TPU v7x, 32 devices: a whole 2x2x4 slice. The times are simulated.
32 devices in a mesh: ctx: 8 (over z, x), head: 4 (over y, core).
Axes of the slice: x: 2, y: 2, z: 4, core: 2. Of those that a mesh axis runs over, the one named last changes fastest.
Arguments:
- queries: bfloat16 [1024, 4096], P('ctx', 'head'), may hold values from -40 to 40
- keys: bfloat16 [1024, 4096], P('ctx', 'head'), may hold values from -40 to 40
- values: bfloat16 [1024, 4096], P('ctx', 'head'), may hold values from -50 to 50
- pattern: int32 [8, 8], replicated, may hold values from -1 to 7, as said below
- upstream: bfloat16 [1024, 4096], P('ctx', 'head'), may hold values from -6 to 6
Outputs:
- normed: bfloat16 [1024, 4096], P('ctx', 'head')
- grad_queries: bfloat16 [1024, 4096], P('ctx', 'head')
- grad_keys: bfloat16 [1024, 4096], P('ctx', 'head')
- grad_values: bfloat16 [1024, 4096], P('ctx', 'head')
Inputs may be any that keep to these rules, and one draw needn't show every extreme that they name: `pattern`: entry [i, k] for k < 7 is either i - 2^k or -1, and always -1 where i < 2^k; entry [i, 7] is i.
All inputs are finite; a program needn't handle non-finite values.
Results may differ from a plain program's by a relative error of at most 0.04.
Values may be sent and summed in bfloat16 or wider, within the bound.
No kernel may reach another device: no remote copies, remote signals or barrier semaphores. Data moves between devices by JAX's collectives and lax.ppermute only.
A program may use at most 64 MiB of HBM per device.

v0:
```python
import jax
import jax.numpy as jnp
from jax import lax
from jax.sharding import PartitionSpec as P

HD = 128
BLOCK = 128
LEVELS = 7
WIDTH = 4096


NEG_BIG = -1e30
EPSILON = 1e-06


def shifted(block, axis, distance):
    devices = range(lax.axis_size(axis))
    route = [(i - distance, i) for i in devices if i - distance in devices]
    return lax.ppermute(block, axis, route)


def for_sending(x):
    return jax.tree.map(lambda a: a.astype(jnp.bfloat16) if a.dtype == jnp.float32 else a, x)


def route_table(blocks, levels):
    routing = []
    for query_block in range(blocks):
        for level_index in range(levels + 1):
            if level_index == levels:
                routing.append((0, query_block))
            else:
                distance = 2**level_index
                routing.append(
                    (-((query_block - distance) // blocks), (query_block - distance) % blocks)
                )
    return routing


def pair_grads(
    query_tiles, grad_tiles, lse_tiles, delta_tiles, key_tiles, value_tiles, keep_mask, score_scale
):
    scores = (
        jnp.einsum("pqhd,pkhd->phqk", query_tiles, key_tiles, preferred_element_type=jnp.float32)
        * score_scale
    )
    scores = jnp.where(keep_mask[:, None], scores, NEG_BIG)
    weights = jnp.exp(scores - lse_tiles[..., None])
    prob_tiles = weights.astype(jnp.bfloat16)
    grad_probs = jnp.einsum(
        "pqhd,pkhd->phqk", grad_tiles, value_tiles, preferred_element_type=jnp.float32
    )
    dscore = (weights * (grad_probs - delta_tiles[..., None]) * score_scale).astype(jnp.bfloat16)
    return (dscore, prob_tiles)


def key_grads(dscore, prob_tiles, query_tiles, grad_tiles):
    key_part = jnp.einsum(
        "phqk,pqhd->pkhd", dscore, query_tiles, preferred_element_type=jnp.float32
    )
    value_part = jnp.einsum(
        "phqk,pqhd->pkhd", prob_tiles, grad_tiles, preferred_element_type=jnp.float32
    )
    return jnp.stack((key_part, value_part))


def collect(partials, targets, blocks):
    pieces = []
    for key_index in range(blocks):
        summed = jnp.zeros((2,) + partials.shape[2:], jnp.float32)
        for row_index, target in enumerate(targets):
            if target == key_index:
                summed = summed + partials[:, row_index]
        pieces.append(summed)
    return jnp.stack(pieces, axis=1)


def shards(queries, keys, values, pattern, upstream):
    tokens_here = queries.shape[0]
    heads_here = queries.shape[1] // HD
    blocks = tokens_here // BLOCK
    slot_count = LEVELS + 1
    pair_count = blocks * slot_count
    score_scale = HD ** (-0.5)
    ctx_count = lax.axis_size("ctx")
    device_index = lax.axis_index("ctx")
    routing = route_table(blocks, LEVELS)
    offsets = sorted(
        set((route_entry[0] for route_entry in routing if 0 < route_entry[0] < ctx_count))
    )
    tile_shape = (blocks, BLOCK, heads_here, HD)
    query_blocks = queries.reshape(tile_shape)
    own_pairs = jnp.stack((keys, values)).reshape((2,) + tile_shape)
    sources = {0: own_pairs}
    for offset in offsets:
        fetched = shifted(jnp.stack((keys, values)), "ctx", offset)
        sources[offset] = fetched.reshape((2,) + tile_shape)
    empty_tile = jnp.zeros((2, BLOCK, heads_here, HD), jnp.bfloat16)
    gathered = []
    for source, key_index in routing:
        if source in sources:
            gathered.append(sources[source][:, key_index])
        else:
            gathered.append(empty_tile)
    pair_kv = jnp.stack(gathered, axis=1)
    key_tiles = pair_kv[0]
    value_tiles = pair_kv[1]
    key_stack = key_tiles.reshape((blocks, slot_count) + tile_shape[1:])
    value_stack = value_tiles.reshape((blocks, slot_count) + tile_shape[1:])
    own_rows = lax.dynamic_slice_in_dim(pattern, device_index * blocks, blocks, 0)
    positions = jnp.arange(BLOCK)
    causal = positions[None, :] <= positions[:, None]
    self_slot = jnp.arange(slot_count) == LEVELS
    tile_keep = (own_rows >= 0)[:, :, None, None] & (
        jnp.logical_not(self_slot)[None, :, None, None] | causal[None, None]
    )
    scores = (
        jnp.einsum("bqhd,bskhd->bhqsk", query_blocks, key_stack, preferred_element_type=jnp.float32)
        * score_scale
    )
    scores = jnp.where(jnp.transpose(tile_keep, (0, 2, 1, 3))[:, None], scores, NEG_BIG)
    highest = jnp.max(scores, axis=(3, 4))
    log_total = highest + jnp.log(jnp.sum(jnp.exp(scores - highest[..., None, None]), axis=(3, 4)))
    prob_stack = jnp.exp(scores - log_total[..., None, None]).astype(jnp.bfloat16)
    attention = jnp.einsum(
        "bhqsk,bskhd->bqhd", prob_stack, value_stack, preferred_element_type=jnp.float32
    ).astype(jnp.bfloat16)
    attn_wide = attention.reshape(tokens_here, heads_here * HD).astype(jnp.float32)
    square_sum = lax.psum(jnp.sum(attn_wide * attn_wide, axis=1), "head")
    inverse = lax.rsqrt(square_sum / WIDTH + EPSILON)
    normed = (attn_wide * inverse[:, None]).astype(jnp.bfloat16)
    upstream_wide = upstream.astype(jnp.float32)
    cross_term = lax.psum(jnp.sum(upstream_wide * attn_wide, axis=1), "head")
    grad_attn = (
        inverse[:, None] * upstream_wide - attn_wide * (inverse**3 * cross_term / WIDTH)[:, None]
    ).astype(jnp.bfloat16)
    row_delta = jnp.sum(
        (grad_attn.astype(jnp.float32) * attn_wide).reshape(tokens_here, heads_here, HD), axis=2
    )
    row_delta = jnp.transpose(row_delta.reshape(blocks, BLOCK, heads_here), (0, 2, 1))

    def spread(array):
        return jnp.broadcast_to(array[:, None], (blocks, slot_count) + array.shape[1:]).reshape(
            (pair_count,) + array.shape[1:]
        )

    grad_blocks = grad_attn.reshape(tile_shape)
    query_pairs = spread(query_blocks)
    grad_pairs = spread(grad_blocks)
    keep_pairs = tile_keep.reshape(pair_count, BLOCK, BLOCK)
    dscore, prob_pairs = pair_grads(
        query_pairs,
        grad_pairs,
        spread(log_total),
        spread(row_delta),
        key_tiles,
        value_tiles,
        keep_pairs,
        score_scale,
    )
    grad_query = jnp.einsum(
        "phqk,pkhd->pqhd", dscore, key_tiles, preferred_element_type=jnp.float32
    )
    grad_query = jnp.sum(grad_query.reshape((blocks, slot_count) + tile_shape[1:]), axis=1)
    grad_queries = grad_query.astype(jnp.bfloat16).reshape(tokens_here, heads_here * HD)
    local_rows = [row_index for row_index in range(pair_count) if routing[row_index][0] == 0]
    chosen = jnp.array(local_rows, jnp.int32)
    local_terms = key_grads(
        dscore[chosen], prob_pairs[chosen], query_pairs[chosen], grad_pairs[chosen]
    )
    key_sum = collect(local_terms, [routing[row_index][1] for row_index in local_rows], blocks)
    for offset in offsets:
        remote_rows = [
            row_index for row_index in range(pair_count) if routing[row_index][0] == offset
        ]
        chosen = jnp.array(remote_rows, jnp.int32)
        remote_terms = key_grads(
            dscore[chosen], prob_pairs[chosen], query_pairs[chosen], grad_pairs[chosen]
        )
        outgoing = collect(
            remote_terms, [routing[row_index][1] for row_index in remote_rows], blocks
        )
        key_sum = key_sum + shifted(for_sending(outgoing), "ctx", -offset).astype(outgoing.dtype)
    grad_keys = key_sum[0].astype(jnp.bfloat16).reshape(tokens_here, heads_here * HD)
    grad_values = key_sum[1].astype(jnp.bfloat16).reshape(tokens_here, heads_here * HD)
    return (normed, grad_queries, grad_keys, grad_values)


def solution(mesh):
    return jax.shard_map(
        shards,
        mesh=mesh,
        in_specs=(P("ctx", "head"), P("ctx", "head"), P("ctx", "head"), P(), P("ctx", "head")),
        out_specs=(P("ctx", "head"), P("ctx", "head"), P("ctx", "head"), P("ctx", "head")),
        check_vma=False,
    )
```

profile of v0, /device:TPU:0, one launch (start us, length us, event | category | flops | bytes accessed | tf_op | source)
XLA Modules:
  0.0 132.0 jit_solution(9039660541150314955)
XLA Ops:
  0.6 1.2 copy.88
  1.8 1.1 copy.89
  3.0 6.0 %collective-permute-start.2 = (bf16[2,128,1024]{1,2,0:T(8,128)(2,1)S(1)}, bf16[2,128,1024]{1,2,0:T(8,128)(2,1)S(1)}, u32[]{:S(2)}, u32[]{:S(2)}) collective-permute-start(bf16[2,128,1024]{1,2,0:T(8,128)(2,1)S(1)} %pad_maximum_fusion), channel_id=1, source_target_pairs={{0,16},{4,20},{8,24},{12,28},{1,17},{5,21},{9,25},{13,29},{2,18},{... | collective-permute-start | bytes 1572872 | tf_op jit(solution)/shard_map/ppermute | solution.py:19
  9.0 3.5 %collective-permute-start.1 = (bf16[2,128,1024]{1,2,0:T(8,128)(2,1)S(1)}, bf16[2,128,1024]{1,2,0:T(8,128)(2,1)S(1)}, u32[]{:S(2)}, u32[]{:S(2)}) collective-permute-start(bf16[2,128,1024]{1,2,0:T(8,128)(2,1)S(1)} %pad_maximum_fusion), channel_id=1, source_target_pairs={{0,8},{4,12},{8,16},{12,20},{16,24},{20,28},{1,9},{5,13},{9,17},{1... | collective-permute-start | bytes 1572872 | tf_op jit(solution)/shard_map/ppermute | solution.py:19
  12.5 3.4 %collective-permute-start = (bf16[2,128,1024]{1,2,0:T(8,128)(2,1)S(1)}, bf16[2,128,1024]{1,2,0:T(8,128)(2,1)S(1)}, u32[]{:S(2)}, u32[]{:S(2)}) collective-permute-start(bf16[2,128,1024]{1,2,0:T(8,128)(2,1)S(1)} %pad_maximum_fusion), channel_id=1, source_target_pairs={{0,4},{4,8},{8,12},{12,16},{16,20},{20,24},{24,28},{1,5},{5,9},{9,... | collective-permute-start | bytes 1572872 | tf_op jit(solution)/shard_map/ppermute | solution.py:19
  18.6 1.5 %or_and_fusion = pred[8,128,128]{2,1,0:T(8,128)(4,1)} fusion(pred[8]{0:T(512)(128)(4,1)} %copy-done.10, pred[128,128]{1,0:T(8,128)(4,1)S(1)} %copy.101, pred[8]{0:T(512)(128)(4,1)} %copy-done.9), kind=kLoop, calls=%fused_computation.60 | loop fusion | flops 262144 | bytes 147472 | tf_op jit(solution)/shard_map/and | solution.py:114
  22.1 1.3 copy.96
  23.4 8.0 %collective-permute-done.1 = bf16[2,128,1024]{1,2,0:T(8,128)(2,1)S(1)} collective-permute-done((bf16[2,128,1024]{1,2,0:T(8,128)(2,1)S(1)}, bf16[2,128,1024]{1,2,0:T(8,128)(2,1)S(1)}, u32[]{:S(2)}, u32[]{:S(2)}) %collective-permute-start.1) | collective-permute-done | bytes 524320 | tf_op jit(solution)/shard_map/ppermute | solution.py:19
  32.2 1.3 copy.95
  34.8 2.0 %slice_bitcast_fusion.1 = (bf16[8,128,8,128]{3,1,0,2:T(8,128)(2,1)S(1)}, bf16[8,128,8,128]{3,1,0,2:T(8,128)(2,1)}) fusion(bf16[2,8,128,8,128]{4,2,1,3,0:T(8,128)(2,1)S(1)} %maximum_dynamic-update-slice_fusion), kind=kLoop, calls=%fused_computation.11 | loop fusion | bytes 8388608 | tf_op jit(solution)/shard_map/reshape.9
  38.5 2.4 %multiply_reduce_fusion = (f32[128]{0:T(128)S(1)}, f32[8,128,128]{2,1,0:T(8,128)}) fusion(f32[8,8,128,128]{3,2,1,0:T(8,128)S(1)} %get-tuple-element.204, f32[8,128]{1,0:T(8,128)S(1)} %log_add_fusion, pred[128,8,128]{0,2,1:T(8,128)(4,1)S(1)} %and_bitcast_fusion, bf16[2,8,128,8,128]{4,2,1,3,0:T(8,128)(2,1)S(1)} %maximum_dynamic-update-slice_fusion), kind=kOutput, calls=%fused_computation.59 | convolution fusion | flops 273153920 | bytes 6951424 | tf_op jit(solution)/shard_map/bhqsk,bskhd->bqhd/dot_general | solution.py:125
  40.9 1.3 copy.100
  42.3 5.7 %all-reduce = (f32[128]{0:T(128)S(1)}, f32[128]{0:T(128)S(1)}) all-reduce(f32[128]{0:T(128)S(1)} %get-tuple-element.205, f32[128]{0:T(128)S(1)} %fusion.36), channel_id=1, replica_groups=mesh['ctx'=8,'head'=4] {'head'}, use_global_device_ids=true, to_apply=%region_3.4 | all-reduce | flops 256 | bytes 2048 | tf_op jit(solution)/shard_map/psum | solution.py:129
  49.4 3.3 %fusion.3 = (bf16[8,8,128,128]{3,2,1,0:T(8,128)(2,1)S(1)}, f32[8,8,128,128]{2,3,1,0:T(8,128)S(1)}) fusion(f32[8,128]{1,0:T(8,128)S(1)} %log_add_fusion, pred[8,128,128]{2,1,0:T(8,128)(4,1)S(1)} %copy-done.8, bf16[128,8,128]{2,0,1:T(8,128)(2,1)} %copy_bitcast_fusion.1, bf16[8,128,8,128]{3,1,0,2:T(8,128)(2,1)} %get-tuple-element.195), kind=kOutput, calls=%fused_computation.8 | convolution fusion | flops 272629760 | bytes 8785920 | tf_op jit(solution)/shard_map/pqhd,pkhd->phqk/dot_general | solution.py:44
  52.7 2.1 %multiply_convert_fusion = bf16[8,8,128,128]{3,2,1,0:T(8,128)(2,1)S(1)} fusion(f32[8,8,128,128]{2,3,1,0:T(8,128)S(1)} %get-tuple-element.208, bf16[8,128,8,128]{3,1,0,2:T(8,128)(2,1)S(1)} %get-tuple-element.194, f32[8,128]{1,0:T(8,128)S(1)} %copy.111, f32[8,128]{1,0:T(8,128)S(1)} %log_add_fusion, pred[8,128,128]{2,1,0:T(8,128)(4,1)S(1)} %copy-done.8, ...), kind=kOutput, calls=%fused_computation.4 | convolution fusion | flops 275775488 | bytes 8790016 | tf_op jit(solution)/shard_map/pqhd,pkhd->phqk/dot_general | solution.py:50
  56.6 1.4 %collective-permute-start.3 = (bf16[2,1,128,8,128]{2,4,3,1,0:T(8,128)(2,1)S(1)}, bf16[2,1,128,8,128]{2,4,3,1,0:T(8,128)(2,1)S(1)}, u32[]{:S(2)}, u32[]{:S(2)}) collective-permute-start(bf16[2,1,128,8,128]{2,4,3,1,0:T(8,128)(2,1)S(1)} %pad_maximum_fusion.1), channel_id=1, source_target_pairs={{4,0},{8,4},{12,8},{16,12},{20,16},{24,20},{28,24},{5,1},{9,5},{13... | collective-permute-start | bytes 1572872 | tf_op jit(solution)/shard_map/ppermute | solution.py:19
  58.1 1.3 collective-permute-start.4
  59.4 1.3 collective-permute-start.5
  62.4 1.2 convolution_bitcast_fusion
  63.6 1.2 convolution_bitcast_fusion.1
  64.8 16.2 %collective-permute-done.3 = bf16[2,1,128,8,128]{2,4,3,1,0:T(8,128)(2,1)S(1)} collective-permute-done((bf16[2,1,128,8,128]{2,4,3,1,0:T(8,128)(2,1)S(1)}, bf16[2,1,128,8,128]{2,4,3,1,0:T(8,128)(2,1)S(1)}, u32[]{:S(2)}, u32[]{:S(2)}) %collective-permute-start.3) | collective-permute-done | bytes 524320 | tf_op jit(solution)/shard_map/ppermute | solution.py:19
  81.1 13.3 %collective-permute-done.4 = bf16[2,1,128,8,128]{2,4,3,1,0:T(8,128)(2,1)S(1)} collective-permute-done((bf16[2,1,128,8,128]{2,4,3,1,0:T(8,128)(2,1)S(1)}, bf16[2,1,128,8,128]{2,4,3,1,0:T(8,128)(2,1)S(1)}, u32[]{:S(2)}, u32[]{:S(2)}) %collective-permute-start.4) | collective-permute-done | bytes 524320 | tf_op jit(solution)/shard_map/ppermute | solution.py:19
  94.4 34.5 %collective-permute-done.5 = bf16[2,1,128,8,128]{2,4,3,1,0:T(8,128)(2,1)} collective-permute-done((bf16[2,1,128,8,128]{2,4,3,1,0:T(8,128)(2,1)S(1)}, bf16[2,1,128,8,128]{2,4,3,1,0:T(8,128)(2,1)}, u32[]{:S(2)}, u32[]{:S(2)}) %collective-permute-start.5) | collective-permute-done | bytes 524320 | tf_op jit(solution)/shard_map/ppermute | solution.py:19
  128.9 1.3 %fusion.31 = bf16[2,1,128,8,128]{2,4,3,1,0:T(8,128)(2,1)S(1)} fusion(f32[1,1,128,8,128]{2,4,3,1,0:T(8,128)S(1)} %convolution_bitcast_fusion.1, f32[1,1,128,8,128]{2,4,3,1,0:T(8,128)S(1)} %convolution_bitcast_fusion, bf16[2,1,128,8,128]{2,4,3,1,0:T(8,128)(2,1)} %collective-permute-done.5, bf16[2,1,128,8,128]{2,4,3,1,0:T(8,128)(2,1)S(1)} %collective-permute-done.4, ...), kind=kLoop, calls=%fused_computation.43 | loop fusion | flops 2097152 | bytes 3145728 | tf_op jit(solution)/shard_map/convert.4
  (64 shorter events, 15.0 us)
Async XLA Ops:
  0.6 19.4 %copy-start = (bf16[128,1024]{1,0:T(8,128)(2,1)S(1)}, bf16[128,1024]{1,0:T(8,128)(2,1)}, u32[]{:S(2)}) copy-start(bf16[128,1024]{1,0:T(8,128)(2,1)} %param.9) | copy-start | bytes 786436
  3.0 18.3 %collective-permute-start.2 = (bf16[2,128,1024]{1,2,0:T(8,128)(2,1)S(1)}, bf16[2,128,1024]{1,2,0:T(8,128)(2,1)S(1)}, u32[]{:S(2)}, u32[]{:S(2)}) collective-permute-start(bf16[2,128,1024]{1,2,0:T(8,128)(2,1)S(1)} %pad_maximum_fusion), channel_id=1, source_target_pairs={{0,16},{4,20},{8,24},{12,28},{1,17},{5,21},{9,25},{13,29},{2,18},{... | collective-permute-start | bytes 1572872 | tf_op jit(solution)/shard_map/ppermute | solution.py:19
  9.0 22.4 %collective-permute-start.1 = (bf16[2,128,1024]{1,2,0:T(8,128)(2,1)S(1)}, bf16[2,128,1024]{1,2,0:T(8,128)(2,1)S(1)}, u32[]{:S(2)}, u32[]{:S(2)}) collective-permute-start(bf16[2,128,1024]{1,2,0:T(8,128)(2,1)S(1)} %pad_maximum_fusion), channel_id=1, source_target_pairs={{0,8},{4,12},{8,16},{12,20},{16,24},{20,28},{1,9},{5,13},{9,17},{1... | collective-permute-start | bytes 1572872 | tf_op jit(solution)/shard_map/ppermute | solution.py:19
  12.5 21.0 %collective-permute-start = (bf16[2,128,1024]{1,2,0:T(8,128)(2,1)S(1)}, bf16[2,128,1024]{1,2,0:T(8,128)(2,1)S(1)}, u32[]{:S(2)}, u32[]{:S(2)}) collective-permute-start(bf16[2,128,1024]{1,2,0:T(8,128)(2,1)S(1)} %pad_maximum_fusion), channel_id=1, source_target_pairs={{0,4},{4,8},{8,12},{12,16},{16,20},{20,24},{24,28},{1,5},{5,9},{9,... | collective-permute-start | bytes 1572872 | tf_op jit(solution)/shard_map/ppermute | solution.py:19
  15.9 1.0 copy-start.9
  16.7 0.5 copy-start.10
  21.3 0.8 copy-start.7
  31.4 0.8 copy-start.6
  34.7 3.7 %copy-start.1 = (bf16[2,8,128,8,128]{4,2,1,3,0:T(8,128)(2,1)}, bf16[2,8,128,8,128]{4,2,1,3,0:T(8,128)(2,1)S(1)}, u32[]{:S(2)}) copy-start(bf16[2,8,128,8,128]{4,2,1,3,0:T(8,128)(2,1)S(1)} %maximum_dynamic-update-slice_fusion) | copy-start | bytes 12582916
  38.5 3.7 %copy-start.3 = (bf16[128,1024]{1,0:T(8,128)(2,1)S(1)}, bf16[128,1024]{1,0:T(8,128)(2,1)}, u32[]{:S(2)}) copy-start(bf16[128,1024]{1,0:T(8,128)(2,1)} %param.13) | copy-start | bytes 786436
  40.9 8.5 %copy-start.8 = (pred[8,128,128]{2,1,0:T(8,128)(4,1)S(1)}, pred[8,128,128]{2,1,0:T(8,128)(4,1)}, u32[]{:S(2)}) copy-start(pred[8,128,128]{2,1,0:T(8,128)(4,1)} %or_and_fusion) | copy-start | bytes 393220
  52.7 3.5 %copy-start.4 = (bf16[8,8,128,128]{3,2,1,0:T(8,128)(2,1)}, bf16[8,8,128,128]{3,2,1,0:T(8,128)(2,1)S(1)}, u32[]{:S(2)}) copy-start(bf16[8,8,128,128]{3,2,1,0:T(8,128)(2,1)S(1)} %get-tuple-element.207) | copy-start | bytes 6291460
  54.8 6.7 %copy-start.5 = (bf16[8,8,128,128]{3,2,1,0:T(8,128)(2,1)}, bf16[8,8,128,128]{3,2,1,0:T(8,128)(2,1)S(1)}, u32[]{:S(2)}) copy-start(bf16[8,8,128,128]{3,2,1,0:T(8,128)(2,1)S(1)} %multiply_convert_fusion) | copy-start | bytes 6291460
  54.8 5.9 %copy-start.2 = (bf16[2,8,128,8,128]{4,2,1,3,0:T(8,128)(2,1)S(1)}, bf16[2,8,128,8,128]{4,2,1,3,0:T(8,128)(2,1)}, u32[]{:S(2)}) copy-start(bf16[2,8,128,8,128]{4,2,1,3,0:T(8,128)(2,1)} %copy-done.1) | copy-start | bytes 12582916
  56.6 24.5 %collective-permute-start.3 = (bf16[2,1,128,8,128]{2,4,3,1,0:T(8,128)(2,1)S(1)}, bf16[2,1,128,8,128]{2,4,3,1,0:T(8,128)(2,1)S(1)}, u32[]{:S(2)}, u32[]{:S(2)}) collective-permute-start(bf16[2,1,128,8,128]{2,4,3,1,0:T(8,128)(2,1)S(1)} %pad_maximum_fusion.1), channel_id=1, source_target_pairs={{4,0},{8,4},{12,8},{16,12},{20,16},{24,20},{28,24},{5,1},{9,5},{13... | collective-permute-start | bytes 1572872 | tf_op jit(solution)/shard_map/ppermute | solution.py:19
  58.1 36.3 %collective-permute-start.4 = (bf16[2,1,128,8,128]{2,4,3,1,0:T(8,128)(2,1)S(1)}, bf16[2,1,128,8,128]{2,4,3,1,0:T(8,128)(2,1)S(1)}, u32[]{:S(2)}, u32[]{:S(2)}) collective-permute-start(bf16[2,1,128,8,128]{2,4,3,1,0:T(8,128)(2,1)S(1)} %pad_maximum_fusion.2), channel_id=1, source_target_pairs={{8,0},{12,4},{16,8},{20,12},{24,16},{28,20},{9,1},{13,5},{17,9},{2... | collective-permute-start | bytes 1572872 | tf_op jit(solution)/shard_map/ppermute | solution.py:19
  59.4 69.5 %collective-permute-start.5 = (bf16[2,1,128,8,128]{2,4,3,1,0:T(8,128)(2,1)S(1)}, bf16[2,1,128,8,128]{2,4,3,1,0:T(8,128)(2,1)}, u32[]{:S(2)}, u32[]{:S(2)}) collective-permute-start(bf16[2,1,128,8,128]{2,4,3,1,0:T(8,128)(2,1)S(1)} %pad_maximum_fusion.3), channel_id=1, source_target_pairs={{16,0},{20,4},{24,8},{28,12},{17,1},{21,5},{25,9},{29,13},{18,2},{... | collective-permute-start | bytes 1572872 | tf_op jit(solution)/shard_map/ppermute | solution.py:19
where the time goes:
time: 133 us; the launch traced here: 132 us
  waiting for transfers between devices  72.6 us (55%)
  starting transfers between devices  16.9 us (13%)
  local copies, waits for them, and re-layouts  16.2 us (12%)
  matrix products  13.4 us (10%)
  other arithmetic  6.09 us (5%)
  blocking collectives  5.73 us (4%)
    ppermute x6, waiting for transfers between devices, shifted(): return lax.ppermute(block, axis, route)  72.6 us
    ppermute x6, starting transfers between devices, shifted(): return lax.ppermute(block, axis, route)  16.9 us
    unnamed x33, local copies, waits for them, and re-layouts  8.6 us
    psum x1, blocking collectives, shards(): square_sum = lax.psum(jnp.sum(attn_wide * attn_wide, axis=1), 'head')  5.73 us
    dot_general x1, matrix products, pair_grads(): jnp.einsum('pqhd,pkhd->phqk', query_tiles, key_tiles, preferred_element_t...  3.27 us
    another operation x3, local copies, waits for them, and re-layouts, shards(): pair_kv = jnp.stack(gathered, axis=1)  2.9 us
    another operation x2, local copies, waits for them, and re-layouts  2.75 us
  transfers between devices with their start and end apart: 6, of which 5 were waited for; matrix products, arithmetic and copies ran while one was open for 9% of the time, Pallas kernels for 0%

commit v1 on v0

--- a/solution.py
+++ b/solution.py
@@ -1,6 +1,10 @@
+import functools
+
 import jax
 import jax.numpy as jnp
 from jax import lax
+from jax.experimental import pallas as pl
+from jax.experimental.pallas import tpu as pltpu
 from jax.sharding import PartitionSpec as P
 
 HD = 128
@@ -75,7 +79,7 @@
     return jnp.stack(pieces, axis=1)
 
 
-def shards(queries, keys, values, pattern, upstream):
+def generic_shards(queries, keys, values, pattern, upstream):
     tokens_here = queries.shape[0]
     heads_here = queries.shape[1] // HD
     blocks = tokens_here // BLOCK
@@ -186,6 +190,346 @@
     return (normed, grad_queries, grad_keys, grad_values)
 
 
+NT = (((1,), (1,)), ((), ()))
+NN = (((1,), (0,)), ((), ()))
+TN = (((0,), (0,)), ((), ()))
+SCALE = HD ** (-0.5)
+PACK = 128
+
+
+def mm(a, b, dims):
+    return lax.dot_general(a, b, dims, preferred_element_type=jnp.float32)
+
+
+def lane_ids(shape):
+    return lax.broadcasted_iota(jnp.int32, shape, len(shape) - 1)
+
+
+def causal_mask():
+    rows = lax.broadcasted_iota(jnp.int32, (BLOCK, BLOCK), 0)
+    return lane_ids((BLOCK, BLOCK)) <= rows
+
+
+def pack_columns(columns):
+    count = len(columns)
+    lanes = lane_ids((BLOCK, PACK))
+    wide = jnp.zeros((BLOCK, PACK), jnp.float32)
+    for index, column in enumerate(columns):
+        wide = jnp.where(lanes % count == index, column, wide)
+    first = wide.astype(jnp.bfloat16)
+    left = wide - first.astype(jnp.float32)
+    second = left.astype(jnp.bfloat16)
+    third = (left - second.astype(jnp.float32)).astype(jnp.bfloat16)
+    return jnp.where(lanes < count, first, jnp.where(lanes < 2 * count, second, third))
+
+
+def unpack_column(tile, count, index):
+    wide = tile.astype(jnp.float32)
+    return (
+        wide[:, index : index + 1]
+        + wide[:, count + index : count + index + 1]
+        + wide[:, 2 * count + index : 2 * count + index + 1]
+    )
+
+
+def pair_flags(me_ref, pattern_ref):
+    me = me_ref[0]
+    blocks = pattern_ref.shape[0]
+    odd = lax.rem(me, 2)
+    ahead = jnp.minimum(me + 2, blocks - 1)
+    partner = me + 1 - 2 * odd
+    near = pattern_ref[me, 1] >= 0
+    far = jnp.logical_and(me + 2 < blocks, pattern_ref[ahead, 2] >= 0)
+    side = jnp.logical_and(jnp.logical_or(odd == 0, me >= 2), pattern_ref[partner, 0] >= 0)
+    return odd, near, far, side
+
+
+def softmax_part(score_list, value_list):
+    highest = score_list[0].max(axis=1, keepdims=True)
+    for scores in score_list[1:]:
+        highest = jnp.maximum(highest, scores.max(axis=1, keepdims=True))
+    total, out = 0.0, 0.0
+    for scores, value in zip(score_list, value_list):
+        weights = jnp.exp(scores - highest)
+        total = total + weights.sum(axis=1, keepdims=True)
+        out = out + mm(weights.astype(jnp.bfloat16), value, NN)
+    return out / total, highest + jnp.log(total)
+
+
+def forward_kernel(
+    heads, me_ref, pattern_ref, q_ref, qz_ref, qx_ref, k_ref, v_ref, k2_ref, v2_ref, own_ref, lse_ref, oz_ref, ox_ref
+):
+    odd, near, _, _ = pair_flags(me_ref, pattern_ref)
+    causal = causal_mask()
+    own_lse, z_lse, x_lse = [], [], []
+    for h in range(heads):
+        at = slice(h * HD, (h + 1) * HD)
+        k, v, k2, v2 = k_ref[:, at], v_ref[:, at], k2_ref[:, at], v2_ref[:, at]
+        q = q_ref[:, at]
+        here = jnp.where(causal, mm(q, k, NT) * SCALE, NEG_BIG)
+        back = jnp.where(near, mm(q, k2, NT) * SCALE, NEG_BIG)
+        out, lse = softmax_part([here, back], [v, v2])
+        own_ref[:, at] = out
+        own_lse.append(lse)
+        out, lse = softmax_part([mm(qz_ref[:, at], k2, NT) * SCALE], [v2])
+        oz_ref[:, at] = out.astype(jnp.bfloat16)
+        z_lse.append(lse)
+        ks, vs = jnp.where(odd == 1, k2, k), jnp.where(odd == 1, v2, v)
+        out, lse = softmax_part([mm(qx_ref[:, at], ks, NT) * SCALE], [vs])
+        ox_ref[:, at] = out.astype(jnp.bfloat16)
+        x_lse.append(lse)
+    oz_ref[:, heads * HD :] = pack_columns(z_lse)
+    ox_ref[:, heads * HD :] = pack_columns(x_lse)
+    lse_ref[...] = pack_columns(own_lse)
+
+
+def merge_kernel(heads, me_ref, pattern_ref, own_ref, lse_ref, rz_ref, rx_ref, u_ref, a_ref, sums_ref):
+    me = me_ref[0]
+    far, side = pattern_ref[me, 2] >= 0, pattern_ref[me, 0] >= 0
+    tail = slice(heads * HD, heads * HD + PACK)
+    own_tile, z_tile, x_tile = lse_ref[...], rz_ref[:, tail], rx_ref[:, tail]
+    totals = []
+    squares = jnp.zeros((BLOCK, HD), jnp.float32)
+    crosses = jnp.zeros((BLOCK, HD), jnp.float32)
+    for h in range(heads):
+        at = slice(h * HD, (h + 1) * HD)
+        own_lse = unpack_column(own_tile, heads, h)
+        z_lse = jnp.where(far, unpack_column(z_tile, heads, h), NEG_BIG)
+        x_lse = jnp.where(side, unpack_column(x_tile, heads, h), NEG_BIG)
+        highest = jnp.maximum(own_lse, jnp.maximum(z_lse, x_lse))
+        total = highest + jnp.log(
+            jnp.exp(own_lse - highest) + jnp.exp(z_lse - highest) + jnp.exp(x_lse - highest)
+        )
+        totals.append(total)
+        out = (
+            own_ref[:, at] * jnp.exp(own_lse - total)
+            + rz_ref[:, at].astype(jnp.float32) * jnp.exp(z_lse - total)
+            + rx_ref[:, at].astype(jnp.float32) * jnp.exp(x_lse - total)
+        ).astype(jnp.bfloat16)
+        a_ref[:, at] = out
+        wide = out.astype(jnp.float32)
+        squares += wide * wide
+        crosses += wide * u_ref[:, at].astype(jnp.float32)
+    a_ref[:, tail] = pack_columns(totals)
+    sums_ref[...] = jnp.concatenate(
+        [
+            jnp.sum(squares.T, axis=0, keepdims=True),
+            jnp.sum(crosses.T, axis=0, keepdims=True),
+            jnp.zeros((6, BLOCK), jnp.float32),
+        ],
+        axis=0,
+    )
+
+
+def norm_columns(sums):
+    inverse = lax.rsqrt(sums[0:1] / WIDTH + EPSILON)
+    factor = inverse**3 * sums[1:2] / WIDTH
+    return (
+        jnp.broadcast_to(inverse, (BLOCK, BLOCK)).T,
+        jnp.broadcast_to(factor, (BLOCK, BLOCK)).T,
+    )
+
+
+def upstream_part(inverse, factor, u, a):
+    wide = a.astype(jnp.float32)
+    grad = (inverse * u.astype(jnp.float32) - wide * factor).astype(jnp.bfloat16)
+    delta = jnp.sum(grad.astype(jnp.float32) * wide, axis=1, keepdims=True)
+    return grad, delta
+
+
+def pair_back(q, k, v, grad, delta, lse, keep):
+    scores = jnp.where(keep, mm(q, k, NT) * SCALE, NEG_BIG)
+    weights = jnp.exp(scores - lse)
+    dscore = (weights * (mm(grad, v, NT) - delta) * SCALE).astype(jnp.bfloat16)
+    return weights.astype(jnp.bfloat16), dscore
+
+
+def far_kernel(
+    heads,
+    me_ref,
+    pattern_ref,
+    sums_ref,
+    sz_ref,
+    sx_ref,
+    q_ref,
+    qz_ref,
+    qx_ref,
+    a_ref,
+    az_ref,
+    ax_ref,
+    u_ref,
+    uz_ref,
+    ux_ref,
+    k_ref,
+    v_ref,
+    k2_ref,
+    v2_ref,
+    dkv_ref,
+    dqz_ref,
+    dqx_ref,
+    dq_ref,
+    dside_ref,
+):
+    odd, near, far, side = pair_flags(me_ref, pattern_ref)
+    tail = slice(heads * HD, heads * HD + PACK)
+    own_norm, z_norm, x_norm = norm_columns(sums_ref), norm_columns(sz_ref), norm_columns(sx_ref)
+    own_tile, z_tile, x_tile = a_ref[:, tail], az_ref[:, tail], ax_ref[:, tail]
+    share = (odd == 1).astype(jnp.float32)
+    for h in range(heads):
+        at = slice(h * HD, (h + 1) * HD)
+        k, v, k2, v2 = k_ref[:, at], v_ref[:, at], k2_ref[:, at], v2_ref[:, at]
+        q, qz, qx = q_ref[:, at], qz_ref[:, at], qx_ref[:, at]
+        grad, delta = upstream_part(*own_norm, u_ref[:, at], a_ref[:, at])
+        gradz, deltaz = upstream_part(*z_norm, uz_ref[:, at], az_ref[:, at])
+        gradx, deltax = upstream_part(*x_norm, ux_ref[:, at], ax_ref[:, at])
+        probs, dscore = pair_back(q, k2, v2, grad, delta, unpack_column(own_tile, heads, h), near)
+        dk2 = mm(dscore, q, TN)
+        dv2 = mm(probs, grad, TN)
+        dq_ref[:, at] = mm(dscore, k2, NN)
+        probs, dscore = pair_back(qz, k2, v2, gradz, deltaz, unpack_column(z_tile, heads, h), far)
+        dk2 += mm(dscore, qz, TN)
+        dv2 += mm(probs, gradz, TN)
+        dqz_ref[:, at] = mm(dscore, k2, NN).astype(jnp.bfloat16)
+        ks, vs = jnp.where(odd == 1, k2, k), jnp.where(odd == 1, v2, v)
+        probs, dscore = pair_back(qx, ks, vs, gradx, deltax, unpack_column(x_tile, heads, h), side)
+        dks = mm(dscore, qx, TN)
+        dvs = mm(probs, gradx, TN)
+        dqx_ref[:, at] = mm(dscore, ks, NN).astype(jnp.bfloat16)
+        dkv_ref[0, :, at] = (dk2 + share * dks).astype(jnp.bfloat16)
+        dkv_ref[1, :, at] = (dv2 + share * dvs).astype(jnp.bfloat16)
+        dside_ref[0, :, at] = (1.0 - share) * dks
+        dside_ref[1, :, at] = (1.0 - share) * dvs
+
+
+def near_kernel(
+    heads,
+    sums_ref,
+    q_ref,
+    a_ref,
+    u_ref,
+    k_ref,
+    v_ref,
+    dq_in_ref,
+    dside_ref,
+    normed_ref,
+    dq_ref,
+    dkv_ref,
+):
+    tail = slice(heads * HD, heads * HD + PACK)
+    inverse, factor = norm_columns(sums_ref)
+    tile = a_ref[:, tail]
+    causal = causal_mask()
+    for h in range(heads):
+        at = slice(h * HD, (h + 1) * HD)
+        q, k, v, a = q_ref[:, at], k_ref[:, at], v_ref[:, at], a_ref[:, at]
+        normed_ref[:, at] = (a.astype(jnp.float32) * inverse).astype(jnp.bfloat16)
+        grad, delta = upstream_part(inverse, factor, u_ref[:, at], a)
+        probs, dscore = pair_back(q, k, v, grad, delta, unpack_column(tile, heads, h), causal)
+        dq_ref[:, at] = dq_in_ref[:, at] + mm(dscore, k, NN)
+        dkv_ref[0, :, at] = dside_ref[0, :, at] + mm(dscore, q, TN)
+        dkv_ref[1, :, at] = dside_ref[1, :, at] + mm(probs, grad, TN)
+
+
+def call(kernel, heads, scalars, arrays, outs, flops):
+    smem = pl.BlockSpec(memory_space=pltpu.SMEM)
+    vmem = pl.BlockSpec(memory_space=pltpu.VMEM)
+    moved = sum(a.size * a.dtype.itemsize for a in arrays) + sum(o.size * o.dtype.itemsize for o in outs)
+    return pl.pallas_call(
+        functools.partial(kernel, heads),
+        out_shape=outs,
+        in_specs=[smem] * len(scalars) + [vmem] * len(arrays),
+        out_specs=[vmem] * len(outs),
+        compiler_params=pltpu.CompilerParams(vmem_limit_bytes=24 * 2**20),
+        cost_estimate=pl.CostEstimate(flops=flops, bytes_accessed=moved, transcendentals=0),
+    )(*scalars, *arrays)
+
+
+def meeting_shards(queries, keys, values, pattern, upstream):
+    tokens, width = queries.shape
+    heads = width // HD
+    count = lax.axis_size("ctx")
+    me = lax.axis_index("ctx").astype(jnp.int32).reshape(1)
+    partners = [(i, i ^ 1) for i in range(count)]
+    unit = heads * 2 * BLOCK**3
+
+    def swap(array):
+        return lax.ppermute(array, "ctx", partners)
+
+    def up(array):
+        return shifted(array, "ctx", 2)
+
+    def down(array):
+        return shifted(array, "ctx", -2)
+
+    def struct(*shape, dtype=jnp.bfloat16):
+        return jax.ShapeDtypeStruct(shape, dtype)
+
+    keys2, values2 = up(keys), up(values)
+    queries_z, queries_x = down(queries), swap(queries)
+    upstream_z, upstream_x = down(upstream), swap(upstream)
+    packed = struct(tokens, width + PACK)
+    own, own_lse, out_z, out_x = call(
+        forward_kernel,
+        heads,
+        (me, pattern),
+        (queries, queries_z, queries_x, keys, values, keys2, values2),
+        (struct(tokens, width, dtype=jnp.float32), struct(tokens, PACK), packed, packed),
+        8 * unit,
+    )
+    back_z, back_x = up(out_z), swap(out_x)
+    attention, sums = call(
+        merge_kernel,
+        heads,
+        (me, pattern),
+        (own, own_lse, back_z, back_x, upstream),
+        (packed, struct(8, BLOCK, dtype=jnp.float32)),
+        unit // 64,
+    )
+    attention_z, attention_x = down(attention), swap(attention)
+    sums = lax.psum(sums, "head")
+    sums_z, sums_x = down(sums), swap(sums)
+    grads2, dq_z, dq_x, dq_own, dside = call(
+        far_kernel,
+        heads,
+        (me, pattern),
+        (sums, sums_z, sums_x, queries, queries_z, queries_x, attention, attention_z, attention_x)
+        + (upstream, upstream_z, upstream_x, keys, values, keys2, values2),
+        (
+            struct(2, tokens, width),
+            struct(tokens, width),
+            struct(tokens, width),
+            struct(tokens, width, dtype=jnp.float32),
+            struct(2, tokens, width, dtype=jnp.float32),
+        ),
+        15 * unit,
+    )
+    grads_back = down(grads2)
+    dq_back_z, dq_back_x = up(dq_z), swap(dq_x)
+    normed, dq_own, grads_own = call(
+        near_kernel,
+        heads,
+        (),
+        (sums, queries, attention, upstream, keys, values, dq_own, dside),
+        (
+            struct(tokens, width),
+            struct(tokens, width, dtype=jnp.float32),
+            struct(2, tokens, width, dtype=jnp.float32),
+        ),
+        5 * unit,
+    )
+    grad_queries = (
+        dq_own + dq_back_z.astype(jnp.float32) + dq_back_x.astype(jnp.float32)
+    ).astype(jnp.bfloat16)
+    grads = (grads_own + grads_back.astype(jnp.float32)).astype(jnp.bfloat16)
+    return (normed, grad_queries, grads[0], grads[1])
+
+
+def shards(queries, keys, values, pattern, upstream):
+    if lax.axis_size("ctx") == 8 and queries.shape[0] == BLOCK:
+        return meeting_shards(queries, keys, values, pattern, upstream)
+    return generic_shards(queries, keys, values, pattern, upstream)
+
+
 def solution(mesh):
     return jax.shard_map(
         shards,

time: 133 us -> 77.9 us (0.59)
  waiting for transfers between devices: 72.6 us -> 23.6 us
  matrix products: 13.4 us -> 0 us
  Pallas kernels: 0 us -> 13.1 us
  local copies, waits for them, and re-layouts: 16.2 us -> 3.69 us
  starting transfers between devices: 16.9 us -> 29.4 us
  other arithmetic: 6.09 us -> 0.96 us
    ppermute x6 -> x9, waiting for transfers between devices: 72.6 us -> 18.7 us  [shifted(): return lax.ppermute(block, axis, route)]
    dot_general x13 -> x0, matrix products: 13.4 us -> none  [the longest x1 3.27 us: pair_grads(): jnp.einsum('pqhd,pkhd->phqk', query_tiles, key_tiles, preferred_element_t...]
    pallas_call x0 -> x4, Pallas kernels: none -> 13.1 us  [call(): pl.pallas_call(functools.partial(kernel, heads), out_shape=outs, in_specs...]
    ppermute x0 -> x6, starting transfers between devices: none -> 6.46 us  [swap(): return lax.ppermute(array, 'ctx', partners)]
    another operation x7 -> x0, local copies, waits for them, and re-layouts: 6.02 us -> none  [the longest x3 2.9 us: shards(): pair_kv = jnp.stack(gathered, axis=1)]
    ppermute x6 -> x9, starting transfers between devices: 16.9 us -> 22.9 us  [shifted(): return lax.ppermute(block, axis, route)]
    unnamed x33 -> x16, local copies, waits for them, and re-layouts: 8.6 us -> 2.87 us
    ppermute x0 -> x6, waiting for transfers between devices: none -> 4.93 us  [swap(): return lax.ppermute(array, 'ctx', partners)]
  transfers between devices with their start and end apart: 6 -> 15, of which waited for: 5 -> 11; matrix products, arithmetic and copies ran while one was open for 9% -> 1% of each run, Pallas kernels for 0% -> 3%
where the time goes in v1:
time: 77.9 us; the launch traced here: 77.4 us
  starting transfers between devices  29.4 us (38%)
  waiting for transfers between devices  23.6 us (30%)
  Pallas kernels  13.1 us (17%)
  blocking collectives  5.97 us (8%)
  local copies, waits for them, and re-layouts  3.69 us (5%)
  other arithmetic  0.96 us (1%)
  between operations  0.78 us (1%)
    ppermute x9, starting transfers between devices, shifted(): return lax.ppermute(block, axis, route)  22.9 us
    ppermute x9, waiting for transfers between devices, shifted(): return lax.ppermute(block, axis, route)  18.7 us
    pallas_call x4, Pallas kernels, call(): pl.pallas_call(functools.partial(kernel, heads), out_shape=outs, in_specs...  13.1 us
    ppermute x6, starting transfers between devices, swap(): return lax.ppermute(array, 'ctx', partners)  6.46 us
    psum x1, blocking collectives, meeting_shards(): sums = lax.psum(sums, 'head')  5.97 us
    ppermute x6, waiting for transfers between devices, swap(): return lax.ppermute(array, 'ctx', partners)  4.93 us
    unnamed x16, local copies, waits for them, and re-layouts  2.87 us
  transfers between devices with their start and end apart: 15, of which 11 were waited for; matrix products, arithmetic and copies ran while one was open for 1% of the time, Pallas kernels for 3%

profile of v1, /device:TPU:0, one launch (start us, length us, event | category | flops | bytes accessed | tf_op | source)
XLA Modules:
  0.0 77.4 jit_solution(10594581860374286283)
XLA Ops:
  0.6 4.9 %collective-permute-start.2 = (bf16[128,1024]{1,0:T(8,128)(2,1)}, bf16[128,1024]{1,0:T(8,128)(2,1)S(1)}, u32[]{:S(2)}, u32[]{:S(2)}) collective-permute-start(bf16[128,1024]{1,0:T(8,128)(2,1)} %k_ref.5), channel_id=1, source_target_pairs={{0,8},{4,12},{8,16},{12,20},{16,24},{20,28},{1,9},{5,13},{9,17},{1... | collective-permute-start | bytes 786440 | tf_op jit(solution)/shard_map/ppermute | solution.py:23
  5.6 3.5 %collective-permute-start.3 = (bf16[128,1024]{1,0:T(8,128)(2,1)}, bf16[128,1024]{1,0:T(8,128)(2,1)S(1)}, u32[]{:S(2)}, u32[]{:S(2)}) collective-permute-start(bf16[128,1024]{1,0:T(8,128)(2,1)} %v_ref.5), channel_id=1, source_target_pairs={{0,8},{4,12},{8,16},{12,20},{16,24},{20,28},{1,9},{5,13},{9,17},{1... | collective-permute-start | bytes 786440 | tf_op jit(solution)/shard_map/ppermute | solution.py:23
  9.1 1.6 %collective-permute-start.1 = (bf16[128,1024]{1,0:T(8,128)(2,1)}, bf16[128,1024]{1,0:T(8,128)(2,1)S(1)}, u32[]{:S(2)}, u32[]{:S(2)}) collective-permute-start(bf16[128,1024]{1,0:T(8,128)(2,1)} %q_ref.5), channel_id=1, source_target_pairs={{0,4},{4,0},{8,12},{12,8},{16,20},{20,16},{24,28},{28,24},{1,5},{5... | collective-permute-start | bytes 786440 | tf_op jit(solution)/shard_map/ppermute | solution.py:456
  10.6 1.3 %collective-permute-start = (bf16[128,1024]{1,0:T(8,128)(2,1)}, bf16[128,1024]{1,0:T(8,128)(2,1)S(1)}, u32[]{:S(2)}, u32[]{:S(2)}) collective-permute-start(bf16[128,1024]{1,0:T(8,128)(2,1)} %q_ref.5), channel_id=1, source_target_pairs={{8,0},{12,4},{16,8},{20,12},{24,16},{28,20},{9,1},{13,5},{17,9},{2... | collective-permute-start | bytes 786440 | tf_op jit(solution)/shard_map/ppermute | solution.py:23
  12.6 4.5 %collective-permute-done.3.v2_ref = bf16[128,1024]{1,0:T(8,128)(2,1)S(1)} collective-permute-done((bf16[128,1024]{1,0:T(8,128)(2,1)}, bf16[128,1024]{1,0:T(8,128)(2,1)S(1)}, u32[]{:S(2)}, u32[]{:S(2)}) %collective-permute-start.3) | collective-permute-done | bytes 262176 | tf_op jit(solution)/shard_map/ppermute | solution.py:23
  17.1 2.9 %collective-permute-done.qz_ref = bf16[128,1024]{1,0:T(8,128)(2,1)S(1)} collective-permute-done((bf16[128,1024]{1,0:T(8,128)(2,1)}, bf16[128,1024]{1,0:T(8,128)(2,1)S(1)}, u32[]{:S(2)}, u32[]{:S(2)}) %collective-permute-start) | collective-permute-done | bytes 262176 | tf_op jit(solution)/shard_map/ppermute | solution.py:23
  22.8 3.2 %shard_map.84 = (f32[128,1024]{1,0:T(8,128)S(1)}, bf16[128,128]{1,0:T(8,128)(2,1)S(1)}, bf16[128,1152]{1,0:T(8,128)(2,1)S(1)}, bf16[128,1152]{1,0:T(8,128)(2,1)S(1)}) custom-call(s32[1]{0:T(128)} %bitcast.me_ref, s32[8,8]{1,0:T(8,128)S(1)} %copy-done.7, bf16[128,1024]{1,0:T(8,128)(2,1)S(1)} %copy-done.1, bf16[128,1024]{1,0:T(8,128)(2,1)S(1)} %collective-permute-done.qz_ref, ...), custom_call_target="tpu_custom_call" | custom-call | flops 268435456 | bytes 2981888 | tf_op jit(solution)/shard_map/pallas_call | solution.py:437
  26.0 3.5 %collective-permute-start.4 = (bf16[128,1152]{1,0:T(8,128)(2,1)S(1)}, bf16[128,1152]{1,0:T(8,128)(2,1)S(1)}, u32[]{:S(2)}, u32[]{:S(2)}) collective-permute-start(bf16[128,1152]{1,0:T(8,128)(2,1)S(1)} %get-tuple-element.20), channel_id=1, source_target_pairs={{0,8},{4,12},{8,16},{12,20},{16,24},{20,28},{1,9},{5,13},{9,17},{1... | collective-permute-start | bytes 884744 | tf_op jit(solution)/shard_map/ppermute | solution.py:23
  30.1 3.9 %collective-permute-done.4.rz_ref = bf16[128,1152]{1,0:T(8,128)(2,1)S(1)} collective-permute-done((bf16[128,1152]{1,0:T(8,128)(2,1)S(1)}, bf16[128,1152]{1,0:T(8,128)(2,1)S(1)}, u32[]{:S(2)}, u32[]{:S(2)}) %collective-permute-start.4) | collective-permute-done | bytes 294944 | tf_op jit(solution)/shard_map/ppermute | solution.py:23
  34.0 2.3 %collective-permute-done.5.rx_ref = bf16[128,1152]{1,0:T(8,128)(2,1)S(1)} collective-permute-done((bf16[128,1152]{1,0:T(8,128)(2,1)S(1)}, bf16[128,1152]{1,0:T(8,128)(2,1)S(1)}, u32[]{:S(2)}, u32[]{:S(2)}) %collective-permute-start.5) | collective-permute-done | bytes 294944 | tf_op jit(solution)/shard_map/ppermute | solution.py:456
  36.3 1.5 %shard_map.85 = (bf16[128,1152]{1,0:T(8,128)(2,1)S(1)}, f32[8,128]{1,0:T(8,128)S(1)}) custom-call(s32[1]{0:T(128)} %bitcast.me_ref, s32[8,8]{1,0:T(8,128)S(1)} %copy-done.7, f32[128,1024]{1,0:T(8,128)S(1)} %get-tuple-element.18.own_ref, bf16[128,128]{1,0:T(8,128)(2,1)S(1)} %get-tuple-element.19.lse_ref, bf16[128,1152]{1,0:T(8,128)(2,1)S(1)} %collective-permute-done.4.rz_ref, ...), custom_call_target="tpu_custom_call" | custom-call | flops 524288 | bytes 1708032 | tf_op jit(solution)/shard_map/pallas_call | solution.py:437
  38.4 1.3 %collective-permute-start.8 = (bf16[128,1152]{1,0:T(8,128)(2,1)S(1)}, bf16[128,1152]{1,0:T(8,128)(2,1)S(1)}, u32[]{:S(2)}, u32[]{:S(2)}) collective-permute-start(bf16[128,1152]{1,0:T(8,128)(2,1)S(1)} %get-tuple-element.23.a_ref), channel_id=1, source_target_pairs={{8,0},{12,4},{16,8},{20,12},{24,16},{28,20},{9,1},{13,5},{17,9},{2... | collective-permute-start | bytes 884744 | tf_op jit(solution)/shard_map/ppermute | solution.py:23
  39.7 1.6 %collective-permute-start.11 = (bf16[128,1024]{1,0:T(8,128)(2,1)S(1)}, bf16[128,1024]{1,0:T(8,128)(2,1)S(1)}, u32[]{:S(2)}, u32[]{:S(2)}) collective-permute-start(bf16[128,1024]{1,0:T(8,128)(2,1)S(1)} %copy-done), channel_id=1, source_target_pairs={{0,4},{4,0},{8,12},{12,8},{16,20},{20,16},{24,28},{28,24},{1,5},{5... | collective-permute-start | bytes 786440 | tf_op jit(solution)/shard_map/ppermute | solution.py:456
  42.6 6.0 %psum.7.sums_ref = f32[8,128]{1,0:T(8,128)S(1)} all-reduce(f32[8,128]{1,0:T(8,128)S(1)} %get-tuple-element.22), channel_id=1, replica_groups=mesh['ctx'=8,'head'=4] {'head'}, use_global_device_ids=true, to_apply=%region_0.0 | all-reduce | flops 1024 | bytes 8192 | tf_op jit(solution)/shard_map/psum | solution.py:489
  49.1 1.3 %collective-permute-start.6 = (f32[8,128]{1,0:T(8,128)S(1)}, f32[8,128]{1,0:T(8,128)S(1)}, u32[]{:S(2)}, u32[]{:S(2)}) collective-permute-start(f32[8,128]{1,0:T(8,128)S(1)} %psum.7.sums_ref), channel_id=1, source_target_pairs={{8,0},{12,4},{16,8},{20,12},{24,16},{28,20},{9,1},{13,5},{17,9},{2... | collective-permute-start | bytes 12296 | tf_op jit(solution)/shard_map/ppermute | solution.py:23
  50.4 1.5 %collective-permute-done.10.uz_ref = bf16[128,1024]{1,0:T(8,128)(2,1)S(1)} collective-permute-done((bf16[128,1024]{1,0:T(8,128)(2,1)S(1)}, bf16[128,1024]{1,0:T(8,128)(2,1)S(1)}, u32[]{:S(2)}, u32[]{:S(2)}) %collective-permute-start.10) | collective-permute-done | bytes 262176 | tf_op jit(solution)/shard_map/ppermute | solution.py:23
  52.2 3.7 %collective-permute-done.6.sz_ref = f32[8,128]{1,0:T(8,128)S(1)} collective-permute-done((f32[8,128]{1,0:T(8,128)S(1)}, f32[8,128]{1,0:T(8,128)S(1)}, u32[]{:S(2)}, u32[]{:S(2)}) %collective-permute-start.6) | collective-permute-done | bytes 4128 | tf_op jit(solution)/shard_map/ppermute | solution.py:23
  55.9 6.1 %shard_map.86 = (bf16[2,128,1024]{2,1,0:T(8,128)(2,1)S(1)}, bf16[128,1024]{1,0:T(8,128)(2,1)S(1)}, bf16[128,1024]{1,0:T(8,128)(2,1)S(1)}, f32[128,1024]{1,0:T(8,128)S(1)}, f32[2,128,1024]{2,1,0:T(8,128)S(1)}) custom-call(s32[1]{0:T(128)} %bitcast.me_ref, s32[8,8]{1,0:T(8,128)S(1)} %copy-done.7, f32[8,128]{1,0:T(8,128)S(1)} %psum.7.sums_ref, ...), custom_call_target="tpu_custom_call" | custom-call | flops 503316480 | bytes 6139904 | tf_op jit(solution)/shard_map/pallas_call | solution.py:437
  62.0 1.3 %collective-permute-start.14 = (bf16[2,128,1024]{2,1,0:T(8,128)(2,1)S(1)}, bf16[2,128,1024]{2,1,0:T(8,128)(2,1)S(1)}, u32[]{:S(2)}, u32[]{:S(2)}) collective-permute-start(bf16[2,128,1024]{2,1,0:T(8,128)(2,1)S(1)} %get-tuple-element.31), channel_id=1, source_target_pairs={{8,0},{12,4},{16,8},{20,12},{24,16},{28,20},{9,1},{13,5},{17,9},{2... | collective-permute-start | bytes 1572872 | tf_op jit(solution)/shard_map/ppermute | solution.py:23
  63.3 4.6 %collective-permute-start.12 = (bf16[128,1024]{1,0:T(8,128)(2,1)S(1)}, bf16[128,1024]{1,0:T(8,128)(2,1)S(1)}, u32[]{:S(2)}, u32[]{:S(2)}) collective-permute-start(bf16[128,1024]{1,0:T(8,128)(2,1)S(1)} %get-tuple-element.28), channel_id=1, source_target_pairs={{0,8},{4,12},{8,16},{12,20},{16,24},{20,28},{1,9},{5,13},{9,17},{1... | collective-permute-start | bytes 786440 | tf_op jit(solution)/shard_map/ppermute | solution.py:23
  67.9 1.6 %collective-permute-start.13 = (bf16[128,1024]{1,0:T(8,128)(2,1)S(1)}, bf16[128,1024]{1,0:T(8,128)(2,1)S(1)}, u32[]{:S(2)}, u32[]{:S(2)}) collective-permute-start(bf16[128,1024]{1,0:T(8,128)(2,1)S(1)} %get-tuple-element.29), channel_id=1, source_target_pairs={{0,4},{4,0},{8,12},{12,8},{16,20},{20,16},{24,28},{28,24},{1,5},{5... | collective-permute-start | bytes 786440 | tf_op jit(solution)/shard_map/ppermute | solution.py:456
  69.4 2.2 %shard_map.87 = (bf16[128,1024]{1,0:T(8,128)(2,1)}, f32[128,1024]{1,0:T(8,128)S(1)}, f32[2,128,1024]{2,1,0:T(8,128)S(1)}) custom-call(f32[8,128]{1,0:T(8,128)S(1)} %psum.7.sums_ref, bf16[128,1024]{1,0:T(8,128)(2,1)S(1)} %copy-done.2, bf16[128,1152]{1,0:T(8,128)(2,1)S(1)} %get-tuple-element.23.a_ref, bf16[128,1024]{1,0:T(8,128)(2,1)S(1)} %copy-done, ...), custom_call_target="tpu_custom_call" | custom-call | flops 167772160 | bytes 4755456 | tf_op jit(solution)/shard_map/pallas_call | solution.py:437
  72.0 2.3 %collective-permute-done.13 = bf16[128,1024]{1,0:T(8,128)(2,1)S(1)} collective-permute-done((bf16[128,1024]{1,0:T(8,128)(2,1)S(1)}, bf16[128,1024]{1,0:T(8,128)(2,1)S(1)}, u32[]{:S(2)}, u32[]{:S(2)}) %collective-permute-start.13) | collective-permute-done | bytes 262176 | tf_op jit(solution)/shard_map/ppermute | solution.py:456
  75.1 1.3 %collective-permute-done.14 = bf16[2,128,1024]{2,1,0:T(8,128)(2,1)S(1)} collective-permute-done((bf16[2,128,1024]{2,1,0:T(8,128)(2,1)S(1)}, bf16[2,128,1024]{2,1,0:T(8,128)(2,1)S(1)}, u32[]{:S(2)}, u32[]{:S(2)}) %collective-permute-start.14) | collective-permute-done | bytes 524320 | tf_op jit(solution)/shard_map/ppermute | solution.py:23
  (30 shorter events, 9.0 us)
Async XLA Ops:
  0.6 11.9 %collective-permute-start.2 = (bf16[128,1024]{1,0:T(8,128)(2,1)}, bf16[128,1024]{1,0:T(8,128)(2,1)S(1)}, u32[]{:S(2)}, u32[]{:S(2)}) collective-permute-start(bf16[128,1024]{1,0:T(8,128)(2,1)} %k_ref.5), channel_id=1, source_target_pairs={{0,8},{4,12},{8,16},{12,20},{16,24},{20,28},{1,9},{5,13},{9,17},{1... | collective-permute-start | bytes 786440 | tf_op jit(solution)/shard_map/ppermute | solution.py:23
  5.6 11.5 %collective-permute-start.3 = (bf16[128,1024]{1,0:T(8,128)(2,1)}, bf16[128,1024]{1,0:T(8,128)(2,1)S(1)}, u32[]{:S(2)}, u32[]{:S(2)}) collective-permute-start(bf16[128,1024]{1,0:T(8,128)(2,1)} %v_ref.5), channel_id=1, source_target_pairs={{0,8},{4,12},{8,16},{12,20},{16,24},{20,28},{1,9},{5,13},{9,17},{1... | collective-permute-start | bytes 786440 | tf_op jit(solution)/shard_map/ppermute | solution.py:23
  9.1 8.0 %collective-permute-start.1 = (bf16[128,1024]{1,0:T(8,128)(2,1)}, bf16[128,1024]{1,0:T(8,128)(2,1)S(1)}, u32[]{:S(2)}, u32[]{:S(2)}) collective-permute-start(bf16[128,1024]{1,0:T(8,128)(2,1)} %q_ref.5), channel_id=1, source_target_pairs={{0,4},{4,0},{8,12},{12,8},{16,20},{20,16},{24,28},{28,24},{1,5},{5... | collective-permute-start | bytes 786440 | tf_op jit(solution)/shard_map/ppermute | solution.py:456
  10.6 9.3 %collective-permute-start = (bf16[128,1024]{1,0:T(8,128)(2,1)}, bf16[128,1024]{1,0:T(8,128)(2,1)S(1)}, u32[]{:S(2)}, u32[]{:S(2)}) collective-permute-start(bf16[128,1024]{1,0:T(8,128)(2,1)} %q_ref.5), channel_id=1, source_target_pairs={{8,0},{12,4},{16,8},{20,12},{24,16},{28,20},{9,1},{13,5},{17,9},{2... | collective-permute-start | bytes 786440 | tf_op jit(solution)/shard_map/ppermute | solution.py:23
  11.9 8.0 %copy-start.7 = (s32[8,8]{1,0:T(8,128)S(1)}, s32[8,8]{1,0:T(8,128)}, u32[]{:S(2)}) copy-start(s32[8,8]{1,0:T(8,128)} %pattern_ref.5) | copy-start | bytes 772
  19.9 1.0 %copy-start.1 = (bf16[128,1024]{1,0:T(8,128)(2,1)S(1)}, bf16[128,1024]{1,0:T(8,128)(2,1)}, u32[]{:S(2)}) copy-start(bf16[128,1024]{1,0:T(8,128)(2,1)} %q_ref.5) | copy-start | bytes 786436
  20.9 0.9 %copy-start.3 = (bf16[128,1024]{1,0:T(8,128)(2,1)S(1)}, bf16[128,1024]{1,0:T(8,128)(2,1)}, u32[]{:S(2)}) copy-start(bf16[128,1024]{1,0:T(8,128)(2,1)} %k_ref.5) | copy-start | bytes 786436
  21.8 0.9 %copy-start.5 = (bf16[128,1024]{1,0:T(8,128)(2,1)S(1)}, bf16[128,1024]{1,0:T(8,128)(2,1)}, u32[]{:S(2)}) copy-start(bf16[128,1024]{1,0:T(8,128)(2,1)} %v_ref.5) | copy-start | bytes 786436
  22.8 13.5 %copy-start = (bf16[128,1024]{1,0:T(8,128)(2,1)S(1)}, bf16[128,1024]{1,0:T(8,128)(2,1)}, u32[]{:S(2)}) copy-start(bf16[128,1024]{1,0:T(8,128)(2,1)} %u_ref.5) | copy-start | bytes 786436
  26.0 8.0 %collective-permute-start.4 = (bf16[128,1152]{1,0:T(8,128)(2,1)S(1)}, bf16[128,1152]{1,0:T(8,128)(2,1)S(1)}, u32[]{:S(2)}, u32[]{:S(2)}) collective-permute-start(bf16[128,1152]{1,0:T(8,128)(2,1)S(1)} %get-tuple-element.20), channel_id=1, source_target_pairs={{0,8},{4,12},{8,16},{12,20},{16,24},{20,28},{1,9},{5,13},{9,17},{1... | collective-permute-start | bytes 884744 | tf_op jit(solution)/shard_map/ppermute | solution.py:23
  29.5 6.8 %collective-permute-start.5 = (bf16[128,1152]{1,0:T(8,128)(2,1)S(1)}, bf16[128,1152]{1,0:T(8,128)(2,1)S(1)}, u32[]{:S(2)}, u32[]{:S(2)}) collective-permute-start(bf16[128,1152]{1,0:T(8,128)(2,1)S(1)} %get-tuple-element.21), channel_id=1, source_target_pairs={{0,4},{4,0},{8,12},{12,8},{16,20},{20,16},{24,28},{28,24},{1,5},{5... | collective-permute-start | bytes 884744 | tf_op jit(solution)/shard_map/ppermute | solution.py:456
  36.3 19.6 %copy-start.2 = (bf16[128,1024]{1,0:T(8,128)(2,1)S(1)}, bf16[128,1024]{1,0:T(8,128)(2,1)}, u32[]{:S(2)}) copy-start(bf16[128,1024]{1,0:T(8,128)(2,1)} %q_ref.5) | copy-start | bytes 786436
  36.3 19.6 %copy-start.4 = (bf16[128,1024]{1,0:T(8,128)(2,1)S(1)}, bf16[128,1024]{1,0:T(8,128)(2,1)}, u32[]{:S(2)}) copy-start(bf16[128,1024]{1,0:T(8,128)(2,1)} %k_ref.5) | copy-start | bytes 786436
  36.3 19.6 %copy-start.6 = (bf16[128,1024]{1,0:T(8,128)(2,1)S(1)}, bf16[128,1024]{1,0:T(8,128)(2,1)}, u32[]{:S(2)}) copy-start(bf16[128,1024]{1,0:T(8,128)(2,1)} %v_ref.5) | copy-start | bytes 786436
  37.8 18.0 %collective-permute-start.9 = (bf16[128,1152]{1,0:T(8,128)(2,1)S(1)}, bf16[128,1152]{1,0:T(8,128)(2,1)S(1)}, u32[]{:S(2)}, u32[]{:S(2)}) collective-permute-start(bf16[128,1152]{1,0:T(8,128)(2,1)S(1)} %get-tuple-element.23.a_ref), channel_id=1, source_target_pairs={{0,4},{4,0},{8,12},{12,8},{16,20},{20,16},{24,28},{28,24},{1,5},{5... | collective-permute-start | bytes 884744 | tf_op jit(solution)/shard_map/ppermute | solution.py:456
  38.4 17.4 %collective-permute-start.8 = (bf16[128,1152]{1,0:T(8,128)(2,1)S(1)}, bf16[128,1152]{1,0:T(8,128)(2,1)S(1)}, u32[]{:S(2)}, u32[]{:S(2)}) collective-permute-start(bf16[128,1152]{1,0:T(8,128)(2,1)S(1)} %get-tuple-element.23.a_ref), channel_id=1, source_target_pairs={{8,0},{12,4},{16,8},{20,12},{24,16},{28,20},{9,1},{13,5},{17,9},{2... | collective-permute-start | bytes 884744 | tf_op jit(solution)/shard_map/ppermute | solution.py:23
  39.7 9.4 %collective-permute-start.11 = (bf16[128,1024]{1,0:T(8,128)(2,1)S(1)}, bf16[128,1024]{1,0:T(8,128)(2,1)S(1)}, u32[]{:S(2)}, u32[]{:S(2)}) collective-permute-start(bf16[128,1024]{1,0:T(8,128)(2,1)S(1)} %copy-done), channel_id=1, source_target_pairs={{0,4},{4,0},{8,12},{12,8},{16,20},{20,16},{24,28},{28,24},{1,5},{5... | collective-permute-start | bytes 786440 | tf_op jit(solution)/shard_map/ppermute | solution.py:456
  41.3 10.6 %collective-permute-start.10 = (bf16[128,1024]{1,0:T(8,128)(2,1)S(1)}, bf16[128,1024]{1,0:T(8,128)(2,1)S(1)}, u32[]{:S(2)}, u32[]{:S(2)}) collective-permute-start(bf16[128,1024]{1,0:T(8,128)(2,1)S(1)} %copy-done), channel_id=1, source_target_pairs={{8,0},{12,4},{16,8},{20,12},{24,16},{28,20},{9,1},{13,5},{17,9},{2... | collective-permute-start | bytes 786440 | tf_op jit(solution)/shard_map/ppermute | solution.py:23
  48.5 3.7 %collective-permute-start.7 = (f32[8,128]{1,0:T(8,128)S(1)}, f32[8,128]{1,0:T(8,128)S(1)}, u32[]{:S(2)}, u32[]{:S(2)}) collective-permute-start(f32[8,128]{1,0:T(8,128)S(1)} %psum.7.sums_ref), channel_id=1, source_target_pairs={{0,4},{4,0},{8,12},{12,8},{16,20},{20,16},{24,28},{28,24},{1,5},{5... | collective-permute-start | bytes 12296 | tf_op jit(solution)/shard_map/ppermute | solution.py:456
  49.1 6.7 %collective-permute-start.6 = (f32[8,128]{1,0:T(8,128)S(1)}, f32[8,128]{1,0:T(8,128)S(1)}, u32[]{:S(2)}, u32[]{:S(2)}) collective-permute-start(f32[8,128]{1,0:T(8,128)S(1)} %psum.7.sums_ref), channel_id=1, source_target_pairs={{8,0},{12,4},{16,8},{20,12},{24,16},{28,20},{9,1},{13,5},{17,9},{2... | collective-permute-start | bytes 12296 | tf_op jit(solution)/shard_map/ppermute | solution.py:23
  62.0 14.4 %collective-permute-start.14 = (bf16[2,128,1024]{2,1,0:T(8,128)(2,1)S(1)}, bf16[2,128,1024]{2,1,0:T(8,128)(2,1)S(1)}, u32[]{:S(2)}, u32[]{:S(2)}) collective-permute-start(bf16[2,128,1024]{2,1,0:T(8,128)(2,1)S(1)} %get-tuple-element.31), channel_id=1, source_target_pairs={{8,0},{12,4},{16,8},{20,12},{24,16},{28,20},{9,1},{13,5},{17,9},{2... | collective-permute-start | bytes 1572872 | tf_op jit(solution)/shard_map/ppermute | solution.py:23
  63.3 8.7 %collective-permute-start.12 = (bf16[128,1024]{1,0:T(8,128)(2,1)S(1)}, bf16[128,1024]{1,0:T(8,128)(2,1)S(1)}, u32[]{:S(2)}, u32[]{:S(2)}) collective-permute-start(bf16[128,1024]{1,0:T(8,128)(2,1)S(1)} %get-tuple-element.28), channel_id=1, source_target_pairs={{0,8},{4,12},{8,16},{12,20},{16,24},{20,28},{1,9},{5,13},{9,17},{1... | collective-permute-start | bytes 786440 | tf_op jit(solution)/shard_map/ppermute | solution.py:23
  67.9 6.4 %collective-permute-start.13 = (bf16[128,1024]{1,0:T(8,128)(2,1)S(1)}, bf16[128,1024]{1,0:T(8,128)(2,1)S(1)}, u32[]{:S(2)}, u32[]{:S(2)}) collective-permute-start(bf16[128,1024]{1,0:T(8,128)(2,1)S(1)} %get-tuple-element.29), channel_id=1, source_target_pairs={{0,4},{4,0},{8,12},{12,8},{16,20},{20,16},{24,28},{28,24},{1,5},{5... | collective-permute-start | bytes 786440 | tf_op jit(solution)/shard_map/ppermute | solution.py:456

commit v2 on v1

--- a/solution.py
+++ b/solution.py
@@ -244,43 +244,89 @@
     return odd, near, far, side
 
 
-def softmax_part(score_list, value_list):
-    highest = score_list[0].max(axis=1, keepdims=True)
-    for scores in score_list[1:]:
-        highest = jnp.maximum(highest, scores.max(axis=1, keepdims=True))
-    total, out = 0.0, 0.0
-    for scores, value in zip(score_list, value_list):
-        weights = jnp.exp(scores - highest)
-        total = total + weights.sum(axis=1, keepdims=True)
-        out = out + mm(weights.astype(jnp.bfloat16), value, NN)
-    return out / total, highest + jnp.log(total)
-
-
-def forward_kernel(
-    heads, me_ref, pattern_ref, q_ref, qz_ref, qx_ref, k_ref, v_ref, k2_ref, v2_ref, own_ref, lse_ref, oz_ref, ox_ref
-):
-    odd, near, _, _ = pair_flags(me_ref, pattern_ref)
+def softmax_pair(scores, value):
+    highest = scores.max(axis=1, keepdims=True)
+    weights = jnp.exp(scores - highest)
+    total = weights.sum(axis=1, keepdims=True)
+    out = mm(weights.astype(jnp.bfloat16), value, NN) / total
+    return out, highest, highest + jnp.log(total), weights
+
+
+def tile_columns(columns):
+    lanes = lane_ids((BLOCK, PACK))
+    wide = jnp.zeros((BLOCK, PACK), jnp.float32)
+    for index, column in enumerate(columns):
+        wide = jnp.where(lanes == index, column, wide)
+    return wide
+
+
+def side_pair(odd, k, v, k2, v2):
+    return jnp.where(odd == 1, k2, k), jnp.where(odd == 1, v2, v)
+
+
+def diagonal_kernel(heads, q_ref, k_ref, v_ref, qc_ref, kc_ref, vc_ref, out_ref, lse_ref):
     causal = causal_mask()
-    own_lse, z_lse, x_lse = [], [], []
+    tops = []
     for h in range(heads):
         at = slice(h * HD, (h + 1) * HD)
-        k, v, k2, v2 = k_ref[:, at], v_ref[:, at], k2_ref[:, at], v2_ref[:, at]
-        q = q_ref[:, at]
-        here = jnp.where(causal, mm(q, k, NT) * SCALE, NEG_BIG)
-        back = jnp.where(near, mm(q, k2, NT) * SCALE, NEG_BIG)
-        out, lse = softmax_part([here, back], [v, v2])
-        own_ref[:, at] = out
-        own_lse.append(lse)
-        out, lse = softmax_part([mm(qz_ref[:, at], k2, NT) * SCALE], [v2])
+        q, k, v = q_ref[:, at], k_ref[:, at], v_ref[:, at]
+        qc_ref[:, at], kc_ref[:, at], vc_ref[:, at] = q, k, v
+        scores = jnp.where(causal, mm(q, k, NT) * SCALE, NEG_BIG)
+        out_ref[:, at], _, lse, _ = softmax_pair(scores, v)
+        tops.append(lse)
+    lse_ref[...] = tile_columns(tops)
+
+
+def helper_kernel(
+    heads,
+    me_ref,
+    qz_ref,
+    qx_ref,
+    k_ref,
+    v_ref,
+    k2_ref,
+    v2_ref,
+    oz_ref,
+    ox_ref,
+    ez_ref,
+    ex_ref,
+    mz_ref,
+    mx_ref,
+):
+    odd = lax.rem(me_ref[0], 2)
+    z_lse, x_lse, z_top, x_top = [], [], [], []
+    for h in range(heads):
+        at = slice(h * HD, (h + 1) * HD)
+        k2, v2 = k2_ref[:, at], v2_ref[:, at]
+        out, top, lse, ez_ref[:, at] = softmax_pair(mm(qz_ref[:, at], k2, NT) * SCALE, v2)
         oz_ref[:, at] = out.astype(jnp.bfloat16)
+        z_top.append(top)
         z_lse.append(lse)
-        ks, vs = jnp.where(odd == 1, k2, k), jnp.where(odd == 1, v2, v)
-        out, lse = softmax_part([mm(qx_ref[:, at], ks, NT) * SCALE], [vs])
+        ks, vs = side_pair(odd, k_ref[:, at], v_ref[:, at], k2, v2)
+        out, top, lse, ex_ref[:, at] = softmax_pair(mm(qx_ref[:, at], ks, NT) * SCALE, vs)
         ox_ref[:, at] = out.astype(jnp.bfloat16)
+        x_top.append(top)
         x_lse.append(lse)
     oz_ref[:, heads * HD :] = pack_columns(z_lse)
     ox_ref[:, heads * HD :] = pack_columns(x_lse)
-    lse_ref[...] = pack_columns(own_lse)
+    mz_ref[...] = tile_columns(z_top)
+    mx_ref[...] = tile_columns(x_top)
+
+
+def own_kernel(heads, me_ref, pattern_ref, q_ref, k2_ref, v2_ref, out_ref, lse_ref, own_ref, total_ref):
+    near = pattern_ref[me_ref[0], 1] >= 0
+    tile = lse_ref[...]
+    totals = []
+    for h in range(heads):
+        at = slice(h * HD, (h + 1) * HD)
+        out, _, lse, _ = softmax_pair(mm(q_ref[:, at], k2_ref[:, at], NT) * SCALE, v2_ref[:, at])
+        lse = jnp.where(near, lse, NEG_BIG)
+        before = tile[:, h : h + 1]
+        highest = jnp.maximum(before, lse)
+        total = highest + jnp.log(jnp.exp(before - highest) + jnp.exp(lse - highest))
+        own_ref[:, at] = out_ref[:, at] * jnp.exp(before - total) + out * jnp.exp(lse - total)
+        totals.append(total)
+    total_ref[...] = tile_columns(totals)
 
 
 def merge_kernel(heads, me_ref, pattern_ref, own_ref, lse_ref, rz_ref, rx_ref, u_ref, a_ref, sums_ref):
@@ -293,7 +339,7 @@
     crosses = jnp.zeros((BLOCK, HD), jnp.float32)
     for h in range(heads):
         at = slice(h * HD, (h + 1) * HD)
-        own_lse = unpack_column(own_tile, heads, h)
+        own_lse = own_tile[:, h : h + 1]
         z_lse = jnp.where(far, unpack_column(z_tile, heads, h), NEG_BIG)
         x_lse = jnp.where(side, unpack_column(x_tile, heads, h), NEG_BIG)
         highest = jnp.maximum(own_lse, jnp.maximum(z_lse, x_lse))
@@ -344,90 +390,110 @@
     return weights.astype(jnp.bfloat16), dscore
 
 
-def far_kernel(
+def own_back_kernel(
     heads,
     me_ref,
     pattern_ref,
-    sums_ref,
-    sz_ref,
-    sx_ref,
-    q_ref,
-    qz_ref,
-    qx_ref,
-    a_ref,
-    az_ref,
-    ax_ref,
-    u_ref,
-    uz_ref,
-    ux_ref,
-    k_ref,
-    v_ref,
-    k2_ref,
-    v2_ref,
-    dkv_ref,
-    dqz_ref,
-    dqx_ref,
-    dq_ref,
-    dside_ref,
-):
-    odd, near, far, side = pair_flags(me_ref, pattern_ref)
-    tail = slice(heads * HD, heads * HD + PACK)
-    own_norm, z_norm, x_norm = norm_columns(sums_ref), norm_columns(sz_ref), norm_columns(sx_ref)
-    own_tile, z_tile, x_tile = a_ref[:, tail], az_ref[:, tail], ax_ref[:, tail]
-    share = (odd == 1).astype(jnp.float32)
-    for h in range(heads):
-        at = slice(h * HD, (h + 1) * HD)
-        k, v, k2, v2 = k_ref[:, at], v_ref[:, at], k2_ref[:, at], v2_ref[:, at]
-        q, qz, qx = q_ref[:, at], qz_ref[:, at], qx_ref[:, at]
-        grad, delta = upstream_part(*own_norm, u_ref[:, at], a_ref[:, at])
-        gradz, deltaz = upstream_part(*z_norm, uz_ref[:, at], az_ref[:, at])
-        gradx, deltax = upstream_part(*x_norm, ux_ref[:, at], ax_ref[:, at])
-        probs, dscore = pair_back(q, k2, v2, grad, delta, unpack_column(own_tile, heads, h), near)
-        dk2 = mm(dscore, q, TN)
-        dv2 = mm(probs, grad, TN)
-        dq_ref[:, at] = mm(dscore, k2, NN)
-        probs, dscore = pair_back(qz, k2, v2, gradz, deltaz, unpack_column(z_tile, heads, h), far)
-        dk2 += mm(dscore, qz, TN)
-        dv2 += mm(probs, gradz, TN)
-        dqz_ref[:, at] = mm(dscore, k2, NN).astype(jnp.bfloat16)
-        ks, vs = jnp.where(odd == 1, k2, k), jnp.where(odd == 1, v2, v)
-        probs, dscore = pair_back(qx, ks, vs, gradx, deltax, unpack_column(x_tile, heads, h), side)
-        dks = mm(dscore, qx, TN)
-        dvs = mm(probs, gradx, TN)
-        dqx_ref[:, at] = mm(dscore, ks, NN).astype(jnp.bfloat16)
-        dkv_ref[0, :, at] = (dk2 + share * dks).astype(jnp.bfloat16)
-        dkv_ref[1, :, at] = (dv2 + share * dvs).astype(jnp.bfloat16)
-        dside_ref[0, :, at] = (1.0 - share) * dks
-        dside_ref[1, :, at] = (1.0 - share) * dvs
-
-
-def near_kernel(
-    heads,
     sums_ref,
     q_ref,
     a_ref,
     u_ref,
     k_ref,
     v_ref,
-    dq_in_ref,
-    dside_ref,
+    k2_ref,
+    v2_ref,
     normed_ref,
     dq_ref,
     dkv_ref,
+    dkv2_ref,
 ):
-    tail = slice(heads * HD, heads * HD + PACK)
+    near = pattern_ref[me_ref[0], 1] >= 0
     inverse, factor = norm_columns(sums_ref)
-    tile = a_ref[:, tail]
+    tile = a_ref[:, heads * HD : heads * HD + PACK]
     causal = causal_mask()
     for h in range(heads):
         at = slice(h * HD, (h + 1) * HD)
-        q, k, v, a = q_ref[:, at], k_ref[:, at], v_ref[:, at], a_ref[:, at]
+        q, k, v, a, k2, v2 = q_ref[:, at], k_ref[:, at], v_ref[:, at], a_ref[:, at], k2_ref[:, at], v2_ref[:, at]
+        lse = unpack_column(tile, heads, h)
         normed_ref[:, at] = (a.astype(jnp.float32) * inverse).astype(jnp.bfloat16)
         grad, delta = upstream_part(inverse, factor, u_ref[:, at], a)
-        probs, dscore = pair_back(q, k, v, grad, delta, unpack_column(tile, heads, h), causal)
-        dq_ref[:, at] = dq_in_ref[:, at] + mm(dscore, k, NN)
-        dkv_ref[0, :, at] = dside_ref[0, :, at] + mm(dscore, q, TN)
-        dkv_ref[1, :, at] = dside_ref[1, :, at] + mm(probs, grad, TN)
+        probs, dscore = pair_back(q, k2, v2, grad, delta, lse, near)
+        dkv2_ref[0, :, at] = mm(dscore, q, TN)
+        dkv2_ref[1, :, at] = mm(probs, grad, TN)
+        dq = mm(dscore, k2, NN)
+        probs, dscore = pair_back(q, k, v, grad, delta, lse, causal)
+        dkv_ref[0, :, at] = mm(dscore, q, TN)
+        dkv_ref[1, :, at] = mm(probs, grad, TN)
+        dq_ref[:, at] = dq + mm(dscore, k, NN)
+
+
+def helper_back_kernel(
+    heads,
+    me_ref,
+    pattern_ref,
+    sz_ref,
+    sx_ref,
+    qz_ref,
+    qx_ref,
+    az_ref,
+    ax_ref,
+    uz_ref,
+    ux_ref,
+    ez_ref,
+    ex_ref,
+    mz_ref,
+    mx_ref,
+    v_ref,
+    v2_ref,
+    own_ref,
+    dkv_ref,
+    dsz_ref,
+    dsx_ref,
+    dside_ref,
+):
+    odd, _, far, side = pair_flags(me_ref, pattern_ref)
+    tail = slice(heads * HD, heads * HD + PACK)
+    z_norm, x_norm = norm_columns(sz_ref), norm_columns(sx_ref)
+    z_tile, x_tile, z_top, x_top = az_ref[:, tail], ax_ref[:, tail], mz_ref[...], mx_ref[...]
+    share = (odd == 1).astype(jnp.float32)
+
+    def one(h, at, norm, u, a, weights, tile, top, value, keep):
+        grad, delta = upstream_part(*norm, u, a)
+        scale = jnp.exp(top[:, h : h + 1] - unpack_column(tile, heads, h))
+        wide = jnp.where(keep, weights * scale, 0.0)
+        dscore = (wide * (mm(grad, value, NT) - delta) * SCALE).astype(jnp.bfloat16)
+        return wide.astype(jnp.bfloat16), dscore, grad
+
+    for h in range(heads):
+        at = slice(h * HD, (h + 1) * HD)
+        v, v2 = v_ref[:, at], v2_ref[:, at]
+        probs, dscore, grad = one(
+            h, at, z_norm, uz_ref[:, at], az_ref[:, at], ez_ref[:, at], z_tile, z_top, v2, far
+        )
+        dk2 = own_ref[0, :, at] + mm(dscore, qz_ref[:, at], TN)
+        dv2 = own_ref[1, :, at] + mm(probs, grad, TN)
+        dsz_ref[:, at] = dscore
+        vs = jnp.where(odd == 1, v2, v)
+        probs, dscore, grad = one(
+            h, at, x_norm, ux_ref[:, at], ax_ref[:, at], ex_ref[:, at], x_tile, x_top, vs, side
+        )
+        dks = mm(dscore, qx_ref[:, at], TN)
+        dvs = mm(probs, grad, TN)
+        dsx_ref[:, at] = dscore
+        dkv_ref[0, :, at] = (dk2 + share * dks).astype(jnp.bfloat16)
+        dkv_ref[1, :, at] = (dv2 + share * dvs).astype(jnp.bfloat16)
+        dside_ref[0, :, at] = (1.0 - share) * dks
+        dside_ref[1, :, at] = (1.0 - share) * dvs
+
+
+def helper_query_kernel(heads, me_ref, dsz_ref, dsx_ref, k_ref, k2_ref, dqz_ref, dqx_ref):
+    odd = lax.rem(me_ref[0], 2)
+    for h in range(heads):
+        at = slice(h * HD, (h + 1) * HD)
+        k2 = k2_ref[:, at]
+        dqz_ref[:, at] = mm(dsz_ref[:, at], k2, NN).astype(jnp.bfloat16)
+        ks = jnp.where(odd == 1, k2, k_ref[:, at])
+        dqx_ref[:, at] = mm(dsx_ref[:, at], ks, NN).astype(jnp.bfloat16)
 
 
 def call(kernel, heads, scalars, arrays, outs, flops):
@@ -464,19 +530,38 @@
     def struct(*shape, dtype=jnp.bfloat16):
         return jax.ShapeDtypeStruct(shape, dtype)
 
+    wide = struct(tokens, width, dtype=jnp.float32)
+    wide_pair = struct(2, tokens, width, dtype=jnp.float32)
+    flat = struct(tokens, width)
+    packed = struct(tokens, width + PACK)
+    tile = struct(tokens, PACK, dtype=jnp.float32)
+
     keys2, values2 = up(keys), up(values)
     queries_z, queries_x = down(queries), swap(queries)
     upstream_z, upstream_x = down(upstream), swap(upstream)
-    packed = struct(tokens, width + PACK)
-    own, own_lse, out_z, out_x = call(
-        forward_kernel,
+    q, k, v, diagonal, diagonal_lse = call(
+        diagonal_kernel, heads, (), (queries, keys, values), (flat, flat, flat, wide, tile), 2 * unit
+    )
+    keys2, values2, queries_z, queries_x, upstream_z, upstream_x = lax.optimization_barrier(
+        (keys2, values2, queries_z, queries_x, upstream_z, upstream_x)
+    )
+    out_z, out_x, ez, ex, mz, mx = call(
+        helper_kernel,
+        heads,
+        (me,),
+        (queries_z, queries_x, k, v, keys2, values2),
+        (packed, packed, wide, wide, tile, tile),
+        4 * unit,
+    )
+    back_z, back_x = up(out_z), swap(out_x)
+    own, own_lse = call(
+        own_kernel,
         heads,
         (me, pattern),
-        (queries, queries_z, queries_x, keys, values, keys2, values2),
-        (struct(tokens, width, dtype=jnp.float32), struct(tokens, PACK), packed, packed),
-        8 * unit,
-    )
-    back_z, back_x = up(out_z), swap(out_x)
+        (q, keys2, values2, diagonal, diagonal_lse),
+        (wide, tile),
+        2 * unit,
+    )
     attention, sums = call(
         merge_kernel,
         heads,
@@ -488,40 +573,33 @@
     attention_z, attention_x = down(attention), swap(attention)
     sums = lax.psum(sums, "head")
     sums_z, sums_x = down(sums), swap(sums)
-    grads2, dq_z, dq_x, dq_own, dside = call(
-        far_kernel,
+    normed, dq_own, grads_own, grads2_own = call(
+        own_back_kernel,
         heads,
         (me, pattern),
-        (sums, sums_z, sums_x, queries, queries_z, queries_x, attention, attention_z, attention_x)
-        + (upstream, upstream_z, upstream_x, keys, values, keys2, values2),
-        (
-            struct(2, tokens, width),
-            struct(tokens, width),
-            struct(tokens, width),
-            struct(tokens, width, dtype=jnp.float32),
-            struct(2, tokens, width, dtype=jnp.float32),
-        ),
-        15 * unit,
+        (sums, q, attention, upstream, k, v, keys2, values2),
+        (flat, wide, wide_pair, wide_pair),
+        10 * unit,
+    )
+    grads2, dsz, dsx, dside = call(
+        helper_back_kernel,
+        heads,
+        (me, pattern),
+        (sums_z, sums_x, queries_z, queries_x, attention_z, attention_x, upstream_z, upstream_x)
+        + (ez, ex, mz, mx, v, values2, grads2_own),
+        (struct(2, tokens, width), flat, flat, wide_pair),
+        6 * unit,
     )
     grads_back = down(grads2)
+    dq_z, dq_x = call(helper_query_kernel, heads, (me,), (dsz, dsx, k, keys2), (flat, flat), 2 * unit)
     dq_back_z, dq_back_x = up(dq_z), swap(dq_x)
-    normed, dq_own, grads_own = call(
-        near_kernel,
-        heads,
-        (),
-        (sums, queries, attention, upstream, keys, values, dq_own, dside),
-        (
-            struct(tokens, width),
-            struct(tokens, width, dtype=jnp.float32),
-            struct(2, tokens, width, dtype=jnp.float32),
-        ),
-        5 * unit,
-    )
     grad_queries = (
         dq_own + dq_back_z.astype(jnp.float32) + dq_back_x.astype(jnp.float32)
     ).astype(jnp.bfloat16)
-    grads = (grads_own + grads_back.astype(jnp.float32)).astype(jnp.bfloat16)
-    return (normed, grad_queries, grads[0], grads[1])
+    grad_keys, grad_values = (
+        (grads_own[n] + dside[n] + grads_back[n].astype(jnp.float32)).astype(jnp.bfloat16) for n in (0, 1)
+    )
+    return (normed, grad_queries, grad_keys, grad_values)
 
 
 def shards(queries, keys, values, pattern, upstream):

time: 77.9 us -> 76.9 us (0.987)
  waiting for transfers between devices: 23.6 us -> 10.6 us
  Pallas kernels: 13.1 us -> 19.3 us
  starting transfers between devices: 29.4 us -> 32.8 us
  local copies, waits for them, and re-layouts: 3.69 us -> 4.89 us
  other arithmetic: 0.96 us -> 1.88 us
    ppermute x9, waiting for transfers between devices: 18.7 us -> 5.79 us  [shifted(): return lax.ppermute(block, axis, route)]
    pallas_call x4 -> x7, Pallas kernels: 13.1 us -> 19.3 us  [call(): pl.pallas_call(functools.partial(kernel, heads), out_shape=outs, in_specs...]
    ppermute x9, starting transfers between devices: 22.9 us -> 25.3 us  [shifted(): return lax.ppermute(block, axis, route)]
    unnamed x16 -> x22, local copies, waits for them, and re-layouts: 2.87 us -> 4.89 us
    ppermute x6, starting transfers between devices: 6.46 us -> 7.42 us  [swap(): return lax.ppermute(array, 'ctx', partners)]
    convert_element_type x1, other arithmetic: 0.15 us -> 1.07 us  [meeting_shards(): (grads_own[n] + dside[n] + grads_back[n].astype(jnp.float32)).astype(jnp....]
    squeeze x1 -> x0, local copies, waits for them, and re-layouts: 0.82 us -> none  [meeting_shards(): return (normed, grad_queries, grads[0], grads[1])]
  transfers between devices with their start and end apart: 15 -> 15, of which waited for: 11 -> 6; matrix products, arithmetic and copies ran while one was open for 1% -> 1% of each run, Pallas kernels for 3% -> 13%
where the time goes in v2:
time: 76.9 us; the launch traced here: 76.4 us
  starting transfers between devices  32.8 us (43%)
  Pallas kernels  19.3 us (25%)
  waiting for transfers between devices  10.6 us (14%)
  blocking collectives  6.07 us (8%)
  local copies, waits for them, and re-layouts  4.89 us (6%)
  other arithmetic  1.88 us (2%)
  between operations  0.89 us (1%)
    ppermute x9, starting transfers between devices, shifted(): return lax.ppermute(block, axis, route)  25.3 us
    pallas_call x7, Pallas kernels, call(): pl.pallas_call(functools.partial(kernel, heads), out_shape=outs, in_specs...  19.3 us
    ppermute x6, starting transfers between devices, swap(): return lax.ppermute(array, 'ctx', partners)  7.42 us
    psum x1, blocking collectives, meeting_shards(): sums = lax.psum(sums, 'head')  6.07 us
    ppermute x9, waiting for transfers between devices, shifted(): return lax.ppermute(block, axis, route)  5.79 us
    unnamed x22, local copies, waits for them, and re-layouts  4.89 us
    ppermute x6, waiting for transfers between devices, swap(): return lax.ppermute(array, 'ctx', partners)  4.86 us
  transfers between devices with their start and end apart: 15, of which 6 were waited for; matrix products, arithmetic and copies ran while one was open for 1% of the time, Pallas kernels for 13%

profile of v2, /device:TPU:0, one launch (start us, length us, event | category | flops | bytes accessed | tf_op | source)
XLA Modules:
  0.0 76.4 jit_solution(7647166001718877612)
XLA Ops:
  0.6 4.9 %collective-permute-start = (bf16[128,1024]{1,0:T(8,128)(2,1)}, bf16[128,1024]{1,0:T(8,128)(2,1)S(1)}, u32[]{:S(2)}, u32[]{:S(2)}) collective-permute-start(bf16[128,1024]{1,0:T(8,128)(2,1)} %k_ref.1), channel_id=1, source_target_pairs={{0,8},{4,12},{8,16},{12,20},{16,24},{20,28},{1,9},{5,13},{9,17},{1... | collective-permute-start | bytes 786440 | tf_op jit(solution)/shard_map/ppermute | solution.py:23
  5.6 1.6 %collective-permute-start.3 = (bf16[128,1024]{1,0:T(8,128)(2,1)}, bf16[128,1024]{1,0:T(8,128)(2,1)S(1)}, u32[]{:S(2)}, u32[]{:S(2)}) collective-permute-start(bf16[128,1024]{1,0:T(8,128)(2,1)} %q_ref.1), channel_id=1, source_target_pairs={{0,4},{4,0},{8,12},{12,8},{16,20},{20,16},{24,28},{28,24},{1,5},{5... | collective-permute-start | bytes 786440 | tf_op jit(solution)/shard_map/ppermute | solution.py:522
  7.1 1.3 %collective-permute-start.2 = (bf16[128,1024]{1,0:T(8,128)(2,1)}, bf16[128,1024]{1,0:T(8,128)(2,1)S(1)}, u32[]{:S(2)}, u32[]{:S(2)}) collective-permute-start(bf16[128,1024]{1,0:T(8,128)(2,1)} %q_ref.1), channel_id=1, source_target_pairs={{8,0},{12,4},{16,8},{20,12},{24,16},{28,20},{9,1},{13,5},{17,9},{2... | collective-permute-start | bytes 786440 | tf_op jit(solution)/shard_map/ppermute | solution.py:23
  8.4 4.6 %collective-permute-start.1 = (bf16[128,1024]{1,0:T(8,128)(2,1)}, bf16[128,1024]{1,0:T(8,128)(2,1)S(1)}, u32[]{:S(2)}, u32[]{:S(2)}) collective-permute-start(bf16[128,1024]{1,0:T(8,128)(2,1)} %v_ref.1), channel_id=1, source_target_pairs={{0,8},{4,12},{8,16},{12,20},{16,24},{20,28},{1,9},{5,13},{9,17},{1... | collective-permute-start | bytes 786440 | tf_op jit(solution)/shard_map/ppermute | solution.py:23
  13.6 1.3 %collective-permute-start.4 = (bf16[128,1024]{1,0:T(8,128)(2,1)}, bf16[128,1024]{1,0:T(8,128)(2,1)S(1)}, u32[]{:S(2)}, u32[]{:S(2)}) collective-permute-start(bf16[128,1024]{1,0:T(8,128)(2,1)} %u_ref.3), channel_id=1, source_target_pairs={{8,0},{12,4},{16,8},{20,12},{24,16},{28,20},{9,1},{13,5},{17,9},{2... | collective-permute-start | bytes 786440 | tf_op jit(solution)/shard_map/ppermute | solution.py:23
  17.7 2.0 %shard_map.84 = (bf16[128,1024]{1,0:T(8,128)(2,1)S(1)}, bf16[128,1024]{1,0:T(8,128)(2,1)S(1)}, bf16[128,1024]{1,0:T(8,128)(2,1)S(1)}, f32[128,1024]{1,0:T(8,128)S(1)}, f32[128,128]{1,0:T(8,128)S(1)}) custom-call(bf16[128,1024]{1,0:T(8,128)(2,1)S(1)} %copy-done.3, bf16[128,1024]{1,0:T(8,128)(2,1)S(1)} %copy-done.1, bf16[128,1024]{1,0:T(8,128)(2,1)S(1)} %copy-done.2), custom_call_target="tpu_custom_call" | custom-call | flops 67108864 | bytes 2162688 | tf_op jit(solution)/shard_map/pallas_call | solution.py:503
  20.9 1.4 %collective-permute-done.4.uz_ref = bf16[128,1024]{1,0:T(8,128)(2,1)S(1)} collective-permute-done((bf16[128,1024]{1,0:T(8,128)(2,1)}, bf16[128,1024]{1,0:T(8,128)(2,1)S(1)}, u32[]{:S(2)}, u32[]{:S(2)}) %collective-permute-start.4) | collective-permute-done | bytes 262176 | tf_op jit(solution)/shard_map/ppermute | solution.py:23
  23.0 3.9 %shard_map.86 = (bf16[128,1152]{1,0:T(8,128)(2,1)S(1)}, bf16[128,1152]{1,0:T(8,128)(2,1)S(1)}, f32[128,1024]{1,0:T(8,128)S(1)}, f32[128,1024]{1,0:T(8,128)S(1)},...) custom-call(s32[1]{0:T(128)} %bitcast.me_ref, bf16[128,1024]{1,0:T(8,128)(2,1)S(1)} %collective-permute-done.2.qz_ref, ...), custom_call_target="tpu_custom_call" | custom-call | flops 134217728 | bytes 3342336 | tf_op jit(solution)/shard_map/pallas_call | solution.py:503
  27.6 3.6 %collective-permute-start.6 = (bf16[128,1152]{1,0:T(8,128)(2,1)S(1)}, bf16[128,1152]{1,0:T(8,128)(2,1)S(1)}, u32[]{:S(2)}, u32[]{:S(2)}) collective-permute-start(bf16[128,1152]{1,0:T(8,128)(2,1)S(1)} %get-tuple-element.46), channel_id=1, source_target_pairs={{0,8},{4,12},{8,16},{12,20},{16,24},{20,28},{1,9},{5,13},{9,17},{1... | collective-permute-start | bytes 884744 | tf_op jit(solution)/shard_map/ppermute | solution.py:23
  31.2 1.6 %collective-permute-start.7 = (bf16[128,1152]{1,0:T(8,128)(2,1)S(1)}, bf16[128,1152]{1,0:T(8,128)(2,1)S(1)}, u32[]{:S(2)}, u32[]{:S(2)}) collective-permute-start(bf16[128,1152]{1,0:T(8,128)(2,1)S(1)} %get-tuple-element.47), channel_id=1, source_target_pairs={{0,4},{4,0},{8,12},{12,8},{16,20},{20,16},{24,28},{28,24},{1,5},{5... | collective-permute-start | bytes 884744 | tf_op jit(solution)/shard_map/ppermute | solution.py:522
  32.8 3.1 %shard_map.85 = (f32[128,1024]{1,0:T(8,128)S(1)}, f32[128,128]{1,0:T(8,128)S(1)}) custom-call(s32[1]{0:T(128)} %bitcast.me_ref, s32[8,8]{1,0:T(8,128)S(1)} %copy-done.10, bf16[128,1024]{1,0:T(8,128)(2,1)S(1)} %get-tuple-element.35.q_ref, bf16[128,1024]{1,0:T(8,128)(2,1)S(1)} %collective-permute-done.k2_ref, ...), custom_call_target="tpu_custom_call" | custom-call | flops 67108864 | bytes 1966080 | tf_op jit(solution)/shard_map/pallas_call | solution.py:503
  35.9 2.2 %collective-permute-done.7.rx_ref = bf16[128,1152]{1,0:T(8,128)(2,1)S(1)} collective-permute-done((bf16[128,1152]{1,0:T(8,128)(2,1)S(1)}, bf16[128,1152]{1,0:T(8,128)(2,1)S(1)}, u32[]{:S(2)}, u32[]{:S(2)}) %collective-permute-start.7) | collective-permute-done | bytes 294944 | tf_op jit(solution)/shard_map/ppermute | solution.py:522
  38.0 1.5 %shard_map.87 = (bf16[128,1152]{1,0:T(8,128)(2,1)S(1)}, f32[8,128]{1,0:T(8,128)S(1)}) custom-call(s32[1]{0:T(128)} %bitcast.me_ref, s32[8,8]{1,0:T(8,128)S(1)} %copy-done.10, f32[128,1024]{1,0:T(8,128)S(1)} %get-tuple-element.40.own_ref, f32[128,128]{1,0:T(8,128)S(1)} %get-tuple-element.41.lse_ref, bf16[128,1152]{1,0:T(8,128)(2,1)S(1)} %collective-permute-done.6.rz_ref, ...), custom_call_target="tpu_custom_call" | custom-call | flops 524288 | bytes 1740800 | tf_op jit(solution)/shard_map/pallas_call | solution.py:503
  39.5 1.6 %collective-permute-start.11 = (bf16[128,1152]{1,0:T(8,128)(2,1)S(1)}, bf16[128,1152]{1,0:T(8,128)(2,1)}, u32[]{:S(2)}, u32[]{:S(2)}) collective-permute-start(bf16[128,1152]{1,0:T(8,128)(2,1)S(1)} %get-tuple-element.49.a_ref), channel_id=1, source_target_pairs={{0,4},{4,0},{8,12},{12,8},{16,20},{20,16},{24,28},{28,24},{1,5},{5... | collective-permute-start | bytes 884744 | tf_op jit(solution)/shard_map/ppermute | solution.py:522
  41.1 1.3 %collective-permute-start.10 = (bf16[128,1152]{1,0:T(8,128)(2,1)S(1)}, bf16[128,1152]{1,0:T(8,128)(2,1)}, u32[]{:S(2)}, u32[]{:S(2)}) collective-permute-start(bf16[128,1152]{1,0:T(8,128)(2,1)S(1)} %get-tuple-element.49.a_ref), channel_id=1, source_target_pairs={{8,0},{12,4},{16,8},{20,12},{24,16},{28,20},{9,1},{13,5},{17,9},{2... | collective-permute-start | bytes 884744 | tf_op jit(solution)/shard_map/ppermute | solution.py:23
  42.4 6.1 %psum.7.sums_ref = f32[8,128]{1,0:T(8,128)S(1)} all-reduce(f32[8,128]{1,0:T(8,128)S(1)} %get-tuple-element.48), channel_id=1, replica_groups=mesh['ctx'=8,'head'=4] {'head'}, use_global_device_ids=true, to_apply=%region_0.0 | all-reduce | flops 1024 | bytes 8192 | tf_op jit(solution)/shard_map/psum | solution.py:574
  49.0 1.3 %collective-permute-start.8 = (f32[8,128]{1,0:T(8,128)S(1)}, f32[8,128]{1,0:T(8,128)S(1)}, u32[]{:S(2)}, u32[]{:S(2)}) collective-permute-start(f32[8,128]{1,0:T(8,128)S(1)} %psum.7.sums_ref), channel_id=1, source_target_pairs={{8,0},{12,4},{16,8},{20,12},{24,16},{28,20},{9,1},{13,5},{17,9},{2... | collective-permute-start | bytes 12296 | tf_op jit(solution)/shard_map/ppermute | solution.py:23
  50.3 4.9 %shard_map.88 = (bf16[128,1024]{1,0:T(8,128)(2,1)}, f32[128,1024]{1,0:T(8,128)S(1)}, f32[2,128,1024]{2,1,0:T(8,128)S(1)}, f32[2,128,1024]{2,1,0:T(8,128)S(1)}) custom-call(s32[1]{0:T(128)} %bitcast.me_ref, s32[8,8]{1,0:T(8,128)S(1)} %copy-done.10, f32[8,128]{1,0:T(8,128)S(1)} %psum.7.sums_ref, bf16[128,1024]{1,0:T(8,128)(2,1)S(1)} %get-tuple-element.35.q_ref, ...), custom_call_target="tpu_custom_call" | custom-call | flops 335544320 | bytes 4755456 | tf_op jit(solution)/shard_map/pallas_call | solution.py:503
  55.3 3.6 %shard_map.89 = (bf16[2,128,1024]{2,1,0:T(8,128)(2,1)S(1)}, bf16[128,1024]{1,0:T(8,128)(2,1)S(1)}, bf16[128,1024]{1,0:T(8,128)(2,1)S(1)}, f32[2,128,1024]{2,1,0:T(8,128)S(1)}) custom-call(s32[1]{0:T(128)} %bitcast.me_ref, s32[8,8]{1,0:T(8,128)S(1)} %copy-done.10, f32[8,128]{1,0:T(8,128)S(1)} %collective-permute-done.8.sz_ref, ...), custom_call_target="tpu_custom_call" | custom-call | flops 201326592 | bytes 6496256 | tf_op jit(solution)/shard_map/pallas_call | solution.py:503
  58.9 1.3 %collective-permute-start.14 = (bf16[2,128,1024]{2,1,0:T(8,128)(2,1)S(1)}, bf16[2,128,1024]{2,1,0:T(8,128)(2,1)S(1)}, u32[]{:S(2)}, u32[]{:S(2)}) collective-permute-start(bf16[2,128,1024]{2,1,0:T(8,128)(2,1)S(1)} %get-tuple-element.65), channel_id=1, source_target_pairs={{8,0},{12,4},{16,8},{20,12},{24,16},{28,20},{9,1},{13,5},{17,9},{2... | collective-permute-start | bytes 1572872 | tf_op jit(solution)/shard_map/ppermute | solution.py:23
  60.5 5.8 %collective-permute-start.12 = (bf16[128,1024]{1,0:T(8,128)(2,1)S(1)}, bf16[128,1024]{1,0:T(8,128)(2,1)S(1)}, u32[]{:S(2)}, u32[]{:S(2)}) collective-permute-start(bf16[128,1024]{1,0:T(8,128)(2,1)S(1)} %get-tuple-element.61), channel_id=1, source_target_pairs={{0,8},{4,12},{8,16},{12,20},{16,24},{20,28},{1,9},{5,13},{9,17},{1... | collective-permute-start | bytes 786440 | tf_op jit(solution)/shard_map/ppermute | solution.py:23
  66.4 1.6 %collective-permute-start.13 = (bf16[128,1024]{1,0:T(8,128)(2,1)S(1)}, bf16[128,1024]{1,0:T(8,128)(2,1)S(1)}, u32[]{:S(2)}, u32[]{:S(2)}) collective-permute-start(bf16[128,1024]{1,0:T(8,128)(2,1)S(1)} %get-tuple-element.62), channel_id=1, source_target_pairs={{0,4},{4,0},{8,12},{12,8},{16,20},{20,16},{24,28},{28,24},{1,5},{5... | collective-permute-start | bytes 786440 | tf_op jit(solution)/shard_map/ppermute | solution.py:522
  67.9 3.3 %collective-permute-done.12 = bf16[128,1024]{1,0:T(8,128)(2,1)S(1)} collective-permute-done((bf16[128,1024]{1,0:T(8,128)(2,1)S(1)}, bf16[128,1024]{1,0:T(8,128)(2,1)S(1)}, u32[]{:S(2)}, u32[]{:S(2)}) %collective-permute-start.12) | collective-permute-done | bytes 262176 | tf_op jit(solution)/shard_map/ppermute | solution.py:23
  71.3 2.3 %collective-permute-done.13 = bf16[128,1024]{1,0:T(8,128)(2,1)S(1)} collective-permute-done((bf16[128,1024]{1,0:T(8,128)(2,1)S(1)}, bf16[128,1024]{1,0:T(8,128)(2,1)S(1)}, u32[]{:S(2)}, u32[]{:S(2)}) %collective-permute-start.13) | collective-permute-done | bytes 262176 | tf_op jit(solution)/shard_map/ppermute | solution.py:522
  (38 shorter events, 9.7 us)
Async XLA Ops:
  0.6 13.0 %collective-permute-start = (bf16[128,1024]{1,0:T(8,128)(2,1)}, bf16[128,1024]{1,0:T(8,128)(2,1)S(1)}, u32[]{:S(2)}, u32[]{:S(2)}) collective-permute-start(bf16[128,1024]{1,0:T(8,128)(2,1)} %k_ref.1), channel_id=1, source_target_pairs={{0,8},{4,12},{8,16},{12,20},{16,24},{20,28},{1,9},{5,13},{9,17},{1... | collective-permute-start | bytes 786440 | tf_op jit(solution)/shard_map/ppermute | solution.py:23
  5.6 14.2 %collective-permute-start.3 = (bf16[128,1024]{1,0:T(8,128)(2,1)}, bf16[128,1024]{1,0:T(8,128)(2,1)S(1)}, u32[]{:S(2)}, u32[]{:S(2)}) collective-permute-start(bf16[128,1024]{1,0:T(8,128)(2,1)} %q_ref.1), channel_id=1, source_target_pairs={{0,4},{4,0},{8,12},{12,8},{16,20},{20,16},{24,28},{28,24},{1,5},{5... | collective-permute-start | bytes 786440 | tf_op jit(solution)/shard_map/ppermute | solution.py:522
  7.1 12.7 %collective-permute-start.2 = (bf16[128,1024]{1,0:T(8,128)(2,1)}, bf16[128,1024]{1,0:T(8,128)(2,1)S(1)}, u32[]{:S(2)}, u32[]{:S(2)}) collective-permute-start(bf16[128,1024]{1,0:T(8,128)(2,1)} %q_ref.1), channel_id=1, source_target_pairs={{8,0},{12,4},{16,8},{20,12},{24,16},{28,20},{9,1},{13,5},{17,9},{2... | collective-permute-start | bytes 786440 | tf_op jit(solution)/shard_map/ppermute | solution.py:23
  8.4 11.4 %collective-permute-start.1 = (bf16[128,1024]{1,0:T(8,128)(2,1)}, bf16[128,1024]{1,0:T(8,128)(2,1)S(1)}, u32[]{:S(2)}, u32[]{:S(2)}) collective-permute-start(bf16[128,1024]{1,0:T(8,128)(2,1)} %v_ref.1), channel_id=1, source_target_pairs={{0,8},{4,12},{8,16},{12,20},{16,24},{20,28},{1,9},{5,13},{9,17},{1... | collective-permute-start | bytes 786440 | tf_op jit(solution)/shard_map/ppermute | solution.py:23
  13.0 7.2 %collective-permute-start.5 = (bf16[128,1024]{1,0:T(8,128)(2,1)}, bf16[128,1024]{1,0:T(8,128)(2,1)S(1)}, u32[]{:S(2)}, u32[]{:S(2)}) collective-permute-start(bf16[128,1024]{1,0:T(8,128)(2,1)} %u_ref.3), channel_id=1, source_target_pairs={{0,4},{4,0},{8,12},{12,8},{16,20},{20,16},{24,28},{28,24},{1,5},{5... | collective-permute-start | bytes 786440 | tf_op jit(solution)/shard_map/ppermute | solution.py:522
  13.6 8.7 %collective-permute-start.4 = (bf16[128,1024]{1,0:T(8,128)(2,1)}, bf16[128,1024]{1,0:T(8,128)(2,1)S(1)}, u32[]{:S(2)}, u32[]{:S(2)}) collective-permute-start(bf16[128,1024]{1,0:T(8,128)(2,1)} %u_ref.3), channel_id=1, source_target_pairs={{8,0},{12,4},{16,8},{20,12},{24,16},{28,20},{9,1},{13,5},{17,9},{2... | collective-permute-start | bytes 786440 | tf_op jit(solution)/shard_map/ppermute | solution.py:23
  14.9 1.0 %copy-start.1 = (bf16[128,1024]{1,0:T(8,128)(2,1)S(1)}, bf16[128,1024]{1,0:T(8,128)(2,1)}, u32[]{:S(2)}) copy-start(bf16[128,1024]{1,0:T(8,128)(2,1)} %k_ref.1) | copy-start | bytes 786436
  15.8 0.9 %copy-start.2 = (bf16[128,1024]{1,0:T(8,128)(2,1)S(1)}, bf16[128,1024]{1,0:T(8,128)(2,1)}, u32[]{:S(2)}) copy-start(bf16[128,1024]{1,0:T(8,128)(2,1)} %v_ref.1) | copy-start | bytes 786436
  16.8 0.9 %copy-start.3 = (bf16[128,1024]{1,0:T(8,128)(2,1)S(1)}, bf16[128,1024]{1,0:T(8,128)(2,1)}, u32[]{:S(2)}) copy-start(bf16[128,1024]{1,0:T(8,128)(2,1)} %q_ref.1) | copy-start | bytes 786436
  20.2 0.7 copy-start.4
  27.6 5.2 %copy-start.10 = (s32[8,8]{1,0:T(8,128)S(1)}, s32[8,8]{1,0:T(8,128)}, u32[]{:S(2)}) copy-start(s32[8,8]{1,0:T(8,128)} %pattern_ref.7) | copy-start | bytes 772
  27.6 8.2 %collective-permute-start.6 = (bf16[128,1152]{1,0:T(8,128)(2,1)S(1)}, bf16[128,1152]{1,0:T(8,128)(2,1)S(1)}, u32[]{:S(2)}, u32[]{:S(2)}) collective-permute-start(bf16[128,1152]{1,0:T(8,128)(2,1)S(1)} %get-tuple-element.46), channel_id=1, source_target_pairs={{0,8},{4,12},{8,16},{12,20},{16,24},{20,28},{1,9},{5,13},{9,17},{1... | collective-permute-start | bytes 884744 | tf_op jit(solution)/shard_map/ppermute | solution.py:23
  31.2 6.8 %collective-permute-start.7 = (bf16[128,1152]{1,0:T(8,128)(2,1)S(1)}, bf16[128,1152]{1,0:T(8,128)(2,1)S(1)}, u32[]{:S(2)}, u32[]{:S(2)}) collective-permute-start(bf16[128,1152]{1,0:T(8,128)(2,1)S(1)} %get-tuple-element.47), channel_id=1, source_target_pairs={{0,4},{4,0},{8,12},{12,8},{16,20},{20,16},{24,28},{28,24},{1,5},{5... | collective-permute-start | bytes 884744 | tf_op jit(solution)/shard_map/ppermute | solution.py:522
  32.8 5.2 %copy-start = (bf16[128,1024]{1,0:T(8,128)(2,1)S(1)}, bf16[128,1024]{1,0:T(8,128)(2,1)}, u32[]{:S(2)}) copy-start(bf16[128,1024]{1,0:T(8,128)(2,1)} %u_ref.3) | copy-start | bytes 786436
  39.5 15.7 %collective-permute-start.11 = (bf16[128,1152]{1,0:T(8,128)(2,1)S(1)}, bf16[128,1152]{1,0:T(8,128)(2,1)}, u32[]{:S(2)}, u32[]{:S(2)}) collective-permute-start(bf16[128,1152]{1,0:T(8,128)(2,1)S(1)} %get-tuple-element.49.a_ref), channel_id=1, source_target_pairs={{0,4},{4,0},{8,12},{12,8},{16,20},{20,16},{24,28},{28,24},{1,5},{5... | collective-permute-start | bytes 884744 | tf_op jit(solution)/shard_map/ppermute | solution.py:522
  41.1 14.2 %collective-permute-start.10 = (bf16[128,1152]{1,0:T(8,128)(2,1)S(1)}, bf16[128,1152]{1,0:T(8,128)(2,1)}, u32[]{:S(2)}, u32[]{:S(2)}) collective-permute-start(bf16[128,1152]{1,0:T(8,128)(2,1)S(1)} %get-tuple-element.49.a_ref), channel_id=1, source_target_pairs={{8,0},{12,4},{16,8},{20,12},{24,16},{28,20},{9,1},{13,5},{17,9},{2... | collective-permute-start | bytes 884744 | tf_op jit(solution)/shard_map/ppermute | solution.py:23
  48.4 6.8 %copy-start.5 = (bf16[128,1024]{1,0:T(8,128)(2,1)S(1)}, bf16[128,1024]{1,0:T(8,128)(2,1)}, u32[]{:S(2)}) copy-start(bf16[128,1024]{1,0:T(8,128)(2,1)} %copy-done.4) | copy-start | bytes 786436
  48.4 6.9 %copy-start.7 = (bf16[128,1024]{1,0:T(8,128)(2,1)S(1)}, bf16[128,1024]{1,0:T(8,128)(2,1)}, u32[]{:S(2)}) copy-start(bf16[128,1024]{1,0:T(8,128)(2,1)} %copy-done.6) | copy-start | bytes 786436
  48.4 6.9 %copy-start.9 = (f32[128,128]{1,0:T(8,128)S(1)}, f32[128,128]{1,0:T(8,128)}, u32[]{:S(2)}) copy-start(f32[128,128]{1,0:T(8,128)} %copy-done.8) | copy-start | bytes 196612
  48.4 6.8 %collective-permute-start.9 = (f32[8,128]{1,0:T(8,128)S(1)}, f32[8,128]{1,0:T(8,128)S(1)}, u32[]{:S(2)}, u32[]{:S(2)}) collective-permute-start(f32[8,128]{1,0:T(8,128)S(1)} %psum.7.sums_ref), channel_id=1, source_target_pairs={{0,4},{4,0},{8,12},{12,8},{16,20},{20,16},{24,28},{28,24},{1,5},{5... | collective-permute-start | bytes 12296 | tf_op jit(solution)/shard_map/ppermute | solution.py:522
  49.0 6.2 %collective-permute-start.8 = (f32[8,128]{1,0:T(8,128)S(1)}, f32[8,128]{1,0:T(8,128)S(1)}, u32[]{:S(2)}, u32[]{:S(2)}) collective-permute-start(f32[8,128]{1,0:T(8,128)S(1)} %psum.7.sums_ref), channel_id=1, source_target_pairs={{8,0},{12,4},{16,8},{20,12},{24,16},{28,20},{9,1},{13,5},{17,9},{2... | collective-permute-start | bytes 12296 | tf_op jit(solution)/shard_map/ppermute | solution.py:23
  58.9 16.4 %collective-permute-start.14 = (bf16[2,128,1024]{2,1,0:T(8,128)(2,1)S(1)}, bf16[2,128,1024]{2,1,0:T(8,128)(2,1)S(1)}, u32[]{:S(2)}, u32[]{:S(2)}) collective-permute-start(bf16[2,128,1024]{2,1,0:T(8,128)(2,1)S(1)} %get-tuple-element.65), channel_id=1, source_target_pairs={{8,0},{12,4},{16,8},{20,12},{24,16},{28,20},{9,1},{13,5},{17,9},{2... | collective-permute-start | bytes 1572872 | tf_op jit(solution)/shard_map/ppermute | solution.py:23
  60.5 10.7 %collective-permute-start.12 = (bf16[128,1024]{1,0:T(8,128)(2,1)S(1)}, bf16[128,1024]{1,0:T(8,128)(2,1)S(1)}, u32[]{:S(2)}, u32[]{:S(2)}) collective-permute-start(bf16[128,1024]{1,0:T(8,128)(2,1)S(1)} %get-tuple-element.61), channel_id=1, source_target_pairs={{0,8},{4,12},{8,16},{12,20},{16,24},{20,28},{1,9},{5,13},{9,17},{1... | collective-permute-start | bytes 786440 | tf_op jit(solution)/shard_map/ppermute | solution.py:23
  66.4 7.2 %collective-permute-start.13 = (bf16[128,1024]{1,0:T(8,128)(2,1)S(1)}, bf16[128,1024]{1,0:T(8,128)(2,1)S(1)}, u32[]{:S(2)}, u32[]{:S(2)}) collective-permute-start(bf16[128,1024]{1,0:T(8,128)(2,1)S(1)} %get-tuple-element.62), channel_id=1, source_target_pairs={{0,4},{4,0},{8,12},{12,8},{16,20},{20,16},{24,28},{28,24},{1,5},{5... | collective-permute-start | bytes 786440 | tf_op jit(solution)/shard_map/ppermute | solution.py:522
  (2 other events, 1.3 us)

commit v3 on v0

--- a/solution.py
+++ b/solution.py
@@ -1,6 +1,11 @@
+import functools
+import math
+
 import jax
 import jax.numpy as jnp
 from jax import lax
+from jax.experimental import pallas as pl
+from jax.experimental.pallas import tpu as pltpu
 from jax.sharding import PartitionSpec as P
 
 HD = 128
@@ -75,7 +80,7 @@
     return jnp.stack(pieces, axis=1)
 
 
-def shards(queries, keys, values, pattern, upstream):
+def generic_shards(queries, keys, values, pattern, upstream):
     tokens_here = queries.shape[0]
     heads_here = queries.shape[1] // HD
     blocks = tokens_here // BLOCK
@@ -186,6 +191,480 @@
     return (normed, grad_queries, grad_keys, grad_values)
 
 
+NT = (((1,), (1,)), ((), ()))
+NN = (((1,), (0,)), ((), ()))
+TN = (((0,), (0,)), ((), ()))
+SCALE = HD ** (-0.5)
+TAIL = 32
+
+
+class Flags:
+    def __init__(self, pattern_ref=None):
+        me, member = lax.axis_index("ctx"), lax.axis_index("head")
+        self.odd = lax.rem(me, 2) == 1
+        self.half = member >= lax.axis_size("head") // 2
+        if pattern_ref is None:
+            return
+        blocks = pattern_ref.shape[0]
+        ahead, partner = jnp.minimum(me + 2, blocks - 1), jnp.where(self.odd, me - 1, me + 1)
+        self.near = pattern_ref[me, 1] >= 0
+        self.far_in, self.side_in = pattern_ref[me, 2] >= 0, pattern_ref[me, 0] >= 0
+        self.ahead = me + 2 < blocks
+        self.far = jnp.logical_and(self.ahead, pattern_ref[ahead, 2] >= 0)
+        self.side = jnp.logical_and(
+            jnp.logical_or(jnp.logical_not(self.odd), me >= 2), pattern_ref[partner, 0] >= 0
+        )
+
+
+def mm(a, b, dims):
+    return lax.dot_general(a, b, dims, preferred_element_type=jnp.float32)
+
+
+def rows_of(h):
+    return slice(h * HD, (h + 1) * HD)
+
+
+def causal_mask():
+    keys = lax.broadcasted_iota(jnp.int32, (BLOCK, BLOCK), 0)
+    return keys <= lax.broadcasted_iota(jnp.int32, (BLOCK, BLOCK), 1)
+
+
+def split_rows(rows):
+    first = rows.astype(jnp.bfloat16).astype(jnp.float32)
+    second = (rows - first).astype(jnp.bfloat16).astype(jnp.float32)
+    third = rows - first - second
+    return jnp.concatenate([first, second, third, jnp.zeros_like(rows)], axis=0).astype(jnp.bfloat16)
+
+
+def joined_rows(tile):
+    wide = tile.astype(jnp.float32)
+    return wide[0:8] + wide[8:16] + wide[16:24]
+
+
+def stack_rows(rows):
+    return jnp.concatenate(rows + [jnp.zeros((1, BLOCK), jnp.float32)] * (8 - len(rows)), axis=0)
+
+
+def score_tile(keys, queries):
+    return mm(keys, queries, NT) * SCALE
+
+
+def softmax_parts(pairs):
+    tops = [scores.max(axis=0, keepdims=True) for scores, _ in pairs]
+    weights = [jnp.exp(scores - top) for (scores, _), top in zip(pairs, tops)]
+    totals = [w.sum(axis=0, keepdims=True) for w in weights]
+    outs = [
+        mm(value, w.astype(jnp.bfloat16), TN) * (1.0 / total)
+        for (_, value), w, total in zip(pairs, weights, totals)
+    ]
+    return [(out, top, top + jnp.log(total), w) for out, top, total, w in zip(outs, tops, totals, weights)]
+
+
+def payload_kernel(heads, q_ref, k_ref, v_ref, u_ref, up_ref, down_ref, sems):
+    half = Flags().half
+    top, bottom = pl.ds(0, BLOCK), pl.ds(BLOCK, BLOCK)
+
+    def move(sources):
+        targets = (up_ref.at[top], up_ref.at[bottom], down_ref.at[top], down_ref.at[bottom])
+        copies = [
+            pltpu.make_async_copy(source, target, sems.at[n])
+            for n, (source, target) in enumerate(zip(sources, targets))
+        ]
+        for copy in copies:
+            copy.start()
+        for copy in copies:
+            copy.wait()
+
+    @pl.when(jnp.logical_not(half))
+    def _():
+        move((k_ref, v_ref, q_ref, u_ref))
+
+    @pl.when(half)
+    def _():
+        move((q_ref, u_ref, k_ref, v_ref))
+
+
+def diagonal_kernel(heads, q_ref, k_ref, v_ref, u_ref, out_ref, lse_ref, ut_ref):
+    causal = causal_mask()
+    rows = []
+    for h in range(heads):
+        at = rows_of(h)
+        scores = jnp.where(causal, score_tile(k_ref[:, at], q_ref[:, at]), NEG_BIG)
+        ((out, _, lse, _),) = softmax_parts([(scores, v_ref[:, at])])
+        out_ref[at] = out
+        rows.append(lse)
+        ut_ref[at] = u_ref[:, at].T
+    lse_ref[...] = stack_rows(rows)
+
+
+def helper_kernel(
+    heads, up_ref, down_ref, qx_ref, k_ref, v_ref, oz_ref, ox_ref, ez_ref, ex_ref, mz_ref, mx_ref
+):
+    flags = Flags()
+    odd, half = flags.odd, flags.half
+    first, second = slice(0, BLOCK), slice(BLOCK, 2 * BLOCK)
+    z_rows, x_rows, z_tops, x_tops = [], [], [], []
+    for start in range(0, heads, 2):
+        pairs = []
+        for h in range(start, start + 2):
+            at = rows_of(h)
+            up_a, down_a = up_ref[first, at], down_ref[first, at]
+            k2, qz = jnp.where(half, down_a, up_a), jnp.where(half, up_a, down_a)
+            v2 = jnp.where(half, down_ref[second, at], up_ref[second, at])
+            pairs.append((score_tile(k2, qz), v2))
+            ks, vs = jnp.where(odd, k2, k_ref[:, at]), jnp.where(odd, v2, v_ref[:, at])
+            pairs.append((score_tile(ks, qx_ref[:, at]), vs))
+        for n, (out, top, lse, weights) in enumerate(softmax_parts(pairs)):
+            at = rows_of(start + n // 2)
+            o_ref, e_ref = ((oz_ref, ez_ref), (ox_ref, ex_ref))[n % 2]
+            o_ref[at] = out.astype(jnp.bfloat16)
+            e_ref[at] = weights
+            (z_rows, x_rows)[n % 2].append(lse)
+            (z_tops, x_tops)[n % 2].append(top)
+    tail = slice(heads * HD, heads * HD + TAIL)
+    oz_ref[tail] = split_rows(stack_rows(z_rows))
+    ox_ref[tail] = split_rows(stack_rows(x_rows))
+    mz_ref[...] = stack_rows(z_tops)
+    mx_ref[...] = stack_rows(x_tops)
+
+
+def own_kernel(
+    heads, pattern_ref, up_ref, down_ref, q_ref, ux_ref, out_ref, lse_ref, own_ref, total_ref, uzt_ref, uxt_ref
+):
+    flags = Flags(pattern_ref)
+    half, near = flags.half, flags.near
+    first, second = slice(0, BLOCK), slice(BLOCK, 2 * BLOCK)
+    before = lse_ref[...]
+    rows = []
+    for h in range(heads):
+        at = rows_of(h)
+        k2 = jnp.where(half, down_ref[first, at], up_ref[first, at])
+        up_b, down_b = up_ref[second, at], down_ref[second, at]
+        v2, uz = jnp.where(half, down_b, up_b), jnp.where(half, up_b, down_b)
+        ((out, _, lse, _),) = softmax_parts([(score_tile(k2, q_ref[:, at]), v2)])
+        lse = jnp.where(near, lse, NEG_BIG)
+        old = before[h : h + 1]
+        highest = jnp.maximum(old, lse)
+        total = highest + jnp.log(jnp.exp(old - highest) + jnp.exp(lse - highest))
+        own_ref[at] = out_ref[at] * jnp.exp(old - total) + out * jnp.exp(lse - total)
+        rows.append(total)
+        uzt_ref[at] = uz.T
+        uxt_ref[at] = ux_ref[:, at].T
+    total_ref[...] = stack_rows(rows)
+
+
+def merge_kernel(heads, pattern_ref, own_ref, lse_ref, rz_ref, rx_ref, ut_ref, a_ref, sums_ref):
+    flags = Flags(pattern_ref)
+    tail = slice(heads * HD, heads * HD + TAIL)
+    own = lse_ref[...]
+    z = jnp.where(flags.far_in, joined_rows(rz_ref[tail]), NEG_BIG)
+    x = jnp.where(flags.side_in, joined_rows(rx_ref[tail]), NEG_BIG)
+    highest = jnp.maximum(own, jnp.maximum(z, x))
+    total = highest + jnp.log(jnp.exp(own - highest) + jnp.exp(z - highest) + jnp.exp(x - highest))
+    own, z, x = jnp.exp(own - total), jnp.exp(z - total), jnp.exp(x - total)
+    squares = jnp.zeros((8, BLOCK), jnp.float32)
+    crosses = jnp.zeros((8, BLOCK), jnp.float32)
+    for h in range(heads):
+        at, row = rows_of(h), slice(h, h + 1)
+        out = (
+            own_ref[at] * own[row]
+            + rz_ref[at].astype(jnp.float32) * z[row]
+            + rx_ref[at].astype(jnp.float32) * x[row]
+        ).astype(jnp.bfloat16)
+        a_ref[at] = out
+        wide = out.astype(jnp.float32)
+        squares += (wide * wide).reshape(HD // 8, 8, BLOCK).sum(axis=0)
+        crosses += (wide * ut_ref[at].astype(jnp.float32)).reshape(HD // 8, 8, BLOCK).sum(axis=0)
+    a_ref[tail] = split_rows(total)
+    sums_ref[...] = stack_rows([squares.sum(axis=0, keepdims=True), crosses.sum(axis=0, keepdims=True)])
+
+
+def norm_rows(sums_ref):
+    inverse = lax.rsqrt(sums_ref[0:1] / WIDTH + EPSILON)
+    return inverse, inverse**3 * sums_ref[1:2] / WIDTH
+
+
+def upstream_part(norm, u, a):
+    inverse, factor = norm
+    wide = a.astype(jnp.float32)
+    grad = (inverse * u.astype(jnp.float32) - wide * factor).astype(jnp.bfloat16)
+    return grad, jnp.sum(grad.astype(jnp.float32) * wide, axis=0, keepdims=True)
+
+
+def pair_back(q, k, v, grad, delta, lse, keep):
+    weights = jnp.exp(jnp.where(keep, score_tile(k, q), NEG_BIG) - lse)
+    dscore = (weights * (mm(v, grad, NN) - delta) * SCALE).astype(jnp.bfloat16)
+    return mm(dscore, q, NN), mm(weights.astype(jnp.bfloat16), grad, NT), mm(dscore, k, TN)
+
+
+def near_back_kernel(
+    heads, pattern_ref, sums_ref, q_ref, up_ref, down_ref, a_ref, ut_ref, dq_ref, dkv2_ref, grad_ref, delta_ref
+):
+    flags = Flags(pattern_ref)
+    half, near = flags.half, flags.near
+    first, second = slice(0, BLOCK), slice(BLOCK, 2 * BLOCK)
+    norm = norm_rows(sums_ref)
+    lse = joined_rows(a_ref[heads * HD : heads * HD + TAIL])
+    deltas = []
+    for h in range(heads):
+        at = rows_of(h)
+        grad, delta = upstream_part(norm, ut_ref[at], a_ref[at])
+        k2 = jnp.where(half, down_ref[first, at], up_ref[first, at])
+        v2 = jnp.where(half, down_ref[second, at], up_ref[second, at])
+        dkv2_ref[0, :, at], dkv2_ref[1, :, at], dq_ref[:, at] = pair_back(
+            q_ref[:, at], k2, v2, grad, delta, lse[h : h + 1], near
+        )
+        grad_ref[at] = grad
+        deltas.append(delta)
+    delta_ref[...] = stack_rows(deltas)
+
+
+def diagonal_back_kernel(
+    heads,
+    sums_ref,
+    q_ref,
+    k_ref,
+    v_ref,
+    a_ref,
+    grad_ref,
+    delta_ref,
+    dq_in_ref,
+    dside_ref,
+    normed_ref,
+    dq_ref,
+    dkv_ref,
+):
+    inverse, _ = norm_rows(sums_ref)
+    lse = joined_rows(a_ref[heads * HD : heads * HD + TAIL])
+    causal = causal_mask()
+    for h in range(heads):
+        at, row = rows_of(h), slice(h, h + 1)
+        normed_ref[:, at] = (a_ref[at].astype(jnp.float32) * inverse).astype(jnp.bfloat16).T
+        dk, dv, dq = pair_back(
+            q_ref[:, at], k_ref[:, at], v_ref[:, at], grad_ref[at], delta_ref[row], lse[row], causal
+        )
+        dkv_ref[0, :, at] = dside_ref[0, :, at] + dk
+        dkv_ref[1, :, at] = dside_ref[1, :, at] + dv
+        dq_ref[:, at] = dq_in_ref[:, at] + dq
+
+
+def helper_back_kernel(
+    heads,
+    pattern_ref,
+    sz_ref,
+    sx_ref,
+    up_ref,
+    down_ref,
+    qx_ref,
+    k_ref,
+    v_ref,
+    az_ref,
+    ax_ref,
+    uzt_ref,
+    uxt_ref,
+    ez_ref,
+    ex_ref,
+    mz_ref,
+    mx_ref,
+    own_ref,
+    up_out_ref,
+    down_out_ref,
+    dqx_ref,
+    dside_ref,
+):
+    flags = Flags(pattern_ref)
+    odd, half = flags.odd, flags.half
+    first, second = slice(0, BLOCK), slice(BLOCK, 2 * BLOCK)
+    tail = slice(heads * HD, heads * HD + TAIL)
+    z_norm, x_norm = norm_rows(sz_ref), norm_rows(sx_ref)
+    z_scale = jnp.where(flags.far, jnp.exp(mz_ref[...] - joined_rows(az_ref[tail])), 0.0)
+    x_scale = jnp.where(flags.side, jnp.exp(mx_ref[...] - joined_rows(ax_ref[tail])), 0.0)
+    share = odd.astype(jnp.float32)
+
+    def one(norm, u, a, weights, value):
+        grad, delta = upstream_part(norm, u, a)
+        dscore = (weights * (mm(value, grad, NN) - delta) * SCALE).astype(jnp.bfloat16)
+        return grad, weights.astype(jnp.bfloat16), dscore
+
+    for h in range(heads):
+        at, row = rows_of(h), slice(h, h + 1)
+        up_a, down_a = up_ref[first, at], down_ref[first, at]
+        k2, qz = jnp.where(half, down_a, up_a), jnp.where(half, up_a, down_a)
+        v2 = jnp.where(half, down_ref[second, at], up_ref[second, at])
+        ks, vs, qx = jnp.where(odd, k2, k_ref[:, at]), jnp.where(odd, v2, v_ref[:, at]), qx_ref[:, at]
+        gz, pz, dz = one(z_norm, uzt_ref[at], az_ref[at], ez_ref[at] * z_scale[row], v2)
+        gx, px, dx = one(x_norm, uxt_ref[at], ax_ref[at], ex_ref[at] * x_scale[row], vs)
+        dks, dvs = mm(dx, qx, NN), mm(px, gx, NT)
+        dk2 = (own_ref[0, :, at] + mm(dz, qz, NN) + share * dks).astype(jnp.bfloat16)
+        dv2 = (own_ref[1, :, at] + mm(pz, gz, NT) + share * dvs).astype(jnp.bfloat16)
+        dqz = mm(dz, k2, TN).astype(jnp.bfloat16)
+        dqx_ref[:, at] = mm(dx, ks, TN).astype(jnp.bfloat16)
+        up_out_ref[first, at] = jnp.where(half, dk2, dqz)
+        up_out_ref[second, at] = dv2
+        down_out_ref[first, at] = jnp.where(half, dqz, dk2)
+        down_out_ref[second, at] = dv2
+        dside_ref[0, :, at] = (1.0 - share) * dks
+        dside_ref[1, :, at] = (1.0 - share) * dvs
+
+
+def final_kernel(heads, pattern_ref, up_ref, down_ref, dqx_ref, dq_own_ref, dkv_own_ref, dq_ref, dk_ref, dv_ref):
+    flags = Flags(pattern_ref)
+    half = flags.half
+    first, second = slice(0, BLOCK), slice(BLOCK, 2 * BLOCK)
+    ahead = flags.ahead.astype(jnp.float32)
+    far = flags.far_in.astype(jnp.float32)
+    for h in range(heads):
+        at = rows_of(h)
+        up_a, down_a = up_ref[first, at], down_ref[first, at]
+        dqz = jnp.where(half, down_a, up_a).astype(jnp.float32) * far
+        dk = jnp.where(half, up_a, down_a).astype(jnp.float32) * ahead
+        dv = jnp.where(half, up_ref[second, at], down_ref[second, at]).astype(jnp.float32) * ahead
+        dq_ref[:, at] = (dq_own_ref[:, at] + dqx_ref[:, at].astype(jnp.float32) + dqz).astype(jnp.bfloat16)
+        dk_ref[:, at] = (dkv_own_ref[0, :, at] + dk).astype(jnp.bfloat16)
+        dv_ref[:, at] = (dkv_own_ref[1, :, at] + dv).astype(jnp.bfloat16)
+
+
+def call(kernel, heads, flags, arrays, outs, flops, space=pltpu.VMEM, scratch=(), limit=24):
+    moved = sum(math.prod(a.shape) * a.dtype.itemsize for a in (*arrays, *outs))
+    return pl.pallas_call(
+        functools.partial(kernel, heads),
+        out_shape=outs,
+        in_specs=[pl.BlockSpec(memory_space=pltpu.SMEM)] * len(flags)
+        + [pl.BlockSpec(memory_space=space)] * len(arrays),
+        out_specs=[pl.BlockSpec(memory_space=pltpu.VMEM)] * len(outs),
+        scratch_shapes=scratch,
+        compiler_params=pltpu.CompilerParams(vmem_limit_bytes=limit * 2**20),
+        cost_estimate=pl.CostEstimate(flops=flops, bytes_accessed=moved, transcendentals=0),
+    )(*flags, *arrays)
+
+
+def cycles(blocks, members):
+    route = []
+    for block in range(blocks):
+        for member in range(members):
+            rising = member < members // 2
+            other = member + members // 2 if rising else member - members // 2
+            target = block + 2 if rising else block - 2
+            inside = 0 <= target < blocks
+            route.append(
+                (block * members + member, target * members + member if inside else block * members + other)
+            )
+    return route
+
+
+def meeting_shards(queries, keys, values, pattern, upstream):
+    tokens, width = queries.shape
+    heads = width // HD
+    blocks, members = lax.axis_size("ctx"), lax.axis_size("head")
+    flags = (pattern,)
+    unit = heads * 2 * BLOCK**3
+    rising = cycles(blocks, members)
+    falling = [(target, source) for source, target in rising]
+
+    def cycle(up_array, down_array):
+        return lax.ppermute(up_array, ("ctx", "head"), rising), lax.ppermute(
+            down_array, ("ctx", "head"), falling
+        )
+
+    def swap(array):
+        return lax.ppermute(array, "ctx", [(i, i ^ 1) for i in range(blocks)])
+
+    def ring(array, distance):
+        return lax.ppermute(array, "ctx", [(i, (i + distance) % blocks) for i in range(blocks)])
+
+    def struct(*shape, dtype=jnp.bfloat16):
+        return jax.ShapeDtypeStruct(shape, dtype)
+
+    wide = struct(tokens, width, dtype=jnp.float32)
+    wide_t = struct(width, tokens, dtype=jnp.float32)
+    wide_pair = struct(2, tokens, width, dtype=jnp.float32)
+    flat, flat_t = struct(tokens, width), struct(width, tokens)
+    double = struct(2 * tokens, width)
+    message = struct(width + TAIL, tokens)
+    rows = struct(8, tokens, dtype=jnp.float32)
+
+    up_out, down_out = call(
+        payload_kernel,
+        heads,
+        (),
+        [pltpu.with_memory_space_constraint(a, pltpu.HBM) for a in (queries, keys, values, upstream)],
+        [pltpu.VMEM((2 * tokens, width), jnp.bfloat16)] * 2,
+        0,
+        space=pltpu.HBM,
+        scratch=(pltpu.SemaphoreType.DMA((4,)),),
+    )
+    up_in, down_in = cycle(up_out, down_out)
+    queries_x, upstream_x = swap(queries), swap(upstream)
+    diagonal, diagonal_lse, upstream_t = call(
+        diagonal_kernel, heads, (), (queries, keys, values, upstream), (wide_t, rows, flat_t), 3 * unit
+    )
+    up_in, down_in, queries_x, upstream_x = lax.optimization_barrier((up_in, down_in, queries_x, upstream_x))
+    out_z, out_x, ez, ex, mz, mx = call(
+        helper_kernel,
+        heads,
+        (),
+        (up_in, down_in, queries_x, keys, values),
+        (message, message, wide_t, wide_t, rows, rows),
+        4 * unit,
+    )
+    back_z, back_x = ring(out_z, 2), swap(out_x)
+    own, own_lse, upstream_zt, upstream_xt = call(
+        own_kernel,
+        heads,
+        flags,
+        (up_in, down_in, queries, upstream_x, diagonal, diagonal_lse),
+        (wide_t, rows, flat_t, flat_t),
+        3 * unit,
+    )
+    attention, sums = call(
+        merge_kernel, heads, flags, (own, own_lse, back_z, back_x, upstream_t), (message, rows), unit // 64
+    )
+    others = [
+        lax.ppermute(sums, "head", [(i, i ^ step) for i in range(members)]) for step in range(1, members)
+    ]
+    attention_z, attention_x = ring(attention, -2), swap(attention)
+    sums = functools.reduce(jnp.add, others, sums)
+    sums_z, sums_x = ring(sums, -2), swap(sums)
+    dq_own, grads2_own, grad_t, delta = call(
+        near_back_kernel,
+        heads,
+        flags,
+        (sums, queries, up_in, down_in, attention, upstream_t),
+        (wide, wide_pair, flat_t, rows),
+        5 * unit,
+    )
+    up_out, down_out, dq_x, dside = call(
+        helper_back_kernel,
+        heads,
+        flags,
+        (sums_z, sums_x, up_in, down_in, queries_x, keys, values, attention_z, attention_x)
+        + (upstream_zt, upstream_xt, ez, ex, mz, mx, grads2_own),
+        (double, double, flat, wide_pair),
+        8 * unit,
+    )
+    up_in, down_in = cycle(up_out, down_out)
+    dq_x = swap(dq_x)
+    normed, dq_own, grads_own = call(
+        diagonal_back_kernel,
+        heads,
+        (),
+        (sums, queries, keys, values, attention, grad_t, delta, dq_own, dside),
+        (flat, wide, wide_pair),
+        6 * unit,
+    )
+    grad_queries, grad_keys, grad_values = call(
+        final_kernel, heads, flags, (up_in, down_in, dq_x, dq_own, grads_own), (flat, flat, flat), 0
+    )
+    return (normed, grad_queries, grad_keys, grad_values)
+
+
+def shards(queries, keys, values, pattern, upstream):
+    fits = lax.axis_size("ctx") == 8 and lax.axis_size("head") == 4 and queries.shape == (BLOCK, 8 * HD)
+    if fits:
+        return meeting_shards(queries, keys, values, pattern, upstream)
+    return generic_shards(queries, keys, values, pattern, upstream)
+
+
 def solution(mesh):
     return jax.shard_map(
         shards,

time: 133 us -> 60 us (0.45)
  waiting for transfers between devices: 72.6 us -> 23 us
  Pallas kernels: 0 us -> 17.1 us
  local copies, waits for them, and re-layouts: 16.2 us -> 0.02 us
  matrix products: 13.4 us -> 0 us
  other arithmetic: 6.09 us -> 0.01 us
  blocking collectives: 5.73 us -> 0 us
  starting transfers between devices: 16.9 us -> 19 us
    ppermute x6 -> x16, waiting for transfers between devices: 72.6 us -> 23 us  [the longest x6 15.5 us: swap(): return lax.ppermute(array, 'ctx', [(i, i ^ 1) for i in range(blocks)])]
    pallas_call x0 -> x9, Pallas kernels: none -> 17.1 us  [call(): pl.pallas_call(functools.partial(kernel, heads), out_shape=outs, in_specs...]
    dot_general x13 -> x0, matrix products: 13.4 us -> none  [the longest x1 3.27 us: pair_grads(): jnp.einsum('pqhd,pkhd->phqk', query_tiles, key_tiles, preferred_element_t...]
    unnamed x33 -> x10, local copies, waits for them, and re-layouts: 8.6 us -> 0.02 us
    another operation x7 -> x0, local copies, waits for them, and re-layouts: 6.02 us -> none  [the longest x3 2.9 us: shards(): pair_kv = jnp.stack(gathered, axis=1)]
    psum x1 -> x0, blocking collectives: 5.73 us -> none  [shards(): square_sum = lax.psum(jnp.sum(attn_wide * attn_wide, axis=1), 'head')]
    and x2 -> x0, other arithmetic: 2.18 us -> none  [shards(): (own_rows >= 0)[:, :, None, None]]
    ppermute x6 -> x16, starting transfers between devices: 16.9 us -> 19 us  [the longest x6 6.59 us: swap(): return lax.ppermute(array, 'ctx', [(i, i ^ 1) for i in range(blocks)])]
  transfers between devices with their start and end apart: 6 -> 16, of which waited for: 5 -> 9; matrix products, arithmetic and copies ran while one was open for 9% -> 0% of each run, Pallas kernels for 0% -> 16%
where the time goes in v3:
time: 60 us; the launch traced here: 59.8 us
  waiting for transfers between devices  23 us (38%)
  starting transfers between devices  19 us (32%)
  Pallas kernels  17.1 us (29%)
  between operations  0.76 us (1%)
    pallas_call x9, Pallas kernels, call(): pl.pallas_call(functools.partial(kernel, heads), out_shape=outs, in_specs...  17.1 us
    ppermute x6, waiting for transfers between devices, swap(): return lax.ppermute(array, 'ctx', [(i, i ^ 1) for i in range(blocks)])  15.5 us
    ppermute x6, starting transfers between devices, swap(): return lax.ppermute(array, 'ctx', [(i, i ^ 1) for i in range(blocks)])  6.59 us
    ppermute x3, starting transfers between devices, ring(): lax.ppermute(array, 'ctx', [(i, (i + distance) % blocks) for i in range(b...  5.34 us
    ppermute x2, waiting for transfers between devices, cycle(): lax.ppermute(up_array, ('ctx', 'head'), rising)  4.15 us
    ppermute x2, starting transfers between devices, cycle(): lax.ppermute(up_array, ('ctx', 'head'), rising)  3.48 us
    ppermute x3, starting transfers between devices, meeting_shards(): lax.ppermute(sums, 'head', [(i, i ^ step) for i in range(members)])  1.86 us
    ppermute x3, waiting for transfers between devices, meeting_shards(): lax.ppermute(sums, 'head', [(i, i ^ step) for i in range(members)])  1.78 us
  transfers between devices with their start and end apart: 16, of which 9 were waited for; matrix products, arithmetic and copies ran while one was open for 0% of the time, Pallas kernels for 16%

profile of v3, /device:TPU:0, one launch (start us, length us, event | category | flops | bytes accessed | tf_op | source)
XLA Modules:
  0.0 59.8 jit_solution(973220062434148843)
XLA Ops:
  0.7 1.3 %shard_map.84 = (bf16[256,1024]{1,0:T(8,128)(2,1)S(1)}, bf16[256,1024]{1,0:T(8,128)(2,1)S(1)}) custom-call(bf16[128,1024]{1,0:T(8,128)(2,1)} %q_ref.9, bf16[128,1024]{1,0:T(8,128)(2,1)} %k_ref.9, bf16[128,1024]{1,0:T(8,128)(2,1)} %v_ref.9, bf16[128,1024]{1,0:T(8,128)(2,1)} %u_ref.3), custom_call_target="tpu_custom_call" | custom-call | bytes 2097152 | tf_op jit(solution)/shard_map/pallas_call | solution.py:529
  2.0 3.1 %collective-permute-start = (bf16[256,1024]{1,0:T(8,128)(2,1)S(1)}, bf16[256,1024]{1,0:T(8,128)(2,1)S(1)}, u32[]{:S(2)}, u32[]{:S(2)}) collective-permute-start(bf16[256,1024]{1,0:T(8,128)(2,1)S(1)} %get-tuple-element.39), channel_id=1, source_target_pairs={{0,8},{1,9},{2,0},{3,1},{4,12},{5,13},{6,4},{7,5},{8,16},{9,17},{1... | collective-permute-start | bytes 1572872 | tf_op jit(solution)/shard_map/ppermute | solution.py:565
  5.1 1.9 %collective-permute-start.2 = (bf16[128,1024]{1,0:T(8,128)(2,1)S(1)}, bf16[128,1024]{1,0:T(8,128)(2,1)S(1)}, u32[]{:S(2)}, u32[]{:S(2)}) collective-permute-start(bf16[128,1024]{1,0:T(8,128)(2,1)S(1)} %copy-done.2), channel_id=1, source_target_pairs={{0,4},{4,0},{8,12},{12,8},{16,20},{20,16},{24,28},{28,24},{1,5},{5... | collective-permute-start | bytes 786440 | tf_op jit(solution)/shard_map/ppermute | solution.py:570
  7.1 7.2 %collective-permute-done.2.qx_ref = bf16[128,1024]{1,0:T(8,128)(2,1)S(1)} collective-permute-done((bf16[128,1024]{1,0:T(8,128)(2,1)S(1)}, bf16[128,1024]{1,0:T(8,128)(2,1)S(1)}, u32[]{:S(2)}, u32[]{:S(2)}) %collective-permute-start.2) | collective-permute-done | bytes 262176 | tf_op jit(solution)/shard_map/ppermute | solution.py:570
  14.3 4.2 %collective-permute-done.3.ux_ref = bf16[128,1024]{1,0:T(8,128)(2,1)S(1)} collective-permute-done((bf16[128,1024]{1,0:T(8,128)(2,1)S(1)}, bf16[128,1024]{1,0:T(8,128)(2,1)S(1)}, u32[]{:S(2)}, u32[]{:S(2)}) %collective-permute-start.3) | collective-permute-done | bytes 262176 | tf_op jit(solution)/shard_map/ppermute | solution.py:570
  18.5 1.1 %shard_map.87 = (bf16[1056,128]{1,0:T(8,128)(2,1)S(1)}, bf16[1056,128]{1,0:T(8,128)(2,1)S(1)}, f32[1024,128]{1,0:T(8,128)S(1)}, f32[1024,128]{1,0:T(8,128)S(1)},...) custom-call(bf16[256,1024]{1,0:T(8,128)(2,1)S(1)} %collective-permute-done.up_ref, ...), custom_call_target="tpu_custom_call" | custom-call | flops 134217728 | bytes 3432448 | tf_op jit(solution)/shard_map/pallas_call | solution.py:529
  19.6 1.8 %collective-permute-start.4 = (bf16[1056,128]{1,0:T(8,128)(2,1)S(1)}, bf16[1056,128]{1,0:T(8,128)(2,1)S(1)}, u32[]{:S(2)}, u32[]{:S(2)}) collective-permute-start(bf16[1056,128]{1,0:T(8,128)(2,1)S(1)} %get-tuple-element.49), channel_id=1, source_target_pairs={{0,8},{4,12},{8,16},{12,20},{16,24},{20,28},{24,0},{28,4},{1,9},{5... | collective-permute-start | bytes 811016 | tf_op jit(solution)/shard_map/ppermute | solution.py:573
  21.4 1.5 %collective-permute-start.5 = (bf16[1056,128]{1,0:T(8,128)(2,1)S(1)}, bf16[1056,128]{1,0:T(8,128)(2,1)S(1)}, u32[]{:S(2)}, u32[]{:S(2)}) collective-permute-start(bf16[1056,128]{1,0:T(8,128)(2,1)S(1)} %get-tuple-element.50), channel_id=1, source_target_pairs={{0,4},{4,0},{8,12},{12,8},{16,20},{20,16},{24,28},{28,24},{1,5},{5... | collective-permute-start | bytes 811016 | tf_op jit(solution)/shard_map/ppermute | solution.py:570
  22.9 1.8 %shard_map.85 = (f32[1024,128]{1,0:T(8,128)S(1)}, f32[8,128]{1,0:T(8,128)S(1)}, bf16[1024,128]{1,0:T(8,128)(2,1)S(1)}) custom-call(bf16[128,1024]{1,0:T(8,128)(2,1)S(1)} %copy-done.2, bf16[128,1024]{1,0:T(8,128)(2,1)S(1)} %copy-done, bf16[128,1024]{1,0:T(8,128)(2,1)S(1)} %copy-done.1, bf16[128,1024]{1,0:T(8,128)(2,1)S(1)} %copy-done.3), custom_call_target="tpu_custom_call" | custom-call | flops 100663296 | bytes 1839104 | tf_op jit(solution)/shard_map/pallas_call | solution.py:529
  24.7 2.4 %shard_map.86 = (f32[1024,128]{1,0:T(8,128)S(1)}, f32[8,128]{1,0:T(8,128)S(1)}, bf16[1024,128]{1,0:T(8,128)(2,1)S(1)}, bf16[1024,128]{1,0:T(8,128)(2,1)S(1)}) custom-call(s32[8,8]{1,0:T(8,128)S(1)} %copy-done.4, bf16[256,1024]{1,0:T(8,128)(2,1)S(1)} %collective-permute-done.up_ref, bf16[256,1024]{1,0:T(8,128)(2,1)S(1)} %collective-permute-done.1.down_ref, ...), custom_call_target="tpu_custom_call" | custom-call | flops 100663296 | bytes 3153920 | tf_op jit(solution)/shard_map/pallas_call | solution.py:529
  27.1 1.5 %collective-permute-done.4.rz_ref = bf16[1056,128]{1,0:T(8,128)(2,1)S(1)} collective-permute-done((bf16[1056,128]{1,0:T(8,128)(2,1)S(1)}, bf16[1056,128]{1,0:T(8,128)(2,1)S(1)}, u32[]{:S(2)}, u32[]{:S(2)}) %collective-permute-start.4) | collective-permute-done | bytes 270368 | tf_op jit(solution)/shard_map/ppermute | solution.py:573
  29.4 1.8 %collective-permute-start.11 = (bf16[1056,128]{1,0:T(8,128)(2,1)S(1)}, bf16[1056,128]{1,0:T(8,128)(2,1)S(1)}, u32[]{:S(2)}, u32[]{:S(2)}) collective-permute-start(bf16[1056,128]{1,0:T(8,128)(2,1)S(1)} %get-tuple-element.53.a_ref), channel_id=1, source_target_pairs={{0,24},{4,28},{8,0},{12,4},{16,8},{20,12},{24,16},{28,20},{1,25},{... | collective-permute-start | bytes 811016 | tf_op jit(solution)/shard_map/ppermute | solution.py:573
  31.3 1.5 %collective-permute-start.12 = (bf16[1056,128]{1,0:T(8,128)(2,1)S(1)}, bf16[1056,128]{1,0:T(8,128)(2,1)S(1)}, u32[]{:S(2)}, u32[]{:S(2)}) collective-permute-start(bf16[1056,128]{1,0:T(8,128)(2,1)S(1)} %get-tuple-element.53.a_ref), channel_id=1, source_target_pairs={{0,4},{4,0},{8,12},{12,8},{16,20},{20,16},{24,28},{28,24},{1,5},{5... | collective-permute-start | bytes 811016 | tf_op jit(solution)/shard_map/ppermute | solution.py:570
  32.8 1.5 %collective-permute-start.7 = (f32[8,128]{1,0:T(8,128)S(1)}, f32[8,128]{1,0:T(8,128)S(1)}, u32[]{:S(2)}, u32[]{:S(2)}) collective-permute-start(f32[8,128]{1,0:T(8,128)S(1)} %get-tuple-element.52), channel_id=1, source_target_pairs={{0,2},{1,3},{2,0},{3,1},{4,6},{5,7},{6,4},{7,5},{8,10},{9,11},{10,... | collective-permute-start | bytes 12296 | tf_op jit(solution)/shard_map/ppermute | solution.py:623
  34.6 1.2 %collective-permute-done.8 = f32[8,128]{1,0:T(8,128)S(1)} collective-permute-done((f32[8,128]{1,0:T(8,128)S(1)}, f32[8,128]{1,0:T(8,128)S(1)}, u32[]{:S(2)}, u32[]{:S(2)}) %collective-permute-start.8) | collective-permute-done | bytes 4128 | tf_op jit(solution)/shard_map/ppermute | solution.py:623
  36.4 1.7 %collective-permute-start.9 = (f32[8,128]{1,0:T(8,128)S(1)}, f32[8,128]{1,0:T(8,128)S(1)}, u32[]{:S(2)}, u32[]{:S(2)}) collective-permute-start(f32[8,128]{1,0:T(8,128)S(1)} %add_add_fusion.sums_ref), channel_id=1, source_target_pairs={{0,24},{4,28},{8,0},{12,4},{16,8},{20,12},{24,16},{28,20},{1,25},{... | collective-permute-start | bytes 12296 | tf_op jit(solution)/shard_map/ppermute | solution.py:573
  38.7 2.6 %shard_map.89 = (f32[128,1024]{1,0:T(8,128)S(1)}, f32[2,128,1024]{2,1,0:T(8,128)S(1)}, bf16[1024,128]{1,0:T(8,128)(2,1)S(1)}, f32[8,128]{1,0:T(8,128)S(1)}) custom-call(s32[8,8]{1,0:T(8,128)S(1)} %copy-done.4, f32[8,128]{1,0:T(8,128)S(1)} %add_add_fusion.sums_ref, bf16[128,1024]{1,0:T(8,128)(2,1)S(1)} %copy-done.2, ...), custom_call_target="tpu_custom_call" | custom-call | flops 167772160 | bytes 3686400 | tf_op jit(solution)/shard_map/pallas_call | solution.py:529
  41.8 2.6 %shard_map.90 = (bf16[256,1024]{1,0:T(8,128)(2,1)S(1)}, bf16[256,1024]{1,0:T(8,128)(2,1)S(1)}, bf16[128,1024]{1,0:T(8,128)(2,1)S(1)}, f32[2,128,1024]{2,1,0:T(8,128)S(1)}) custom-call(s32[8,8]{1,0:T(8,128)S(1)} %copy-done.4, f32[8,128]{1,0:T(8,128)S(1)} %collective-permute-done.9.sz_ref, f32[8,128]{1,0:T(8,128)S(1)} %collective-permute-done.10.sx_ref, ...), custom_call_target="tpu_custom_call" | custom-call | flops 268435456 | bytes 7372800 | tf_op jit(solution)/shard_map/pallas_call | solution.py:529
  44.7 1.7 %collective-permute-start.14 = (bf16[256,1024]{1,0:T(8,128)(2,1)S(1)}, bf16[256,1024]{1,0:T(8,128)(2,1)S(1)}, u32[]{:S(2)}, u32[]{:S(2)}) collective-permute-start(bf16[256,1024]{1,0:T(8,128)(2,1)S(1)} %get-tuple-element.67), channel_id=1, source_target_pairs={{8,0},{9,1},{0,2},{1,3},{12,4},{13,5},{4,6},{5,7},{16,8},{17,9},{2... | collective-permute-start | bytes 1572872 | tf_op jit(solution)/shard_map/ppermute | solution.py:565
  46.4 1.1 %collective-permute-start.15 = (bf16[128,1024]{1,0:T(8,128)(2,1)S(1)}, bf16[128,1024]{1,0:T(8,128)(2,1)S(1)}, u32[]{:S(2)}, u32[]{:S(2)}) collective-permute-start(bf16[128,1024]{1,0:T(8,128)(2,1)S(1)} %get-tuple-element.68), channel_id=1, source_target_pairs={{0,4},{4,0},{8,12},{12,8},{16,20},{20,16},{24,28},{28,24},{1,5},{5... | collective-permute-start | bytes 786440 | tf_op jit(solution)/shard_map/ppermute | solution.py:570
  47.4 2.6 %shard_map.91 = (bf16[128,1024]{1,0:T(8,128)(2,1)}, f32[128,1024]{1,0:T(8,128)S(1)}, f32[2,128,1024]{2,1,0:T(8,128)S(1)}) custom-call(f32[8,128]{1,0:T(8,128)S(1)} %add_add_fusion.sums_ref, bf16[128,1024]{1,0:T(8,128)(2,1)S(1)} %copy-done.2, bf16[128,1024]{1,0:T(8,128)(2,1)S(1)} %copy-done, bf16[128,1024]{1,0:T(8,128)(2,1)S(1)} %copy-done.1, ...), custom_call_target="tpu_custom_call" | custom-call | flops 201326592 | bytes 4734976 | tf_op jit(solution)/shard_map/pallas_call | solution.py:529
  50.1 3.7 %collective-permute-done.15.dqx_ref = bf16[128,1024]{1,0:T(8,128)(2,1)S(1)} collective-permute-done((bf16[128,1024]{1,0:T(8,128)(2,1)S(1)}, bf16[128,1024]{1,0:T(8,128)(2,1)S(1)}, u32[]{:S(2)}, u32[]{:S(2)}) %collective-permute-start.15) | collective-permute-done | bytes 262176 | tf_op jit(solution)/shard_map/ppermute | solution.py:570
  53.8 4.2 %collective-permute-done.13.up_ref = bf16[256,1024]{1,0:T(8,128)(2,1)S(1)} collective-permute-done((bf16[256,1024]{1,0:T(8,128)(2,1)S(1)}, bf16[256,1024]{1,0:T(8,128)(2,1)S(1)}, u32[]{:S(2)}, u32[]{:S(2)}) %collective-permute-start.13) | collective-permute-done | bytes 524320 | tf_op jit(solution)/shard_map/ppermute | solution.py:565
  58.0 1.8 %shard_map.92 = (bf16[128,1024]{1,0:T(8,128)(2,1)}, bf16[128,1024]{1,0:T(8,128)(2,1)}, bf16[128,1024]{1,0:T(8,128)(2,1)}) custom-call(s32[8,8]{1,0:T(8,128)S(1)} %copy-done.4, bf16[256,1024]{1,0:T(8,128)(2,1)S(1)} %collective-permute-done.13.up_ref, bf16[256,1024]{1,0:T(8,128)(2,1)S(1)} %collective-permute-done.14.down_ref, ...), custom_call_target="tpu_custom_call" | custom-call | bytes 3670016 | tf_op jit(solution)/shard_map/pallas_call | solution.py:529
  (28 shorter events, 3.5 us)
Async XLA Ops:
  0.6 4.5 %copy-start.2 = (bf16[128,1024]{1,0:T(8,128)(2,1)S(1)}, bf16[128,1024]{1,0:T(8,128)(2,1)}, u32[]{:S(2)}) copy-start(bf16[128,1024]{1,0:T(8,128)(2,1)} %q_ref.9) | copy-start | bytes 786436
  0.6 17.8 %copy-start = (bf16[128,1024]{1,0:T(8,128)(2,1)S(1)}, bf16[128,1024]{1,0:T(8,128)(2,1)}, u32[]{:S(2)}) copy-start(bf16[128,1024]{1,0:T(8,128)(2,1)} %k_ref.9) | copy-start | bytes 786436
  0.7 17.8 %copy-start.1 = (bf16[128,1024]{1,0:T(8,128)(2,1)S(1)}, bf16[128,1024]{1,0:T(8,128)(2,1)}, u32[]{:S(2)}) copy-start(bf16[128,1024]{1,0:T(8,128)(2,1)} %v_ref.9) | copy-start | bytes 786436
  0.7 6.3 %copy-start.3 = (bf16[128,1024]{1,0:T(8,128)(2,1)S(1)}, bf16[128,1024]{1,0:T(8,128)(2,1)}, u32[]{:S(2)}) copy-start(bf16[128,1024]{1,0:T(8,128)(2,1)} %u_ref.3) | copy-start | bytes 786436
  2.0 16.5 %collective-permute-start = (bf16[256,1024]{1,0:T(8,128)(2,1)S(1)}, bf16[256,1024]{1,0:T(8,128)(2,1)S(1)}, u32[]{:S(2)}, u32[]{:S(2)}) collective-permute-start(bf16[256,1024]{1,0:T(8,128)(2,1)S(1)} %get-tuple-element.39), channel_id=1, source_target_pairs={{0,8},{1,9},{2,0},{3,1},{4,12},{5,13},{6,4},{7,5},{8,16},{9,17},{1... | collective-permute-start | bytes 1572872 | tf_op jit(solution)/shard_map/ppermute | solution.py:565
  5.1 13.4 %collective-permute-start.1 = (bf16[256,1024]{1,0:T(8,128)(2,1)S(1)}, bf16[256,1024]{1,0:T(8,128)(2,1)S(1)}, u32[]{:S(2)}, u32[]{:S(2)}) collective-permute-start(bf16[256,1024]{1,0:T(8,128)(2,1)S(1)} %get-tuple-element.40), channel_id=1, source_target_pairs={{8,0},{9,1},{0,2},{1,3},{12,4},{13,5},{4,6},{5,7},{16,8},{17,9},{2... | collective-permute-start | bytes 1572872 | tf_op jit(solution)/shard_map/ppermute | solution.py:565
  5.1 9.2 %collective-permute-start.2 = (bf16[128,1024]{1,0:T(8,128)(2,1)S(1)}, bf16[128,1024]{1,0:T(8,128)(2,1)S(1)}, u32[]{:S(2)}, u32[]{:S(2)}) collective-permute-start(bf16[128,1024]{1,0:T(8,128)(2,1)S(1)} %copy-done.2), channel_id=1, source_target_pairs={{0,4},{4,0},{8,12},{12,8},{16,20},{20,16},{24,28},{28,24},{1,5},{5... | collective-permute-start | bytes 786440 | tf_op jit(solution)/shard_map/ppermute | solution.py:570
  7.0 11.5 %collective-permute-start.3 = (bf16[128,1024]{1,0:T(8,128)(2,1)S(1)}, bf16[128,1024]{1,0:T(8,128)(2,1)S(1)}, u32[]{:S(2)}, u32[]{:S(2)}) collective-permute-start(bf16[128,1024]{1,0:T(8,128)(2,1)S(1)} %copy-done.3), channel_id=1, source_target_pairs={{0,4},{4,0},{8,12},{12,8},{16,20},{20,16},{24,28},{28,24},{1,5},{5... | collective-permute-start | bytes 786440 | tf_op jit(solution)/shard_map/ppermute | solution.py:570
  19.6 8.9 %collective-permute-start.4 = (bf16[1056,128]{1,0:T(8,128)(2,1)S(1)}, bf16[1056,128]{1,0:T(8,128)(2,1)S(1)}, u32[]{:S(2)}, u32[]{:S(2)}) collective-permute-start(bf16[1056,128]{1,0:T(8,128)(2,1)S(1)} %get-tuple-element.49), channel_id=1, source_target_pairs={{0,8},{4,12},{8,16},{12,20},{16,24},{20,28},{24,0},{28,4},{1,9},{5... | collective-permute-start | bytes 811016 | tf_op jit(solution)/shard_map/ppermute | solution.py:573
  21.4 7.1 %collective-permute-start.5 = (bf16[1056,128]{1,0:T(8,128)(2,1)S(1)}, bf16[1056,128]{1,0:T(8,128)(2,1)S(1)}, u32[]{:S(2)}, u32[]{:S(2)}) collective-permute-start(bf16[1056,128]{1,0:T(8,128)(2,1)S(1)} %get-tuple-element.50), channel_id=1, source_target_pairs={{0,4},{4,0},{8,12},{12,8},{16,20},{20,16},{24,28},{28,24},{1,5},{5... | collective-permute-start | bytes 811016 | tf_op jit(solution)/shard_map/ppermute | solution.py:570
  22.9 1.8 %copy-start.4 = (s32[8,8]{1,0:T(8,128)S(1)}, s32[8,8]{1,0:T(8,128)}, u32[]{:S(2)}) copy-start(s32[8,8]{1,0:T(8,128)} %pattern_ref.9) | copy-start | bytes 772
  29.4 12.3 %collective-permute-start.11 = (bf16[1056,128]{1,0:T(8,128)(2,1)S(1)}, bf16[1056,128]{1,0:T(8,128)(2,1)S(1)}, u32[]{:S(2)}, u32[]{:S(2)}) collective-permute-start(bf16[1056,128]{1,0:T(8,128)(2,1)S(1)} %get-tuple-element.53.a_ref), channel_id=1, source_target_pairs={{0,24},{4,28},{8,0},{12,4},{16,8},{20,12},{24,16},{28,20},{1,25},{... | collective-permute-start | bytes 811016 | tf_op jit(solution)/shard_map/ppermute | solution.py:573
  31.3 10.5 %collective-permute-start.12 = (bf16[1056,128]{1,0:T(8,128)(2,1)S(1)}, bf16[1056,128]{1,0:T(8,128)(2,1)S(1)}, u32[]{:S(2)}, u32[]{:S(2)}) collective-permute-start(bf16[1056,128]{1,0:T(8,128)(2,1)S(1)} %get-tuple-element.53.a_ref), channel_id=1, source_target_pairs={{0,4},{4,0},{8,12},{12,8},{16,20},{20,16},{24,28},{28,24},{1,5},{5... | collective-permute-start | bytes 811016 | tf_op jit(solution)/shard_map/ppermute | solution.py:570
  32.8 3.1 %collective-permute-start.8 = (f32[8,128]{1,0:T(8,128)S(1)}, f32[8,128]{1,0:T(8,128)S(1)}, u32[]{:S(2)}, u32[]{:S(2)}) collective-permute-start(f32[8,128]{1,0:T(8,128)S(1)} %get-tuple-element.52), channel_id=1, source_target_pairs={{0,3},{1,2},{2,1},{3,0},{4,7},{5,6},{6,5},{7,4},{8,11},{9,10},{10,... | collective-permute-start | bytes 12296 | tf_op jit(solution)/shard_map/ppermute | solution.py:623
  32.8 3.6 %collective-permute-start.7 = (f32[8,128]{1,0:T(8,128)S(1)}, f32[8,128]{1,0:T(8,128)S(1)}, u32[]{:S(2)}, u32[]{:S(2)}) collective-permute-start(f32[8,128]{1,0:T(8,128)S(1)} %get-tuple-element.52), channel_id=1, source_target_pairs={{0,2},{1,3},{2,0},{3,1},{4,6},{5,7},{6,4},{7,5},{8,10},{9,11},{10,... | collective-permute-start | bytes 12296 | tf_op jit(solution)/shard_map/ppermute | solution.py:623
  34.3 2.1 %collective-permute-start.6 = (f32[8,128]{1,0:T(8,128)S(1)}, f32[8,128]{1,0:T(8,128)S(1)}, u32[]{:S(2)}, u32[]{:S(2)}) collective-permute-start(f32[8,128]{1,0:T(8,128)S(1)} %get-tuple-element.52), channel_id=1, source_target_pairs={{0,1},{1,0},{2,3},{3,2},{4,5},{5,4},{6,7},{7,6},{8,9},{9,8},{10,11... | collective-permute-start | bytes 12296 | tf_op jit(solution)/shard_map/ppermute | solution.py:623
  36.4 4.8 %collective-permute-start.9 = (f32[8,128]{1,0:T(8,128)S(1)}, f32[8,128]{1,0:T(8,128)S(1)}, u32[]{:S(2)}, u32[]{:S(2)}) collective-permute-start(f32[8,128]{1,0:T(8,128)S(1)} %add_add_fusion.sums_ref), channel_id=1, source_target_pairs={{0,24},{4,28},{8,0},{12,4},{16,8},{20,12},{24,16},{28,20},{1,25},{... | collective-permute-start | bytes 12296 | tf_op jit(solution)/shard_map/ppermute | solution.py:573
  38.1 3.6 %collective-permute-start.10 = (f32[8,128]{1,0:T(8,128)S(1)}, f32[8,128]{1,0:T(8,128)S(1)}, u32[]{:S(2)}, u32[]{:S(2)}) collective-permute-start(f32[8,128]{1,0:T(8,128)S(1)} %add_add_fusion.sums_ref), channel_id=1, source_target_pairs={{0,4},{4,0},{8,12},{12,8},{16,20},{20,16},{24,28},{28,24},{1,5},{5... | collective-permute-start | bytes 12296 | tf_op jit(solution)/shard_map/ppermute | solution.py:570
  44.3 13.6 %collective-permute-start.13 = (bf16[256,1024]{1,0:T(8,128)(2,1)S(1)}, bf16[256,1024]{1,0:T(8,128)(2,1)S(1)}, u32[]{:S(2)}, u32[]{:S(2)}) collective-permute-start(bf16[256,1024]{1,0:T(8,128)(2,1)S(1)} %get-tuple-element.66), channel_id=1, source_target_pairs={{0,8},{1,9},{2,0},{3,1},{4,12},{5,13},{6,4},{7,5},{8,16},{9,17},{1... | collective-permute-start | bytes 1572872 | tf_op jit(solution)/shard_map/ppermute | solution.py:565
  44.7 13.3 %collective-permute-start.14 = (bf16[256,1024]{1,0:T(8,128)(2,1)S(1)}, bf16[256,1024]{1,0:T(8,128)(2,1)S(1)}, u32[]{:S(2)}, u32[]{:S(2)}) collective-permute-start(bf16[256,1024]{1,0:T(8,128)(2,1)S(1)} %get-tuple-element.67), channel_id=1, source_target_pairs={{8,0},{9,1},{0,2},{1,3},{12,4},{13,5},{4,6},{5,7},{16,8},{17,9},{2... | collective-permute-start | bytes 1572872 | tf_op jit(solution)/shard_map/ppermute | solution.py:565
  46.4 7.4 %collective-permute-start.15 = (bf16[128,1024]{1,0:T(8,128)(2,1)S(1)}, bf16[128,1024]{1,0:T(8,128)(2,1)S(1)}, u32[]{:S(2)}, u32[]{:S(2)}) collective-permute-start(bf16[128,1024]{1,0:T(8,128)(2,1)S(1)} %get-tuple-element.68), channel_id=1, source_target_pairs={{0,4},{4,0},{8,12},{12,8},{16,20},{20,16},{24,28},{28,24},{1,5},{5... | collective-permute-start | bytes 786440 | tf_op jit(solution)/shard_map/ppermute | solution.py:570

commit v4 on v3

--- a/solution.py
+++ b/solution.py
@@ -206,14 +206,17 @@
         if pattern_ref is None:
             return
         blocks = pattern_ref.shape[0]
-        ahead, partner = jnp.minimum(me + 2, blocks - 1), jnp.where(self.odd, me - 1, me + 1)
+        even = jnp.logical_not(self.odd)
+        ahead = jnp.minimum(me + 2, blocks - 1)
+        self.ahead = me + 2 < blocks
         self.near = pattern_ref[me, 1] >= 0
-        self.far_in, self.side_in = pattern_ref[me, 2] >= 0, pattern_ref[me, 0] >= 0
-        self.ahead = me + 2 < blocks
         self.far = jnp.logical_and(self.ahead, pattern_ref[ahead, 2] >= 0)
-        self.side = jnp.logical_and(
-            jnp.logical_or(jnp.logical_not(self.odd), me >= 2), pattern_ref[partner, 0] >= 0
+        ahead_side = jnp.logical_and(self.ahead, pattern_ref[ahead, 0] >= 0)
+        own_side = pattern_ref[me, 0] >= 0
+        self.side = jnp.logical_or(
+            jnp.logical_and(self.odd, own_side), jnp.logical_and(even, ahead_side)
         )
+        self.helped = jnp.logical_or(pattern_ref[me, 2] >= 0, jnp.logical_and(even, own_side))
 
 
 def mm(a, b, dims):
@@ -258,6 +261,9 @@
         for (_, value), w, total in zip(pairs, weights, totals)
     ]
     return [(out, top, top + jnp.log(total), w) for out, top, total, w in zip(outs, tops, totals, weights)]
+
+
+FIRST, SECOND = slice(0, BLOCK), slice(BLOCK, 2 * BLOCK)
 
 
 def payload_kernel(heads, q_ref, k_ref, v_ref, u_ref, up_ref, down_ref, sems):
@@ -297,80 +303,118 @@
     lse_ref[...] = stack_rows(rows)
 
 
+def merged(parts):
+    highest = functools.reduce(jnp.maximum, [lse for _, lse in parts])
+    total = highest + jnp.log(functools.reduce(jnp.add, [jnp.exp(lse - highest) for _, lse in parts]))
+    return functools.reduce(jnp.add, [out * jnp.exp(lse - total) for out, lse in parts]), total
+
+
 def helper_kernel(
-    heads, up_ref, down_ref, qx_ref, k_ref, v_ref, oz_ref, ox_ref, ez_ref, ex_ref, mz_ref, mx_ref
+    heads,
+    pattern_ref,
+    up_ref,
+    down_ref,
+    q_ref,
+    kx_ref,
+    vx_ref,
+    oz_ref,
+    ez_ref,
+    ex_ref,
+    outx_ref,
+    mz_ref,
+    mx_ref,
+    lsex_ref,
 ):
-    flags = Flags()
+    flags = Flags(pattern_ref)
     odd, half = flags.odd, flags.half
-    first, second = slice(0, BLOCK), slice(BLOCK, 2 * BLOCK)
+    joins = jnp.logical_and(flags.side, jnp.logical_not(odd))
     z_rows, x_rows, z_tops, x_tops = [], [], [], []
     for start in range(0, heads, 2):
         pairs = []
         for h in range(start, start + 2):
             at = rows_of(h)
-            up_a, down_a = up_ref[first, at], down_ref[first, at]
+            up_a, down_a = up_ref[FIRST, at], down_ref[FIRST, at]
             k2, qz = jnp.where(half, down_a, up_a), jnp.where(half, up_a, down_a)
-            v2 = jnp.where(half, down_ref[second, at], up_ref[second, at])
+            v2 = jnp.where(half, down_ref[SECOND, at], up_ref[SECOND, at])
             pairs.append((score_tile(k2, qz), v2))
-            ks, vs = jnp.where(odd, k2, k_ref[:, at]), jnp.where(odd, v2, v_ref[:, at])
-            pairs.append((score_tile(ks, qx_ref[:, at]), vs))
-        for n, (out, top, lse, weights) in enumerate(softmax_parts(pairs)):
-            at = rows_of(start + n // 2)
-            o_ref, e_ref = ((oz_ref, ez_ref), (ox_ref, ex_ref))[n % 2]
-            o_ref[at] = out.astype(jnp.bfloat16)
-            e_ref[at] = weights
-            (z_rows, x_rows)[n % 2].append(lse)
-            (z_tops, x_tops)[n % 2].append(top)
-    tail = slice(heads * HD, heads * HD + TAIL)
-    oz_ref[tail] = split_rows(stack_rows(z_rows))
-    ox_ref[tail] = split_rows(stack_rows(x_rows))
+            pairs.append((score_tile(kx_ref[:, at], jnp.where(odd, q_ref[:, at], qz)), vx_ref[:, at]))
+        parts = softmax_parts(pairs)
+        for n, h in enumerate(range(start, start + 2)):
+            at = rows_of(h)
+            (z_out, z_top, z_lse, ez_ref[at]), (x_out, x_top, x_lse, ex_ref[at]) = parts[2 * n : 2 * n + 2]
+            out, lse = merged(
+                [(z_out, jnp.where(flags.far, z_lse, NEG_BIG)), (x_out, jnp.where(joins, x_lse, NEG_BIG))]
+            )
+            oz_ref[at] = out.astype(jnp.bfloat16)
+            outx_ref[at] = x_out
+            z_rows.append(lse)
+            x_rows.append(x_lse)
+            z_tops.append(z_top)
+            x_tops.append(x_top)
+    oz_ref[heads * HD :] = split_rows(stack_rows(z_rows))
+    lsex_ref[...] = stack_rows(x_rows)
     mz_ref[...] = stack_rows(z_tops)
     mx_ref[...] = stack_rows(x_tops)
 
 
 def own_kernel(
-    heads, pattern_ref, up_ref, down_ref, q_ref, ux_ref, out_ref, lse_ref, own_ref, total_ref, uzt_ref, uxt_ref
+    heads,
+    pattern_ref,
+    up_ref,
+    down_ref,
+    q_ref,
+    out_ref,
+    lse_ref,
+    outx_ref,
+    lsex_ref,
+    own_ref,
+    total_ref,
+    uzt_ref,
+    e_ref,
+    m_ref,
 ):
     flags = Flags(pattern_ref)
-    half, near = flags.half, flags.near
-    first, second = slice(0, BLOCK), slice(BLOCK, 2 * BLOCK)
-    before = lse_ref[...]
-    rows = []
-    for h in range(heads):
-        at = rows_of(h)
-        k2 = jnp.where(half, down_ref[first, at], up_ref[first, at])
-        up_b, down_b = up_ref[second, at], down_ref[second, at]
-        v2, uz = jnp.where(half, down_b, up_b), jnp.where(half, up_b, down_b)
-        ((out, _, lse, _),) = softmax_parts([(score_tile(k2, q_ref[:, at]), v2)])
-        lse = jnp.where(near, lse, NEG_BIG)
-        old = before[h : h + 1]
-        highest = jnp.maximum(old, lse)
-        total = highest + jnp.log(jnp.exp(old - highest) + jnp.exp(lse - highest))
-        own_ref[at] = out_ref[at] * jnp.exp(old - total) + out * jnp.exp(lse - total)
-        rows.append(total)
-        uzt_ref[at] = uz.T
-        uxt_ref[at] = ux_ref[:, at].T
+    half = flags.half
+    local = jnp.logical_and(flags.odd, flags.side)
+    before, side = lse_ref[...], jnp.where(local, lsex_ref[...], NEG_BIG)
+    rows, tops = [], []
+    for start in range(0, heads, 2):
+        group = range(start, start + 2)
+        pairs = []
+        for h in group:
+            at = rows_of(h)
+            k2 = jnp.where(half, down_ref[FIRST, at], up_ref[FIRST, at])
+            up_b, down_b = up_ref[SECOND, at], down_ref[SECOND, at]
+            uzt_ref[at] = jnp.where(half, up_b, down_b).T
+            pairs.append((score_tile(k2, q_ref[:, at]), jnp.where(half, down_b, up_b)))
+        for h, (out, top, lse, e_ref[rows_of(h)]) in zip(group, softmax_parts(pairs)):
+            at, row = rows_of(h), slice(h, h + 1)
+            own_ref[at], total = merged(
+                [
+                    (out_ref[at], before[row]),
+                    (out, jnp.where(flags.near, lse, NEG_BIG)),
+                    (outx_ref[at], side[row]),
+                ]
+            )
+            rows.append(total)
+            tops.append(top)
     total_ref[...] = stack_rows(rows)
-
-
-def merge_kernel(heads, pattern_ref, own_ref, lse_ref, rz_ref, rx_ref, ut_ref, a_ref, sums_ref):
+    m_ref[...] = stack_rows(tops)
+
+
+def merge_kernel(heads, pattern_ref, own_ref, lse_ref, rz_ref, ut_ref, a_ref, sums_ref):
     flags = Flags(pattern_ref)
     tail = slice(heads * HD, heads * HD + TAIL)
-    own = lse_ref[...]
-    z = jnp.where(flags.far_in, joined_rows(rz_ref[tail]), NEG_BIG)
-    x = jnp.where(flags.side_in, joined_rows(rx_ref[tail]), NEG_BIG)
-    highest = jnp.maximum(own, jnp.maximum(z, x))
-    total = highest + jnp.log(jnp.exp(own - highest) + jnp.exp(z - highest) + jnp.exp(x - highest))
-    own, z, x = jnp.exp(own - total), jnp.exp(z - total), jnp.exp(x - total)
     squares = jnp.zeros((8, BLOCK), jnp.float32)
     crosses = jnp.zeros((8, BLOCK), jnp.float32)
+    own = lse_ref[...]
+    z = jnp.where(flags.helped, joined_rows(rz_ref[tail]), NEG_BIG)
+    highest = jnp.maximum(own, z)
+    total = highest + jnp.log(jnp.exp(own - highest) + jnp.exp(z - highest))
+    own, z = jnp.exp(own - total), jnp.exp(z - total)
     for h in range(heads):
         at, row = rows_of(h), slice(h, h + 1)
-        out = (
-            own_ref[at] * own[row]
-            + rz_ref[at].astype(jnp.float32) * z[row]
-            + rx_ref[at].astype(jnp.float32) * x[row]
-        ).astype(jnp.bfloat16)
+        out = (own_ref[at] * own[row] + rz_ref[at].astype(jnp.float32) * z[row]).astype(jnp.bfloat16)
         a_ref[at] = out
         wide = out.astype(jnp.float32)
         squares += (wide * wide).reshape(HD // 8, 8, BLOCK).sum(axis=0)
@@ -384,6 +428,10 @@
     return inverse, inverse**3 * sums_ref[1:2] / WIDTH
 
 
+def total_rows(a_ref):
+    return joined_rows(a_ref[a_ref.shape[0] - TAIL :])
+
+
 def upstream_part(norm, u, a):
     inverse, factor = norm
     wide = a.astype(jnp.float32)
@@ -391,32 +439,119 @@
     return grad, jnp.sum(grad.astype(jnp.float32) * wide, axis=0, keepdims=True)
 
 
-def pair_back(q, k, v, grad, delta, lse, keep):
-    weights = jnp.exp(jnp.where(keep, score_tile(k, q), NEG_BIG) - lse)
-    dscore = (weights * (mm(v, grad, NN) - delta) * SCALE).astype(jnp.bfloat16)
-    return mm(dscore, q, NN), mm(weights.astype(jnp.bfloat16), grad, NT), mm(dscore, k, TN)
-
-
 def near_back_kernel(
-    heads, pattern_ref, sums_ref, q_ref, up_ref, down_ref, a_ref, ut_ref, dq_ref, dkv2_ref, grad_ref, delta_ref
+    heads,
+    pattern_ref,
+    sums_ref,
+    q_ref,
+    a_ref,
+    ut_ref,
+    up_ref,
+    down_ref,
+    e_ref,
+    m_ref,
+    grad_ref,
+    delta_ref,
+    ds_ref,
+    dkv2_ref,
 ):
     flags = Flags(pattern_ref)
-    half, near = flags.half, flags.near
-    first, second = slice(0, BLOCK), slice(BLOCK, 2 * BLOCK)
+    half = flags.half
     norm = norm_rows(sums_ref)
-    lse = joined_rows(a_ref[heads * HD : heads * HD + TAIL])
+    scale = jnp.where(flags.near, jnp.exp(m_ref[...] - total_rows(a_ref)), 0.0)
     deltas = []
-    for h in range(heads):
-        at = rows_of(h)
-        grad, delta = upstream_part(norm, ut_ref[at], a_ref[at])
-        k2 = jnp.where(half, down_ref[first, at], up_ref[first, at])
-        v2 = jnp.where(half, down_ref[second, at], up_ref[second, at])
-        dkv2_ref[0, :, at], dkv2_ref[1, :, at], dq_ref[:, at] = pair_back(
-            q_ref[:, at], k2, v2, grad, delta, lse[h : h + 1], near
-        )
-        grad_ref[at] = grad
-        deltas.append(delta)
+    for start in range(0, heads, 4):
+        group = range(start, start + 4)
+        parts = [upstream_part(norm, ut_ref[rows_of(h)], a_ref[rows_of(h)]) for h in group]
+        for h, (grad, delta) in zip(group, parts):
+            grad_ref[rows_of(h)] = grad
+            deltas.append(delta)
+        products = []
+        for h, (grad, _) in zip(group, parts):
+            v2 = jnp.where(half, down_ref[SECOND, rows_of(h)], up_ref[SECOND, rows_of(h)])
+            products.append(mm(v2, grad, NN))
+        scores = []
+        for h, product, (_, delta) in zip(group, products, parts):
+            weights = e_ref[rows_of(h)] * scale[h : h + 1]
+            dscore = (weights * (product - delta) * SCALE).astype(jnp.bfloat16)
+            scores.append((dscore, weights.astype(jnp.bfloat16)))
+        for h, (dscore, probs), (grad, _) in zip(group, scores, parts):
+            at = rows_of(h)
+            ds_ref[at] = dscore
+            dkv2_ref[0, :, at] = mm(dscore, q_ref[:, at], NN)
+            dkv2_ref[1, :, at] = mm(probs, grad, NT)
     delta_ref[...] = stack_rows(deltas)
+
+
+def helper_back_kernel(
+    heads,
+    pattern_ref,
+    sz_ref,
+    az_ref,
+    uzt_ref,
+    a_ref,
+    grad_ref,
+    delta_ref,
+    up_ref,
+    down_ref,
+    q_ref,
+    kx_ref,
+    vx_ref,
+    ez_ref,
+    ex_ref,
+    mz_ref,
+    mx_ref,
+    near_ref,
+    up_out_ref,
+    down_out_ref,
+    side_out_ref,
+    dsx_ref,
+):
+    flags = Flags(pattern_ref)
+    odd, half = flags.odd, flags.half
+    norm = norm_rows(sz_ref)
+    z_lse = total_rows(az_ref)
+    scales = (
+        jnp.where(flags.far, jnp.exp(mz_ref[...] - z_lse), 0.0),
+        jnp.where(flags.side, jnp.exp(mx_ref[...] - jnp.where(odd, total_rows(a_ref), z_lse)), 0.0),
+    )
+    own_deltas = delta_ref[...]
+    for start in range(0, heads, 2):
+        group = range(start, start + 2)
+        parts, products, scores = [], [], []
+        for h in group:
+            grad, delta = upstream_part(norm, uzt_ref[rows_of(h)], az_ref[rows_of(h)])
+            parts.append((grad, delta))
+            parts.append(
+                (jnp.where(odd, grad_ref[rows_of(h)], grad), jnp.where(odd, own_deltas[h : h + 1], delta))
+            )
+        for n, h in enumerate(group):
+            at = rows_of(h)
+            v2 = jnp.where(half, down_ref[SECOND, at], up_ref[SECOND, at])
+            products.append(mm(v2, parts[2 * n][0], NN))
+            products.append(mm(vx_ref[:, at], parts[2 * n + 1][0], NN))
+        for n, ((_, delta), product) in enumerate(zip(parts, products)):
+            h = group[n // 2]
+            weights = (ez_ref, ex_ref)[n % 2][rows_of(h)] * scales[n % 2][h : h + 1]
+            dscore = (weights * (product - delta) * SCALE).astype(jnp.bfloat16)
+            scores.append((dscore, weights.astype(jnp.bfloat16)))
+        for n, h in enumerate(group):
+            at = rows_of(h)
+            (gz, _), (gx, _) = parts[2 * n : 2 * n + 2]
+            (dz, pz), (dx, px) = scores[2 * n : 2 * n + 2]
+            up_a, down_a = up_ref[FIRST, at], down_ref[FIRST, at]
+            k2, qz = jnp.where(half, down_a, up_a), jnp.where(half, up_a, down_a)
+            dsx_ref[at] = dx
+            dk2 = (near_ref[0, :, at] + mm(dz, qz, NN)).astype(jnp.bfloat16)
+            dv2 = (near_ref[1, :, at] + mm(pz, gz, NT)).astype(jnp.bfloat16)
+            side_out_ref[FIRST, at] = mm(dx, jnp.where(odd, q_ref[:, at], qz), NN).astype(jnp.bfloat16)
+            side_out_ref[SECOND, at] = mm(px, gx, NT).astype(jnp.bfloat16)
+            joined = jnp.concatenate([dz, jnp.where(odd, jnp.zeros_like(dx), dx)], axis=0)
+            dqz = mm(joined, jnp.concatenate([k2, kx_ref[:, at]], axis=0), TN).astype(jnp.bfloat16)
+            up_out_ref[FIRST, at] = jnp.where(half, dk2, dqz)
+            up_out_ref[SECOND, at] = dv2
+            down_out_ref[FIRST, at] = jnp.where(half, dqz, dk2)
+            down_out_ref[SECOND, at] = dv2
 
 
 def diagonal_back_kernel(
@@ -428,114 +563,66 @@
     a_ref,
     grad_ref,
     delta_ref,
-    dq_in_ref,
-    dside_ref,
+    ds_ref,
+    dsx_ref,
+    kx_ref,
+    up_ref,
+    down_ref,
     normed_ref,
     dq_ref,
     dkv_ref,
 ):
+    flags = Flags()
+    half, odd = flags.half, flags.odd
     inverse, _ = norm_rows(sums_ref)
-    lse = joined_rows(a_ref[heads * HD : heads * HD + TAIL])
+    lse = total_rows(a_ref)
     causal = causal_mask()
     for h in range(heads):
         at, row = rows_of(h), slice(h, h + 1)
         normed_ref[:, at] = (a_ref[at].astype(jnp.float32) * inverse).astype(jnp.bfloat16).T
-        dk, dv, dq = pair_back(
-            q_ref[:, at], k_ref[:, at], v_ref[:, at], grad_ref[at], delta_ref[row], lse[row], causal
+        q, k, v, grad = q_ref[:, at], k_ref[:, at], v_ref[:, at], grad_ref[at]
+        weights = jnp.exp(jnp.where(causal, score_tile(k, q), NEG_BIG) - lse[row])
+        dscore = (weights * (mm(v, grad, NN) - delta_ref[row]) * SCALE).astype(jnp.bfloat16)
+        dkv_ref[0, :, at] = mm(dscore, q, NN)
+        dkv_ref[1, :, at] = mm(weights.astype(jnp.bfloat16), grad, NT)
+        k2 = jnp.where(half, down_ref[FIRST, at], up_ref[FIRST, at])
+        dsx = jnp.where(odd, dsx_ref[at], jnp.zeros_like(dsx_ref[at]))
+        dq_ref[:, at] = mm(dscore, k, TN) + mm(
+            jnp.concatenate([ds_ref[at], dsx], axis=0), jnp.concatenate([k2, kx_ref[:, at]], axis=0), TN
         )
-        dkv_ref[0, :, at] = dside_ref[0, :, at] + dk
-        dkv_ref[1, :, at] = dside_ref[1, :, at] + dv
-        dq_ref[:, at] = dq_in_ref[:, at] + dq
-
-
-def helper_back_kernel(
-    heads,
-    pattern_ref,
-    sz_ref,
-    sx_ref,
-    up_ref,
-    down_ref,
-    qx_ref,
-    k_ref,
-    v_ref,
-    az_ref,
-    ax_ref,
-    uzt_ref,
-    uxt_ref,
-    ez_ref,
-    ex_ref,
-    mz_ref,
-    mx_ref,
-    own_ref,
-    up_out_ref,
-    down_out_ref,
-    dqx_ref,
-    dside_ref,
+
+
+def final_kernel(
+    heads, pattern_ref, dq_own_ref, dkv_own_ref, side_ref, up_ref, down_ref, dq_ref, dk_ref, dv_ref
 ):
     flags = Flags(pattern_ref)
-    odd, half = flags.odd, flags.half
-    first, second = slice(0, BLOCK), slice(BLOCK, 2 * BLOCK)
-    tail = slice(heads * HD, heads * HD + TAIL)
-    z_norm, x_norm = norm_rows(sz_ref), norm_rows(sx_ref)
-    z_scale = jnp.where(flags.far, jnp.exp(mz_ref[...] - joined_rows(az_ref[tail])), 0.0)
-    x_scale = jnp.where(flags.side, jnp.exp(mx_ref[...] - joined_rows(ax_ref[tail])), 0.0)
-    share = odd.astype(jnp.float32)
-
-    def one(norm, u, a, weights, value):
-        grad, delta = upstream_part(norm, u, a)
-        dscore = (weights * (mm(value, grad, NN) - delta) * SCALE).astype(jnp.bfloat16)
-        return grad, weights.astype(jnp.bfloat16), dscore
-
-    for h in range(heads):
-        at, row = rows_of(h), slice(h, h + 1)
-        up_a, down_a = up_ref[first, at], down_ref[first, at]
-        k2, qz = jnp.where(half, down_a, up_a), jnp.where(half, up_a, down_a)
-        v2 = jnp.where(half, down_ref[second, at], up_ref[second, at])
-        ks, vs, qx = jnp.where(odd, k2, k_ref[:, at]), jnp.where(odd, v2, v_ref[:, at]), qx_ref[:, at]
-        gz, pz, dz = one(z_norm, uzt_ref[at], az_ref[at], ez_ref[at] * z_scale[row], v2)
-        gx, px, dx = one(x_norm, uxt_ref[at], ax_ref[at], ex_ref[at] * x_scale[row], vs)
-        dks, dvs = mm(dx, qx, NN), mm(px, gx, NT)
-        dk2 = (own_ref[0, :, at] + mm(dz, qz, NN) + share * dks).astype(jnp.bfloat16)
-        dv2 = (own_ref[1, :, at] + mm(pz, gz, NT) + share * dvs).astype(jnp.bfloat16)
-        dqz = mm(dz, k2, TN).astype(jnp.bfloat16)
-        dqx_ref[:, at] = mm(dx, ks, TN).astype(jnp.bfloat16)
-        up_out_ref[first, at] = jnp.where(half, dk2, dqz)
-        up_out_ref[second, at] = dv2
-        down_out_ref[first, at] = jnp.where(half, dqz, dk2)
-        down_out_ref[second, at] = dv2
-        dside_ref[0, :, at] = (1.0 - share) * dks
-        dside_ref[1, :, at] = (1.0 - share) * dvs
-
-
-def final_kernel(heads, pattern_ref, up_ref, down_ref, dqx_ref, dq_own_ref, dkv_own_ref, dq_ref, dk_ref, dv_ref):
-    flags = Flags(pattern_ref)
     half = flags.half
-    first, second = slice(0, BLOCK), slice(BLOCK, 2 * BLOCK)
     ahead = flags.ahead.astype(jnp.float32)
-    far = flags.far_in.astype(jnp.float32)
+    helped = flags.helped.astype(jnp.float32)
     for h in range(heads):
         at = rows_of(h)
-        up_a, down_a = up_ref[first, at], down_ref[first, at]
-        dqz = jnp.where(half, down_a, up_a).astype(jnp.float32) * far
+        up_a, down_a = up_ref[FIRST, at], down_ref[FIRST, at]
+        dqz = jnp.where(half, down_a, up_a).astype(jnp.float32) * helped
         dk = jnp.where(half, up_a, down_a).astype(jnp.float32) * ahead
-        dv = jnp.where(half, up_ref[second, at], down_ref[second, at]).astype(jnp.float32) * ahead
-        dq_ref[:, at] = (dq_own_ref[:, at] + dqx_ref[:, at].astype(jnp.float32) + dqz).astype(jnp.bfloat16)
-        dk_ref[:, at] = (dkv_own_ref[0, :, at] + dk).astype(jnp.bfloat16)
-        dv_ref[:, at] = (dkv_own_ref[1, :, at] + dv).astype(jnp.bfloat16)
-
-
-def call(kernel, heads, flags, arrays, outs, flops, space=pltpu.VMEM, scratch=(), limit=24):
+        dv = jnp.where(half, up_ref[SECOND, at], down_ref[SECOND, at]).astype(jnp.float32) * ahead
+        dq_ref[:, at] = (dq_own_ref[:, at] + dqz).astype(jnp.bfloat16)
+        dk_ref[:, at] = (dkv_own_ref[0, :, at] + side_ref[FIRST, at].astype(jnp.float32) + dk).astype(jnp.bfloat16)
+        dv_ref[:, at] = (dkv_own_ref[1, :, at] + side_ref[SECOND, at].astype(jnp.float32) + dv).astype(jnp.bfloat16)
+
+
+def call(kernel, heads, flags, arrays, outs, flops, space=pltpu.VMEM, scratch=(), after=()):
     moved = sum(math.prod(a.shape) * a.dtype.itemsize for a in (*arrays, *outs))
     return pl.pallas_call(
-        functools.partial(kernel, heads),
+        lambda *refs: kernel(heads, *refs[len(after) :]),
         out_shape=outs,
-        in_specs=[pl.BlockSpec(memory_space=pltpu.SMEM)] * len(flags)
+        in_specs=[pl.BlockSpec(memory_space=pl.ANY)] * len(after)
+        + [pl.BlockSpec(memory_space=pltpu.SMEM)] * len(flags)
         + [pl.BlockSpec(memory_space=space)] * len(arrays),
         out_specs=[pl.BlockSpec(memory_space=pltpu.VMEM)] * len(outs),
         scratch_shapes=scratch,
-        compiler_params=pltpu.CompilerParams(vmem_limit_bytes=limit * 2**20),
+        compiler_params=pltpu.CompilerParams(vmem_limit_bytes=24 * 2**20),
         cost_estimate=pl.CostEstimate(flops=flops, bytes_accessed=moved, transcendentals=0),
-    )(*flags, *arrays)
+    )(*after, *flags, *arrays)
 
 
 def cycles(blocks, members):
@@ -583,7 +670,7 @@
     message = struct(width + TAIL, tokens)
     rows = struct(8, tokens, dtype=jnp.float32)
 
-    up_out, down_out = call(
+    payload = call(
         payload_kernel,
         heads,
         (),
@@ -593,67 +680,73 @@
         space=pltpu.HBM,
         scratch=(pltpu.SemaphoreType.DMA((4,)),),
     )
-    up_in, down_in = cycle(up_out, down_out)
-    queries_x, upstream_x = swap(queries), swap(upstream)
+    received = cycle(*payload)
+    keys_x, values_x = swap(keys), swap(values)
     diagonal, diagonal_lse, upstream_t = call(
-        diagonal_kernel, heads, (), (queries, keys, values, upstream), (wide_t, rows, flat_t), 3 * unit
-    )
-    up_in, down_in, queries_x, upstream_x = lax.optimization_barrier((up_in, down_in, queries_x, upstream_x))
-    out_z, out_x, ez, ex, mz, mx = call(
+        diagonal_kernel,
+        heads,
+        (),
+        (queries, keys, values, upstream),
+        (wide_t, rows, flat_t),
+        3 * unit,
+        after=(payload[0],),
+    )
+    out_z, ez, ex, out_x, mz, mx, lse_x = call(
         helper_kernel,
         heads,
-        (),
-        (up_in, down_in, queries_x, keys, values),
-        (message, message, wide_t, wide_t, rows, rows),
+        flags,
+        (*received, queries, keys_x, values_x),
+        (message, wide_t, wide_t, wide_t, rows, rows, rows),
         4 * unit,
-    )
-    back_z, back_x = ring(out_z, 2), swap(out_x)
-    own, own_lse, upstream_zt, upstream_xt = call(
+        after=(diagonal_lse,),
+    )
+    back_z = ring(out_z, 2)
+    own, own_lse, upstream_zt, e2, m2 = call(
         own_kernel,
         heads,
         flags,
-        (up_in, down_in, queries, upstream_x, diagonal, diagonal_lse),
-        (wide_t, rows, flat_t, flat_t),
+        (*received, queries, diagonal, diagonal_lse, out_x, lse_x),
+        (wide_t, rows, flat_t, wide_t, rows),
         3 * unit,
     )
     attention, sums = call(
-        merge_kernel, heads, flags, (own, own_lse, back_z, back_x, upstream_t), (message, rows), unit // 64
+        merge_kernel, heads, flags, (own, own_lse, back_z, upstream_t), (message, rows), unit // 64
     )
     others = [
         lax.ppermute(sums, "head", [(i, i ^ step) for i in range(members)]) for step in range(1, members)
     ]
-    attention_z, attention_x = ring(attention, -2), swap(attention)
+    attention_z = ring(attention, -2)
     sums = functools.reduce(jnp.add, others, sums)
-    sums_z, sums_x = ring(sums, -2), swap(sums)
-    dq_own, grads2_own, grad_t, delta = call(
+    sums_z = ring(sums, -2)
+    grad_t, delta, near_ds, near_grads = call(
         near_back_kernel,
         heads,
         flags,
-        (sums, queries, up_in, down_in, attention, upstream_t),
-        (wide, wide_pair, flat_t, rows),
-        5 * unit,
-    )
-    up_out, down_out, dq_x, dside = call(
+        (sums, queries, attention, upstream_t, *received, e2, m2),
+        (flat_t, rows, flat_t, wide_pair),
+        3 * unit,
+    )
+    up_out, down_out, side_out, side_ds = call(
         helper_back_kernel,
         heads,
         flags,
-        (sums_z, sums_x, up_in, down_in, queries_x, keys, values, attention_z, attention_x)
-        + (upstream_zt, upstream_xt, ez, ex, mz, mx, grads2_own),
-        (double, double, flat, wide_pair),
+        (sums_z, attention_z, upstream_zt, attention, grad_t, delta, *received, queries, keys_x, values_x)
+        + (ez, ex, mz, mx, near_grads),
+        (double, double, double, flat_t),
         8 * unit,
     )
-    up_in, down_in = cycle(up_out, down_out)
-    dq_x = swap(dq_x)
+    returned = cycle(up_out, down_out)
+    side_grads = swap(side_out)
     normed, dq_own, grads_own = call(
         diagonal_back_kernel,
         heads,
         (),
-        (sums, queries, keys, values, attention, grad_t, delta, dq_own, dside),
+        (sums, queries, keys, values, attention, grad_t, delta, near_ds, side_ds, keys_x, *received),
         (flat, wide, wide_pair),
-        6 * unit,
+        7 * unit,
     )
     grad_queries, grad_keys, grad_values = call(
-        final_kernel, heads, flags, (up_in, down_in, dq_x, dq_own, grads_own), (flat, flat, flat), 0
+        final_kernel, heads, flags, (dq_own, grads_own, side_grads, *returned), (flat, flat, flat), 0
     )
     return (normed, grad_queries, grad_keys, grad_values)
 

time: 60 us -> 58.1 us (0.968)
  waiting for transfers between devices: 23 us -> 27.6 us
  starting transfers between devices: 19 us -> 14.7 us
  Pallas kernels: 17.1 us -> 14.9 us
    ppermute x3, waiting for transfers between devices: 1.47 us -> 7.33 us  [ring(): lax.ppermute(array, 'ctx', [(i, (i + distance) % blocks) for i in range(b...]
    ppermute x6 -> x3, starting transfers between devices: 6.59 us -> 3.58 us  [swap(): return lax.ppermute(array, 'ctx', [(i, i ^ 1) for i in range(blocks)])]
    ppermute x2, waiting for transfers between devices: 4.15 us -> 1.21 us  [cycle(): lax.ppermute(up_array, ('ctx', 'head'), rising)]
    pallas_call x9, Pallas kernels: 17.1 us -> 14.9 us  [call(): pl.pallas_call(lambda *refs: kernel(heads, *refs[len(after):]), out_shape...]
    ppermute x6 -> x3, waiting for transfers between devices: 15.5 us -> 17 us  [swap(): return lax.ppermute(array, 'ctx', [(i, i ^ 1) for i in range(blocks)])]
    ppermute x3, starting transfers between devices: 5.34 us -> 4.12 us  [ring(): lax.ppermute(array, 'ctx', [(i, (i + distance) % blocks) for i in range(b...]
  transfers between devices with their start and end apart: 16 -> 13, of which waited for: 9 -> 9; matrix products, arithmetic and copies ran while one was open for 0% -> 0% of each run, Pallas kernels for 16% -> 12%
where the time goes in v4:
time: 58.1 us; the launch traced here: 58 us
  waiting for transfers between devices  27.6 us (48%)
  Pallas kernels  14.9 us (26%)
  starting transfers between devices  14.7 us (25%)
  between operations  0.72 us (1%)
    ppermute x3, waiting for transfers between devices, swap(): return lax.ppermute(array, 'ctx', [(i, i ^ 1) for i in range(blocks)])  17 us
    pallas_call x9, Pallas kernels, call(): pl.pallas_call(lambda *refs: kernel(heads, *refs[len(after):]), out_shape...  14.9 us
    ppermute x3, waiting for transfers between devices, ring(): lax.ppermute(array, 'ctx', [(i, (i + distance) % blocks) for i in range(b...  7.33 us
    ppermute x3, starting transfers between devices, ring(): lax.ppermute(array, 'ctx', [(i, (i + distance) % blocks) for i in range(b...  4.12 us
    ppermute x3, starting transfers between devices, swap(): return lax.ppermute(array, 'ctx', [(i, i ^ 1) for i in range(blocks)])  3.58 us
    ppermute x2, starting transfers between devices, cycle(): lax.ppermute(up_array, ('ctx', 'head'), rising)  3.36 us
    ppermute x3, starting transfers between devices, meeting_shards(): lax.ppermute(sums, 'head', [(i, i ^ step) for i in range(members)])  1.86 us
    ppermute x3, waiting for transfers between devices, meeting_shards(): lax.ppermute(sums, 'head', [(i, i ^ step) for i in range(members)])  1.78 us
  transfers between devices with their start and end apart: 13, of which 9 were waited for; matrix products, arithmetic and copies ran while one was open for 0% of the time, Pallas kernels for 12%

profile of v4, /device:TPU:0, one launch (start us, length us, event | category | flops | bytes accessed | tf_op | source)
XLA Modules:
  0.0 58.0 jit_solution(6567398547766626256)
XLA Ops:
  0.7 1.3 %shard_map.84 = (bf16[256,1024]{1,0:T(8,128)(2,1)S(1)}, bf16[256,1024]{1,0:T(8,128)(2,1)S(1)}) custom-call(bf16[128,1024]{1,0:T(8,128)(2,1)} %refs_1_.7, bf16[128,1024]{1,0:T(8,128)(2,1)} %refs_2_.7, bf16[128,1024]{1,0:T(8,128)(2,1)} %refs_3_.7, bf16[128,1024]{1,0:T(8,128)(2,1)} %refs_4_.2), custom_call_target="tpu_custom_call" | custom-call | bytes 2097152 | tf_op jit(solution)/shard_map/pallas_call | solution.py:615
  2.0 3.1 %collective-permute-start = (bf16[256,1024]{1,0:T(8,128)(2,1)S(1)}, bf16[256,1024]{1,0:T(8,128)(2,1)S(1)}, u32[]{:S(2)}, u32[]{:S(2)}) collective-permute-start(bf16[256,1024]{1,0:T(8,128)(2,1)S(1)} %get-tuple-element.37.refs_0_), channel_id=1, source_target_pairs={{0,8},{1,9},{2,0},{3,1},{4,12},{5,13},{6,4},{7,5},{8,16},{9,17},{1... | collective-permute-start | bytes 1572872 | tf_op jit(solution)/shard_map/ppermute | solution.py:652
  5.1 1.9 %collective-permute-start.2 = (bf16[128,1024]{1,0:T(8,128)(2,1)S(1)}, bf16[128,1024]{1,0:T(8,128)(2,1)S(1)}, u32[]{:S(2)}, u32[]{:S(2)}) collective-permute-start(bf16[128,1024]{1,0:T(8,128)(2,1)S(1)} %copy-done.1), channel_id=1, source_target_pairs={{0,4},{4,0},{8,12},{12,8},{16,20},{20,16},{24,28},{28,24},{1,5},{5... | collective-permute-start | bytes 786440 | tf_op jit(solution)/shard_map/ppermute | solution.py:657
  7.1 1.8 %shard_map.85 = (f32[1024,128]{1,0:T(8,128)S(1)}, f32[8,128]{1,0:T(8,128)S(1)}, bf16[1024,128]{1,0:T(8,128)(2,1)S(1)}) custom-call(bf16[256,1024]{1,0:T(8,128)(2,1)S(1)} %get-tuple-element.37.refs_0_, bf16[128,1024]{1,0:T(8,128)(2,1)S(1)} %copy-done, bf16[128,1024]{1,0:T(8,128)(2,1)S(1)} %copy-done.1, bf16[128,1024]{1,0:T(8,128)(2,1)S(1)} %copy-done.2, ...), custom_call_target="tpu_custom_call" | custom-call | flops 100663296 | bytes 1839104 | tf_op jit(solution)/shard_map/pallas_call | solution.py:615
  8.9 5.4 %collective-permute-done.2.refs_5_.refs_10_.refs_9_ = bf16[128,1024]{1,0:T(8,128)(2,1)S(1)} collective-permute-done((bf16[128,1024]{1,0:T(8,128)(2,1)S(1)}, bf16[128,1024]{1,0:T(8,128)(2,1)S(1)}, u32[]{:S(2)}, u32[]{:S(2)}) %collective-permute-start.2) | collective-permute-done | bytes 262176 | tf_op jit(solution)/shard_map/ppermute | solution.py:657
  14.3 4.2 %collective-permute-done.3.refs_6_.refs_11_ = bf16[128,1024]{1,0:T(8,128)(2,1)S(1)} collective-permute-done((bf16[128,1024]{1,0:T(8,128)(2,1)S(1)}, bf16[128,1024]{1,0:T(8,128)(2,1)S(1)}, u32[]{:S(2)}, u32[]{:S(2)}) %collective-permute-start.3) | collective-permute-done | bytes 262176 | tf_op jit(solution)/shard_map/ppermute | solution.py:657
  18.5 1.9 %shard_map.86 = (bf16[1056,128]{1,0:T(8,128)(2,1)S(1)}, f32[1024,128]{1,0:T(8,128)S(1)}, f32[1024,128]{1,0:T(8,128)S(1)}, f32[1024,128]{1,0:T(8,128)S(1)}, f32[8...) custom-call(f32[8,128]{1,0:T(8,128)S(1)} %get-tuple-element.40.refs_0_.refs_5_, s32[8,8]{1,0:T(8,128)S(1)} %copy-done.4, ...), custom_call_target="tpu_custom_call" | custom-call | flops 134217728 | bytes 3690496 | tf_op jit(solution)/shard_map/pallas_call | solution.py:615
  20.3 1.8 %collective-permute-start.4 = (bf16[1056,128]{1,0:T(8,128)(2,1)S(1)}, bf16[1056,128]{1,0:T(8,128)(2,1)S(1)}, u32[]{:S(2)}, u32[]{:S(2)}) collective-permute-start(bf16[1056,128]{1,0:T(8,128)(2,1)S(1)} %get-tuple-element.45), channel_id=1, source_target_pairs={{0,8},{4,12},{8,16},{12,20},{16,24},{20,28},{24,0},{28,4},{1,9},{5... | collective-permute-start | bytes 811016 | tf_op jit(solution)/shard_map/ppermute | solution.py:660
  22.1 1.6 %shard_map.87 = (f32[1024,128]{1,0:T(8,128)S(1)}, f32[8,128]{1,0:T(8,128)S(1)}, bf16[1024,128]{1,0:T(8,128)(2,1)S(1)}, f32[1024,128]{1,0:T(8,128)S(1)}, f32[8,128]{1,0:T(8,128)S(1)}) custom-call(s32[8,8]{1,0:T(8,128)S(1)} %copy-done.4, bf16[256,1024]{1,0:T(8,128)(2,1)S(1)} %collective-permute-done.refs_2_.refs_1_.refs_5_.refs_7_.refs_10_, ...), custom_call_target="tpu_custom_call" | custom-call | flops 100663296 | bytes 3686400 | tf_op jit(solution)/shard_map/pallas_call | solution.py:615
  23.7 5.5 %collective-permute-done.4.refs_3_ = bf16[1056,128]{1,0:T(8,128)(2,1)S(1)} collective-permute-done((bf16[1056,128]{1,0:T(8,128)(2,1)S(1)}, bf16[1056,128]{1,0:T(8,128)(2,1)S(1)}, u32[]{:S(2)}, u32[]{:S(2)}) %collective-permute-start.4) | collective-permute-done | bytes 270368 | tf_op jit(solution)/shard_map/ppermute | solution.py:660
  29.2 0.8 %shard_map.88 = (bf16[1056,128]{1,0:T(8,128)(2,1)S(1)}, f32[8,128]{1,0:T(8,128)S(1)}) custom-call(s32[8,8]{1,0:T(8,128)S(1)} %copy-done.4, f32[1024,128]{1,0:T(8,128)S(1)} %get-tuple-element.43.refs_1_, f32[8,128]{1,0:T(8,128)S(1)} %get-tuple-element.44.refs_2_, bf16[1056,128]{1,0:T(8,128)(2,1)S(1)} %collective-permute-done.4.refs_3_, ...), custom_call_target="tpu_custom_call" | custom-call | flops 524288 | bytes 1335296 | tf_op jit(solution)/shard_map/pallas_call | solution.py:615
  30.1 1.8 %collective-permute-start.9 = (bf16[1056,128]{1,0:T(8,128)(2,1)S(1)}, bf16[1056,128]{1,0:T(8,128)(2,1)S(1)}, u32[]{:S(2)}, u32[]{:S(2)}) collective-permute-start(bf16[1056,128]{1,0:T(8,128)(2,1)S(1)} %get-tuple-element.48.refs_3_.refs_4_), channel_id=1, source_target_pairs={{0,24},{4,28},{8,0},{12,4},{16,8},{20,12},{24,16},{28,20},{1,25},{... | collective-permute-start | bytes 811016 | tf_op jit(solution)/shard_map/ppermute | solution.py:660
  31.8 1.5 %collective-permute-start.6 = (f32[8,128]{1,0:T(8,128)S(1)}, f32[8,128]{1,0:T(8,128)S(1)}, u32[]{:S(2)}, u32[]{:S(2)}) collective-permute-start(f32[8,128]{1,0:T(8,128)S(1)} %get-tuple-element.47), channel_id=1, source_target_pairs={{0,2},{1,3},{2,0},{3,1},{4,6},{5,7},{6,4},{7,5},{8,10},{9,11},{10,... | collective-permute-start | bytes 12296 | tf_op jit(solution)/shard_map/ppermute | solution.py:716
  33.7 1.2 %collective-permute-done.7 = f32[8,128]{1,0:T(8,128)S(1)} collective-permute-done((f32[8,128]{1,0:T(8,128)S(1)}, f32[8,128]{1,0:T(8,128)S(1)}, u32[]{:S(2)}, u32[]{:S(2)}) %collective-permute-start.7) | collective-permute-done | bytes 4128 | tf_op jit(solution)/shard_map/ppermute | solution.py:716
  34.9 0.6 %collective-permute-done.6 = f32[8,128]{1,0:T(8,128)S(1)} collective-permute-done((f32[8,128]{1,0:T(8,128)S(1)}, f32[8,128]{1,0:T(8,128)S(1)}, u32[]{:S(2)}, u32[]{:S(2)}) %collective-permute-start.6) | collective-permute-done | bytes 4128 | tf_op jit(solution)/shard_map/ppermute | solution.py:716
  36.0 1.2 %shard_map.89 = (bf16[1024,128]{1,0:T(8,128)(2,1)S(1)}, f32[8,128]{1,0:T(8,128)S(1)}, bf16[1024,128]{1,0:T(8,128)(2,1)S(1)}, f32[2,128,1024]{2,1,0:T(8,128)S(1)}) custom-call(s32[8,8]{1,0:T(8,128)S(1)} %copy-done.4, f32[8,128]{1,0:T(8,128)S(1)} %add_add_fusion.refs_1_.refs_0_, bf16[128,1024]{1,0:T(8,128)(2,1)S(1)} %copy-done, ...), custom_call_target="tpu_custom_call" | custom-call | flops 100663296 | bytes 3952640 | tf_op jit(solution)/shard_map/pallas_call | solution.py:615
  37.3 1.9 %collective-permute-done.8.refs_1_ = f32[8,128]{1,0:T(8,128)S(1)} collective-permute-done((f32[8,128]{1,0:T(8,128)S(1)}, f32[8,128]{1,0:T(8,128)S(1)}, u32[]{:S(2)}, u32[]{:S(2)}) %collective-permute-start.8) | collective-permute-done | bytes 4128 | tf_op jit(solution)/shard_map/ppermute | solution.py:660
  39.2 2.0 %shard_map.90 = (bf16[256,1024]{1,0:T(8,128)(2,1)S(1)}, bf16[256,1024]{1,0:T(8,128)(2,1)S(1)}, bf16[256,1024]{1,0:T(8,128)(2,1)S(1)}, bf16[1024,128]{1,0:T(8,128)(2,1)S(1)}) custom-call(s32[8,8]{1,0:T(8,128)S(1)} %copy-done.4, f32[8,128]{1,0:T(8,128)S(1)} %collective-permute-done.8.refs_1_, bf16[1056,128]{1,0:T(8,128)(2,1)S(1)} %collective-permute-done.9.refs_2_, ...), custom_call_target="tpu_custom_call" | custom-call | flops 268435456 | bytes 6848512 | tf_op jit(solution)/shard_map/pallas_call | solution.py:615
  41.2 1.6 %collective-permute-start.10 = (bf16[256,1024]{1,0:T(8,128)(2,1)S(1)}, bf16[256,1024]{1,0:T(8,128)(2,1)S(1)}, u32[]{:S(2)}, u32[]{:S(2)}) collective-permute-start(bf16[256,1024]{1,0:T(8,128)(2,1)S(1)} %get-tuple-element.64), channel_id=1, source_target_pairs={{0,4},{4,0},{8,12},{12,8},{16,20},{20,16},{24,28},{28,24},{1,5},{5... | collective-permute-start | bytes 1572872 | tf_op jit(solution)/shard_map/ppermute | solution.py:657
  43.0 1.7 %collective-permute-start.12 = (bf16[256,1024]{1,0:T(8,128)(2,1)S(1)}, bf16[256,1024]{1,0:T(8,128)(2,1)S(1)}, u32[]{:S(2)}, u32[]{:S(2)}) collective-permute-start(bf16[256,1024]{1,0:T(8,128)(2,1)S(1)} %get-tuple-element.66), channel_id=1, source_target_pairs={{8,0},{9,1},{0,2},{1,3},{12,4},{13,5},{4,6},{5,7},{16,8},{17,9},{2... | collective-permute-start | bytes 1572872 | tf_op jit(solution)/shard_map/ppermute | solution.py:652
  44.8 2.4 %shard_map.91 = (bf16[128,1024]{1,0:T(8,128)(2,1)}, f32[128,1024]{1,0:T(8,128)S(1)}, f32[2,128,1024]{2,1,0:T(8,128)S(1)}) custom-call(f32[8,128]{1,0:T(8,128)S(1)} %add_add_fusion.refs_1_.refs_0_, bf16[128,1024]{1,0:T(8,128)(2,1)S(1)} %copy-done, bf16[128,1024]{1,0:T(8,128)(2,1)S(1)} %copy-done.1, bf16[128,1024]{1,0:T(8,128)(2,1)S(1)} %copy-done.2, ...), custom_call_target="tpu_custom_call" | custom-call | flops 234881024 | bytes 4997120 | tf_op jit(solution)/shard_map/pallas_call | solution.py:615
  47.2 7.4 %collective-permute-done.10.refs_3_ = bf16[256,1024]{1,0:T(8,128)(2,1)S(1)} collective-permute-done((bf16[256,1024]{1,0:T(8,128)(2,1)S(1)}, bf16[256,1024]{1,0:T(8,128)(2,1)S(1)}, u32[]{:S(2)}, u32[]{:S(2)}) %collective-permute-start.10) | collective-permute-done | bytes 524320 | tf_op jit(solution)/shard_map/ppermute | solution.py:657
  54.6 1.2 %collective-permute-done.11.refs_4_ = bf16[256,1024]{1,0:T(8,128)(2,1)S(1)} collective-permute-done((bf16[256,1024]{1,0:T(8,128)(2,1)S(1)}, bf16[256,1024]{1,0:T(8,128)(2,1)S(1)}, u32[]{:S(2)}, u32[]{:S(2)}) %collective-permute-start.11) | collective-permute-done | bytes 524320 | tf_op jit(solution)/shard_map/ppermute | solution.py:652
  56.1 1.9 %shard_map.92 = (bf16[128,1024]{1,0:T(8,128)(2,1)}, bf16[128,1024]{1,0:T(8,128)(2,1)}, bf16[128,1024]{1,0:T(8,128)(2,1)}) custom-call(s32[8,8]{1,0:T(8,128)S(1)} %copy-done.4, f32[128,1024]{1,0:T(8,128)S(1)} %get-tuple-element.62.refs_1_, f32[2,128,1024]{2,1,0:T(8,128)S(1)} %get-tuple-element.63.refs_2_, ...), custom_call_target="tpu_custom_call" | custom-call | bytes 3932160 | tf_op jit(solution)/shard_map/pallas_call | solution.py:615
  (22 shorter events, 1.6 us)
Async XLA Ops:
  0.6 6.5 %copy-start = (bf16[128,1024]{1,0:T(8,128)(2,1)S(1)}, bf16[128,1024]{1,0:T(8,128)(2,1)}, u32[]{:S(2)}) copy-start(bf16[128,1024]{1,0:T(8,128)(2,1)} %refs_1_.7) | copy-start | bytes 786436
  0.6 4.4 %copy-start.1 = (bf16[128,1024]{1,0:T(8,128)(2,1)S(1)}, bf16[128,1024]{1,0:T(8,128)(2,1)}, u32[]{:S(2)}) copy-start(bf16[128,1024]{1,0:T(8,128)(2,1)} %refs_2_.7) | copy-start | bytes 786436
  0.7 6.4 %copy-start.2 = (bf16[128,1024]{1,0:T(8,128)(2,1)S(1)}, bf16[128,1024]{1,0:T(8,128)(2,1)}, u32[]{:S(2)}) copy-start(bf16[128,1024]{1,0:T(8,128)(2,1)} %refs_3_.7) | copy-start | bytes 786436
  0.7 6.5 %copy-start.3 = (bf16[128,1024]{1,0:T(8,128)(2,1)S(1)}, bf16[128,1024]{1,0:T(8,128)(2,1)}, u32[]{:S(2)}) copy-start(bf16[128,1024]{1,0:T(8,128)(2,1)} %refs_4_.2) | copy-start | bytes 786436
  2.0 16.5 %collective-permute-start = (bf16[256,1024]{1,0:T(8,128)(2,1)S(1)}, bf16[256,1024]{1,0:T(8,128)(2,1)S(1)}, u32[]{:S(2)}, u32[]{:S(2)}) collective-permute-start(bf16[256,1024]{1,0:T(8,128)(2,1)S(1)} %get-tuple-element.37.refs_0_), channel_id=1, source_target_pairs={{0,8},{1,9},{2,0},{3,1},{4,12},{5,13},{6,4},{7,5},{8,16},{9,17},{1... | collective-permute-start | bytes 1572872 | tf_op jit(solution)/shard_map/ppermute | solution.py:652
  5.1 13.4 %collective-permute-start.1 = (bf16[256,1024]{1,0:T(8,128)(2,1)S(1)}, bf16[256,1024]{1,0:T(8,128)(2,1)S(1)}, u32[]{:S(2)}, u32[]{:S(2)}) collective-permute-start(bf16[256,1024]{1,0:T(8,128)(2,1)S(1)} %get-tuple-element.38), channel_id=1, source_target_pairs={{8,0},{9,1},{0,2},{1,3},{12,4},{13,5},{4,6},{5,7},{16,8},{17,9},{2... | collective-permute-start | bytes 1572872 | tf_op jit(solution)/shard_map/ppermute | solution.py:652
  5.1 9.2 %collective-permute-start.2 = (bf16[128,1024]{1,0:T(8,128)(2,1)S(1)}, bf16[128,1024]{1,0:T(8,128)(2,1)S(1)}, u32[]{:S(2)}, u32[]{:S(2)}) collective-permute-start(bf16[128,1024]{1,0:T(8,128)(2,1)S(1)} %copy-done.1), channel_id=1, source_target_pairs={{0,4},{4,0},{8,12},{12,8},{16,20},{20,16},{24,28},{28,24},{1,5},{5... | collective-permute-start | bytes 786440 | tf_op jit(solution)/shard_map/ppermute | solution.py:657
  7.0 11.5 %collective-permute-start.3 = (bf16[128,1024]{1,0:T(8,128)(2,1)S(1)}, bf16[128,1024]{1,0:T(8,128)(2,1)S(1)}, u32[]{:S(2)}, u32[]{:S(2)}) collective-permute-start(bf16[128,1024]{1,0:T(8,128)(2,1)S(1)} %copy-done.2), channel_id=1, source_target_pairs={{0,4},{4,0},{8,12},{12,8},{16,20},{20,16},{24,28},{28,24},{1,5},{5... | collective-permute-start | bytes 786440 | tf_op jit(solution)/shard_map/ppermute | solution.py:657
  7.1 11.4 %copy-start.4 = (s32[8,8]{1,0:T(8,128)S(1)}, s32[8,8]{1,0:T(8,128)}, u32[]{:S(2)}) copy-start(s32[8,8]{1,0:T(8,128)} %refs_0_.11) | copy-start | bytes 772
  20.3 8.9 %collective-permute-start.4 = (bf16[1056,128]{1,0:T(8,128)(2,1)S(1)}, bf16[1056,128]{1,0:T(8,128)(2,1)S(1)}, u32[]{:S(2)}, u32[]{:S(2)}) collective-permute-start(bf16[1056,128]{1,0:T(8,128)(2,1)S(1)} %get-tuple-element.45), channel_id=1, source_target_pairs={{0,8},{4,12},{8,16},{12,20},{16,24},{20,28},{24,0},{28,4},{1,9},{5... | collective-permute-start | bytes 811016 | tf_op jit(solution)/shard_map/ppermute | solution.py:660
  30.1 9.1 %collective-permute-start.9 = (bf16[1056,128]{1,0:T(8,128)(2,1)S(1)}, bf16[1056,128]{1,0:T(8,128)(2,1)S(1)}, u32[]{:S(2)}, u32[]{:S(2)}) collective-permute-start(bf16[1056,128]{1,0:T(8,128)(2,1)S(1)} %get-tuple-element.48.refs_3_.refs_4_), channel_id=1, source_target_pairs={{0,24},{4,28},{8,0},{12,4},{16,8},{20,12},{24,16},{28,20},{1,25},{... | collective-permute-start | bytes 811016 | tf_op jit(solution)/shard_map/ppermute | solution.py:660
  31.8 3.1 %collective-permute-start.7 = (f32[8,128]{1,0:T(8,128)S(1)}, f32[8,128]{1,0:T(8,128)S(1)}, u32[]{:S(2)}, u32[]{:S(2)}) collective-permute-start(f32[8,128]{1,0:T(8,128)S(1)} %get-tuple-element.47), channel_id=1, source_target_pairs={{0,3},{1,2},{2,1},{3,0},{4,7},{5,6},{6,5},{7,4},{8,11},{9,10},{10,... | collective-permute-start | bytes 12296 | tf_op jit(solution)/shard_map/ppermute | solution.py:716
  31.8 3.6 %collective-permute-start.6 = (f32[8,128]{1,0:T(8,128)S(1)}, f32[8,128]{1,0:T(8,128)S(1)}, u32[]{:S(2)}, u32[]{:S(2)}) collective-permute-start(f32[8,128]{1,0:T(8,128)S(1)} %get-tuple-element.47), channel_id=1, source_target_pairs={{0,2},{1,3},{2,0},{3,1},{4,6},{5,7},{6,4},{7,5},{8,10},{9,11},{10,... | collective-permute-start | bytes 12296 | tf_op jit(solution)/shard_map/ppermute | solution.py:716
  33.3 2.1 %collective-permute-start.5 = (f32[8,128]{1,0:T(8,128)S(1)}, f32[8,128]{1,0:T(8,128)S(1)}, u32[]{:S(2)}, u32[]{:S(2)}) collective-permute-start(f32[8,128]{1,0:T(8,128)S(1)} %get-tuple-element.47), channel_id=1, source_target_pairs={{0,1},{1,0},{2,3},{3,2},{4,5},{5,4},{6,7},{7,6},{8,9},{9,8},{10,11... | collective-permute-start | bytes 12296 | tf_op jit(solution)/shard_map/ppermute | solution.py:716
  35.5 3.7 %collective-permute-start.8 = (f32[8,128]{1,0:T(8,128)S(1)}, f32[8,128]{1,0:T(8,128)S(1)}, u32[]{:S(2)}, u32[]{:S(2)}) collective-permute-start(f32[8,128]{1,0:T(8,128)S(1)} %add_add_fusion.refs_1_.refs_0_), channel_id=1, source_target_pairs={{0,24},{4,28},{8,0},{12,4},{16,8},{20,12},{24,16},{28,20},{1,25},{... | collective-permute-start | bytes 12296 | tf_op jit(solution)/shard_map/ppermute | solution.py:660
  41.2 13.4 %collective-permute-start.10 = (bf16[256,1024]{1,0:T(8,128)(2,1)S(1)}, bf16[256,1024]{1,0:T(8,128)(2,1)S(1)}, u32[]{:S(2)}, u32[]{:S(2)}) collective-permute-start(bf16[256,1024]{1,0:T(8,128)(2,1)S(1)} %get-tuple-element.64), channel_id=1, source_target_pairs={{0,4},{4,0},{8,12},{12,8},{16,20},{20,16},{24,28},{28,24},{1,5},{5... | collective-permute-start | bytes 1572872 | tf_op jit(solution)/shard_map/ppermute | solution.py:657
  42.7 13.1 %collective-permute-start.11 = (bf16[256,1024]{1,0:T(8,128)(2,1)S(1)}, bf16[256,1024]{1,0:T(8,128)(2,1)S(1)}, u32[]{:S(2)}, u32[]{:S(2)}) collective-permute-start(bf16[256,1024]{1,0:T(8,128)(2,1)S(1)} %get-tuple-element.65), channel_id=1, source_target_pairs={{0,8},{1,9},{2,0},{3,1},{4,12},{5,13},{6,4},{7,5},{8,16},{9,17},{1... | collective-permute-start | bytes 1572872 | tf_op jit(solution)/shard_map/ppermute | solution.py:652
  43.0 13.1 %collective-permute-start.12 = (bf16[256,1024]{1,0:T(8,128)(2,1)S(1)}, bf16[256,1024]{1,0:T(8,128)(2,1)S(1)}, u32[]{:S(2)}, u32[]{:S(2)}) collective-permute-start(bf16[256,1024]{1,0:T(8,128)(2,1)S(1)} %get-tuple-element.66), channel_id=1, source_target_pairs={{8,0},{9,1},{0,2},{1,3},{12,4},{13,5},{4,6},{5,7},{16,8},{17,9},{2... | collective-permute-start | bytes 1572872 | tf_op jit(solution)/shard_map/ppermute | solution.py:652

commit v5 on v4

--- a/solution.py
+++ b/solution.py
@@ -198,25 +198,37 @@
 TAIL = 32
 
 
-class Flags:
-    def __init__(self, pattern_ref=None):
-        me, member = lax.axis_index("ctx"), lax.axis_index("head")
-        self.odd = lax.rem(me, 2) == 1
-        self.half = member >= lax.axis_size("head") // 2
-        if pattern_ref is None:
-            return
-        blocks = pattern_ref.shape[0]
-        even = jnp.logical_not(self.odd)
-        ahead = jnp.minimum(me + 2, blocks - 1)
-        self.ahead = me + 2 < blocks
-        self.near = pattern_ref[me, 1] >= 0
-        self.far = jnp.logical_and(self.ahead, pattern_ref[ahead, 2] >= 0)
-        ahead_side = jnp.logical_and(self.ahead, pattern_ref[ahead, 0] >= 0)
-        own_side = pattern_ref[me, 0] >= 0
-        self.side = jnp.logical_or(
-            jnp.logical_and(self.odd, own_side), jnp.logical_and(even, ahead_side)
-        )
-        self.helped = jnp.logical_or(pattern_ref[me, 2] >= 0, jnp.logical_and(even, own_side))
+NEAR, FAR, SIDE, HELPED, LOCAL = range(5)
+
+
+class Place:
+    def __init__(self):
+        self.me = lax.axis_index("ctx")
+        self.odd = lax.rem(self.me, 2) == 1
+        self.half = lax.axis_index("head") >= lax.axis_size("head") // 2
+
+
+def bias_rows(pattern_ref):
+    place = Place()
+    me, odd, even = place.me, place.odd, jnp.logical_not(place.odd)
+    blocks = pattern_ref.shape[0]
+    ahead = jnp.minimum(me + 2, blocks - 1)
+    has_ahead = me + 2 < blocks
+    ahead_side = jnp.logical_and(has_ahead, pattern_ref[ahead, 0] >= 0)
+    own_side = pattern_ref[me, 0] >= 0
+    local = jnp.logical_and(odd, own_side)
+    held = {
+        NEAR: pattern_ref[me, 1] >= 0,
+        FAR: jnp.logical_and(has_ahead, pattern_ref[ahead, 2] >= 0),
+        SIDE: jnp.logical_or(local, jnp.logical_and(even, ahead_side)),
+        HELPED: jnp.logical_or(pattern_ref[me, 2] >= 0, jnp.logical_and(even, own_side)),
+        LOCAL: local,
+    }
+    row = lax.broadcasted_iota(jnp.int32, (8, BLOCK), 0)
+    rows = jnp.zeros((8, BLOCK), jnp.float32)
+    for index, flag in held.items():
+        rows = jnp.where(row == index, jnp.where(flag, 0.0, NEG_BIG), rows)
+    return rows
 
 
 def mm(a, b, dims):
@@ -267,7 +279,7 @@
 
 
 def payload_kernel(heads, q_ref, k_ref, v_ref, u_ref, up_ref, down_ref, sems):
-    half = Flags().half
+    half = Place().half
     top, bottom = pl.ds(0, BLOCK), pl.ds(BLOCK, BLOCK)
 
     def move(sources):
@@ -290,7 +302,8 @@
         move((q_ref, u_ref, k_ref, v_ref))
 
 
-def diagonal_kernel(heads, q_ref, k_ref, v_ref, u_ref, out_ref, lse_ref, ut_ref):
+def diagonal_kernel(heads, pattern_ref, q_ref, k_ref, v_ref, u_ref, out_ref, lse_ref, ut_ref, bias_ref):
+    bias_ref[...] = bias_rows(pattern_ref)
     causal = causal_mask()
     rows = []
     for h in range(heads):
@@ -310,73 +323,65 @@
 
 
 def helper_kernel(
-    heads,
-    pattern_ref,
-    up_ref,
-    down_ref,
-    q_ref,
-    kx_ref,
-    vx_ref,
-    oz_ref,
-    ez_ref,
-    ex_ref,
-    outx_ref,
-    mz_ref,
-    mx_ref,
-    lsex_ref,
+    heads, bias_ref, up_ref, down_ref, q_ref, kx_ref, vx_ref, oz_ref, ez_ref, ex_ref, mz_ref, mx_ref
 ):
-    flags = Flags(pattern_ref)
-    odd, half = flags.odd, flags.half
-    joins = jnp.logical_and(flags.side, jnp.logical_not(odd))
-    z_rows, x_rows, z_tops, x_tops = [], [], [], []
-    for start in range(0, heads, 2):
-        pairs = []
-        for h in range(start, start + 2):
+    place = Place()
+    odd, half = place.odd, place.half
+    far, side = bias_ref[FAR : FAR + 1], bias_ref[SIDE : SIDE + 1]
+    step = 4
+    z_rows, z_tops, x_tops = [], [], []
+    for start in range(0, heads, step):
+        group = range(start, start + step)
+        scores, weights, totals = [], [], []
+        for h in group:
             at = rows_of(h)
             up_a, down_a = up_ref[FIRST, at], down_ref[FIRST, at]
             k2, qz = jnp.where(half, down_a, up_a), jnp.where(half, up_a, down_a)
-            v2 = jnp.where(half, down_ref[SECOND, at], up_ref[SECOND, at])
-            pairs.append((score_tile(k2, qz), v2))
-            pairs.append((score_tile(kx_ref[:, at], jnp.where(odd, q_ref[:, at], qz)), vx_ref[:, at]))
-        parts = softmax_parts(pairs)
-        for n, h in enumerate(range(start, start + 2)):
-            at = rows_of(h)
-            (z_out, z_top, z_lse, ez_ref[at]), (x_out, x_top, x_lse, ex_ref[at]) = parts[2 * n : 2 * n + 2]
-            out, lse = merged(
-                [(z_out, jnp.where(flags.far, z_lse, NEG_BIG)), (x_out, jnp.where(joins, x_lse, NEG_BIG))]
-            )
-            oz_ref[at] = out.astype(jnp.bfloat16)
-            outx_ref[at] = x_out
-            z_rows.append(lse)
-            x_rows.append(x_lse)
+            qx = jnp.where(odd, q_ref[:, at], qz)
+            scores.append((score_tile(k2, qz) + far, score_tile(kx_ref[:, at], qx) + side))
+        for h, (z, x) in zip(group, scores):
+            z_top, x_top = z.max(axis=0, keepdims=True), x.max(axis=0, keepdims=True)
+            both = jnp.maximum(z_top, x_top)
+            z_top, x_top = jnp.where(odd, z_top, both), jnp.where(odd, x_top, both)
+            z, x = jnp.exp(z - z_top), jnp.exp(x - x_top)
+            ez_ref[rows_of(h)], ex_ref[rows_of(h)] = z, x
+            x = jnp.where(odd, 0.0, x)
+            total = z.sum(axis=0, keepdims=True) + x.sum(axis=0, keepdims=True)
+            weights.append(jnp.concatenate([z, x], axis=0).astype(jnp.bfloat16))
+            totals.append(total)
+            z_rows.append(z_top + jnp.log(total))
             z_tops.append(z_top)
             x_tops.append(x_top)
+        for h, w, total in zip(group, weights, totals):
+            at = rows_of(h)
+            v2 = jnp.where(half, down_ref[SECOND, at], up_ref[SECOND, at])
+            out = mm(jnp.concatenate([v2, vx_ref[:, at]], axis=0), w, TN) * (1.0 / total)
+            oz_ref[at] = out.astype(jnp.bfloat16)
     oz_ref[heads * HD :] = split_rows(stack_rows(z_rows))
-    lsex_ref[...] = stack_rows(x_rows)
     mz_ref[...] = stack_rows(z_tops)
     mx_ref[...] = stack_rows(x_tops)
 
 
 def own_kernel(
     heads,
-    pattern_ref,
+    bias_ref,
     up_ref,
     down_ref,
     q_ref,
     out_ref,
     lse_ref,
-    outx_ref,
-    lsex_ref,
+    vx_ref,
+    ex_ref,
+    mx_ref,
     own_ref,
     total_ref,
     uzt_ref,
     e_ref,
     m_ref,
 ):
-    flags = Flags(pattern_ref)
-    half = flags.half
-    local = jnp.logical_and(flags.odd, flags.side)
-    before, side = lse_ref[...], jnp.where(local, lsex_ref[...], NEG_BIG)
+    half = Place().half
+    near, local = bias_ref[NEAR : NEAR + 1], bias_ref[LOCAL : LOCAL + 1]
+    before = lse_ref[...]
     rows, tops = [], []
     for start in range(0, heads, 2):
         group = range(start, start + 2)
@@ -389,11 +394,14 @@
             pairs.append((score_tile(k2, q_ref[:, at]), jnp.where(half, down_b, up_b)))
         for h, (out, top, lse, e_ref[rows_of(h)]) in zip(group, softmax_parts(pairs)):
             at, row = rows_of(h), slice(h, h + 1)
+            weights = ex_ref[at]
+            side = jnp.maximum(weights.sum(axis=0, keepdims=True), 1.0)
+            side_out = mm(vx_ref[:, at], weights.astype(jnp.bfloat16), TN) * (1.0 / side)
             own_ref[at], total = merged(
                 [
                     (out_ref[at], before[row]),
-                    (out, jnp.where(flags.near, lse, NEG_BIG)),
-                    (outx_ref[at], side[row]),
+                    (out, lse + near),
+                    (side_out, mx_ref[row] + jnp.log(side) + local),
                 ]
             )
             rows.append(total)
@@ -402,13 +410,12 @@
     m_ref[...] = stack_rows(tops)
 
 
-def merge_kernel(heads, pattern_ref, own_ref, lse_ref, rz_ref, ut_ref, a_ref, sums_ref):
-    flags = Flags(pattern_ref)
+def merge_kernel(heads, bias_ref, own_ref, lse_ref, rz_ref, ut_ref, a_ref, sums_ref):
     tail = slice(heads * HD, heads * HD + TAIL)
     squares = jnp.zeros((8, BLOCK), jnp.float32)
     crosses = jnp.zeros((8, BLOCK), jnp.float32)
     own = lse_ref[...]
-    z = jnp.where(flags.helped, joined_rows(rz_ref[tail]), NEG_BIG)
+    z = joined_rows(rz_ref[tail]) + bias_ref[HELPED : HELPED + 1]
     highest = jnp.maximum(own, z)
     total = highest + jnp.log(jnp.exp(own - highest) + jnp.exp(z - highest))
     own, z = jnp.exp(own - total), jnp.exp(z - total)
@@ -441,7 +448,7 @@
 
 def near_back_kernel(
     heads,
-    pattern_ref,
+    bias_ref,
     sums_ref,
     q_ref,
     a_ref,
@@ -453,12 +460,12 @@
     grad_ref,
     delta_ref,
     ds_ref,
-    dkv2_ref,
+    dk2_ref,
+    dv2_ref,
 ):
-    flags = Flags(pattern_ref)
-    half = flags.half
+    half = Place().half
     norm = norm_rows(sums_ref)
-    scale = jnp.where(flags.near, jnp.exp(m_ref[...] - total_rows(a_ref)), 0.0)
+    scale = jnp.exp(m_ref[...] - total_rows(a_ref) + bias_ref[NEAR : NEAR + 1])
     deltas = []
     for start in range(0, heads, 4):
         group = range(start, start + 4)
@@ -478,14 +485,14 @@
         for h, (dscore, probs), (grad, _) in zip(group, scores, parts):
             at = rows_of(h)
             ds_ref[at] = dscore
-            dkv2_ref[0, :, at] = mm(dscore, q_ref[:, at], NN)
-            dkv2_ref[1, :, at] = mm(probs, grad, NT)
+            dk2_ref[:, at] = mm(dscore, q_ref[:, at], NN)
+            dv2_ref[:, at] = mm(probs, grad, NT)
     delta_ref[...] = stack_rows(deltas)
 
 
 def helper_back_kernel(
     heads,
-    pattern_ref,
+    bias_ref,
     sz_ref,
     az_ref,
     uzt_ref,
@@ -494,7 +501,6 @@
     delta_ref,
     up_ref,
     down_ref,
-    q_ref,
     kx_ref,
     vx_ref,
     ez_ref,
@@ -504,20 +510,22 @@
     near_ref,
     up_out_ref,
     down_out_ref,
-    side_out_ref,
+    dvx_ref,
+    dsz_ref,
     dsx_ref,
 ):
-    flags = Flags(pattern_ref)
-    odd, half = flags.odd, flags.half
+    place = Place()
+    odd, half = place.odd, place.half
     norm = norm_rows(sz_ref)
     z_lse = total_rows(az_ref)
     scales = (
-        jnp.where(flags.far, jnp.exp(mz_ref[...] - z_lse), 0.0),
-        jnp.where(flags.side, jnp.exp(mx_ref[...] - jnp.where(odd, total_rows(a_ref), z_lse)), 0.0),
+        jnp.exp(mz_ref[...] - z_lse + bias_ref[FAR : FAR + 1]),
+        jnp.exp(mx_ref[...] - jnp.where(odd, total_rows(a_ref), z_lse) + bias_ref[SIDE : SIDE + 1]),
     )
     own_deltas = delta_ref[...]
-    for start in range(0, heads, 2):
-        group = range(start, start + 2)
+    step = 2
+    for start in range(0, heads, step):
+        group = range(start, start + step)
         parts, products, scores = [], [], []
         for h in group:
             grad, delta = upstream_part(norm, uzt_ref[rows_of(h)], az_ref[rows_of(h)])
@@ -539,19 +547,24 @@
             at = rows_of(h)
             (gz, _), (gx, _) = parts[2 * n : 2 * n + 2]
             (dz, pz), (dx, px) = scores[2 * n : 2 * n + 2]
-            up_a, down_a = up_ref[FIRST, at], down_ref[FIRST, at]
-            k2, qz = jnp.where(half, down_a, up_a), jnp.where(half, up_a, down_a)
-            dsx_ref[at] = dx
-            dk2 = (near_ref[0, :, at] + mm(dz, qz, NN)).astype(jnp.bfloat16)
-            dv2 = (near_ref[1, :, at] + mm(pz, gz, NT)).astype(jnp.bfloat16)
-            side_out_ref[FIRST, at] = mm(dx, jnp.where(odd, q_ref[:, at], qz), NN).astype(jnp.bfloat16)
-            side_out_ref[SECOND, at] = mm(px, gx, NT).astype(jnp.bfloat16)
+            k2 = jnp.where(half, down_ref[FIRST, at], up_ref[FIRST, at])
+            dsz_ref[at], dsx_ref[at] = dz, dx
+            dv2 = (near_ref[:, at] + mm(pz, gz, NT)).astype(jnp.bfloat16)
+            dvx_ref[:, at] = mm(px, gx, NT).astype(jnp.bfloat16)
             joined = jnp.concatenate([dz, jnp.where(odd, jnp.zeros_like(dx), dx)], axis=0)
             dqz = mm(joined, jnp.concatenate([k2, kx_ref[:, at]], axis=0), TN).astype(jnp.bfloat16)
-            up_out_ref[FIRST, at] = jnp.where(half, dk2, dqz)
-            up_out_ref[SECOND, at] = dv2
-            down_out_ref[FIRST, at] = jnp.where(half, dqz, dk2)
-            down_out_ref[SECOND, at] = dv2
+            up_out_ref[:, at] = jnp.where(half, dv2, dqz)
+            down_out_ref[:, at] = jnp.where(half, dqz, dv2)
+
+
+def helper_keys_kernel(heads, q_ref, up_ref, down_ref, dsz_ref, dsx_ref, near_ref, dk_ref, dkx_ref):
+    place = Place()
+    for h in range(heads):
+        at = rows_of(h)
+        qz = jnp.where(place.half, up_ref[FIRST, at], down_ref[FIRST, at])
+        qx = jnp.where(place.odd, q_ref[:, at], qz)
+        dk_ref[:, at] = (near_ref[:, at] + mm(dsz_ref[at], qz, NN)).astype(jnp.bfloat16)
+        dkx_ref[:, at] = mm(dsx_ref[at], qx, NN).astype(jnp.bfloat16)
 
 
 def diagonal_back_kernel(
@@ -570,10 +583,11 @@
     down_ref,
     normed_ref,
     dq_ref,
-    dkv_ref,
+    dk_ref,
+    dv_ref,
 ):
-    flags = Flags()
-    half, odd = flags.half, flags.odd
+    place = Place()
+    half, odd = place.half, place.odd
     inverse, _ = norm_rows(sums_ref)
     lse = total_rows(a_ref)
     causal = causal_mask()
@@ -583,8 +597,8 @@
         q, k, v, grad = q_ref[:, at], k_ref[:, at], v_ref[:, at], grad_ref[at]
         weights = jnp.exp(jnp.where(causal, score_tile(k, q), NEG_BIG) - lse[row])
         dscore = (weights * (mm(v, grad, NN) - delta_ref[row]) * SCALE).astype(jnp.bfloat16)
-        dkv_ref[0, :, at] = mm(dscore, q, NN)
-        dkv_ref[1, :, at] = mm(weights.astype(jnp.bfloat16), grad, NT)
+        dk_ref[:, at] = mm(dscore, q, NN)
+        dv_ref[:, at] = mm(weights.astype(jnp.bfloat16), grad, NT)
         k2 = jnp.where(half, down_ref[FIRST, at], up_ref[FIRST, at])
         dsx = jnp.where(odd, dsx_ref[at], jnp.zeros_like(dsx_ref[at]))
         dq_ref[:, at] = mm(dscore, k, TN) + mm(
@@ -592,22 +606,27 @@
         )
 
 
-def final_kernel(
-    heads, pattern_ref, dq_own_ref, dkv_own_ref, side_ref, up_ref, down_ref, dq_ref, dk_ref, dv_ref
-):
-    flags = Flags(pattern_ref)
-    half = flags.half
-    ahead = flags.ahead.astype(jnp.float32)
-    helped = flags.helped.astype(jnp.float32)
+def final_first_kernel(heads, dq_own_ref, dv_own_ref, side_ref, up_ref, down_ref, dq_ref, dv_ref, token_ref):
+    place = Place()
+    half = place.half
+    ahead = (place.me + 2 < lax.axis_size("ctx")).astype(jnp.float32)
+    behind = (place.me >= 2).astype(jnp.float32)
     for h in range(heads):
         at = rows_of(h)
-        up_a, down_a = up_ref[FIRST, at], down_ref[FIRST, at]
-        dqz = jnp.where(half, down_a, up_a).astype(jnp.float32) * helped
-        dk = jnp.where(half, up_a, down_a).astype(jnp.float32) * ahead
-        dv = jnp.where(half, up_ref[SECOND, at], down_ref[SECOND, at]).astype(jnp.float32) * ahead
+        up, down = up_ref[:, at], down_ref[:, at]
+        dqz = jnp.where(half, down, up).astype(jnp.float32) * behind
+        dv = jnp.where(half, up, down).astype(jnp.float32) * ahead
         dq_ref[:, at] = (dq_own_ref[:, at] + dqz).astype(jnp.bfloat16)
-        dk_ref[:, at] = (dkv_own_ref[0, :, at] + side_ref[FIRST, at].astype(jnp.float32) + dk).astype(jnp.bfloat16)
-        dv_ref[:, at] = (dkv_own_ref[1, :, at] + side_ref[SECOND, at].astype(jnp.float32) + dv).astype(jnp.bfloat16)
+        dv_ref[:, at] = (dv_own_ref[:, at] + side_ref[:, at].astype(jnp.float32) + dv).astype(jnp.bfloat16)
+    token_ref[...] = jnp.zeros_like(token_ref)
+
+
+def final_keys_kernel(heads, dk_own_ref, side_ref, back_ref, dk_ref):
+    ahead = (Place().me + 2 < lax.axis_size("ctx")).astype(jnp.float32)
+    for h in range(heads):
+        at = rows_of(h)
+        dk = back_ref[:, at].astype(jnp.float32) * ahead
+        dk_ref[:, at] = (dk_own_ref[:, at] + side_ref[:, at].astype(jnp.float32) + dk).astype(jnp.bfloat16)
 
 
 def call(kernel, heads, flags, arrays, outs, flops, space=pltpu.VMEM, scratch=(), after=()):
@@ -643,7 +662,6 @@
     tokens, width = queries.shape
     heads = width // HD
     blocks, members = lax.axis_size("ctx"), lax.axis_size("head")
-    flags = (pattern,)
     unit = heads * 2 * BLOCK**3
     rising = cycles(blocks, members)
     falling = [(target, source) for source, target in rising]
@@ -664,9 +682,7 @@
 
     wide = struct(tokens, width, dtype=jnp.float32)
     wide_t = struct(width, tokens, dtype=jnp.float32)
-    wide_pair = struct(2, tokens, width, dtype=jnp.float32)
     flat, flat_t = struct(tokens, width), struct(width, tokens)
-    double = struct(2 * tokens, width)
     message = struct(width + TAIL, tokens)
     rows = struct(8, tokens, dtype=jnp.float32)
 
@@ -682,35 +698,34 @@
     )
     received = cycle(*payload)
     keys_x, values_x = swap(keys), swap(values)
-    diagonal, diagonal_lse, upstream_t = call(
+    diagonal, diagonal_lse, upstream_t, bias = call(
         diagonal_kernel,
         heads,
-        (),
+        (pattern,),
         (queries, keys, values, upstream),
-        (wide_t, rows, flat_t),
+        (wide_t, rows, flat_t, rows),
         3 * unit,
         after=(payload[0],),
     )
-    out_z, ez, ex, out_x, mz, mx, lse_x = call(
+    out_z, ez, ex, mz, mx = call(
         helper_kernel,
         heads,
-        flags,
-        (*received, queries, keys_x, values_x),
-        (message, wide_t, wide_t, wide_t, rows, rows, rows),
+        (),
+        (bias, *received, queries, keys_x, values_x),
+        (message, wide_t, wide_t, rows, rows),
         4 * unit,
-        after=(diagonal_lse,),
     )
     back_z = ring(out_z, 2)
     own, own_lse, upstream_zt, e2, m2 = call(
         own_kernel,
         heads,
-        flags,
-        (*received, queries, diagonal, diagonal_lse, out_x, lse_x),
+        (),
+        (bias, *received, queries, diagonal, diagonal_lse, values_x, ex, mx),
         (wide_t, rows, flat_t, wide_t, rows),
         3 * unit,
     )
     attention, sums = call(
-        merge_kernel, heads, flags, (own, own_lse, back_z, upstream_t), (message, rows), unit // 64
+        merge_kernel, heads, (), (bias, own, own_lse, back_z, upstream_t), (message, rows), unit // 64
     )
     others = [
         lax.ppermute(sums, "head", [(i, i ^ step) for i in range(members)]) for step in range(1, members)
@@ -718,36 +733,46 @@
     attention_z = ring(attention, -2)
     sums = functools.reduce(jnp.add, others, sums)
     sums_z = ring(sums, -2)
-    grad_t, delta, near_ds, near_grads = call(
+    grad_t, delta, near_ds, near_dk, near_dv = call(
         near_back_kernel,
         heads,
-        flags,
-        (sums, queries, attention, upstream_t, *received, e2, m2),
-        (flat_t, rows, flat_t, wide_pair),
+        (),
+        (bias, sums, queries, attention, upstream_t, *received, e2, m2),
+        (flat_t, rows, flat_t, wide, wide),
         3 * unit,
     )
-    up_out, down_out, side_out, side_ds = call(
+    up_out, down_out, side_dv, far_ds, side_ds = call(
         helper_back_kernel,
         heads,
-        flags,
-        (sums_z, attention_z, upstream_zt, attention, grad_t, delta, *received, queries, keys_x, values_x)
-        + (ez, ex, mz, mx, near_grads),
-        (double, double, double, flat_t),
-        8 * unit,
+        (),
+        (bias, sums_z, attention_z, upstream_zt, attention, grad_t, delta, *received, keys_x, values_x)
+        + (ez, ex, mz, mx, near_dv),
+        (flat, flat, flat, flat_t, flat_t),
+        6 * unit,
     )
     returned = cycle(up_out, down_out)
-    side_grads = swap(side_out)
-    normed, dq_own, grads_own = call(
+    out_dk, side_dk = call(
+        helper_keys_kernel,
+        heads,
+        (),
+        (queries, *received, far_ds, side_ds, near_dk),
+        (flat, flat),
+        2 * unit,
+    )
+    back_dk = ring(out_dk, -2)
+    side_dv, side_dk = swap(side_dv), swap(side_dk)
+    normed, dq_own, dk_own, dv_own = call(
         diagonal_back_kernel,
         heads,
         (),
         (sums, queries, keys, values, attention, grad_t, delta, near_ds, side_ds, keys_x, *received),
-        (flat, wide, wide_pair),
+        (flat, wide, wide, wide),
         7 * unit,
     )
-    grad_queries, grad_keys, grad_values = call(
-        final_kernel, heads, flags, (dq_own, grads_own, side_grads, *returned), (flat, flat, flat), 0
-    )
+    grad_queries, grad_values, token = call(
+        final_first_kernel, heads, (), (dq_own, dv_own, side_dv, *returned), (flat, flat, rows), 0
+    )
+    (grad_keys,) = call(final_keys_kernel, heads, (), (dk_own, side_dk, back_dk), (flat,), 0, after=(token,))
     return (normed, grad_queries, grad_keys, grad_values)
 
 

time: 58.1 us -> 54.6 us (0.940)
  waiting for transfers between devices: 27.6 us -> 23.2 us
  starting transfers between devices: 14.7 us -> 17.3 us
  Pallas kernels: 14.9 us -> 12.5 us
  local copies, waits for them, and re-layouts: 0.02 us -> 0.7 us
    ppermute x3 -> x4, waiting for transfers between devices: 17 us -> 9.71 us  [swap(): return lax.ppermute(array, 'ctx', [(i, i ^ 1) for i in range(blocks)])]
    ppermute x2, starting transfers between devices: 1.75 us -> 4.71 us  [cycle(): lax.ppermute(down_array, ('ctx', 'head'), falling)]
    ppermute x2, starting transfers between devices: 3.36 us -> 0.46 us  [cycle(): lax.ppermute(up_array, ('ctx', 'head'), rising)]
    ppermute x3 -> x4, waiting for transfers between devices: 7.33 us -> 9.82 us  [ring(): lax.ppermute(array, 'ctx', [(i, (i + distance) % blocks) for i in range(b...]
    pallas_call x9 -> x11, Pallas kernels: 14.9 us -> 12.5 us  [call(): pl.pallas_call(lambda *refs: kernel(heads, *refs[len(after):]), out_shape...]
    ppermute x3 -> x4, starting transfers between devices: 4.12 us -> 6.08 us  [ring(): lax.ppermute(array, 'ctx', [(i, (i + distance) % blocks) for i in range(b...]
    ppermute x2, waiting for transfers between devices: 0.29 us -> 1.86 us  [cycle(): lax.ppermute(down_array, ('ctx', 'head'), falling)]
    ppermute x2, waiting for transfers between devices: 1.21 us -> 0.01 us  [cycle(): lax.ppermute(up_array, ('ctx', 'head'), rising)]
  transfers between devices with their start and end apart: 13 -> 15, of which waited for: 9 -> 10; matrix products, arithmetic and copies ran while one was open for 0% -> 0% of each run, Pallas kernels for 12% -> 15%
where the time goes in v5:
time: 54.6 us; the launch traced here: 54.4 us
  waiting for transfers between devices  23.2 us (42%)
  starting transfers between devices  17.3 us (32%)
  Pallas kernels  12.5 us (23%)
  between operations  0.74 us (1%)
  local copies, waits for them, and re-layouts  0.7 us (1%)
    pallas_call x11, Pallas kernels, call(): pl.pallas_call(lambda *refs: kernel(heads, *refs[len(after):]), out_shape...  12.5 us
    ppermute x4, waiting for transfers between devices, ring(): lax.ppermute(array, 'ctx', [(i, (i + distance) % blocks) for i in range(b...  9.82 us
    ppermute x4, waiting for transfers between devices, swap(): return lax.ppermute(array, 'ctx', [(i, i ^ 1) for i in range(blocks)])  9.71 us
    ppermute x4, starting transfers between devices, ring(): lax.ppermute(array, 'ctx', [(i, (i + distance) % blocks) for i in range(b...  6.08 us
    ppermute x2, starting transfers between devices, cycle(): lax.ppermute(down_array, ('ctx', 'head'), falling)  4.71 us
    ppermute x4, starting transfers between devices, swap(): return lax.ppermute(array, 'ctx', [(i, i ^ 1) for i in range(blocks)])  4.18 us
    ppermute x3, starting transfers between devices, meeting_shards(): lax.ppermute(sums, 'head', [(i, i ^ step) for i in range(members)])  1.86 us
    ppermute x2, waiting for transfers between devices, cycle(): lax.ppermute(down_array, ('ctx', 'head'), falling)  1.86 us
  transfers between devices with their start and end apart: 15, of which 10 were waited for; matrix products, arithmetic and copies ran while one was open for 0% of the time, Pallas kernels for 15%

profile of v5, /device:TPU:0, one launch (start us, length us, event | category | flops | bytes accessed | tf_op | source)
XLA Modules:
  0.0 54.4 jit_solution(15353070136399975887)
XLA Ops:
  0.7 1.3 %shard_map.84 = (bf16[256,1024]{1,0:T(8,128)(2,1)S(1)}, bf16[256,1024]{1,0:T(8,128)(2,1)S(1)}) custom-call(bf16[128,1024]{1,0:T(8,128)(2,1)} %refs_0_.3, bf16[128,1024]{1,0:T(8,128)(2,1)} %refs_2_.7, bf16[128,1024]{1,0:T(8,128)(2,1)} %refs_3_.9, bf16[128,1024]{1,0:T(8,128)(2,1)} %refs_5_.1), custom_call_target="tpu_custom_call" | custom-call | bytes 2097152 | tf_op jit(solution)/shard_map/pallas_call | solution.py:634
  2.0 3.0 %collective-permute-start.1 = (bf16[256,1024]{1,0:T(8,128)(2,1)S(1)}, bf16[256,1024]{1,0:T(8,128)(2,1)S(1)}, u32[]{:S(2)}, u32[]{:S(2)}) collective-permute-start(bf16[256,1024]{1,0:T(8,128)(2,1)S(1)} %get-tuple-element.43), channel_id=1, source_target_pairs={{8,0},{9,1},{0,2},{1,3},{12,4},{13,5},{4,6},{5,7},{16,8},{17,9},{2... | collective-permute-start | bytes 1572872 | tf_op jit(solution)/shard_map/ppermute | solution.py:670
  5.1 1.9 %collective-permute-start.3 = (bf16[128,1024]{1,0:T(8,128)(2,1)S(1)}, bf16[128,1024]{1,0:T(8,128)(2,1)S(1)}, u32[]{:S(2)}, u32[]{:S(2)}) collective-permute-start(bf16[128,1024]{1,0:T(8,128)(2,1)S(1)} %copy-done.1), channel_id=1, source_target_pairs={{0,4},{4,0},{8,12},{12,8},{16,20},{20,16},{24,28},{28,24},{1,5},{5... | collective-permute-start | bytes 786440 | tf_op jit(solution)/shard_map/ppermute | solution.py:675
  7.9 2.4 %shard_map.85 = (f32[1024,128]{1,0:T(8,128)S(1)}, f32[8,128]{1,0:T(8,128)S(1)}, bf16[1024,128]{1,0:T(8,128)(2,1)S(1)}, f32[8,128]{1,0:T(8,128)S(1)}) custom-call(bf16[256,1024]{1,0:T(8,128)(2,1)S(1)} %get-tuple-element.41.refs_0_, s32[8,8]{1,0:T(8,128)S(1)} %copy-done.4, bf16[128,1024]{1,0:T(8,128)(2,1)S(1)} %copy-done, bf16[128,1024]{1,0:T(8,128)(2,1)S(1)} %copy-done.1, ...), custom_call_target="tpu_custom_call" | custom-call | flops 100663296 | bytes 1843200 | tf_op jit(solution)/shard_map/pallas_call | solution.py:634
  10.2 4.1 %collective-permute-done.3.refs_4_.refs_9_ = bf16[128,1024]{1,0:T(8,128)(2,1)S(1)} collective-permute-done((bf16[128,1024]{1,0:T(8,128)(2,1)S(1)}, bf16[128,1024]{1,0:T(8,128)(2,1)S(1)}, u32[]{:S(2)}, u32[]{:S(2)}) %collective-permute-start.3) | collective-permute-done | bytes 262176 | tf_op jit(solution)/shard_map/ppermute | solution.py:675
  14.4 4.2 %collective-permute-done.2.refs_5_.refs_6_.refs_10_ = bf16[128,1024]{1,0:T(8,128)(2,1)S(1)} collective-permute-done((bf16[128,1024]{1,0:T(8,128)(2,1)S(1)}, bf16[128,1024]{1,0:T(8,128)(2,1)S(1)}, u32[]{:S(2)}, u32[]{:S(2)}) %collective-permute-start.2) | collective-permute-done | bytes 262176 | tf_op jit(solution)/shard_map/ppermute | solution.py:675
  18.5 0.9 %shard_map.86 = (bf16[1056,128]{1,0:T(8,128)(2,1)S(1)}, f32[1024,128]{1,0:T(8,128)S(1)}, f32[1024,128]{1,0:T(8,128)S(1)}, f32[8,128]{1,0:T(8,128)S(1)}, f32[8,128]{1,0:T(8,128)S(1)}) custom-call(f32[8,128]{1,0:T(8,128)S(1)} %get-tuple-element.42.refs_0_, bf16[256,1024]{1,0:T(8,128)(2,1)S(1)} %collective-permute-done.refs_1_.refs_5_.refs_7_.refs_10_, ...), custom_call_target="tpu_custom_call" | custom-call | flops 134217728 | bytes 3166208 | tf_op jit(solution)/shard_map/pallas_call | solution.py:634
  19.5 1.7 %collective-permute-start.4 = (bf16[1056,128]{1,0:T(8,128)(2,1)S(1)}, bf16[1056,128]{1,0:T(8,128)(2,1)S(1)}, u32[]{:S(2)}, u32[]{:S(2)}) collective-permute-start(bf16[1056,128]{1,0:T(8,128)(2,1)S(1)} %get-tuple-element.50), channel_id=1, source_target_pairs={{0,8},{4,12},{8,16},{12,20},{16,24},{20,28},{24,0},{28,4},{1,9},{5... | collective-permute-start | bytes 811016 | tf_op jit(solution)/shard_map/ppermute | solution.py:678
  21.2 1.1 %shard_map.87 = (f32[1024,128]{1,0:T(8,128)S(1)}, f32[8,128]{1,0:T(8,128)S(1)}, bf16[1024,128]{1,0:T(8,128)(2,1)S(1)}, f32[1024,128]{1,0:T(8,128)S(1)}, f32[8,128]{1,0:T(8,128)S(1)}) custom-call(f32[8,128]{1,0:T(8,128)S(1)} %get-tuple-element.42.refs_0_, bf16[256,1024]{1,0:T(8,128)(2,1)S(1)} %collective-permute-done.refs_1_.refs_5_.refs_7_.refs_10_, ...), custom_call_target="tpu_custom_call" | custom-call | flops 100663296 | bytes 3952640 | tf_op jit(solution)/shard_map/pallas_call | solution.py:634
  22.3 6.1 %collective-permute-done.4.refs_3_ = bf16[1056,128]{1,0:T(8,128)(2,1)S(1)} collective-permute-done((bf16[1056,128]{1,0:T(8,128)(2,1)S(1)}, bf16[1056,128]{1,0:T(8,128)(2,1)S(1)}, u32[]{:S(2)}, u32[]{:S(2)}) %collective-permute-start.4) | collective-permute-done | bytes 270368 | tf_op jit(solution)/shard_map/ppermute | solution.py:678
  28.7 1.6 %collective-permute-start.9 = (bf16[1056,128]{1,0:T(8,128)(2,1)S(1)}, bf16[1056,128]{1,0:T(8,128)(2,1)S(1)}, u32[]{:S(2)}, u32[]{:S(2)}) collective-permute-start(bf16[1056,128]{1,0:T(8,128)(2,1)S(1)} %get-tuple-element.53.refs_3_.refs_4_), channel_id=1, source_target_pairs={{0,24},{4,28},{8,0},{12,4},{16,8},{20,12},{24,16},{28,20},{1,25},{... | collective-permute-start | bytes 811016 | tf_op jit(solution)/shard_map/ppermute | solution.py:678
  30.3 1.6 %collective-permute-start.6 = (f32[8,128]{1,0:T(8,128)S(1)}, f32[8,128]{1,0:T(8,128)S(1)}, u32[]{:S(2)}, u32[]{:S(2)}) collective-permute-start(f32[8,128]{1,0:T(8,128)S(1)} %get-tuple-element.52), channel_id=1, source_target_pairs={{0,2},{1,3},{2,0},{3,1},{4,6},{5,7},{6,4},{7,5},{8,10},{9,11},{10,... | collective-permute-start | bytes 12296 | tf_op jit(solution)/shard_map/ppermute | solution.py:731
  32.1 1.2 %collective-permute-done.7 = f32[8,128]{1,0:T(8,128)S(1)} collective-permute-done((f32[8,128]{1,0:T(8,128)S(1)}, f32[8,128]{1,0:T(8,128)S(1)}, u32[]{:S(2)}, u32[]{:S(2)}) %collective-permute-start.7) | collective-permute-done | bytes 4128 | tf_op jit(solution)/shard_map/ppermute | solution.py:731
  35.0 2.5 %collective-permute-done.8.refs_1_ = f32[8,128]{1,0:T(8,128)S(1)} collective-permute-done((f32[8,128]{1,0:T(8,128)S(1)}, f32[8,128]{1,0:T(8,128)S(1)}, u32[]{:S(2)}, u32[]{:S(2)}) %collective-permute-start.8) | collective-permute-done | bytes 4128 | tf_op jit(solution)/shard_map/ppermute | solution.py:678
  37.6 1.3 %shard_map.90 = (bf16[128,1024]{1,0:T(8,128)(2,1)S(1)}, bf16[128,1024]{1,0:T(8,128)(2,1)S(1)}, bf16[128,1024]{1,0:T(8,128)(2,1)S(1)}, bf16[1024,128]{1,0:T(8,128)(2,1)S(1)}, bf16[1024,128]{1,0:T(8,128)(2,1)S(1)}) custom-call(f32[8,128]{1,0:T(8,128)S(1)} %get-tuple-element.42.refs_0_, f32[8,128]{1,0:T(8,128)S(1)} %collective-permute-done.8.refs_1_, ...), custom_call_target="tpu_custom_call" | custom-call | flops 201326592 | bytes 5541888 | tf_op jit(solution)/shard_map/pallas_call | solution.py:634
  38.8 1.6 %collective-permute-start.10 = (bf16[128,1024]{1,0:T(8,128)(2,1)S(1)}, bf16[128,1024]{1,0:T(8,128)(2,1)S(1)}, u32[]{:S(2)}, u32[]{:S(2)}) collective-permute-start(bf16[128,1024]{1,0:T(8,128)(2,1)S(1)} %get-tuple-element.67), channel_id=1, source_target_pairs={{0,4},{4,0},{8,12},{12,8},{16,20},{20,16},{24,28},{28,24},{1,5},{5... | collective-permute-start | bytes 786440 | tf_op jit(solution)/shard_map/ppermute | solution.py:675
  40.7 1.7 %collective-permute-start.12 = (bf16[128,1024]{1,0:T(8,128)(2,1)S(1)}, bf16[128,1024]{1,0:T(8,128)(2,1)S(1)}, u32[]{:S(2)}, u32[]{:S(2)}) collective-permute-start(bf16[128,1024]{1,0:T(8,128)(2,1)S(1)} %get-tuple-element.69), channel_id=1, source_target_pairs={{8,0},{9,1},{0,2},{1,3},{12,4},{13,5},{4,6},{5,7},{16,8},{17,9},{2... | collective-permute-start | bytes 786440 | tf_op jit(solution)/shard_map/ppermute | solution.py:670
  43.4 2.2 %collective-permute-start.14 = (bf16[128,1024]{1,0:T(8,128)(2,1)S(1)}, bf16[128,1024]{1,0:T(8,128)(2,1)S(1)}, u32[]{:S(2)}, u32[]{:S(2)}) collective-permute-start(bf16[128,1024]{1,0:T(8,128)(2,1)S(1)} %get-tuple-element.76), channel_id=1, source_target_pairs={{0,24},{4,28},{8,0},{12,4},{16,8},{20,12},{24,16},{28,20},{1,25},{... | collective-permute-start | bytes 786440 | tf_op jit(solution)/shard_map/ppermute | solution.py:678
  45.6 2.4 %shard_map.91 = (bf16[128,1024]{1,0:T(8,128)(2,1)}, f32[128,1024]{1,0:T(8,128)S(1)}, f32[128,1024]{1,0:T(8,128)S(1)}, f32[128,1024]{1,0:T(8,128)S(1)}) custom-call(f32[8,128]{1,0:T(8,128)S(1)} %add_add_fusion.refs_1_.refs_0_, bf16[128,1024]{1,0:T(8,128)(2,1)S(1)} %copy-done, bf16[128,1024]{1,0:T(8,128)(2,1)S(1)} %copy-done.1, ...), custom_call_target="tpu_custom_call" | custom-call | flops 234881024 | bytes 4997120 | tf_op jit(solution)/shard_map/pallas_call | solution.py:634
  48.1 1.9 %collective-permute-done.12.refs_4_ = bf16[128,1024]{1,0:T(8,128)(2,1)S(1)} collective-permute-done((bf16[128,1024]{1,0:T(8,128)(2,1)S(1)}, bf16[128,1024]{1,0:T(8,128)(2,1)S(1)}, u32[]{:S(2)}, u32[]{:S(2)}) %collective-permute-start.12) | collective-permute-done | bytes 262176 | tf_op jit(solution)/shard_map/ppermute | solution.py:670
  50.0 1.0 %shard_map.92 = (bf16[128,1024]{1,0:T(8,128)(2,1)}, bf16[128,1024]{1,0:T(8,128)(2,1)}, f32[8,128]{1,0:T(8,128)S(1)}) custom-call(f32[128,1024]{1,0:T(8,128)S(1)} %get-tuple-element.65.refs_0_, f32[128,1024]{1,0:T(8,128)S(1)} %get-tuple-element.66.refs_1_, bf16[128,1024]{1,0:T(8,128)(2,1)S(1)} %collective-permute-done.10.refs_2_, ...), custom_call_target="tpu_custom_call" | custom-call | bytes 2363392 | tf_op jit(solution)/shard_map/pallas_call | solution.py:634
  51.0 1.3 %collective-permute-done.13.refs_2_ = bf16[128,1024]{1,0:T(8,128)(2,1)S(1)} collective-permute-done((bf16[128,1024]{1,0:T(8,128)(2,1)S(1)}, bf16[128,1024]{1,0:T(8,128)(2,1)S(1)}, u32[]{:S(2)}, u32[]{:S(2)}) %collective-permute-start.13) | collective-permute-done | bytes 262176 | tf_op jit(solution)/shard_map/ppermute | solution.py:675
  52.3 1.2 %collective-permute-done.14.refs_3_ = bf16[128,1024]{1,0:T(8,128)(2,1)S(1)} collective-permute-done((bf16[128,1024]{1,0:T(8,128)(2,1)S(1)}, bf16[128,1024]{1,0:T(8,128)(2,1)S(1)}, u32[]{:S(2)}, u32[]{:S(2)}) %collective-permute-start.14) | collective-permute-done | bytes 262176 | tf_op jit(solution)/shard_map/ppermute | solution.py:678
  53.6 0.8 %shard_map.94 = bf16[128,1024]{1,0:T(8,128)(2,1)} custom-call(f32[8,128]{1,0:T(8,128)S(1)} %get-tuple-element.71.refs_0_, f32[128,1024]{1,0:T(8,128)S(1)} %get-tuple-element.72.refs_1_, bf16[128,1024]{1,0:T(8,128)(2,1)S(1)} %collective-permute-done.13.refs_2_, bf16[128,1024]{1,0:T(8,128)(2,1)S(1)} %collective-permute-done.14.refs_3_), custom_call_target="tpu_custom_call" | custom-call | bytes 1310720 | tf_op jit(solution)/shard_map/pallas_call | solution.py:634
  (28 shorter events, 4.6 us)
Async XLA Ops:
  0.6 6.5 %copy-start = (bf16[128,1024]{1,0:T(8,128)(2,1)S(1)}, bf16[128,1024]{1,0:T(8,128)(2,1)}, u32[]{:S(2)}) copy-start(bf16[128,1024]{1,0:T(8,128)(2,1)} %refs_0_.3) | copy-start | bytes 786436
  0.6 6.4 %copy-start.2 = (bf16[128,1024]{1,0:T(8,128)(2,1)S(1)}, bf16[128,1024]{1,0:T(8,128)(2,1)}, u32[]{:S(2)}) copy-start(bf16[128,1024]{1,0:T(8,128)(2,1)} %refs_3_.9) | copy-start | bytes 786436
  0.7 4.5 %copy-start.1 = (bf16[128,1024]{1,0:T(8,128)(2,1)S(1)}, bf16[128,1024]{1,0:T(8,128)(2,1)}, u32[]{:S(2)}) copy-start(bf16[128,1024]{1,0:T(8,128)(2,1)} %refs_2_.7) | copy-start | bytes 786436
  0.7 6.5 %copy-start.3 = (bf16[128,1024]{1,0:T(8,128)(2,1)S(1)}, bf16[128,1024]{1,0:T(8,128)(2,1)}, u32[]{:S(2)}) copy-start(bf16[128,1024]{1,0:T(8,128)(2,1)} %refs_5_.1) | copy-start | bytes 786436
  2.0 16.5 %collective-permute-start.1 = (bf16[256,1024]{1,0:T(8,128)(2,1)S(1)}, bf16[256,1024]{1,0:T(8,128)(2,1)S(1)}, u32[]{:S(2)}, u32[]{:S(2)}) collective-permute-start(bf16[256,1024]{1,0:T(8,128)(2,1)S(1)} %get-tuple-element.43), channel_id=1, source_target_pairs={{8,0},{9,1},{0,2},{1,3},{12,4},{13,5},{4,6},{5,7},{16,8},{17,9},{2... | collective-permute-start | bytes 1572872 | tf_op jit(solution)/shard_map/ppermute | solution.py:670
  5.0 13.5 %collective-permute-start = (bf16[256,1024]{1,0:T(8,128)(2,1)S(1)}, bf16[256,1024]{1,0:T(8,128)(2,1)S(1)}, u32[]{:S(2)}, u32[]{:S(2)}) collective-permute-start(bf16[256,1024]{1,0:T(8,128)(2,1)S(1)} %get-tuple-element.41.refs_0_), channel_id=1, source_target_pairs={{0,8},{1,9},{2,0},{3,1},{4,12},{5,13},{6,4},{7,5},{8,16},{9,17},{1... | collective-permute-start | bytes 1572872 | tf_op jit(solution)/shard_map/ppermute | solution.py:670
  5.1 9.2 %collective-permute-start.3 = (bf16[128,1024]{1,0:T(8,128)(2,1)S(1)}, bf16[128,1024]{1,0:T(8,128)(2,1)S(1)}, u32[]{:S(2)}, u32[]{:S(2)}) collective-permute-start(bf16[128,1024]{1,0:T(8,128)(2,1)S(1)} %copy-done.1), channel_id=1, source_target_pairs={{0,4},{4,0},{8,12},{12,8},{16,20},{20,16},{24,28},{28,24},{1,5},{5... | collective-permute-start | bytes 786440 | tf_op jit(solution)/shard_map/ppermute | solution.py:675
  7.0 11.5 %collective-permute-start.2 = (bf16[128,1024]{1,0:T(8,128)(2,1)S(1)}, bf16[128,1024]{1,0:T(8,128)(2,1)S(1)}, u32[]{:S(2)}, u32[]{:S(2)}) collective-permute-start(bf16[128,1024]{1,0:T(8,128)(2,1)S(1)} %copy-done.2), channel_id=1, source_target_pairs={{0,4},{4,0},{8,12},{12,8},{16,20},{20,16},{24,28},{28,24},{1,5},{5... | collective-permute-start | bytes 786440 | tf_op jit(solution)/shard_map/ppermute | solution.py:675
  7.2 0.7 %copy-start.4 = (s32[8,8]{1,0:T(8,128)S(1)}, s32[8,8]{1,0:T(8,128)}, u32[]{:S(2)}) copy-start(s32[8,8]{1,0:T(8,128)} %refs_1_.4) | copy-start | bytes 772
  19.5 9.0 %collective-permute-start.4 = (bf16[1056,128]{1,0:T(8,128)(2,1)S(1)}, bf16[1056,128]{1,0:T(8,128)(2,1)S(1)}, u32[]{:S(2)}, u32[]{:S(2)}) collective-permute-start(bf16[1056,128]{1,0:T(8,128)(2,1)S(1)} %get-tuple-element.50), channel_id=1, source_target_pairs={{0,8},{4,12},{8,16},{12,20},{16,24},{20,28},{24,0},{28,4},{1,9},{5... | collective-permute-start | bytes 811016 | tf_op jit(solution)/shard_map/ppermute | solution.py:678
  28.7 8.9 %collective-permute-start.9 = (bf16[1056,128]{1,0:T(8,128)(2,1)S(1)}, bf16[1056,128]{1,0:T(8,128)(2,1)S(1)}, u32[]{:S(2)}, u32[]{:S(2)}) collective-permute-start(bf16[1056,128]{1,0:T(8,128)(2,1)S(1)} %get-tuple-element.53.refs_3_.refs_4_), channel_id=1, source_target_pairs={{0,24},{4,28},{8,0},{12,4},{16,8},{20,12},{24,16},{28,20},{1,25},{... | collective-permute-start | bytes 811016 | tf_op jit(solution)/shard_map/ppermute | solution.py:678
  30.3 3.0 %collective-permute-start.7 = (f32[8,128]{1,0:T(8,128)S(1)}, f32[8,128]{1,0:T(8,128)S(1)}, u32[]{:S(2)}, u32[]{:S(2)}) collective-permute-start(f32[8,128]{1,0:T(8,128)S(1)} %get-tuple-element.52), channel_id=1, source_target_pairs={{0,3},{1,2},{2,1},{3,0},{4,7},{5,6},{6,5},{7,4},{8,11},{9,10},{10,... | collective-permute-start | bytes 12296 | tf_op jit(solution)/shard_map/ppermute | solution.py:731
  30.3 3.6 %collective-permute-start.6 = (f32[8,128]{1,0:T(8,128)S(1)}, f32[8,128]{1,0:T(8,128)S(1)}, u32[]{:S(2)}, u32[]{:S(2)}) collective-permute-start(f32[8,128]{1,0:T(8,128)S(1)} %get-tuple-element.52), channel_id=1, source_target_pairs={{0,2},{1,3},{2,0},{3,1},{4,6},{5,7},{6,4},{7,5},{8,10},{9,11},{10,... | collective-permute-start | bytes 12296 | tf_op jit(solution)/shard_map/ppermute | solution.py:731
  31.8 2.1 %collective-permute-start.5 = (f32[8,128]{1,0:T(8,128)S(1)}, f32[8,128]{1,0:T(8,128)S(1)}, u32[]{:S(2)}, u32[]{:S(2)}) collective-permute-start(f32[8,128]{1,0:T(8,128)S(1)} %get-tuple-element.52), channel_id=1, source_target_pairs={{0,1},{1,0},{2,3},{3,2},{4,5},{5,4},{6,7},{7,6},{8,9},{9,8},{10,11... | collective-permute-start | bytes 12296 | tf_op jit(solution)/shard_map/ppermute | solution.py:731
  33.9 3.7 %collective-permute-start.8 = (f32[8,128]{1,0:T(8,128)S(1)}, f32[8,128]{1,0:T(8,128)S(1)}, u32[]{:S(2)}, u32[]{:S(2)}) collective-permute-start(f32[8,128]{1,0:T(8,128)S(1)} %add_add_fusion.refs_1_.refs_0_), channel_id=1, source_target_pairs={{0,24},{4,28},{8,0},{12,4},{16,8},{20,12},{24,16},{28,20},{1,25},{... | collective-permute-start | bytes 12296 | tf_op jit(solution)/shard_map/ppermute | solution.py:678
  38.8 9.3 %collective-permute-start.10 = (bf16[128,1024]{1,0:T(8,128)(2,1)S(1)}, bf16[128,1024]{1,0:T(8,128)(2,1)S(1)}, u32[]{:S(2)}, u32[]{:S(2)}) collective-permute-start(bf16[128,1024]{1,0:T(8,128)(2,1)S(1)} %get-tuple-element.67), channel_id=1, source_target_pairs={{0,4},{4,0},{8,12},{12,8},{16,20},{20,16},{24,28},{28,24},{1,5},{5... | collective-permute-start | bytes 786440 | tf_op jit(solution)/shard_map/ppermute | solution.py:675
  40.4 7.7 %collective-permute-start.11 = (bf16[128,1024]{1,0:T(8,128)(2,1)S(1)}, bf16[128,1024]{1,0:T(8,128)(2,1)S(1)}, u32[]{:S(2)}, u32[]{:S(2)}) collective-permute-start(bf16[128,1024]{1,0:T(8,128)(2,1)S(1)} %get-tuple-element.68), channel_id=1, source_target_pairs={{0,8},{1,9},{2,0},{3,1},{4,12},{5,13},{6,4},{7,5},{8,16},{9,17},{1... | collective-permute-start | bytes 786440 | tf_op jit(solution)/shard_map/ppermute | solution.py:670
  40.7 9.2 %collective-permute-start.12 = (bf16[128,1024]{1,0:T(8,128)(2,1)S(1)}, bf16[128,1024]{1,0:T(8,128)(2,1)S(1)}, u32[]{:S(2)}, u32[]{:S(2)}) collective-permute-start(bf16[128,1024]{1,0:T(8,128)(2,1)S(1)} %get-tuple-element.69), channel_id=1, source_target_pairs={{8,0},{9,1},{0,2},{1,3},{12,4},{13,5},{4,6},{5,7},{16,8},{17,9},{2... | collective-permute-start | bytes 786440 | tf_op jit(solution)/shard_map/ppermute | solution.py:670
  42.8 9.6 %collective-permute-start.13 = (bf16[128,1024]{1,0:T(8,128)(2,1)S(1)}, bf16[128,1024]{1,0:T(8,128)(2,1)S(1)}, u32[]{:S(2)}, u32[]{:S(2)}) collective-permute-start(bf16[128,1024]{1,0:T(8,128)(2,1)S(1)} %get-tuple-element.75), channel_id=1, source_target_pairs={{0,4},{4,0},{8,12},{12,8},{16,20},{20,16},{24,28},{28,24},{1,5},{5... | collective-permute-start | bytes 786440 | tf_op jit(solution)/shard_map/ppermute | solution.py:675
  43.4 10.2 %collective-permute-start.14 = (bf16[128,1024]{1,0:T(8,128)(2,1)S(1)}, bf16[128,1024]{1,0:T(8,128)(2,1)S(1)}, u32[]{:S(2)}, u32[]{:S(2)}) collective-permute-start(bf16[128,1024]{1,0:T(8,128)(2,1)S(1)} %get-tuple-element.76), channel_id=1, source_target_pairs={{0,24},{4,28},{8,0},{12,4},{16,8},{20,12},{24,16},{28,20},{1,25},{... | collective-permute-start | bytes 786440 | tf_op jit(solution)/shard_map/ppermute | solution.py:678

commit v6 on v5

--- a/solution.py
+++ b/solution.py
@@ -322,121 +322,148 @@
     return functools.reduce(jnp.add, [out * jnp.exp(lse - total) for out, lse in parts]), total
 
 
-def helper_kernel(
-    heads, bias_ref, up_ref, down_ref, q_ref, kx_ref, vx_ref, oz_ref, ez_ref, ex_ref, mz_ref, mx_ref
-):
-    place = Place()
-    odd, half = place.odd, place.half
-    far, side = bias_ref[FAR : FAR + 1], bias_ref[SIDE : SIDE + 1]
-    step = 4
-    z_rows, z_tops, x_tops = [], [], []
-    for start in range(0, heads, step):
-        group = range(start, start + step)
-        scores, weights, totals = [], [], []
-        for h in group:
-            at = rows_of(h)
-            up_a, down_a = up_ref[FIRST, at], down_ref[FIRST, at]
-            k2, qz = jnp.where(half, down_a, up_a), jnp.where(half, up_a, down_a)
-            qx = jnp.where(odd, q_ref[:, at], qz)
-            scores.append((score_tile(k2, qz) + far, score_tile(kx_ref[:, at], qx) + side))
-        for h, (z, x) in zip(group, scores):
-            z_top, x_top = z.max(axis=0, keepdims=True), x.max(axis=0, keepdims=True)
-            both = jnp.maximum(z_top, x_top)
-            z_top, x_top = jnp.where(odd, z_top, both), jnp.where(odd, x_top, both)
-            z, x = jnp.exp(z - z_top), jnp.exp(x - x_top)
-            ez_ref[rows_of(h)], ex_ref[rows_of(h)] = z, x
-            x = jnp.where(odd, 0.0, x)
-            total = z.sum(axis=0, keepdims=True) + x.sum(axis=0, keepdims=True)
-            weights.append(jnp.concatenate([z, x], axis=0).astype(jnp.bfloat16))
-            totals.append(total)
-            z_rows.append(z_top + jnp.log(total))
-            z_tops.append(z_top)
-            x_tops.append(x_top)
-        for h, w, total in zip(group, weights, totals):
-            at = rows_of(h)
-            v2 = jnp.where(half, down_ref[SECOND, at], up_ref[SECOND, at])
-            out = mm(jnp.concatenate([v2, vx_ref[:, at]], axis=0), w, TN) * (1.0 / total)
-            oz_ref[at] = out.astype(jnp.bfloat16)
-    oz_ref[heads * HD :] = split_rows(stack_rows(z_rows))
-    mz_ref[...] = stack_rows(z_tops)
-    mx_ref[...] = stack_rows(x_tops)
-
-
-def own_kernel(
+def forward_kernel(
     heads,
     bias_ref,
     up_ref,
     down_ref,
     q_ref,
+    kx_ref,
+    vx_ref,
     out_ref,
     lse_ref,
-    vx_ref,
+    up_out_ref,
+    down_out_ref,
+    ez_ref,
     ex_ref,
+    en_ref,
+    mz_ref,
     mx_ref,
-    own_ref,
-    total_ref,
+    mn_ref,
+):
+    place = Place()
+    odd, half = place.odd, place.half
+    near, far, side, local = (bias_ref[n : n + 1] for n in (NEAR, FAR, SIDE, LOCAL))
+    before = lse_ref[...]
+    step = 2
+    z_rows, own_rows, z_tops, x_tops, n_tops = [], [], [], [], []
+    for start in range(0, heads, step):
+        group = range(start, start + step)
+        scores, weights = [], []
+        for h in group:
+            at = rows_of(h)
+            up_a, down_a = up_ref[FIRST, at], down_ref[FIRST, at]
+            k2, qz = jnp.where(half, down_a, up_a), jnp.where(half, up_a, down_a)
+            q = q_ref[:, at]
+            scores.append(
+                (
+                    score_tile(k2, qz) + far,
+                    score_tile(kx_ref[:, at], jnp.where(odd, q, qz)) + side,
+                    score_tile(k2, q) + near,
+                )
+            )
+        for h, (z, x, n) in zip(group, scores):
+            z_top, x_top, n_top = (tile.max(axis=0, keepdims=True) for tile in (z, x, n))
+            both = jnp.maximum(z_top, x_top)
+            z_top, x_top = jnp.where(odd, z_top, both), jnp.where(odd, x_top, both)
+            z, x, n = jnp.exp(z - z_top), jnp.exp(x - x_top), jnp.exp(n - n_top)
+            at = rows_of(h)
+            ez_ref[at], ex_ref[at], en_ref[at] = z, x, n
+            z_sum, x_sum, n_sum = (tile.sum(axis=0, keepdims=True) for tile in (z, x, n))
+            z_sum = z_sum + jnp.where(odd, 0.0, x_sum)
+            x_sum = jnp.maximum(x_sum, 1.0)
+            for kept, top in ((z_tops, z_top), (x_tops, x_top), (n_tops, n_top)):
+                kept.append(top)
+            z_rows.append(z_top + jnp.log(z_sum))
+            parts = (before[h : h + 1], n_top + jnp.log(n_sum) + near, x_top + jnp.log(x_sum) + local)
+            highest = functools.reduce(jnp.maximum, parts)
+            total = highest + jnp.log(functools.reduce(jnp.add, [jnp.exp(part - highest) for part in parts]))
+            own_rows.append(total)
+            d_share, n_share, x_share = (jnp.exp(part - total) for part in parts)
+            xb = x.astype(jnp.bfloat16)
+            joined = jnp.concatenate([z.astype(jnp.bfloat16), jnp.where(odd, jnp.zeros_like(xb), xb)], axis=0)
+            weights.append(
+                (joined, xb, n.astype(jnp.bfloat16), 1.0 / z_sum, d_share, n_share / n_sum, x_share / x_sum)
+            )
+        for h, (joined, xb, nb, z_scale, d_share, n_share, x_share) in zip(group, weights):
+            at = rows_of(h)
+            v2, vx = jnp.where(half, down_ref[SECOND, at], up_ref[SECOND, at]), vx_ref[:, at]
+            out_z = mm(jnp.concatenate([v2, vx], axis=0), joined, TN) * z_scale
+            own = out_ref[at] * d_share + mm(v2, nb, TN) * n_share + mm(vx, xb, TN) * x_share
+            out_z, own = out_z.astype(jnp.bfloat16), own.astype(jnp.bfloat16)
+            up_out_ref[at] = jnp.where(half, own, out_z)
+            down_out_ref[at] = jnp.where(half, out_z, own)
+    tail = slice(heads * HD, heads * HD + TAIL)
+    z_tail, own_tail = split_rows(stack_rows(z_rows)), split_rows(stack_rows(own_rows))
+    up_out_ref[tail] = jnp.where(half, own_tail, z_tail)
+    down_out_ref[tail] = jnp.where(half, z_tail, own_tail)
+    mz_ref[...] = stack_rows(z_tops)
+    mx_ref[...] = stack_rows(x_tops)
+    mn_ref[...] = stack_rows(n_tops)
+
+
+def transpose_kernel(heads, up_ref, down_ref, out_ref):
+    half = Place().half
+    for h in range(heads):
+        at = rows_of(h)
+        out_ref[at] = jnp.where(half, up_ref[SECOND, at], down_ref[SECOND, at]).T
+
+
+def merge_kernel(
+    heads,
+    bias_ref,
+    up_ref,
+    down_ref,
+    up_in_ref,
+    down_in_ref,
+    ut_ref,
     uzt_ref,
-    e_ref,
-    m_ref,
+    a_ref,
+    az_ref,
+    lse_ref,
+    lsez_ref,
+    sums_ref,
 ):
     half = Place().half
-    near, local = bias_ref[NEAR : NEAR + 1], bias_ref[LOCAL : LOCAL + 1]
-    before = lse_ref[...]
-    rows, tops = [], []
-    for start in range(0, heads, 2):
-        group = range(start, start + 2)
-        pairs = []
-        for h in group:
-            at = rows_of(h)
-            k2 = jnp.where(half, down_ref[FIRST, at], up_ref[FIRST, at])
-            up_b, down_b = up_ref[SECOND, at], down_ref[SECOND, at]
-            uzt_ref[at] = jnp.where(half, up_b, down_b).T
-            pairs.append((score_tile(k2, q_ref[:, at]), jnp.where(half, down_b, up_b)))
-        for h, (out, top, lse, e_ref[rows_of(h)]) in zip(group, softmax_parts(pairs)):
-            at, row = rows_of(h), slice(h, h + 1)
-            weights = ex_ref[at]
-            side = jnp.maximum(weights.sum(axis=0, keepdims=True), 1.0)
-            side_out = mm(vx_ref[:, at], weights.astype(jnp.bfloat16), TN) * (1.0 / side)
-            own_ref[at], total = merged(
-                [
-                    (out_ref[at], before[row]),
-                    (out, lse + near),
-                    (side_out, mx_ref[row] + jnp.log(side) + local),
-                ]
-            )
-            rows.append(total)
-            tops.append(top)
-    total_ref[...] = stack_rows(rows)
-    m_ref[...] = stack_rows(tops)
-
-
-def merge_kernel(heads, bias_ref, own_ref, lse_ref, rz_ref, ut_ref, a_ref, sums_ref):
     tail = slice(heads * HD, heads * HD + TAIL)
-    squares = jnp.zeros((8, BLOCK), jnp.float32)
-    crosses = jnp.zeros((8, BLOCK), jnp.float32)
-    own = lse_ref[...]
-    z = joined_rows(rz_ref[tail]) + bias_ref[HELPED : HELPED + 1]
-    highest = jnp.maximum(own, z)
-    total = highest + jnp.log(jnp.exp(own - highest) + jnp.exp(z - highest))
-    own, z = jnp.exp(own - total), jnp.exp(z - total)
+
+    def select(rising, falling, at):
+        first, second = rising[at], falling[at]
+        return jnp.where(half, second, first), jnp.where(half, first, second)
+
+    z_part, own_part = select(up_ref, down_ref, tail)
+    help_part, ahead_part = select(up_in_ref, down_in_ref, tail)
+    rows, shares = [], []
+    for first, second in (
+        (joined_rows(own_part), joined_rows(help_part) + bias_ref[HELPED : HELPED + 1]),
+        (joined_rows(ahead_part), joined_rows(z_part)),
+    ):
+        highest = jnp.maximum(first, second)
+        total = highest + jnp.log(jnp.exp(first - highest) + jnp.exp(second - highest))
+        rows.append(total)
+        shares.append((jnp.exp(first - total), jnp.exp(second - total)))
+    lse_ref[...], lsez_ref[...] = rows
+    sums = [jnp.zeros((8, BLOCK), jnp.float32)] * 4
     for h in range(heads):
         at, row = rows_of(h), slice(h, h + 1)
-        out = (own_ref[at] * own[row] + rz_ref[at].astype(jnp.float32) * z[row]).astype(jnp.bfloat16)
-        a_ref[at] = out
-        wide = out.astype(jnp.float32)
-        squares += (wide * wide).reshape(HD // 8, 8, BLOCK).sum(axis=0)
-        crosses += (wide * ut_ref[at].astype(jnp.float32)).reshape(HD // 8, 8, BLOCK).sum(axis=0)
-    a_ref[tail] = split_rows(total)
-    sums_ref[...] = stack_rows([squares.sum(axis=0, keepdims=True), crosses.sum(axis=0, keepdims=True)])
-
-
-def norm_rows(sums_ref):
-    inverse = lax.rsqrt(sums_ref[0:1] / WIDTH + EPSILON)
-    return inverse, inverse**3 * sums_ref[1:2] / WIDTH
-
-
-def total_rows(a_ref):
-    return joined_rows(a_ref[a_ref.shape[0] - TAIL :])
+        z_out, own_out = select(up_ref, down_ref, at)
+        help_out, ahead_out = select(up_in_ref, down_in_ref, at)
+        for n, (first, second, u_ref, target) in enumerate(
+            ((own_out, help_out, ut_ref, a_ref), (ahead_out, z_out, uzt_ref, az_ref))
+        ):
+            out = (
+                first.astype(jnp.float32) * shares[n][0][row] + second.astype(jnp.float32) * shares[n][1][row]
+            ).astype(jnp.bfloat16)
+            target[at] = out
+            wide = out.astype(jnp.float32)
+            sums[2 * n] += (wide * wide).reshape(HD // 8, 8, BLOCK).sum(axis=0)
+            sums[2 * n + 1] += (wide * u_ref[at].astype(jnp.float32)).reshape(HD // 8, 8, BLOCK).sum(axis=0)
+    sums_ref[...] = stack_rows([part.sum(axis=0, keepdims=True) for part in sums])
+
+
+def norm_rows(sums, first):
+    inverse = lax.rsqrt(sums[first : first + 1] / WIDTH + EPSILON)
+    return inverse, inverse**3 * sums[first + 1 : first + 2] / WIDTH
 
 
 def upstream_part(norm, u, a):
@@ -446,125 +473,95 @@
     return grad, jnp.sum(grad.astype(jnp.float32) * wide, axis=0, keepdims=True)
 
 
-def near_back_kernel(
+def back_kernel(
     heads,
     bias_ref,
     sums_ref,
-    q_ref,
     a_ref,
+    az_ref,
+    lse_ref,
+    lsez_ref,
     ut_ref,
-    up_ref,
-    down_ref,
-    e_ref,
-    m_ref,
-    grad_ref,
-    delta_ref,
-    ds_ref,
-    dk2_ref,
-    dv2_ref,
-):
-    half = Place().half
-    norm = norm_rows(sums_ref)
-    scale = jnp.exp(m_ref[...] - total_rows(a_ref) + bias_ref[NEAR : NEAR + 1])
-    deltas = []
-    for start in range(0, heads, 4):
-        group = range(start, start + 4)
-        parts = [upstream_part(norm, ut_ref[rows_of(h)], a_ref[rows_of(h)]) for h in group]
-        for h, (grad, delta) in zip(group, parts):
-            grad_ref[rows_of(h)] = grad
-            deltas.append(delta)
-        products = []
-        for h, (grad, _) in zip(group, parts):
-            v2 = jnp.where(half, down_ref[SECOND, rows_of(h)], up_ref[SECOND, rows_of(h)])
-            products.append(mm(v2, grad, NN))
-        scores = []
-        for h, product, (_, delta) in zip(group, products, parts):
-            weights = e_ref[rows_of(h)] * scale[h : h + 1]
-            dscore = (weights * (product - delta) * SCALE).astype(jnp.bfloat16)
-            scores.append((dscore, weights.astype(jnp.bfloat16)))
-        for h, (dscore, probs), (grad, _) in zip(group, scores, parts):
-            at = rows_of(h)
-            ds_ref[at] = dscore
-            dk2_ref[:, at] = mm(dscore, q_ref[:, at], NN)
-            dv2_ref[:, at] = mm(probs, grad, NT)
-    delta_ref[...] = stack_rows(deltas)
-
-
-def helper_back_kernel(
-    heads,
-    bias_ref,
-    sz_ref,
-    az_ref,
     uzt_ref,
-    a_ref,
-    grad_ref,
-    delta_ref,
     up_ref,
     down_ref,
     kx_ref,
     vx_ref,
     ez_ref,
     ex_ref,
+    en_ref,
     mz_ref,
     mx_ref,
-    near_ref,
+    mn_ref,
     up_out_ref,
     down_out_ref,
     dvx_ref,
     dsz_ref,
     dsx_ref,
+    dsn_ref,
+    grad_ref,
+    delta_ref,
 ):
     place = Place()
     odd, half = place.odd, place.half
-    norm = norm_rows(sz_ref)
-    z_lse = total_rows(az_ref)
+    sums = sums_ref[...]
+    own_norm, z_norm = norm_rows(sums, 0), norm_rows(sums, 2)
+    lse, z_lse = lse_ref[...], lsez_ref[...]
     scales = (
+        jnp.exp(mn_ref[...] - lse + bias_ref[NEAR : NEAR + 1]),
         jnp.exp(mz_ref[...] - z_lse + bias_ref[FAR : FAR + 1]),
-        jnp.exp(mx_ref[...] - jnp.where(odd, total_rows(a_ref), z_lse) + bias_ref[SIDE : SIDE + 1]),
-    )
-    own_deltas = delta_ref[...]
+        jnp.exp(mx_ref[...] - jnp.where(odd, lse, z_lse) + bias_ref[SIDE : SIDE + 1]),
+    )
+    deltas = []
     step = 2
     for start in range(0, heads, step):
         group = range(start, start + step)
         parts, products, scores = [], [], []
         for h in group:
-            grad, delta = upstream_part(norm, uzt_ref[rows_of(h)], az_ref[rows_of(h)])
-            parts.append((grad, delta))
-            parts.append(
-                (jnp.where(odd, grad_ref[rows_of(h)], grad), jnp.where(odd, own_deltas[h : h + 1], delta))
-            )
-        for n, h in enumerate(group):
+            at = rows_of(h)
+            grad, delta = upstream_part(own_norm, ut_ref[at], a_ref[at])
+            gz, deltaz = upstream_part(z_norm, uzt_ref[at], az_ref[at])
+            grad_ref[at] = grad
+            deltas.append(delta)
+            gx, deltax = jnp.where(odd, grad, gz), jnp.where(odd, delta, deltaz)
+            parts.append(((grad, gz, gx), (delta, deltaz, deltax)))
+        for h, ((grad, gz, gx), _) in zip(group, parts):
             at = rows_of(h)
             v2 = jnp.where(half, down_ref[SECOND, at], up_ref[SECOND, at])
-            products.append(mm(v2, parts[2 * n][0], NN))
-            products.append(mm(vx_ref[:, at], parts[2 * n + 1][0], NN))
-        for n, ((_, delta), product) in enumerate(zip(parts, products)):
-            h = group[n // 2]
-            weights = (ez_ref, ex_ref)[n % 2][rows_of(h)] * scales[n % 2][h : h + 1]
-            dscore = (weights * (product - delta) * SCALE).astype(jnp.bfloat16)
-            scores.append((dscore, weights.astype(jnp.bfloat16)))
-        for n, h in enumerate(group):
+            both = mm(v2, jnp.concatenate([grad, gz], axis=1), NN)
+            products.append((both[:, :BLOCK], both[:, BLOCK:], mm(vx_ref[:, at], gx, NN)))
+        for h, (_, delta), product in zip(group, parts, products):
             at = rows_of(h)
-            (gz, _), (gx, _) = parts[2 * n : 2 * n + 2]
-            (dz, pz), (dx, px) = scores[2 * n : 2 * n + 2]
+            tiles = []
+            for n, (e_ref, ds_ref) in enumerate(((en_ref, dsn_ref), (ez_ref, dsz_ref), (ex_ref, dsx_ref))):
+                weights = e_ref[at] * scales[n][h : h + 1]
+                dscore = (weights * (product[n] - delta[n]) * SCALE).astype(jnp.bfloat16)
+                ds_ref[at] = dscore
+                tiles.append((weights.astype(jnp.bfloat16), dscore))
+            scores.append(tiles)
+        for h, ((grad, gz, gx), _), ((pn, _), (pz, dz), (px, dx)) in zip(group, parts, scores):
+            at = rows_of(h)
             k2 = jnp.where(half, down_ref[FIRST, at], up_ref[FIRST, at])
-            dsz_ref[at], dsx_ref[at] = dz, dx
-            dv2 = (near_ref[:, at] + mm(pz, gz, NT)).astype(jnp.bfloat16)
+            dv2 = mm(jnp.concatenate([pn, pz], axis=1), jnp.concatenate([grad, gz], axis=1), NT)
             dvx_ref[:, at] = mm(px, gx, NT).astype(jnp.bfloat16)
             joined = jnp.concatenate([dz, jnp.where(odd, jnp.zeros_like(dx), dx)], axis=0)
             dqz = mm(joined, jnp.concatenate([k2, kx_ref[:, at]], axis=0), TN).astype(jnp.bfloat16)
+            dv2 = dv2.astype(jnp.bfloat16)
             up_out_ref[:, at] = jnp.where(half, dv2, dqz)
             down_out_ref[:, at] = jnp.where(half, dqz, dv2)
-
-
-def helper_keys_kernel(heads, q_ref, up_ref, down_ref, dsz_ref, dsx_ref, near_ref, dk_ref, dkx_ref):
+    delta_ref[...] = stack_rows(deltas)
+
+
+def helper_keys_kernel(heads, q_ref, up_ref, down_ref, dsz_ref, dsx_ref, dsn_ref, dk_ref, dkx_ref):
     place = Place()
     for h in range(heads):
         at = rows_of(h)
-        qz = jnp.where(place.half, up_ref[FIRST, at], down_ref[FIRST, at])
-        qx = jnp.where(place.odd, q_ref[:, at], qz)
-        dk_ref[:, at] = (near_ref[:, at] + mm(dsz_ref[at], qz, NN)).astype(jnp.bfloat16)
-        dkx_ref[:, at] = mm(dsx_ref[at], qx, NN).astype(jnp.bfloat16)
+        q, qz = q_ref[:, at], jnp.where(place.half, up_ref[FIRST, at], down_ref[FIRST, at])
+        dk2 = mm(
+            jnp.concatenate([dsn_ref[at], dsz_ref[at]], axis=1), jnp.concatenate([q, qz], axis=0), NN
+        )
+        dk_ref[:, at] = dk2.astype(jnp.bfloat16)
+        dkx_ref[:, at] = mm(dsx_ref[at], jnp.where(place.odd, q, qz), NN).astype(jnp.bfloat16)
 
 
 def diagonal_back_kernel(
@@ -574,6 +571,7 @@
     k_ref,
     v_ref,
     a_ref,
+    lse_ref,
     grad_ref,
     delta_ref,
     ds_ref,
@@ -588,8 +586,8 @@
 ):
     place = Place()
     half, odd = place.half, place.odd
-    inverse, _ = norm_rows(sums_ref)
-    lse = total_rows(a_ref)
+    inverse, _ = norm_rows(sums_ref[...], 0)
+    lse = lse_ref[...]
     causal = causal_mask()
     for h in range(heads):
         at, row = rows_of(h), slice(h, h + 1)
@@ -707,57 +705,45 @@
         3 * unit,
         after=(payload[0],),
     )
-    out_z, ez, ex, mz, mx = call(
-        helper_kernel,
+    up_out, down_out, *kept = call(
+        forward_kernel,
         heads,
         (),
-        (bias, *received, queries, keys_x, values_x),
-        (message, wide_t, wide_t, rows, rows),
-        4 * unit,
-    )
-    back_z = ring(out_z, 2)
-    own, own_lse, upstream_zt, e2, m2 = call(
-        own_kernel,
+        (bias, *received, queries, keys_x, values_x, diagonal, diagonal_lse),
+        (message, message, wide_t, wide_t, wide_t, rows, rows, rows),
+        6 * unit,
+    )
+    up_in, down_in = cycle(up_out, down_out)
+    (upstream_zt,) = call(transpose_kernel, heads, (), received, (flat_t,), 0, after=(kept[-1],))
+    attention, attention_z, lse, lse_z, sums = call(
+        merge_kernel,
         heads,
         (),
-        (bias, *received, queries, diagonal, diagonal_lse, values_x, ex, mx),
-        (wide_t, rows, flat_t, wide_t, rows),
-        3 * unit,
-    )
-    attention, sums = call(
-        merge_kernel, heads, (), (bias, own, own_lse, back_z, upstream_t), (message, rows), unit // 64
+        (bias, up_out, down_out, up_in, down_in, upstream_t, upstream_zt),
+        (flat_t, flat_t, rows, rows, rows),
+        unit // 64,
     )
     others = [
         lax.ppermute(sums, "head", [(i, i ^ step) for i in range(members)]) for step in range(1, members)
     ]
-    attention_z = ring(attention, -2)
     sums = functools.reduce(jnp.add, others, sums)
-    sums_z = ring(sums, -2)
-    grad_t, delta, near_ds, near_dk, near_dv = call(
-        near_back_kernel,
+    up_out, down_out, side_dv, far_ds, side_ds, near_ds, grad_t, delta = call(
+        back_kernel,
         heads,
         (),
-        (bias, sums, queries, attention, upstream_t, *received, e2, m2),
-        (flat_t, rows, flat_t, wide, wide),
-        3 * unit,
-    )
-    up_out, down_out, side_dv, far_ds, side_ds = call(
-        helper_back_kernel,
-        heads,
-        (),
-        (bias, sums_z, attention_z, upstream_zt, attention, grad_t, delta, *received, keys_x, values_x)
-        + (ez, ex, mz, mx, near_dv),
-        (flat, flat, flat, flat_t, flat_t),
-        6 * unit,
+        (bias, sums, attention, attention_z, lse, lse_z, upstream_t, upstream_zt, *received, keys_x, values_x)
+        + tuple(kept),
+        (flat, flat, flat, flat_t, flat_t, flat_t, flat_t, rows),
+        8 * unit,
     )
     returned = cycle(up_out, down_out)
     out_dk, side_dk = call(
         helper_keys_kernel,
         heads,
         (),
-        (queries, *received, far_ds, side_ds, near_dk),
+        (queries, *received, far_ds, side_ds, near_ds),
         (flat, flat),
-        2 * unit,
+        3 * unit,
     )
     back_dk = ring(out_dk, -2)
     side_dv, side_dk = swap(side_dv), swap(side_dk)
@@ -765,7 +751,7 @@
         diagonal_back_kernel,
         heads,
         (),
-        (sums, queries, keys, values, attention, grad_t, delta, near_ds, side_ds, keys_x, *received),
+        (sums, queries, keys, values, attention, lse, grad_t, delta, near_ds, side_ds, keys_x, *received),
         (flat, wide, wide, wide),
         7 * unit,
     )

time: 54.6 us -> 50.7 us (0.929)
  waiting for transfers between devices: 23.2 us -> 20.4 us
  Pallas kernels: 12.5 us -> 11.8 us
    ppermute x4 -> x1, waiting for transfers between devices: 9.82 us -> 2.43 us  [ring(): lax.ppermute(array, 'ctx', [(i, (i + distance) % blocks) for i in range(b...]
    ppermute x2 -> x3, waiting for transfers between devices: 0.01 us -> 4.89 us  [cycle(): lax.ppermute(up_array, ('ctx', 'head'), rising)]
    ppermute x2 -> x3, starting transfers between devices: 0.46 us -> 3.43 us  [cycle(): lax.ppermute(up_array, ('ctx', 'head'), rising)]
    ppermute x4 -> x1, starting transfers between devices: 6.08 us -> 3.55 us  [ring(): lax.ppermute(array, 'ctx', [(i, (i + distance) % blocks) for i in range(b...]
    ppermute x4, waiting for transfers between devices: 9.71 us -> 8.3 us  [swap(): return lax.ppermute(array, 'ctx', [(i, i ^ 1) for i in range(blocks)])]
    ppermute x2 -> x3, waiting for transfers between devices: 1.86 us -> 2.92 us  [cycle(): lax.ppermute(down_array, ('ctx', 'head'), falling)]
    ppermute x2 -> x3, starting transfers between devices: 4.71 us -> 3.82 us  [cycle(): lax.ppermute(down_array, ('ctx', 'head'), falling)]
    pallas_call x11 -> x10, Pallas kernels: 12.5 us -> 11.8 us  [call(): pl.pallas_call(lambda *refs: kernel(heads, *refs[len(after):]), out_shape...]
  transfers between devices with their start and end apart: 15 -> 14, of which waited for: 10 -> 8; matrix products, arithmetic and copies ran while one was open for 0% -> 0% of each run, Pallas kernels for 15% -> 13%
where the time goes in v6:
time: 50.7 us; the launch traced here: 50.5 us
  waiting for transfers between devices  20.4 us (40%)
  starting transfers between devices  16.9 us (33%)
  Pallas kernels  11.8 us (23%)
  between operations  0.73 us (1%)
  local copies, waits for them, and re-layouts  0.7 us (1%)
    pallas_call x10, Pallas kernels, call(): pl.pallas_call(lambda *refs: kernel(heads, *refs[len(after):]), out_shape...  11.8 us
    ppermute x4, waiting for transfers between devices, swap(): return lax.ppermute(array, 'ctx', [(i, i ^ 1) for i in range(blocks)])  8.3 us
    ppermute x3, waiting for transfers between devices, cycle(): lax.ppermute(up_array, ('ctx', 'head'), rising)  4.89 us
    ppermute x4, starting transfers between devices, swap(): return lax.ppermute(array, 'ctx', [(i, i ^ 1) for i in range(blocks)])  4.18 us
    ppermute x3, starting transfers between devices, cycle(): lax.ppermute(down_array, ('ctx', 'head'), falling)  3.82 us
    ppermute x1, starting transfers between devices, ring(): lax.ppermute(array, 'ctx', [(i, (i + distance) % blocks) for i in range(b...  3.55 us
    ppermute x3, starting transfers between devices, cycle(): lax.ppermute(up_array, ('ctx', 'head'), rising)  3.43 us
    ppermute x3, waiting for transfers between devices, cycle(): lax.ppermute(down_array, ('ctx', 'head'), falling)  2.92 us
  transfers between devices with their start and end apart: 14, of which 8 were waited for; matrix products, arithmetic and copies ran while one was open for 0% of the time, Pallas kernels for 13%

profile of v6, /device:TPU:0, one launch (start us, length us, event | category | flops | bytes accessed | tf_op | source)
XLA Modules:
  0.0 50.5 jit_solution(1000514439752210766)
XLA Ops:
  0.7 1.3 %shard_map.84 = (bf16[256,1024]{1,0:T(8,128)(2,1)S(1)}, bf16[256,1024]{1,0:T(8,128)(2,1)S(1)}) custom-call(bf16[128,1024]{1,0:T(8,128)(2,1)} %refs_0_.3, bf16[128,1024]{1,0:T(8,128)(2,1)} %refs_2_.5, bf16[128,1024]{1,0:T(8,128)(2,1)} %refs_3_.7, bf16[128,1024]{1,0:T(8,128)(2,1)} %refs_5_.1), custom_call_target="tpu_custom_call" | custom-call | bytes 2097152 | tf_op jit(solution)/shard_map/pallas_call | solution.py:632
  2.0 3.0 %collective-permute-start.1 = (bf16[256,1024]{1,0:T(8,128)(2,1)S(1)}, bf16[256,1024]{1,0:T(8,128)(2,1)S(1)}, u32[]{:S(2)}, u32[]{:S(2)}) collective-permute-start(bf16[256,1024]{1,0:T(8,128)(2,1)S(1)} %get-tuple-element.42), channel_id=1, source_target_pairs={{8,0},{9,1},{0,2},{1,3},{12,4},{13,5},{4,6},{5,7},{16,8},{17,9},{2... | collective-permute-start | bytes 1572872 | tf_op jit(solution)/shard_map/ppermute | solution.py:668
  5.1 1.9 %collective-permute-start.2 = (bf16[128,1024]{1,0:T(8,128)(2,1)S(1)}, bf16[128,1024]{1,0:T(8,128)(2,1)S(1)}, u32[]{:S(2)}, u32[]{:S(2)}) collective-permute-start(bf16[128,1024]{1,0:T(8,128)(2,1)S(1)} %copy-done.1), channel_id=1, source_target_pairs={{0,4},{4,0},{8,12},{12,8},{16,20},{20,16},{24,28},{28,24},{1,5},{5... | collective-permute-start | bytes 786440 | tf_op jit(solution)/shard_map/ppermute | solution.py:673
  7.2 0.7 %copy-done.4 = s32[8,8]{1,0:T(8,128)S(1)} copy-done((s32[8,8]{1,0:T(8,128)S(1)}, s32[8,8]{1,0:T(8,128)}, u32[]{:S(2)}) %copy-start.4) | copy-done | bytes 280
  7.9 2.4 %shard_map.85 = (f32[1024,128]{1,0:T(8,128)S(1)}, f32[8,128]{1,0:T(8,128)S(1)}, bf16[1024,128]{1,0:T(8,128)(2,1)S(1)}, f32[8,128]{1,0:T(8,128)S(1)}) custom-call(bf16[256,1024]{1,0:T(8,128)(2,1)S(1)} %get-tuple-element.40.refs_0_, s32[8,8]{1,0:T(8,128)S(1)} %copy-done.4, bf16[128,1024]{1,0:T(8,128)(2,1)S(1)} %copy-done, bf16[128,1024]{1,0:T(8,128)(2,1)S(1)} %copy-done.1, ...), custom_call_target="tpu_custom_call" | custom-call | flops 100663296 | bytes 1843200 | tf_op jit(solution)/shard_map/pallas_call | solution.py:632
  10.2 4.1 %collective-permute-done.2.refs_4_.refs_10_ = bf16[128,1024]{1,0:T(8,128)(2,1)S(1)} collective-permute-done((bf16[128,1024]{1,0:T(8,128)(2,1)S(1)}, bf16[128,1024]{1,0:T(8,128)(2,1)S(1)}, u32[]{:S(2)}, u32[]{:S(2)}) %collective-permute-start.2) | collective-permute-done | bytes 262176 | tf_op jit(solution)/shard_map/ppermute | solution.py:673
  14.4 4.2 %collective-permute-done.3.refs_5_.refs_11_ = bf16[128,1024]{1,0:T(8,128)(2,1)S(1)} collective-permute-done((bf16[128,1024]{1,0:T(8,128)(2,1)S(1)}, bf16[128,1024]{1,0:T(8,128)(2,1)S(1)}, u32[]{:S(2)}, u32[]{:S(2)}) %collective-permute-start.3) | collective-permute-done | bytes 262176 | tf_op jit(solution)/shard_map/ppermute | solution.py:673
  18.5 1.5 %shard_map.86 = (bf16[1056,128]{1,0:T(8,128)(2,1)S(1)}, bf16[1056,128]{1,0:T(8,128)(2,1)S(1)}, f32[1024,128]{1,0:T(8,128)S(1)}, f32[1024,128]{1,0:T(8,128)S(1)},...) custom-call(f32[8,128]{1,0:T(8,128)S(1)} %get-tuple-element.41.refs_0_, ...), custom_call_target="tpu_custom_call" | custom-call | flops 201326592 | bytes 4493312 | tf_op jit(solution)/shard_map/pallas_call | solution.py:632
  20.0 1.7 %collective-permute-start.4 = (bf16[1056,128]{1,0:T(8,128)(2,1)S(1)}, bf16[1056,128]{1,0:T(8,128)(2,1)S(1)}, u32[]{:S(2)}, u32[]{:S(2)}) collective-permute-start(bf16[1056,128]{1,0:T(8,128)(2,1)S(1)} %get-tuple-element.45.refs_1_), channel_id=1, source_target_pairs={{0,8},{1,9},{2,0},{3,1},{4,12},{5,13},{6,4},{7,5},{8,16},{9,17},{1... | collective-permute-start | bytes 811016 | tf_op jit(solution)/shard_map/ppermute | solution.py:668
  22.2 4.9 %collective-permute-done.4.refs_3_ = bf16[1056,128]{1,0:T(8,128)(2,1)S(1)} collective-permute-done((bf16[1056,128]{1,0:T(8,128)(2,1)S(1)}, bf16[1056,128]{1,0:T(8,128)(2,1)S(1)}, u32[]{:S(2)}, u32[]{:S(2)}) %collective-permute-start.4) | collective-permute-done | bytes 270368 | tf_op jit(solution)/shard_map/ppermute | solution.py:668
  27.1 1.1 %collective-permute-done.5.refs_4_ = bf16[1056,128]{1,0:T(8,128)(2,1)S(1)} collective-permute-done((bf16[1056,128]{1,0:T(8,128)(2,1)S(1)}, bf16[1056,128]{1,0:T(8,128)(2,1)S(1)}, u32[]{:S(2)}, u32[]{:S(2)}) %collective-permute-start.5) | collective-permute-done | bytes 270368 | tf_op jit(solution)/shard_map/ppermute | solution.py:668
  28.8 0.7 %collective-permute-start.7 = (f32[8,128]{1,0:T(8,128)S(1)}, f32[8,128]{1,0:T(8,128)S(1)}, u32[]{:S(2)}, u32[]{:S(2)}) collective-permute-start(f32[8,128]{1,0:T(8,128)S(1)} %get-tuple-element.49), channel_id=1, source_target_pairs={{0,2},{1,3},{2,0},{3,1},{4,6},{5,7},{6,4},{7,5},{8,10},{9,11},{10,... | collective-permute-start | bytes 12296 | tf_op jit(solution)/shard_map/ppermute | solution.py:727
  29.5 1.1 %collective-permute-start.6 = (f32[8,128]{1,0:T(8,128)S(1)}, f32[8,128]{1,0:T(8,128)S(1)}, u32[]{:S(2)}, u32[]{:S(2)}) collective-permute-start(f32[8,128]{1,0:T(8,128)S(1)} %get-tuple-element.49), channel_id=1, source_target_pairs={{0,1},{1,0},{2,3},{3,2},{4,5},{5,4},{6,7},{7,6},{8,9},{9,8},{10,11... | collective-permute-start | bytes 12296 | tf_op jit(solution)/shard_map/ppermute | solution.py:727
  30.7 1.2 %collective-permute-done.8 = f32[8,128]{1,0:T(8,128)S(1)} collective-permute-done((f32[8,128]{1,0:T(8,128)S(1)}, f32[8,128]{1,0:T(8,128)S(1)}, u32[]{:S(2)}, u32[]{:S(2)}) %collective-permute-start.8) | collective-permute-done | bytes 4128 | tf_op jit(solution)/shard_map/ppermute | solution.py:727
  31.8 0.7 %collective-permute-done.7 = f32[8,128]{1,0:T(8,128)S(1)} collective-permute-done((f32[8,128]{1,0:T(8,128)S(1)}, f32[8,128]{1,0:T(8,128)S(1)}, u32[]{:S(2)}, u32[]{:S(2)}) %collective-permute-start.7) | collective-permute-done | bytes 4128 | tf_op jit(solution)/shard_map/ppermute | solution.py:727
  32.5 1.3 %shard_map.89 = (bf16[128,1024]{1,0:T(8,128)(2,1)S(1)}, bf16[128,1024]{1,0:T(8,128)(2,1)S(1)}, bf16[128,1024]{1,0:T(8,128)(2,1)S(1)}, bf16[1024,128]{1,0:T(8,128...) custom-call(f32[8,128]{1,0:T(8,128)S(1)} %get-tuple-element.41.refs_, ...), custom_call_target="tpu_custom_call" | custom-call | flops 268435456 | bytes 6062080 | tf_op jit(solution)/shard_map/pallas_call | solution.py:632
  33.8 1.6 %collective-permute-start.9 = (bf16[128,1024]{1,0:T(8,128)(2,1)S(1)}, bf16[128,1024]{1,0:T(8,128)(2,1)S(1)}, u32[]{:S(2)}, u32[]{:S(2)}) collective-permute-start(bf16[128,1024]{1,0:T(8,128)(2,1)S(1)} %get-tuple-element.66), channel_id=1, source_target_pairs={{0,4},{4,0},{8,12},{12,8},{16,20},{20,16},{24,28},{28,24},{1,5},{5... | collective-permute-start | bytes 786440 | tf_op jit(solution)/shard_map/ppermute | solution.py:673
  35.3 1.6 %collective-permute-start.10 = (bf16[128,1024]{1,0:T(8,128)(2,1)S(1)}, bf16[128,1024]{1,0:T(8,128)(2,1)S(1)}, u32[]{:S(2)}, u32[]{:S(2)}) collective-permute-start(bf16[128,1024]{1,0:T(8,128)(2,1)S(1)} %get-tuple-element.67), channel_id=1, source_target_pairs={{0,8},{1,9},{2,0},{3,1},{4,12},{5,13},{6,4},{7,5},{8,16},{9,17},{1... | collective-permute-start | bytes 786440 | tf_op jit(solution)/shard_map/ppermute | solution.py:668
  38.4 3.6 %collective-permute-start.13 = (bf16[128,1024]{1,0:T(8,128)(2,1)S(1)}, bf16[128,1024]{1,0:T(8,128)(2,1)S(1)}, u32[]{:S(2)}, u32[]{:S(2)}) collective-permute-start(bf16[128,1024]{1,0:T(8,128)(2,1)S(1)} %get-tuple-element.74), channel_id=1, source_target_pairs={{0,24},{4,28},{8,0},{12,4},{16,8},{20,12},{24,16},{28,20},{1,25},{... | collective-permute-start | bytes 786440 | tf_op jit(solution)/shard_map/ppermute | solution.py:676
  41.9 2.4 %shard_map.90 = (bf16[128,1024]{1,0:T(8,128)(2,1)}, f32[128,1024]{1,0:T(8,128)S(1)}, f32[128,1024]{1,0:T(8,128)S(1)}, f32[128,1024]{1,0:T(8,128)S(1)}) custom-call(f32[8,128]{1,0:T(8,128)S(1)} %add_add_fusion.refs_1_.refs_0_, bf16[128,1024]{1,0:T(8,128)(2,1)S(1)} %copy-done, bf16[128,1024]{1,0:T(8,128)(2,1)S(1)} %copy-done.1, ...), custom_call_target="tpu_custom_call" | custom-call | flops 234881024 | bytes 4993024 | tf_op jit(solution)/shard_map/pallas_call | solution.py:632
  44.4 1.8 %collective-permute-done.11.refs_4_ = bf16[128,1024]{1,0:T(8,128)(2,1)S(1)} collective-permute-done((bf16[128,1024]{1,0:T(8,128)(2,1)S(1)}, bf16[128,1024]{1,0:T(8,128)(2,1)S(1)}, u32[]{:S(2)}, u32[]{:S(2)}) %collective-permute-start.11) | collective-permute-done | bytes 262176 | tf_op jit(solution)/shard_map/ppermute | solution.py:668
  46.2 1.1 %shard_map.91 = (bf16[128,1024]{1,0:T(8,128)(2,1)}, bf16[128,1024]{1,0:T(8,128)(2,1)}, f32[8,128]{1,0:T(8,128)S(1)}) custom-call(f32[128,1024]{1,0:T(8,128)S(1)} %get-tuple-element.64.refs_0_, f32[128,1024]{1,0:T(8,128)S(1)} %get-tuple-element.65.refs_1_, bf16[128,1024]{1,0:T(8,128)(2,1)S(1)} %collective-permute-done.9.refs_2_, ...), custom_call_target="tpu_custom_call" | custom-call | bytes 2363392 | tf_op jit(solution)/shard_map/pallas_call | solution.py:632
  47.2 2.4 %collective-permute-done.13.refs_3_ = bf16[128,1024]{1,0:T(8,128)(2,1)S(1)} collective-permute-done((bf16[128,1024]{1,0:T(8,128)(2,1)S(1)}, bf16[128,1024]{1,0:T(8,128)(2,1)S(1)}, u32[]{:S(2)}, u32[]{:S(2)}) %collective-permute-start.13) | collective-permute-done | bytes 262176 | tf_op jit(solution)/shard_map/ppermute | solution.py:676
  49.7 0.8 %shard_map.93 = bf16[128,1024]{1,0:T(8,128)(2,1)} custom-call(f32[8,128]{1,0:T(8,128)S(1)} %get-tuple-element.70.refs_0_, f32[128,1024]{1,0:T(8,128)S(1)} %get-tuple-element.71.refs_1_, bf16[128,1024]{1,0:T(8,128)(2,1)S(1)} %collective-permute-done.12.refs_2_, bf16[128,1024]{1,0:T(8,128)(2,1)S(1)} %collective-permute-done.13.refs_3_), custom_call_target="tpu_custom_call" | custom-call | bytes 1310720 | tf_op jit(solution)/shard_map/pallas_call | solution.py:632
  (25 shorter events, 2.8 us)
Async XLA Ops:
  0.6 6.5 %copy-start = (bf16[128,1024]{1,0:T(8,128)(2,1)S(1)}, bf16[128,1024]{1,0:T(8,128)(2,1)}, u32[]{:S(2)}) copy-start(bf16[128,1024]{1,0:T(8,128)(2,1)} %refs_0_.3) | copy-start | bytes 786436
  0.6 6.4 %copy-start.2 = (bf16[128,1024]{1,0:T(8,128)(2,1)S(1)}, bf16[128,1024]{1,0:T(8,128)(2,1)}, u32[]{:S(2)}) copy-start(bf16[128,1024]{1,0:T(8,128)(2,1)} %refs_3_.7) | copy-start | bytes 786436
  0.7 4.5 %copy-start.1 = (bf16[128,1024]{1,0:T(8,128)(2,1)S(1)}, bf16[128,1024]{1,0:T(8,128)(2,1)}, u32[]{:S(2)}) copy-start(bf16[128,1024]{1,0:T(8,128)(2,1)} %refs_2_.5) | copy-start | bytes 786436
  0.7 6.5 %copy-start.3 = (bf16[128,1024]{1,0:T(8,128)(2,1)S(1)}, bf16[128,1024]{1,0:T(8,128)(2,1)}, u32[]{:S(2)}) copy-start(bf16[128,1024]{1,0:T(8,128)(2,1)} %refs_5_.1) | copy-start | bytes 786436
  2.0 16.5 %collective-permute-start.1 = (bf16[256,1024]{1,0:T(8,128)(2,1)S(1)}, bf16[256,1024]{1,0:T(8,128)(2,1)S(1)}, u32[]{:S(2)}, u32[]{:S(2)}) collective-permute-start(bf16[256,1024]{1,0:T(8,128)(2,1)S(1)} %get-tuple-element.42), channel_id=1, source_target_pairs={{8,0},{9,1},{0,2},{1,3},{12,4},{13,5},{4,6},{5,7},{16,8},{17,9},{2... | collective-permute-start | bytes 1572872 | tf_op jit(solution)/shard_map/ppermute | solution.py:668
  5.0 13.5 %collective-permute-start = (bf16[256,1024]{1,0:T(8,128)(2,1)S(1)}, bf16[256,1024]{1,0:T(8,128)(2,1)S(1)}, u32[]{:S(2)}, u32[]{:S(2)}) collective-permute-start(bf16[256,1024]{1,0:T(8,128)(2,1)S(1)} %get-tuple-element.40.refs_0_), channel_id=1, source_target_pairs={{0,8},{1,9},{2,0},{3,1},{4,12},{5,13},{6,4},{7,5},{8,16},{9,17},{1... | collective-permute-start | bytes 1572872 | tf_op jit(solution)/shard_map/ppermute | solution.py:668
  5.1 9.2 %collective-permute-start.2 = (bf16[128,1024]{1,0:T(8,128)(2,1)S(1)}, bf16[128,1024]{1,0:T(8,128)(2,1)S(1)}, u32[]{:S(2)}, u32[]{:S(2)}) collective-permute-start(bf16[128,1024]{1,0:T(8,128)(2,1)S(1)} %copy-done.1), channel_id=1, source_target_pairs={{0,4},{4,0},{8,12},{12,8},{16,20},{20,16},{24,28},{28,24},{1,5},{5... | collective-permute-start | bytes 786440 | tf_op jit(solution)/shard_map/ppermute | solution.py:673
  7.0 11.5 %collective-permute-start.3 = (bf16[128,1024]{1,0:T(8,128)(2,1)S(1)}, bf16[128,1024]{1,0:T(8,128)(2,1)S(1)}, u32[]{:S(2)}, u32[]{:S(2)}) collective-permute-start(bf16[128,1024]{1,0:T(8,128)(2,1)S(1)} %copy-done.2), channel_id=1, source_target_pairs={{0,4},{4,0},{8,12},{12,8},{16,20},{20,16},{24,28},{28,24},{1,5},{5... | collective-permute-start | bytes 786440 | tf_op jit(solution)/shard_map/ppermute | solution.py:673
  7.2 0.7 %copy-start.4 = (s32[8,8]{1,0:T(8,128)S(1)}, s32[8,8]{1,0:T(8,128)}, u32[]{:S(2)}) copy-start(s32[8,8]{1,0:T(8,128)} %refs_1_.4) | copy-start | bytes 772
  20.0 7.1 %collective-permute-start.4 = (bf16[1056,128]{1,0:T(8,128)(2,1)S(1)}, bf16[1056,128]{1,0:T(8,128)(2,1)S(1)}, u32[]{:S(2)}, u32[]{:S(2)}) collective-permute-start(bf16[1056,128]{1,0:T(8,128)(2,1)S(1)} %get-tuple-element.45.refs_1_), channel_id=1, source_target_pairs={{0,8},{1,9},{2,0},{3,1},{4,12},{5,13},{6,4},{7,5},{8,16},{9,17},{1... | collective-permute-start | bytes 811016 | tf_op jit(solution)/shard_map/ppermute | solution.py:668
  21.8 6.5 %collective-permute-start.5 = (bf16[1056,128]{1,0:T(8,128)(2,1)S(1)}, bf16[1056,128]{1,0:T(8,128)(2,1)S(1)}, u32[]{:S(2)}, u32[]{:S(2)}) collective-permute-start(bf16[1056,128]{1,0:T(8,128)(2,1)S(1)} %get-tuple-element.46.refs_2_), channel_id=1, source_target_pairs={{8,0},{9,1},{0,2},{1,3},{12,4},{13,5},{4,6},{5,7},{16,8},{17,9},{2... | collective-permute-start | bytes 811016 | tf_op jit(solution)/shard_map/ppermute | solution.py:668
  28.7 3.1 %collective-permute-start.8 = (f32[8,128]{1,0:T(8,128)S(1)}, f32[8,128]{1,0:T(8,128)S(1)}, u32[]{:S(2)}, u32[]{:S(2)}) collective-permute-start(f32[8,128]{1,0:T(8,128)S(1)} %get-tuple-element.49), channel_id=1, source_target_pairs={{0,3},{1,2},{2,1},{3,0},{4,7},{5,6},{6,5},{7,4},{8,11},{9,10},{10,... | collective-permute-start | bytes 12296 | tf_op jit(solution)/shard_map/ppermute | solution.py:727
  28.8 3.7 %collective-permute-start.7 = (f32[8,128]{1,0:T(8,128)S(1)}, f32[8,128]{1,0:T(8,128)S(1)}, u32[]{:S(2)}, u32[]{:S(2)}) collective-permute-start(f32[8,128]{1,0:T(8,128)S(1)} %get-tuple-element.49), channel_id=1, source_target_pairs={{0,2},{1,3},{2,0},{3,1},{4,6},{5,7},{6,4},{7,5},{8,10},{9,11},{10,... | collective-permute-start | bytes 12296 | tf_op jit(solution)/shard_map/ppermute | solution.py:727
  29.5 3.0 %collective-permute-start.6 = (f32[8,128]{1,0:T(8,128)S(1)}, f32[8,128]{1,0:T(8,128)S(1)}, u32[]{:S(2)}, u32[]{:S(2)}) collective-permute-start(f32[8,128]{1,0:T(8,128)S(1)} %get-tuple-element.49), channel_id=1, source_target_pairs={{0,1},{1,0},{2,3},{3,2},{4,5},{5,4},{6,7},{7,6},{8,9},{9,8},{10,11... | collective-permute-start | bytes 12296 | tf_op jit(solution)/shard_map/ppermute | solution.py:727
  33.8 10.6 %collective-permute-start.9 = (bf16[128,1024]{1,0:T(8,128)(2,1)S(1)}, bf16[128,1024]{1,0:T(8,128)(2,1)S(1)}, u32[]{:S(2)}, u32[]{:S(2)}) collective-permute-start(bf16[128,1024]{1,0:T(8,128)(2,1)S(1)} %get-tuple-element.66), channel_id=1, source_target_pairs={{0,4},{4,0},{8,12},{12,8},{16,20},{20,16},{24,28},{28,24},{1,5},{5... | collective-permute-start | bytes 786440 | tf_op jit(solution)/shard_map/ppermute | solution.py:673
  35.3 9.0 %collective-permute-start.10 = (bf16[128,1024]{1,0:T(8,128)(2,1)S(1)}, bf16[128,1024]{1,0:T(8,128)(2,1)S(1)}, u32[]{:S(2)}, u32[]{:S(2)}) collective-permute-start(bf16[128,1024]{1,0:T(8,128)(2,1)S(1)} %get-tuple-element.67), channel_id=1, source_target_pairs={{0,8},{1,9},{2,0},{3,1},{4,12},{5,13},{6,4},{7,5},{8,16},{9,17},{1... | collective-permute-start | bytes 786440 | tf_op jit(solution)/shard_map/ppermute | solution.py:668
  36.9 9.2 %collective-permute-start.11 = (bf16[128,1024]{1,0:T(8,128)(2,1)S(1)}, bf16[128,1024]{1,0:T(8,128)(2,1)S(1)}, u32[]{:S(2)}, u32[]{:S(2)}) collective-permute-start(bf16[128,1024]{1,0:T(8,128)(2,1)S(1)} %get-tuple-element.68), channel_id=1, source_target_pairs={{8,0},{9,1},{0,2},{1,3},{12,4},{13,5},{4,6},{5,7},{16,8},{17,9},{2... | collective-permute-start | bytes 786440 | tf_op jit(solution)/shard_map/ppermute | solution.py:668
  37.8 9.5 %collective-permute-start.12 = (bf16[128,1024]{1,0:T(8,128)(2,1)S(1)}, bf16[128,1024]{1,0:T(8,128)(2,1)S(1)}, u32[]{:S(2)}, u32[]{:S(2)}) collective-permute-start(bf16[128,1024]{1,0:T(8,128)(2,1)S(1)} %get-tuple-element.73), channel_id=1, source_target_pairs={{0,4},{4,0},{8,12},{12,8},{16,20},{20,16},{24,28},{28,24},{1,5},{5... | collective-permute-start | bytes 786440 | tf_op jit(solution)/shard_map/ppermute | solution.py:673
  38.4 11.3 %collective-permute-start.13 = (bf16[128,1024]{1,0:T(8,128)(2,1)S(1)}, bf16[128,1024]{1,0:T(8,128)(2,1)S(1)}, u32[]{:S(2)}, u32[]{:S(2)}) collective-permute-start(bf16[128,1024]{1,0:T(8,128)(2,1)S(1)} %get-tuple-element.74), channel_id=1, source_target_pairs={{0,24},{4,28},{8,0},{12,4},{16,8},{20,12},{24,16},{28,20},{1,25},{... | collective-permute-start | bytes 786440 | tf_op jit(solution)/shard_map/ppermute | solution.py:676

commit v7 on v6

--- a/solution.py
+++ b/solution.py
@@ -604,7 +604,7 @@
         )
 
 
-def final_first_kernel(heads, dq_own_ref, dv_own_ref, side_ref, up_ref, down_ref, dq_ref, dv_ref, token_ref):
+def final_first_kernel(heads, up_ref, down_ref, side_ref, dq_own_ref, dv_own_ref, dq_ref, dv_ref, token_ref):
     place = Place()
     half = place.half
     ahead = (place.me + 2 < lax.axis_size("ctx")).astype(jnp.float32)
@@ -619,7 +619,7 @@
     token_ref[...] = jnp.zeros_like(token_ref)
 
 
-def final_keys_kernel(heads, dk_own_ref, side_ref, back_ref, dk_ref):
+def final_keys_kernel(heads, back_ref, side_ref, dk_own_ref, dk_ref):
     ahead = (Place().me + 2 < lax.axis_size("ctx")).astype(jnp.float32)
     for h in range(heads):
         at = rows_of(h)
@@ -756,9 +756,9 @@
         7 * unit,
     )
     grad_queries, grad_values, token = call(
-        final_first_kernel, heads, (), (dq_own, dv_own, side_dv, *returned), (flat, flat, rows), 0
-    )
-    (grad_keys,) = call(final_keys_kernel, heads, (), (dk_own, side_dk, back_dk), (flat,), 0, after=(token,))
+        final_first_kernel, heads, (), (*returned, side_dv, dq_own, dv_own), (flat, flat, rows), 0
+    )
+    (grad_keys,) = call(final_keys_kernel, heads, (), (back_dk, side_dk, dk_own), (flat,), 0, after=(token,))
     return (normed, grad_queries, grad_keys, grad_values)
 
 

time: 50.7 us -> 49.7 us (0.980)
  waiting for transfers between devices: 20.4 us -> 19.4 us
    ppermute x3, waiting for transfers between devices: 2.92 us -> 1.44 us  [cycle(): lax.ppermute(down_array, ('ctx', 'head'), falling)]
  transfers between devices with their start and end apart: 14 -> 14, of which waited for: 8 -> 9; matrix products, arithmetic and copies ran while one was open for 0% -> 0% of each run, Pallas kernels for 13% -> 13%
where the time goes in v7:
time: 49.7 us; the launch traced here: 49.5 us
  waiting for transfers between devices  19.4 us (39%)
  starting transfers between devices  16.9 us (34%)
  Pallas kernels  11.8 us (24%)
  between operations  0.73 us (1%)
  local copies, waits for them, and re-layouts  0.7 us (1%)
    pallas_call x10, Pallas kernels, call(): pl.pallas_call(lambda *refs: kernel(heads, *refs[len(after):]), out_shape...  11.8 us
    ppermute x4, waiting for transfers between devices, swap(): return lax.ppermute(array, 'ctx', [(i, i ^ 1) for i in range(blocks)])  8.53 us
    ppermute x3, waiting for transfers between devices, cycle(): lax.ppermute(up_array, ('ctx', 'head'), rising)  4.89 us
    ppermute x4, starting transfers between devices, swap(): return lax.ppermute(array, 'ctx', [(i, i ^ 1) for i in range(blocks)])  4.05 us
    ppermute x3, starting transfers between devices, cycle(): lax.ppermute(down_array, ('ctx', 'head'), falling)  3.82 us
    ppermute x1, starting transfers between devices, ring(): lax.ppermute(array, 'ctx', [(i, (i + distance) % blocks) for i in range(b...  3.6 us
    ppermute x3, starting transfers between devices, cycle(): lax.ppermute(up_array, ('ctx', 'head'), rising)  3.48 us
    ppermute x1, waiting for transfers between devices, ring(): lax.ppermute(array, 'ctx', [(i, (i + distance) % blocks) for i in range(b...  2.72 us
  transfers between devices with their start and end apart: 14, of which 9 were waited for; matrix products, arithmetic and copies ran while one was open for 0% of the time, Pallas kernels for 13%

profile of v7, /device:TPU:0, one launch (start us, length us, event | category | flops | bytes accessed | tf_op | source)
XLA Modules:
  0.0 49.5 jit_solution(12780667614076091420)
XLA Ops:
  0.7 1.3 %shard_map.84 = (bf16[256,1024]{1,0:T(8,128)(2,1)S(1)}, bf16[256,1024]{1,0:T(8,128)(2,1)S(1)}) custom-call(bf16[128,1024]{1,0:T(8,128)(2,1)} %refs_0_.3, bf16[128,1024]{1,0:T(8,128)(2,1)} %refs_2_.5, bf16[128,1024]{1,0:T(8,128)(2,1)} %refs_3_.7, bf16[128,1024]{1,0:T(8,128)(2,1)} %refs_5_.1), custom_call_target="tpu_custom_call" | custom-call | bytes 2097152 | tf_op jit(solution)/shard_map/pallas_call | solution.py:632
  2.0 3.0 %collective-permute-start.1 = (bf16[256,1024]{1,0:T(8,128)(2,1)S(1)}, bf16[256,1024]{1,0:T(8,128)(2,1)S(1)}, u32[]{:S(2)}, u32[]{:S(2)}) collective-permute-start(bf16[256,1024]{1,0:T(8,128)(2,1)S(1)} %get-tuple-element.42), channel_id=1, source_target_pairs={{8,0},{9,1},{0,2},{1,3},{12,4},{13,5},{4,6},{5,7},{16,8},{17,9},{2... | collective-permute-start | bytes 1572872 | tf_op jit(solution)/shard_map/ppermute | solution.py:668
  5.1 1.9 %collective-permute-start.2 = (bf16[128,1024]{1,0:T(8,128)(2,1)S(1)}, bf16[128,1024]{1,0:T(8,128)(2,1)S(1)}, u32[]{:S(2)}, u32[]{:S(2)}) collective-permute-start(bf16[128,1024]{1,0:T(8,128)(2,1)S(1)} %copy-done.1), channel_id=1, source_target_pairs={{0,4},{4,0},{8,12},{12,8},{16,20},{20,16},{24,28},{28,24},{1,5},{5... | collective-permute-start | bytes 786440 | tf_op jit(solution)/shard_map/ppermute | solution.py:673
  7.2 0.7 %copy-done.4 = s32[8,8]{1,0:T(8,128)S(1)} copy-done((s32[8,8]{1,0:T(8,128)S(1)}, s32[8,8]{1,0:T(8,128)}, u32[]{:S(2)}) %copy-start.4) | copy-done | bytes 280
  7.9 2.4 %shard_map.85 = (f32[1024,128]{1,0:T(8,128)S(1)}, f32[8,128]{1,0:T(8,128)S(1)}, bf16[1024,128]{1,0:T(8,128)(2,1)S(1)}, f32[8,128]{1,0:T(8,128)S(1)}) custom-call(bf16[256,1024]{1,0:T(8,128)(2,1)S(1)} %get-tuple-element.40.refs_0_, s32[8,8]{1,0:T(8,128)S(1)} %copy-done.4, bf16[128,1024]{1,0:T(8,128)(2,1)S(1)} %copy-done, bf16[128,1024]{1,0:T(8,128)(2,1)S(1)} %copy-done.1, ...), custom_call_target="tpu_custom_call" | custom-call | flops 100663296 | bytes 1843200 | tf_op jit(solution)/shard_map/pallas_call | solution.py:632
  10.2 4.1 %collective-permute-done.2.refs_4_.refs_10_ = bf16[128,1024]{1,0:T(8,128)(2,1)S(1)} collective-permute-done((bf16[128,1024]{1,0:T(8,128)(2,1)S(1)}, bf16[128,1024]{1,0:T(8,128)(2,1)S(1)}, u32[]{:S(2)}, u32[]{:S(2)}) %collective-permute-start.2) | collective-permute-done | bytes 262176 | tf_op jit(solution)/shard_map/ppermute | solution.py:673
  14.4 4.2 %collective-permute-done.3.refs_5_.refs_11_ = bf16[128,1024]{1,0:T(8,128)(2,1)S(1)} collective-permute-done((bf16[128,1024]{1,0:T(8,128)(2,1)S(1)}, bf16[128,1024]{1,0:T(8,128)(2,1)S(1)}, u32[]{:S(2)}, u32[]{:S(2)}) %collective-permute-start.3) | collective-permute-done | bytes 262176 | tf_op jit(solution)/shard_map/ppermute | solution.py:673
  18.5 1.5 %shard_map.86 = (bf16[1056,128]{1,0:T(8,128)(2,1)S(1)}, bf16[1056,128]{1,0:T(8,128)(2,1)S(1)}, f32[1024,128]{1,0:T(8,128)S(1)}, f32[1024,128]{1,0:T(8,128)S(1)},...) custom-call(f32[8,128]{1,0:T(8,128)S(1)} %get-tuple-element.41.refs_0_, ...), custom_call_target="tpu_custom_call" | custom-call | flops 201326592 | bytes 4493312 | tf_op jit(solution)/shard_map/pallas_call | solution.py:632
  20.0 1.7 %collective-permute-start.4 = (bf16[1056,128]{1,0:T(8,128)(2,1)S(1)}, bf16[1056,128]{1,0:T(8,128)(2,1)S(1)}, u32[]{:S(2)}, u32[]{:S(2)}) collective-permute-start(bf16[1056,128]{1,0:T(8,128)(2,1)S(1)} %get-tuple-element.45.refs_1_), channel_id=1, source_target_pairs={{0,8},{1,9},{2,0},{3,1},{4,12},{5,13},{6,4},{7,5},{8,16},{9,17},{1... | collective-permute-start | bytes 811016 | tf_op jit(solution)/shard_map/ppermute | solution.py:668
  22.2 4.9 %collective-permute-done.4.refs_3_ = bf16[1056,128]{1,0:T(8,128)(2,1)S(1)} collective-permute-done((bf16[1056,128]{1,0:T(8,128)(2,1)S(1)}, bf16[1056,128]{1,0:T(8,128)(2,1)S(1)}, u32[]{:S(2)}, u32[]{:S(2)}) %collective-permute-start.4) | collective-permute-done | bytes 270368 | tf_op jit(solution)/shard_map/ppermute | solution.py:668
  27.1 1.1 %collective-permute-done.5.refs_4_ = bf16[1056,128]{1,0:T(8,128)(2,1)S(1)} collective-permute-done((bf16[1056,128]{1,0:T(8,128)(2,1)S(1)}, bf16[1056,128]{1,0:T(8,128)(2,1)S(1)}, u32[]{:S(2)}, u32[]{:S(2)}) %collective-permute-start.5) | collective-permute-done | bytes 270368 | tf_op jit(solution)/shard_map/ppermute | solution.py:668
  28.8 0.7 %collective-permute-start.7 = (f32[8,128]{1,0:T(8,128)S(1)}, f32[8,128]{1,0:T(8,128)S(1)}, u32[]{:S(2)}, u32[]{:S(2)}) collective-permute-start(f32[8,128]{1,0:T(8,128)S(1)} %get-tuple-element.49), channel_id=1, source_target_pairs={{0,2},{1,3},{2,0},{3,1},{4,6},{5,7},{6,4},{7,5},{8,10},{9,11},{10,... | collective-permute-start | bytes 12296 | tf_op jit(solution)/shard_map/ppermute | solution.py:727
  29.5 1.1 %collective-permute-start.6 = (f32[8,128]{1,0:T(8,128)S(1)}, f32[8,128]{1,0:T(8,128)S(1)}, u32[]{:S(2)}, u32[]{:S(2)}) collective-permute-start(f32[8,128]{1,0:T(8,128)S(1)} %get-tuple-element.49), channel_id=1, source_target_pairs={{0,1},{1,0},{2,3},{3,2},{4,5},{5,4},{6,7},{7,6},{8,9},{9,8},{10,11... | collective-permute-start | bytes 12296 | tf_op jit(solution)/shard_map/ppermute | solution.py:727
  30.7 1.2 %collective-permute-done.8 = f32[8,128]{1,0:T(8,128)S(1)} collective-permute-done((f32[8,128]{1,0:T(8,128)S(1)}, f32[8,128]{1,0:T(8,128)S(1)}, u32[]{:S(2)}, u32[]{:S(2)}) %collective-permute-start.8) | collective-permute-done | bytes 4128 | tf_op jit(solution)/shard_map/ppermute | solution.py:727
  31.8 0.7 %collective-permute-done.7 = f32[8,128]{1,0:T(8,128)S(1)} collective-permute-done((f32[8,128]{1,0:T(8,128)S(1)}, f32[8,128]{1,0:T(8,128)S(1)}, u32[]{:S(2)}, u32[]{:S(2)}) %collective-permute-start.7) | collective-permute-done | bytes 4128 | tf_op jit(solution)/shard_map/ppermute | solution.py:727
  32.5 1.3 %shard_map.89 = (bf16[128,1024]{1,0:T(8,128)(2,1)S(1)}, bf16[128,1024]{1,0:T(8,128)(2,1)S(1)}, bf16[128,1024]{1,0:T(8,128)(2,1)S(1)}, bf16[1024,128]{1,0:T(8,128...) custom-call(f32[8,128]{1,0:T(8,128)S(1)} %get-tuple-element.41.refs_, ...), custom_call_target="tpu_custom_call" | custom-call | flops 268435456 | bytes 6062080 | tf_op jit(solution)/shard_map/pallas_call | solution.py:632
  33.8 1.6 %collective-permute-start.9 = (bf16[128,1024]{1,0:T(8,128)(2,1)S(1)}, bf16[128,1024]{1,0:T(8,128)(2,1)S(1)}, u32[]{:S(2)}, u32[]{:S(2)}) collective-permute-start(bf16[128,1024]{1,0:T(8,128)(2,1)S(1)} %get-tuple-element.64), channel_id=1, source_target_pairs={{0,8},{1,9},{2,0},{3,1},{4,12},{5,13},{6,4},{7,5},{8,16},{9,17},{1... | collective-permute-start | bytes 786440 | tf_op jit(solution)/shard_map/ppermute | solution.py:668
  35.9 1.5 %collective-permute-start.11 = (bf16[128,1024]{1,0:T(8,128)(2,1)S(1)}, bf16[128,1024]{1,0:T(8,128)(2,1)S(1)}, u32[]{:S(2)}, u32[]{:S(2)}) collective-permute-start(bf16[128,1024]{1,0:T(8,128)(2,1)S(1)} %get-tuple-element.66), channel_id=1, source_target_pairs={{0,4},{4,0},{8,12},{12,8},{16,20},{20,16},{24,28},{28,24},{1,5},{5... | collective-permute-start | bytes 786440 | tf_op jit(solution)/shard_map/ppermute | solution.py:673
  37.8 3.6 %collective-permute-start.12 = (bf16[128,1024]{1,0:T(8,128)(2,1)S(1)}, bf16[128,1024]{1,0:T(8,128)(2,1)S(1)}, u32[]{:S(2)}, u32[]{:S(2)}) collective-permute-start(bf16[128,1024]{1,0:T(8,128)(2,1)S(1)} %get-tuple-element.72), channel_id=1, source_target_pairs={{0,24},{4,28},{8,0},{12,4},{16,8},{20,12},{24,16},{28,20},{1,25},{... | collective-permute-start | bytes 786440 | tf_op jit(solution)/shard_map/ppermute | solution.py:676
  41.4 0.5 %collective-permute-start.13 = (bf16[128,1024]{1,0:T(8,128)(2,1)S(1)}, bf16[128,1024]{1,0:T(8,128)(2,1)S(1)}, u32[]{:S(2)}, u32[]{:S(2)}) collective-permute-start(bf16[128,1024]{1,0:T(8,128)(2,1)S(1)} %get-tuple-element.73), channel_id=1, source_target_pairs={{0,4},{4,0},{8,12},{12,8},{16,20},{20,16},{24,28},{28,24},{1,5},{5... | collective-permute-start | bytes 786440 | tf_op jit(solution)/shard_map/ppermute | solution.py:673
  41.9 2.4 %shard_map.90 = (bf16[128,1024]{1,0:T(8,128)(2,1)}, f32[128,1024]{1,0:T(8,128)S(1)}, f32[128,1024]{1,0:T(8,128)S(1)}, f32[128,1024]{1,0:T(8,128)S(1)}) custom-call(f32[8,128]{1,0:T(8,128)S(1)} %add_add_fusion.refs_1_.refs_0_, bf16[128,1024]{1,0:T(8,128)(2,1)S(1)} %copy-done, bf16[128,1024]{1,0:T(8,128)(2,1)S(1)} %copy-done.1, ...), custom_call_target="tpu_custom_call" | custom-call | flops 234881024 | bytes 4993024 | tf_op jit(solution)/shard_map/pallas_call | solution.py:632
  44.7 1.0 %shard_map.91 = (bf16[128,1024]{1,0:T(8,128)(2,1)}, bf16[128,1024]{1,0:T(8,128)(2,1)}, f32[8,128]{1,0:T(8,128)S(1)}) custom-call(bf16[128,1024]{1,0:T(8,128)(2,1)S(1)} %collective-permute-done.9.refs_0_, bf16[128,1024]{1,0:T(8,128)(2,1)S(1)} %collective-permute-done.10.refs_1_, bf16[128,1024]{1,0:T(8,128)(2,1)S(1)} %collective-permute-done.11.refs_2_, ...), custom_call_target="tpu_custom_call" | custom-call | bytes 2363392 | tf_op jit(solution)/shard_map/pallas_call | solution.py:632
  45.7 2.7 %collective-permute-done.12.refs_1_ = bf16[128,1024]{1,0:T(8,128)(2,1)S(1)} collective-permute-done((bf16[128,1024]{1,0:T(8,128)(2,1)S(1)}, bf16[128,1024]{1,0:T(8,128)(2,1)S(1)}, u32[]{:S(2)}, u32[]{:S(2)}) %collective-permute-start.12) | collective-permute-done | bytes 262176 | tf_op jit(solution)/shard_map/ppermute | solution.py:676
  48.7 0.8 %shard_map.93 = bf16[128,1024]{1,0:T(8,128)(2,1)} custom-call(f32[8,128]{1,0:T(8,128)S(1)} %get-tuple-element.70.refs_0_, bf16[128,1024]{1,0:T(8,128)(2,1)S(1)} %collective-permute-done.12.refs_1_, bf16[128,1024]{1,0:T(8,128)(2,1)S(1)} %collective-permute-done.13.refs_2_, f32[128,1024]{1,0:T(8,128)S(1)} %get-tuple-element.74.refs_3_), custom_call_target="tpu_custom_call" | custom-call | bytes 1310720 | tf_op jit(solution)/shard_map/pallas_call | solution.py:632
  (25 shorter events, 2.8 us)
Async XLA Ops:
  0.6 6.5 %copy-start = (bf16[128,1024]{1,0:T(8,128)(2,1)S(1)}, bf16[128,1024]{1,0:T(8,128)(2,1)}, u32[]{:S(2)}) copy-start(bf16[128,1024]{1,0:T(8,128)(2,1)} %refs_0_.3) | copy-start | bytes 786436
  0.6 6.4 %copy-start.2 = (bf16[128,1024]{1,0:T(8,128)(2,1)S(1)}, bf16[128,1024]{1,0:T(8,128)(2,1)}, u32[]{:S(2)}) copy-start(bf16[128,1024]{1,0:T(8,128)(2,1)} %refs_3_.7) | copy-start | bytes 786436
  0.7 4.5 %copy-start.1 = (bf16[128,1024]{1,0:T(8,128)(2,1)S(1)}, bf16[128,1024]{1,0:T(8,128)(2,1)}, u32[]{:S(2)}) copy-start(bf16[128,1024]{1,0:T(8,128)(2,1)} %refs_2_.5) | copy-start | bytes 786436
  0.7 6.5 %copy-start.3 = (bf16[128,1024]{1,0:T(8,128)(2,1)S(1)}, bf16[128,1024]{1,0:T(8,128)(2,1)}, u32[]{:S(2)}) copy-start(bf16[128,1024]{1,0:T(8,128)(2,1)} %refs_5_.1) | copy-start | bytes 786436
  2.0 16.5 %collective-permute-start.1 = (bf16[256,1024]{1,0:T(8,128)(2,1)S(1)}, bf16[256,1024]{1,0:T(8,128)(2,1)S(1)}, u32[]{:S(2)}, u32[]{:S(2)}) collective-permute-start(bf16[256,1024]{1,0:T(8,128)(2,1)S(1)} %get-tuple-element.42), channel_id=1, source_target_pairs={{8,0},{9,1},{0,2},{1,3},{12,4},{13,5},{4,6},{5,7},{16,8},{17,9},{2... | collective-permute-start | bytes 1572872 | tf_op jit(solution)/shard_map/ppermute | solution.py:668
  5.0 13.5 %collective-permute-start = (bf16[256,1024]{1,0:T(8,128)(2,1)S(1)}, bf16[256,1024]{1,0:T(8,128)(2,1)S(1)}, u32[]{:S(2)}, u32[]{:S(2)}) collective-permute-start(bf16[256,1024]{1,0:T(8,128)(2,1)S(1)} %get-tuple-element.40.refs_0_), channel_id=1, source_target_pairs={{0,8},{1,9},{2,0},{3,1},{4,12},{5,13},{6,4},{7,5},{8,16},{9,17},{1... | collective-permute-start | bytes 1572872 | tf_op jit(solution)/shard_map/ppermute | solution.py:668
  5.1 9.2 %collective-permute-start.2 = (bf16[128,1024]{1,0:T(8,128)(2,1)S(1)}, bf16[128,1024]{1,0:T(8,128)(2,1)S(1)}, u32[]{:S(2)}, u32[]{:S(2)}) collective-permute-start(bf16[128,1024]{1,0:T(8,128)(2,1)S(1)} %copy-done.1), channel_id=1, source_target_pairs={{0,4},{4,0},{8,12},{12,8},{16,20},{20,16},{24,28},{28,24},{1,5},{5... | collective-permute-start | bytes 786440 | tf_op jit(solution)/shard_map/ppermute | solution.py:673
  7.0 11.5 %collective-permute-start.3 = (bf16[128,1024]{1,0:T(8,128)(2,1)S(1)}, bf16[128,1024]{1,0:T(8,128)(2,1)S(1)}, u32[]{:S(2)}, u32[]{:S(2)}) collective-permute-start(bf16[128,1024]{1,0:T(8,128)(2,1)S(1)} %copy-done.2), channel_id=1, source_target_pairs={{0,4},{4,0},{8,12},{12,8},{16,20},{20,16},{24,28},{28,24},{1,5},{5... | collective-permute-start | bytes 786440 | tf_op jit(solution)/shard_map/ppermute | solution.py:673
  7.2 0.7 %copy-start.4 = (s32[8,8]{1,0:T(8,128)S(1)}, s32[8,8]{1,0:T(8,128)}, u32[]{:S(2)}) copy-start(s32[8,8]{1,0:T(8,128)} %refs_1_.4) | copy-start | bytes 772
  20.0 7.1 %collective-permute-start.4 = (bf16[1056,128]{1,0:T(8,128)(2,1)S(1)}, bf16[1056,128]{1,0:T(8,128)(2,1)S(1)}, u32[]{:S(2)}, u32[]{:S(2)}) collective-permute-start(bf16[1056,128]{1,0:T(8,128)(2,1)S(1)} %get-tuple-element.45.refs_1_), channel_id=1, source_target_pairs={{0,8},{1,9},{2,0},{3,1},{4,12},{5,13},{6,4},{7,5},{8,16},{9,17},{1... | collective-permute-start | bytes 811016 | tf_op jit(solution)/shard_map/ppermute | solution.py:668
  21.8 6.5 %collective-permute-start.5 = (bf16[1056,128]{1,0:T(8,128)(2,1)S(1)}, bf16[1056,128]{1,0:T(8,128)(2,1)S(1)}, u32[]{:S(2)}, u32[]{:S(2)}) collective-permute-start(bf16[1056,128]{1,0:T(8,128)(2,1)S(1)} %get-tuple-element.46.refs_2_), channel_id=1, source_target_pairs={{8,0},{9,1},{0,2},{1,3},{12,4},{13,5},{4,6},{5,7},{16,8},{17,9},{2... | collective-permute-start | bytes 811016 | tf_op jit(solution)/shard_map/ppermute | solution.py:668
  28.7 3.1 %collective-permute-start.8 = (f32[8,128]{1,0:T(8,128)S(1)}, f32[8,128]{1,0:T(8,128)S(1)}, u32[]{:S(2)}, u32[]{:S(2)}) collective-permute-start(f32[8,128]{1,0:T(8,128)S(1)} %get-tuple-element.49), channel_id=1, source_target_pairs={{0,3},{1,2},{2,1},{3,0},{4,7},{5,6},{6,5},{7,4},{8,11},{9,10},{10,... | collective-permute-start | bytes 12296 | tf_op jit(solution)/shard_map/ppermute | solution.py:727
  28.8 3.7 %collective-permute-start.7 = (f32[8,128]{1,0:T(8,128)S(1)}, f32[8,128]{1,0:T(8,128)S(1)}, u32[]{:S(2)}, u32[]{:S(2)}) collective-permute-start(f32[8,128]{1,0:T(8,128)S(1)} %get-tuple-element.49), channel_id=1, source_target_pairs={{0,2},{1,3},{2,0},{3,1},{4,6},{5,7},{6,4},{7,5},{8,10},{9,11},{10,... | collective-permute-start | bytes 12296 | tf_op jit(solution)/shard_map/ppermute | solution.py:727
  29.5 3.0 %collective-permute-start.6 = (f32[8,128]{1,0:T(8,128)S(1)}, f32[8,128]{1,0:T(8,128)S(1)}, u32[]{:S(2)}, u32[]{:S(2)}) collective-permute-start(f32[8,128]{1,0:T(8,128)S(1)} %get-tuple-element.49), channel_id=1, source_target_pairs={{0,1},{1,0},{2,3},{3,2},{4,5},{5,4},{6,7},{7,6},{8,9},{9,8},{10,11... | collective-permute-start | bytes 12296 | tf_op jit(solution)/shard_map/ppermute | solution.py:727
  33.8 10.5 %collective-permute-start.9 = (bf16[128,1024]{1,0:T(8,128)(2,1)S(1)}, bf16[128,1024]{1,0:T(8,128)(2,1)S(1)}, u32[]{:S(2)}, u32[]{:S(2)}) collective-permute-start(bf16[128,1024]{1,0:T(8,128)(2,1)S(1)} %get-tuple-element.64), channel_id=1, source_target_pairs={{0,8},{1,9},{2,0},{3,1},{4,12},{5,13},{6,4},{7,5},{8,16},{9,17},{1... | collective-permute-start | bytes 786440 | tf_op jit(solution)/shard_map/ppermute | solution.py:668
  35.4 9.2 %collective-permute-start.10 = (bf16[128,1024]{1,0:T(8,128)(2,1)S(1)}, bf16[128,1024]{1,0:T(8,128)(2,1)S(1)}, u32[]{:S(2)}, u32[]{:S(2)}) collective-permute-start(bf16[128,1024]{1,0:T(8,128)(2,1)S(1)} %get-tuple-element.65), channel_id=1, source_target_pairs={{8,0},{9,1},{0,2},{1,3},{12,4},{13,5},{4,6},{5,7},{16,8},{17,9},{2... | collective-permute-start | bytes 786440 | tf_op jit(solution)/shard_map/ppermute | solution.py:668
  35.9 8.8 %collective-permute-start.11 = (bf16[128,1024]{1,0:T(8,128)(2,1)S(1)}, bf16[128,1024]{1,0:T(8,128)(2,1)S(1)}, u32[]{:S(2)}, u32[]{:S(2)}) collective-permute-start(bf16[128,1024]{1,0:T(8,128)(2,1)S(1)} %get-tuple-element.66), channel_id=1, source_target_pairs={{0,4},{4,0},{8,12},{12,8},{16,20},{20,16},{24,28},{28,24},{1,5},{5... | collective-permute-start | bytes 786440 | tf_op jit(solution)/shard_map/ppermute | solution.py:673
  37.8 10.7 %collective-permute-start.12 = (bf16[128,1024]{1,0:T(8,128)(2,1)S(1)}, bf16[128,1024]{1,0:T(8,128)(2,1)S(1)}, u32[]{:S(2)}, u32[]{:S(2)}) collective-permute-start(bf16[128,1024]{1,0:T(8,128)(2,1)S(1)} %get-tuple-element.72), channel_id=1, source_target_pairs={{0,24},{4,28},{8,0},{12,4},{16,8},{20,12},{24,16},{28,20},{1,25},{... | collective-permute-start | bytes 786440 | tf_op jit(solution)/shard_map/ppermute | solution.py:676
  41.4 7.3 %collective-permute-start.13 = (bf16[128,1024]{1,0:T(8,128)(2,1)S(1)}, bf16[128,1024]{1,0:T(8,128)(2,1)S(1)}, u32[]{:S(2)}, u32[]{:S(2)}) collective-permute-start(bf16[128,1024]{1,0:T(8,128)(2,1)S(1)} %get-tuple-element.73), channel_id=1, source_target_pairs={{0,4},{4,0},{8,12},{12,8},{16,20},{20,16},{24,28},{28,24},{1,5},{5... | collective-permute-start | bytes 786440 | tf_op jit(solution)/shard_map/ppermute | solution.py:673

commit v8 on v7

--- a/solution.py
+++ b/solution.py
@@ -345,7 +345,7 @@
     odd, half = place.odd, place.half
     near, far, side, local = (bias_ref[n : n + 1] for n in (NEAR, FAR, SIDE, LOCAL))
     before = lse_ref[...]
-    step = 2
+    step = heads
     z_rows, own_rows, z_tops, x_tops, n_tops = [], [], [], [], []
     for start in range(0, heads, step):
         group = range(start, start + step)
@@ -355,13 +355,9 @@
             up_a, down_a = up_ref[FIRST, at], down_ref[FIRST, at]
             k2, qz = jnp.where(half, down_a, up_a), jnp.where(half, up_a, down_a)
             q = q_ref[:, at]
-            scores.append(
-                (
-                    score_tile(k2, qz) + far,
-                    score_tile(kx_ref[:, at], jnp.where(odd, q, qz)) + side,
-                    score_tile(k2, q) + near,
-                )
-            )
+            both = score_tile(k2, jnp.concatenate([qz, q], axis=0))
+            x = score_tile(kx_ref[:, at], jnp.where(odd, q, qz))
+            scores.append((both[:, :BLOCK] + far, x + side, both[:, BLOCK:] + near))
         for h, (z, x, n) in zip(group, scores):
             z_top, x_top, n_top = (tile.max(axis=0, keepdims=True) for tile in (z, x, n))
             both = jnp.maximum(z_top, x_top)
@@ -372,25 +368,25 @@
             z_sum, x_sum, n_sum = (tile.sum(axis=0, keepdims=True) for tile in (z, x, n))
             z_sum = z_sum + jnp.where(odd, 0.0, x_sum)
             x_sum = jnp.maximum(x_sum, 1.0)
-            for kept, top in ((z_tops, z_top), (x_tops, x_top), (n_tops, n_top)):
-                kept.append(top)
+            for tops, top in ((z_tops, z_top), (x_tops, x_top), (n_tops, n_top)):
+                tops.append(top)
             z_rows.append(z_top + jnp.log(z_sum))
             parts = (before[h : h + 1], n_top + jnp.log(n_sum) + near, x_top + jnp.log(x_sum) + local)
             highest = functools.reduce(jnp.maximum, parts)
             total = highest + jnp.log(functools.reduce(jnp.add, [jnp.exp(part - highest) for part in parts]))
             own_rows.append(total)
             d_share, n_share, x_share = (jnp.exp(part - total) for part in parts)
-            xb = x.astype(jnp.bfloat16)
-            joined = jnp.concatenate([z.astype(jnp.bfloat16), jnp.where(odd, jnp.zeros_like(xb), xb)], axis=0)
-            weights.append(
-                (joined, xb, n.astype(jnp.bfloat16), 1.0 / z_sum, d_share, n_share / n_sum, x_share / x_sum)
-            )
-        for h, (joined, xb, nb, z_scale, d_share, n_share, x_share) in zip(group, weights):
+            z_scale = 1.0 / z_sum
+            sent = [z * z_scale, x * jnp.where(odd, 0.0, z_scale)]
+            kept = [n * (n_share / n_sum), x * (x_share / x_sum)]
+            joined = [jnp.concatenate(tiles, axis=0).astype(jnp.bfloat16) for tiles in (sent, kept)]
+            weights.append((jnp.concatenate(joined, axis=1), d_share))
+        for h, (joined, d_share) in zip(group, weights):
             at = rows_of(h)
-            v2, vx = jnp.where(half, down_ref[SECOND, at], up_ref[SECOND, at]), vx_ref[:, at]
-            out_z = mm(jnp.concatenate([v2, vx], axis=0), joined, TN) * z_scale
-            own = out_ref[at] * d_share + mm(v2, nb, TN) * n_share + mm(vx, xb, TN) * x_share
-            out_z, own = out_z.astype(jnp.bfloat16), own.astype(jnp.bfloat16)
+            v2 = jnp.where(half, down_ref[SECOND, at], up_ref[SECOND, at])
+            out = mm(jnp.concatenate([v2, vx_ref[:, at]], axis=0), joined, TN)
+            out_z = out[:, :BLOCK].astype(jnp.bfloat16)
+            own = (out_ref[at] * d_share + out[:, BLOCK:]).astype(jnp.bfloat16)
             up_out_ref[at] = jnp.where(half, own, out_z)
             down_out_ref[at] = jnp.where(half, out_z, own)
     tail = slice(heads * HD, heads * HD + TAIL)
@@ -513,7 +509,7 @@
         jnp.exp(mx_ref[...] - jnp.where(odd, lse, z_lse) + bias_ref[SIDE : SIDE + 1]),
     )
     deltas = []
-    step = 2
+    step = heads
     for start in range(0, heads, step):
         group = range(start, start + step)
         parts, products, scores = [], [], []

time: 49.7 us -> 49.2 us (0.990)
  Pallas kernels: 11.8 us -> 11.3 us
    pallas_call x10, Pallas kernels: 11.8 us -> 11.3 us  [call(): pl.pallas_call(lambda *refs: kernel(heads, *refs[len(after):]), out_shape...]
where the time goes in v8:
time: 49.2 us; the launch traced here: 49 us
  waiting for transfers between devices  19.4 us (39%)
  starting transfers between devices  16.9 us (34%)
  Pallas kernels  11.3 us (23%)
  between operations  0.73 us (1%)
  local copies, waits for them, and re-layouts  0.7 us (1%)
    pallas_call x10, Pallas kernels, call(): pl.pallas_call(lambda *refs: kernel(heads, *refs[len(after):]), out_shape...  11.3 us
    ppermute x4, waiting for transfers between devices, swap(): return lax.ppermute(array, 'ctx', [(i, i ^ 1) for i in range(blocks)])  8.52 us
    ppermute x3, waiting for transfers between devices, cycle(): lax.ppermute(up_array, ('ctx', 'head'), rising)  4.88 us
    ppermute x4, starting transfers between devices, swap(): return lax.ppermute(array, 'ctx', [(i, i ^ 1) for i in range(blocks)])  4.05 us
    ppermute x3, starting transfers between devices, cycle(): lax.ppermute(down_array, ('ctx', 'head'), falling)  3.82 us
    ppermute x1, starting transfers between devices, ring(): lax.ppermute(array, 'ctx', [(i, (i + distance) % blocks) for i in range(b...  3.61 us
    ppermute x3, starting transfers between devices, cycle(): lax.ppermute(up_array, ('ctx', 'head'), rising)  3.48 us
    ppermute x1, waiting for transfers between devices, ring(): lax.ppermute(array, 'ctx', [(i, (i + distance) % blocks) for i in range(b...  2.72 us
  transfers between devices with their start and end apart: 14, of which 9 were waited for; matrix products, arithmetic and copies ran while one was open for 0% of the time, Pallas kernels for 13%

profile of v8, /device:TPU:0, one launch (start us, length us, event | category | flops | bytes accessed | tf_op | source)
XLA Modules:
  0.0 49.0 jit_solution(2269187363525785819)
XLA Ops:
  0.7 1.3 %shard_map.84 = (bf16[256,1024]{1,0:T(8,128)(2,1)S(1)}, bf16[256,1024]{1,0:T(8,128)(2,1)S(1)}) custom-call(bf16[128,1024]{1,0:T(8,128)(2,1)} %refs_0_.3, bf16[128,1024]{1,0:T(8,128)(2,1)} %refs_2_.5, bf16[128,1024]{1,0:T(8,128)(2,1)} %refs_3_.7, bf16[128,1024]{1,0:T(8,128)(2,1)} %refs_5_.1), custom_call_target="tpu_custom_call" | custom-call | bytes 2097152 | tf_op jit(solution)/shard_map/pallas_call | solution.py:628
  2.0 3.0 %collective-permute-start.1 = (bf16[256,1024]{1,0:T(8,128)(2,1)S(1)}, bf16[256,1024]{1,0:T(8,128)(2,1)S(1)}, u32[]{:S(2)}, u32[]{:S(2)}) collective-permute-start(bf16[256,1024]{1,0:T(8,128)(2,1)S(1)} %get-tuple-element.42), channel_id=1, source_target_pairs={{8,0},{9,1},{0,2},{1,3},{12,4},{13,5},{4,6},{5,7},{16,8},{17,9},{2... | collective-permute-start | bytes 1572872 | tf_op jit(solution)/shard_map/ppermute | solution.py:664
  5.1 1.9 %collective-permute-start.2 = (bf16[128,1024]{1,0:T(8,128)(2,1)S(1)}, bf16[128,1024]{1,0:T(8,128)(2,1)S(1)}, u32[]{:S(2)}, u32[]{:S(2)}) collective-permute-start(bf16[128,1024]{1,0:T(8,128)(2,1)S(1)} %copy-done.1), channel_id=1, source_target_pairs={{0,4},{4,0},{8,12},{12,8},{16,20},{20,16},{24,28},{28,24},{1,5},{5... | collective-permute-start | bytes 786440 | tf_op jit(solution)/shard_map/ppermute | solution.py:669
  7.2 0.7 %copy-done.4 = s32[8,8]{1,0:T(8,128)S(1)} copy-done((s32[8,8]{1,0:T(8,128)S(1)}, s32[8,8]{1,0:T(8,128)}, u32[]{:S(2)}) %copy-start.4) | copy-done | bytes 280
  7.9 2.4 %shard_map.85 = (f32[1024,128]{1,0:T(8,128)S(1)}, f32[8,128]{1,0:T(8,128)S(1)}, bf16[1024,128]{1,0:T(8,128)(2,1)S(1)}, f32[8,128]{1,0:T(8,128)S(1)}) custom-call(bf16[256,1024]{1,0:T(8,128)(2,1)S(1)} %get-tuple-element.40.refs_0_, s32[8,8]{1,0:T(8,128)S(1)} %copy-done.4, bf16[128,1024]{1,0:T(8,128)(2,1)S(1)} %copy-done, bf16[128,1024]{1,0:T(8,128)(2,1)S(1)} %copy-done.1, ...), custom_call_target="tpu_custom_call" | custom-call | flops 100663296 | bytes 1843200 | tf_op jit(solution)/shard_map/pallas_call | solution.py:628
  10.2 4.1 %collective-permute-done.2.refs_4_.refs_10_ = bf16[128,1024]{1,0:T(8,128)(2,1)S(1)} collective-permute-done((bf16[128,1024]{1,0:T(8,128)(2,1)S(1)}, bf16[128,1024]{1,0:T(8,128)(2,1)S(1)}, u32[]{:S(2)}, u32[]{:S(2)}) %collective-permute-start.2) | collective-permute-done | bytes 262176 | tf_op jit(solution)/shard_map/ppermute | solution.py:669
  14.4 4.2 %collective-permute-done.3.refs_5_.refs_11_ = bf16[128,1024]{1,0:T(8,128)(2,1)S(1)} collective-permute-done((bf16[128,1024]{1,0:T(8,128)(2,1)S(1)}, bf16[128,1024]{1,0:T(8,128)(2,1)S(1)}, u32[]{:S(2)}, u32[]{:S(2)}) %collective-permute-start.3) | collective-permute-done | bytes 262176 | tf_op jit(solution)/shard_map/ppermute | solution.py:669
  18.5 1.1 %shard_map.86 = (bf16[1056,128]{1,0:T(8,128)(2,1)S(1)}, bf16[1056,128]{1,0:T(8,128)(2,1)S(1)}, f32[1024,128]{1,0:T(8,128)S(1)}, f32[1024,128]{1,0:T(8,128)S(1)},...) custom-call(f32[8,128]{1,0:T(8,128)S(1)} %get-tuple-element.41.refs_0_, ...), custom_call_target="tpu_custom_call" | custom-call | flops 201326592 | bytes 4493312 | tf_op jit(solution)/shard_map/pallas_call | solution.py:628
  19.7 1.7 %collective-permute-start.4 = (bf16[1056,128]{1,0:T(8,128)(2,1)S(1)}, bf16[1056,128]{1,0:T(8,128)(2,1)S(1)}, u32[]{:S(2)}, u32[]{:S(2)}) collective-permute-start(bf16[1056,128]{1,0:T(8,128)(2,1)S(1)} %get-tuple-element.45.refs_1_), channel_id=1, source_target_pairs={{0,8},{1,9},{2,0},{3,1},{4,12},{5,13},{6,4},{7,5},{8,16},{9,17},{1... | collective-permute-start | bytes 811016 | tf_op jit(solution)/shard_map/ppermute | solution.py:664
  21.9 4.9 %collective-permute-done.4.refs_3_ = bf16[1056,128]{1,0:T(8,128)(2,1)S(1)} collective-permute-done((bf16[1056,128]{1,0:T(8,128)(2,1)S(1)}, bf16[1056,128]{1,0:T(8,128)(2,1)S(1)}, u32[]{:S(2)}, u32[]{:S(2)}) %collective-permute-start.4) | collective-permute-done | bytes 270368 | tf_op jit(solution)/shard_map/ppermute | solution.py:664
  26.7 1.1 %collective-permute-done.5.refs_4_ = bf16[1056,128]{1,0:T(8,128)(2,1)S(1)} collective-permute-done((bf16[1056,128]{1,0:T(8,128)(2,1)S(1)}, bf16[1056,128]{1,0:T(8,128)(2,1)S(1)}, u32[]{:S(2)}, u32[]{:S(2)}) %collective-permute-start.5) | collective-permute-done | bytes 270368 | tf_op jit(solution)/shard_map/ppermute | solution.py:664
  28.4 0.7 %collective-permute-start.7 = (f32[8,128]{1,0:T(8,128)S(1)}, f32[8,128]{1,0:T(8,128)S(1)}, u32[]{:S(2)}, u32[]{:S(2)}) collective-permute-start(f32[8,128]{1,0:T(8,128)S(1)} %get-tuple-element.49), channel_id=1, source_target_pairs={{0,2},{1,3},{2,0},{3,1},{4,6},{5,7},{6,4},{7,5},{8,10},{9,11},{10,... | collective-permute-start | bytes 12296 | tf_op jit(solution)/shard_map/ppermute | solution.py:723
  29.1 1.1 %collective-permute-start.6 = (f32[8,128]{1,0:T(8,128)S(1)}, f32[8,128]{1,0:T(8,128)S(1)}, u32[]{:S(2)}, u32[]{:S(2)}) collective-permute-start(f32[8,128]{1,0:T(8,128)S(1)} %get-tuple-element.49), channel_id=1, source_target_pairs={{0,1},{1,0},{2,3},{3,2},{4,5},{5,4},{6,7},{7,6},{8,9},{9,8},{10,11... | collective-permute-start | bytes 12296 | tf_op jit(solution)/shard_map/ppermute | solution.py:723
  30.3 1.2 %collective-permute-done.8 = f32[8,128]{1,0:T(8,128)S(1)} collective-permute-done((f32[8,128]{1,0:T(8,128)S(1)}, f32[8,128]{1,0:T(8,128)S(1)}, u32[]{:S(2)}, u32[]{:S(2)}) %collective-permute-start.8) | collective-permute-done | bytes 4128 | tf_op jit(solution)/shard_map/ppermute | solution.py:723
  31.5 0.7 %collective-permute-done.7 = f32[8,128]{1,0:T(8,128)S(1)} collective-permute-done((f32[8,128]{1,0:T(8,128)S(1)}, f32[8,128]{1,0:T(8,128)S(1)}, u32[]{:S(2)}, u32[]{:S(2)}) %collective-permute-start.7) | collective-permute-done | bytes 4128 | tf_op jit(solution)/shard_map/ppermute | solution.py:723
  32.1 1.1 %shard_map.89 = (bf16[128,1024]{1,0:T(8,128)(2,1)S(1)}, bf16[128,1024]{1,0:T(8,128)(2,1)S(1)}, bf16[128,1024]{1,0:T(8,128)(2,1)S(1)}, bf16[1024,128]{1,0:T(8,128...) custom-call(f32[8,128]{1,0:T(8,128)S(1)} %get-tuple-element.41.refs_, ...), custom_call_target="tpu_custom_call" | custom-call | flops 268435456 | bytes 6062080 | tf_op jit(solution)/shard_map/pallas_call | solution.py:628
  33.3 1.6 %collective-permute-start.9 = (bf16[128,1024]{1,0:T(8,128)(2,1)S(1)}, bf16[128,1024]{1,0:T(8,128)(2,1)S(1)}, u32[]{:S(2)}, u32[]{:S(2)}) collective-permute-start(bf16[128,1024]{1,0:T(8,128)(2,1)S(1)} %get-tuple-element.64), channel_id=1, source_target_pairs={{0,8},{1,9},{2,0},{3,1},{4,12},{5,13},{6,4},{7,5},{8,16},{9,17},{1... | collective-permute-start | bytes 786440 | tf_op jit(solution)/shard_map/ppermute | solution.py:664
  35.3 1.5 %collective-permute-start.11 = (bf16[128,1024]{1,0:T(8,128)(2,1)S(1)}, bf16[128,1024]{1,0:T(8,128)(2,1)S(1)}, u32[]{:S(2)}, u32[]{:S(2)}) collective-permute-start(bf16[128,1024]{1,0:T(8,128)(2,1)S(1)} %get-tuple-element.66), channel_id=1, source_target_pairs={{0,4},{4,0},{8,12},{12,8},{16,20},{20,16},{24,28},{28,24},{1,5},{5... | collective-permute-start | bytes 786440 | tf_op jit(solution)/shard_map/ppermute | solution.py:669
  37.2 3.6 %collective-permute-start.12 = (bf16[128,1024]{1,0:T(8,128)(2,1)S(1)}, bf16[128,1024]{1,0:T(8,128)(2,1)S(1)}, u32[]{:S(2)}, u32[]{:S(2)}) collective-permute-start(bf16[128,1024]{1,0:T(8,128)(2,1)S(1)} %get-tuple-element.72), channel_id=1, source_target_pairs={{0,24},{4,28},{8,0},{12,4},{16,8},{20,12},{24,16},{28,20},{1,25},{... | collective-permute-start | bytes 786440 | tf_op jit(solution)/shard_map/ppermute | solution.py:672
  40.8 0.5 %collective-permute-start.13 = (bf16[128,1024]{1,0:T(8,128)(2,1)S(1)}, bf16[128,1024]{1,0:T(8,128)(2,1)S(1)}, u32[]{:S(2)}, u32[]{:S(2)}) collective-permute-start(bf16[128,1024]{1,0:T(8,128)(2,1)S(1)} %get-tuple-element.73), channel_id=1, source_target_pairs={{0,4},{4,0},{8,12},{12,8},{16,20},{20,16},{24,28},{28,24},{1,5},{5... | collective-permute-start | bytes 786440 | tf_op jit(solution)/shard_map/ppermute | solution.py:669
  41.4 2.4 %shard_map.90 = (bf16[128,1024]{1,0:T(8,128)(2,1)}, f32[128,1024]{1,0:T(8,128)S(1)}, f32[128,1024]{1,0:T(8,128)S(1)}, f32[128,1024]{1,0:T(8,128)S(1)}) custom-call(f32[8,128]{1,0:T(8,128)S(1)} %add_add_fusion.refs_1_.refs_0_, bf16[128,1024]{1,0:T(8,128)(2,1)S(1)} %copy-done, bf16[128,1024]{1,0:T(8,128)(2,1)S(1)} %copy-done.1, ...), custom_call_target="tpu_custom_call" | custom-call | flops 234881024 | bytes 4993024 | tf_op jit(solution)/shard_map/pallas_call | solution.py:628
  44.1 1.0 %shard_map.91 = (bf16[128,1024]{1,0:T(8,128)(2,1)}, bf16[128,1024]{1,0:T(8,128)(2,1)}, f32[8,128]{1,0:T(8,128)S(1)}) custom-call(bf16[128,1024]{1,0:T(8,128)(2,1)S(1)} %collective-permute-done.9.refs_0_, bf16[128,1024]{1,0:T(8,128)(2,1)S(1)} %collective-permute-done.10.refs_1_, bf16[128,1024]{1,0:T(8,128)(2,1)S(1)} %collective-permute-done.11.refs_2_, ...), custom_call_target="tpu_custom_call" | custom-call | bytes 2363392 | tf_op jit(solution)/shard_map/pallas_call | solution.py:628
  45.2 2.7 %collective-permute-done.12.refs_1_ = bf16[128,1024]{1,0:T(8,128)(2,1)S(1)} collective-permute-done((bf16[128,1024]{1,0:T(8,128)(2,1)S(1)}, bf16[128,1024]{1,0:T(8,128)(2,1)S(1)}, u32[]{:S(2)}, u32[]{:S(2)}) %collective-permute-start.12) | collective-permute-done | bytes 262176 | tf_op jit(solution)/shard_map/ppermute | solution.py:672
  48.1 0.8 %shard_map.93 = bf16[128,1024]{1,0:T(8,128)(2,1)} custom-call(f32[8,128]{1,0:T(8,128)S(1)} %get-tuple-element.70.refs_0_, bf16[128,1024]{1,0:T(8,128)(2,1)S(1)} %collective-permute-done.12.refs_1_, bf16[128,1024]{1,0:T(8,128)(2,1)S(1)} %collective-permute-done.13.refs_2_, f32[128,1024]{1,0:T(8,128)S(1)} %get-tuple-element.74.refs_3_), custom_call_target="tpu_custom_call" | custom-call | bytes 1310720 | tf_op jit(solution)/shard_map/pallas_call | solution.py:628
  (25 shorter events, 2.8 us)
Async XLA Ops:
  0.6 6.5 %copy-start = (bf16[128,1024]{1,0:T(8,128)(2,1)S(1)}, bf16[128,1024]{1,0:T(8,128)(2,1)}, u32[]{:S(2)}) copy-start(bf16[128,1024]{1,0:T(8,128)(2,1)} %refs_0_.3) | copy-start | bytes 786436
  0.6 6.4 %copy-start.2 = (bf16[128,1024]{1,0:T(8,128)(2,1)S(1)}, bf16[128,1024]{1,0:T(8,128)(2,1)}, u32[]{:S(2)}) copy-start(bf16[128,1024]{1,0:T(8,128)(2,1)} %refs_3_.7) | copy-start | bytes 786436
  0.7 4.5 %copy-start.1 = (bf16[128,1024]{1,0:T(8,128)(2,1)S(1)}, bf16[128,1024]{1,0:T(8,128)(2,1)}, u32[]{:S(2)}) copy-start(bf16[128,1024]{1,0:T(8,128)(2,1)} %refs_2_.5) | copy-start | bytes 786436
  0.7 6.5 %copy-start.3 = (bf16[128,1024]{1,0:T(8,128)(2,1)S(1)}, bf16[128,1024]{1,0:T(8,128)(2,1)}, u32[]{:S(2)}) copy-start(bf16[128,1024]{1,0:T(8,128)(2,1)} %refs_5_.1) | copy-start | bytes 786436
  2.0 16.5 %collective-permute-start.1 = (bf16[256,1024]{1,0:T(8,128)(2,1)S(1)}, bf16[256,1024]{1,0:T(8,128)(2,1)S(1)}, u32[]{:S(2)}, u32[]{:S(2)}) collective-permute-start(bf16[256,1024]{1,0:T(8,128)(2,1)S(1)} %get-tuple-element.42), channel_id=1, source_target_pairs={{8,0},{9,1},{0,2},{1,3},{12,4},{13,5},{4,6},{5,7},{16,8},{17,9},{2... | collective-permute-start | bytes 1572872 | tf_op jit(solution)/shard_map/ppermute | solution.py:664
  5.0 13.5 %collective-permute-start = (bf16[256,1024]{1,0:T(8,128)(2,1)S(1)}, bf16[256,1024]{1,0:T(8,128)(2,1)S(1)}, u32[]{:S(2)}, u32[]{:S(2)}) collective-permute-start(bf16[256,1024]{1,0:T(8,128)(2,1)S(1)} %get-tuple-element.40.refs_0_), channel_id=1, source_target_pairs={{0,8},{1,9},{2,0},{3,1},{4,12},{5,13},{6,4},{7,5},{8,16},{9,17},{1... | collective-permute-start | bytes 1572872 | tf_op jit(solution)/shard_map/ppermute | solution.py:664
  5.1 9.2 %collective-permute-start.2 = (bf16[128,1024]{1,0:T(8,128)(2,1)S(1)}, bf16[128,1024]{1,0:T(8,128)(2,1)S(1)}, u32[]{:S(2)}, u32[]{:S(2)}) collective-permute-start(bf16[128,1024]{1,0:T(8,128)(2,1)S(1)} %copy-done.1), channel_id=1, source_target_pairs={{0,4},{4,0},{8,12},{12,8},{16,20},{20,16},{24,28},{28,24},{1,5},{5... | collective-permute-start | bytes 786440 | tf_op jit(solution)/shard_map/ppermute | solution.py:669
  7.0 11.5 %collective-permute-start.3 = (bf16[128,1024]{1,0:T(8,128)(2,1)S(1)}, bf16[128,1024]{1,0:T(8,128)(2,1)S(1)}, u32[]{:S(2)}, u32[]{:S(2)}) collective-permute-start(bf16[128,1024]{1,0:T(8,128)(2,1)S(1)} %copy-done.2), channel_id=1, source_target_pairs={{0,4},{4,0},{8,12},{12,8},{16,20},{20,16},{24,28},{28,24},{1,5},{5... | collective-permute-start | bytes 786440 | tf_op jit(solution)/shard_map/ppermute | solution.py:669
  7.2 0.7 %copy-start.4 = (s32[8,8]{1,0:T(8,128)S(1)}, s32[8,8]{1,0:T(8,128)}, u32[]{:S(2)}) copy-start(s32[8,8]{1,0:T(8,128)} %refs_1_.4) | copy-start | bytes 772
  19.7 7.1 %collective-permute-start.4 = (bf16[1056,128]{1,0:T(8,128)(2,1)S(1)}, bf16[1056,128]{1,0:T(8,128)(2,1)S(1)}, u32[]{:S(2)}, u32[]{:S(2)}) collective-permute-start(bf16[1056,128]{1,0:T(8,128)(2,1)S(1)} %get-tuple-element.45.refs_1_), channel_id=1, source_target_pairs={{0,8},{1,9},{2,0},{3,1},{4,12},{5,13},{6,4},{7,5},{8,16},{9,17},{1... | collective-permute-start | bytes 811016 | tf_op jit(solution)/shard_map/ppermute | solution.py:664
  21.4 6.5 %collective-permute-start.5 = (bf16[1056,128]{1,0:T(8,128)(2,1)S(1)}, bf16[1056,128]{1,0:T(8,128)(2,1)S(1)}, u32[]{:S(2)}, u32[]{:S(2)}) collective-permute-start(bf16[1056,128]{1,0:T(8,128)(2,1)S(1)} %get-tuple-element.46.refs_2_), channel_id=1, source_target_pairs={{8,0},{9,1},{0,2},{1,3},{12,4},{13,5},{4,6},{5,7},{16,8},{17,9},{2... | collective-permute-start | bytes 811016 | tf_op jit(solution)/shard_map/ppermute | solution.py:664
  28.4 3.1 %collective-permute-start.8 = (f32[8,128]{1,0:T(8,128)S(1)}, f32[8,128]{1,0:T(8,128)S(1)}, u32[]{:S(2)}, u32[]{:S(2)}) collective-permute-start(f32[8,128]{1,0:T(8,128)S(1)} %get-tuple-element.49), channel_id=1, source_target_pairs={{0,3},{1,2},{2,1},{3,0},{4,7},{5,6},{6,5},{7,4},{8,11},{9,10},{10,... | collective-permute-start | bytes 12296 | tf_op jit(solution)/shard_map/ppermute | solution.py:723
  28.4 3.7 %collective-permute-start.7 = (f32[8,128]{1,0:T(8,128)S(1)}, f32[8,128]{1,0:T(8,128)S(1)}, u32[]{:S(2)}, u32[]{:S(2)}) collective-permute-start(f32[8,128]{1,0:T(8,128)S(1)} %get-tuple-element.49), channel_id=1, source_target_pairs={{0,2},{1,3},{2,0},{3,1},{4,6},{5,7},{6,4},{7,5},{8,10},{9,11},{10,... | collective-permute-start | bytes 12296 | tf_op jit(solution)/shard_map/ppermute | solution.py:723
  29.1 3.0 %collective-permute-start.6 = (f32[8,128]{1,0:T(8,128)S(1)}, f32[8,128]{1,0:T(8,128)S(1)}, u32[]{:S(2)}, u32[]{:S(2)}) collective-permute-start(f32[8,128]{1,0:T(8,128)S(1)} %get-tuple-element.49), channel_id=1, source_target_pairs={{0,1},{1,0},{2,3},{3,2},{4,5},{5,4},{6,7},{7,6},{8,9},{9,8},{10,11... | collective-permute-start | bytes 12296 | tf_op jit(solution)/shard_map/ppermute | solution.py:723
  33.3 10.5 %collective-permute-start.9 = (bf16[128,1024]{1,0:T(8,128)(2,1)S(1)}, bf16[128,1024]{1,0:T(8,128)(2,1)S(1)}, u32[]{:S(2)}, u32[]{:S(2)}) collective-permute-start(bf16[128,1024]{1,0:T(8,128)(2,1)S(1)} %get-tuple-element.64), channel_id=1, source_target_pairs={{0,8},{1,9},{2,0},{3,1},{4,12},{5,13},{6,4},{7,5},{8,16},{9,17},{1... | collective-permute-start | bytes 786440 | tf_op jit(solution)/shard_map/ppermute | solution.py:664
  34.9 9.2 %collective-permute-start.10 = (bf16[128,1024]{1,0:T(8,128)(2,1)S(1)}, bf16[128,1024]{1,0:T(8,128)(2,1)S(1)}, u32[]{:S(2)}, u32[]{:S(2)}) collective-permute-start(bf16[128,1024]{1,0:T(8,128)(2,1)S(1)} %get-tuple-element.65), channel_id=1, source_target_pairs={{8,0},{9,1},{0,2},{1,3},{12,4},{13,5},{4,6},{5,7},{16,8},{17,9},{2... | collective-permute-start | bytes 786440 | tf_op jit(solution)/shard_map/ppermute | solution.py:664
  35.3 8.8 %collective-permute-start.11 = (bf16[128,1024]{1,0:T(8,128)(2,1)S(1)}, bf16[128,1024]{1,0:T(8,128)(2,1)S(1)}, u32[]{:S(2)}, u32[]{:S(2)}) collective-permute-start(bf16[128,1024]{1,0:T(8,128)(2,1)S(1)} %get-tuple-element.66), channel_id=1, source_target_pairs={{0,4},{4,0},{8,12},{12,8},{16,20},{20,16},{24,28},{28,24},{1,5},{5... | collective-permute-start | bytes 786440 | tf_op jit(solution)/shard_map/ppermute | solution.py:669
  37.2 10.7 %collective-permute-start.12 = (bf16[128,1024]{1,0:T(8,128)(2,1)S(1)}, bf16[128,1024]{1,0:T(8,128)(2,1)S(1)}, u32[]{:S(2)}, u32[]{:S(2)}) collective-permute-start(bf16[128,1024]{1,0:T(8,128)(2,1)S(1)} %get-tuple-element.72), channel_id=1, source_target_pairs={{0,24},{4,28},{8,0},{12,4},{16,8},{20,12},{24,16},{28,20},{1,25},{... | collective-permute-start | bytes 786440 | tf_op jit(solution)/shard_map/ppermute | solution.py:672
  40.8 7.3 %collective-permute-start.13 = (bf16[128,1024]{1,0:T(8,128)(2,1)S(1)}, bf16[128,1024]{1,0:T(8,128)(2,1)S(1)}, u32[]{:S(2)}, u32[]{:S(2)}) collective-permute-start(bf16[128,1024]{1,0:T(8,128)(2,1)S(1)} %get-tuple-element.73), channel_id=1, source_target_pairs={{0,4},{4,0},{8,12},{12,8},{16,20},{20,16},{24,28},{28,24},{1,5},{5... | collective-permute-start | bytes 786440 | tf_op jit(solution)/shard_map/ppermute | solution.py:669

commit v9 on v8

--- a/solution.py
+++ b/solution.py
@@ -198,7 +198,7 @@
 TAIL = 32
 
 
-NEAR, FAR, SIDE, HELPED, LOCAL = range(5)
+NEAR, FAR, SIDE, HELPED, LOCAL, KEY_NEAR, KEY_FAR, KEY_SIDE = range(8)
 
 
 class Place:
@@ -217,12 +217,20 @@
     ahead_side = jnp.logical_and(has_ahead, pattern_ref[ahead, 0] >= 0)
     own_side = pattern_ref[me, 0] >= 0
     local = jnp.logical_and(odd, own_side)
+
+    def ahead_holds(distance, level):
+        entry = pattern_ref[jnp.minimum(me + distance, blocks - 1), level]
+        return jnp.logical_and(me + distance < blocks, entry >= 0)
+
     held = {
         NEAR: pattern_ref[me, 1] >= 0,
         FAR: jnp.logical_and(has_ahead, pattern_ref[ahead, 2] >= 0),
         SIDE: jnp.logical_or(local, jnp.logical_and(even, ahead_side)),
         HELPED: jnp.logical_or(pattern_ref[me, 2] >= 0, jnp.logical_and(even, own_side)),
         LOCAL: local,
+        KEY_NEAR: ahead_holds(2, 1),
+        KEY_FAR: ahead_holds(4, 2),
+        KEY_SIDE: ahead_holds(1, 0),
     }
     row = lax.broadcasted_iota(jnp.int32, (8, BLOCK), 0)
     rows = jnp.zeros((8, BLOCK), jnp.float32)
@@ -438,7 +446,7 @@
         total = highest + jnp.log(jnp.exp(first - highest) + jnp.exp(second - highest))
         rows.append(total)
         shares.append((jnp.exp(first - total), jnp.exp(second - total)))
-    lse_ref[...], lsez_ref[...] = rows
+    lse_ref[...], lsez_ref[...] = (jnp.maximum(total, -1e9) for total in rows)
     sums = [jnp.zeros((8, BLOCK), jnp.float32)] * 4
     for h in range(heads):
         at, row = rows_of(h), slice(h, h + 1)
@@ -469,6 +477,22 @@
     return grad, jnp.sum(grad.astype(jnp.float32) * wide, axis=0, keepdims=True)
 
 
+def side_queries_kernel(heads, q_ref, up_ref, down_ref, out_ref):
+    place = Place()
+    for h in range(heads):
+        at = rows_of(h)
+        qz = jnp.where(place.half, up_ref[FIRST, at], down_ref[FIRST, at])
+        out_ref[:, at] = jnp.where(place.odd, q_ref[:, at], qz)
+
+
+def relay_kernel(heads, up_ref, down_ref, out_ref):
+    half = Place().half
+    for h in range(heads):
+        at = rows_of(h)
+        out_ref[FIRST, at] = jnp.where(half, up_ref[FIRST, at], down_ref[FIRST, at])
+    out_ref[BLOCK:] = jnp.zeros_like(out_ref[BLOCK:])
+
+
 def back_kernel(
     heads,
     bias_ref,
@@ -485,18 +509,16 @@
     vx_ref,
     ez_ref,
     ex_ref,
-    en_ref,
     mz_ref,
     mx_ref,
-    mn_ref,
     up_out_ref,
     down_out_ref,
-    dvx_ref,
-    dsz_ref,
+    side_out_ref,
     dsx_ref,
-    dsn_ref,
     grad_ref,
+    gz_ref,
     delta_ref,
+    deltaz_ref,
 ):
     place = Place()
     odd, half = place.odd, place.half
@@ -504,73 +526,66 @@
     own_norm, z_norm = norm_rows(sums, 0), norm_rows(sums, 2)
     lse, z_lse = lse_ref[...], lsez_ref[...]
     scales = (
-        jnp.exp(mn_ref[...] - lse + bias_ref[NEAR : NEAR + 1]),
         jnp.exp(mz_ref[...] - z_lse + bias_ref[FAR : FAR + 1]),
         jnp.exp(mx_ref[...] - jnp.where(odd, lse, z_lse) + bias_ref[SIDE : SIDE + 1]),
     )
-    deltas = []
-    step = heads
-    for start in range(0, heads, step):
-        group = range(start, start + step)
-        parts, products, scores = [], [], []
-        for h in group:
-            at = rows_of(h)
-            grad, delta = upstream_part(own_norm, ut_ref[at], a_ref[at])
-            gz, deltaz = upstream_part(z_norm, uzt_ref[at], az_ref[at])
-            grad_ref[at] = grad
-            deltas.append(delta)
-            gx, deltax = jnp.where(odd, grad, gz), jnp.where(odd, delta, deltaz)
-            parts.append(((grad, gz, gx), (delta, deltaz, deltax)))
-        for h, ((grad, gz, gx), _) in zip(group, parts):
-            at = rows_of(h)
-            v2 = jnp.where(half, down_ref[SECOND, at], up_ref[SECOND, at])
-            both = mm(v2, jnp.concatenate([grad, gz], axis=1), NN)
-            products.append((both[:, :BLOCK], both[:, BLOCK:], mm(vx_ref[:, at], gx, NN)))
-        for h, (_, delta), product in zip(group, parts, products):
-            at = rows_of(h)
-            tiles = []
-            for n, (e_ref, ds_ref) in enumerate(((en_ref, dsn_ref), (ez_ref, dsz_ref), (ex_ref, dsx_ref))):
-                weights = e_ref[at] * scales[n][h : h + 1]
-                dscore = (weights * (product[n] - delta[n]) * SCALE).astype(jnp.bfloat16)
-                ds_ref[at] = dscore
-                tiles.append((weights.astype(jnp.bfloat16), dscore))
-            scores.append(tiles)
-        for h, ((grad, gz, gx), _), ((pn, _), (pz, dz), (px, dx)) in zip(group, parts, scores):
-            at = rows_of(h)
-            k2 = jnp.where(half, down_ref[FIRST, at], up_ref[FIRST, at])
-            dv2 = mm(jnp.concatenate([pn, pz], axis=1), jnp.concatenate([grad, gz], axis=1), NT)
-            dvx_ref[:, at] = mm(px, gx, NT).astype(jnp.bfloat16)
-            joined = jnp.concatenate([dz, jnp.where(odd, jnp.zeros_like(dx), dx)], axis=0)
-            dqz = mm(joined, jnp.concatenate([k2, kx_ref[:, at]], axis=0), TN).astype(jnp.bfloat16)
-            dv2 = dv2.astype(jnp.bfloat16)
-            up_out_ref[:, at] = jnp.where(half, dv2, dqz)
-            down_out_ref[:, at] = jnp.where(half, dqz, dv2)
-    delta_ref[...] = stack_rows(deltas)
-
-
-def helper_keys_kernel(heads, q_ref, up_ref, down_ref, dsz_ref, dsx_ref, dsn_ref, dk_ref, dkx_ref):
-    place = Place()
-    for h in range(heads):
-        at = rows_of(h)
-        q, qz = q_ref[:, at], jnp.where(place.half, up_ref[FIRST, at], down_ref[FIRST, at])
-        dk2 = mm(
-            jnp.concatenate([dsn_ref[at], dsz_ref[at]], axis=1), jnp.concatenate([q, qz], axis=0), NN
-        )
-        dk_ref[:, at] = dk2.astype(jnp.bfloat16)
-        dkx_ref[:, at] = mm(dsx_ref[at], jnp.where(place.odd, q, qz), NN).astype(jnp.bfloat16)
-
-
-def diagonal_back_kernel(
+    group = range(heads)
+    deltas, z_deltas = [], []
+    parts, products, scores = [], [], []
+    for h in group:
+        at = rows_of(h)
+        grad, delta = upstream_part(own_norm, ut_ref[at], a_ref[at])
+        gz, deltaz = upstream_part(z_norm, uzt_ref[at], az_ref[at])
+        grad_ref[at], gz_ref[at] = grad, gz
+        deltas.append(delta)
+        z_deltas.append(deltaz)
+        gx, deltax = jnp.where(odd, grad, gz), jnp.where(odd, delta, deltaz)
+        side_out_ref[at] = gx
+        parts.append(((gz, gx), (deltaz, deltax)))
+    for h, ((gz, gx), _) in zip(group, parts):
+        at = rows_of(h)
+        v2 = jnp.where(half, down_ref[SECOND, at], up_ref[SECOND, at])
+        products.append((mm(v2, gz, NN), mm(vx_ref[:, at], gx, NN)))
+    for h, (_, delta), product in zip(group, parts, products):
+        tiles = []
+        for n, e_ref in enumerate((ez_ref, ex_ref)):
+            weights = e_ref[rows_of(h)] * scales[n][h : h + 1]
+            tiles.append((weights * (product[n] - delta[n]) * SCALE).astype(jnp.bfloat16))
+        dsx_ref[rows_of(h)] = tiles[1]
+        scores.append(tiles)
+    for h, ((gz, _), _), (dz, dx) in zip(group, parts, scores):
+        at = rows_of(h)
+        k2 = jnp.where(half, down_ref[FIRST, at], up_ref[FIRST, at])
+        joined = jnp.concatenate([dz, jnp.where(odd, jnp.zeros_like(dx), dx)], axis=0)
+        dqz = mm(jnp.concatenate([k2, kx_ref[:, at]], axis=0), joined, TN).astype(jnp.bfloat16)
+        up_out_ref[at] = jnp.where(half, gz, dqz)
+        down_out_ref[at] = jnp.where(half, dqz, gz)
+    delta, deltaz = stack_rows(deltas), stack_rows(z_deltas)
+    delta_ref[...], deltaz_ref[...] = delta, deltaz
+    tail = slice(heads * HD, heads * HD + 2 * TAIL)
+    z_tail = jnp.concatenate([split_rows(z_lse), split_rows(deltaz)], axis=0)
+    own_tail = jnp.concatenate([split_rows(lse), split_rows(delta)], axis=0)
+    up_out_ref[tail] = jnp.where(half, z_tail, jnp.zeros_like(z_tail))
+    down_out_ref[tail] = jnp.where(half, jnp.zeros_like(z_tail), z_tail)
+    side_out_ref[tail] = jnp.where(odd, own_tail, z_tail)
+
+
+def local_back_kernel(
     heads,
+    bias_ref,
     sums_ref,
     q_ref,
     k_ref,
     v_ref,
     a_ref,
     lse_ref,
+    lsez_ref,
     grad_ref,
+    gz_ref,
     delta_ref,
-    ds_ref,
+    deltaz_ref,
+    en_ref,
+    mn_ref,
     dsx_ref,
     kx_ref,
     up_ref,
@@ -581,50 +596,95 @@
     dv_ref,
 ):
     place = Place()
-    half, odd = place.half, place.odd
+    odd, half = place.odd, place.half
     inverse, _ = norm_rows(sums_ref[...], 0)
-    lse = lse_ref[...]
+    lse, z_lse = lse_ref[...], lsez_ref[...] - bias_ref[KEY_NEAR : KEY_NEAR + 1]
+    near_scale = jnp.exp(mn_ref[...] - lse + bias_ref[NEAR : NEAR + 1])
     causal = causal_mask()
     for h in range(heads):
         at, row = rows_of(h), slice(h, h + 1)
         normed_ref[:, at] = (a_ref[at].astype(jnp.float32) * inverse).astype(jnp.bfloat16).T
-        q, k, v, grad = q_ref[:, at], k_ref[:, at], v_ref[:, at], grad_ref[at]
-        weights = jnp.exp(jnp.where(causal, score_tile(k, q), NEG_BIG) - lse[row])
-        dscore = (weights * (mm(v, grad, NN) - delta_ref[row]) * SCALE).astype(jnp.bfloat16)
-        dk_ref[:, at] = mm(dscore, q, NN)
-        dv_ref[:, at] = mm(weights.astype(jnp.bfloat16), grad, NT)
-        k2 = jnp.where(half, down_ref[FIRST, at], up_ref[FIRST, at])
+        up_a, down_a = up_ref[FIRST, at], down_ref[FIRST, at]
+        k2, qz = jnp.where(half, down_a, up_a), jnp.where(half, up_a, down_a)
+        v2 = jnp.where(half, down_ref[SECOND, at], up_ref[SECOND, at])
+        q, k, v, grad, gz = q_ref[:, at], k_ref[:, at], v_ref[:, at], grad_ref[at], gz_ref[at]
+        queries, grads = jnp.concatenate([q, qz], axis=0), jnp.concatenate([grad, gz], axis=1)
+        both = score_tile(k, queries)
+        products = mm(v, grads, NN)
+        own = jnp.exp(jnp.where(causal, both[:, :BLOCK], NEG_BIG) - lse[row])
+        ahead = jnp.exp(both[:, BLOCK:] - z_lse[row])
+        near = en_ref[at] * near_scale[row]
+        own_ds = (own * (products[:, :BLOCK] - delta_ref[row]) * SCALE).astype(jnp.bfloat16)
+        ahead_ds = (ahead * (products[:, BLOCK:] - deltaz_ref[row]) * SCALE).astype(jnp.bfloat16)
+        near_ds = (near * (mm(v2, grad, NN) - delta_ref[row]) * SCALE).astype(jnp.bfloat16)
+        dk_ref[:, at] = mm(jnp.concatenate([own_ds, ahead_ds], axis=1), queries, NN)
+        probs = jnp.concatenate([own, ahead], axis=1).astype(jnp.bfloat16)
+        dv_ref[:, at] = mm(probs, grads, NT)
         dsx = jnp.where(odd, dsx_ref[at], jnp.zeros_like(dsx_ref[at]))
-        dq_ref[:, at] = mm(dscore, k, TN) + mm(
-            jnp.concatenate([ds_ref[at], dsx], axis=0), jnp.concatenate([k2, kx_ref[:, at]], axis=0), TN
+        dq_ref[:, at] = mm(own_ds, k, TN) + mm(
+            jnp.concatenate([near_ds, dsx], axis=0), jnp.concatenate([k2, kx_ref[:, at]], axis=0), TN
         )
 
 
-def final_first_kernel(heads, up_ref, down_ref, side_ref, dq_own_ref, dv_own_ref, dq_ref, dv_ref, token_ref):
+def key_scores_kernel(heads, bias_ref, k_ref, far_ref, side_ref, out_ref):
+    for h in range(heads):
+        at = rows_of(h)
+        both = score_tile(k_ref[:, at], jnp.concatenate([far_ref[FIRST, at], side_ref[:, at]], axis=0))
+        out_ref[0, at] = both[:, :BLOCK] + bias_ref[KEY_FAR : KEY_FAR + 1]
+        out_ref[1, at] = both[:, BLOCK:] + bias_ref[KEY_SIDE : KEY_SIDE + 1]
+
+
+def final_kernel(
+    heads,
+    scores_ref,
+    far_ref,
+    sideq_ref,
+    up_ref,
+    down_ref,
+    side_ref,
+    v_ref,
+    dq_own_ref,
+    dk_own_ref,
+    dv_own_ref,
+    dq_ref,
+    dk_ref,
+    dv_ref,
+):
     place = Place()
     half = place.half
-    ahead = (place.me + 2 < lax.axis_size("ctx")).astype(jnp.float32)
     behind = (place.me >= 2).astype(jnp.float32)
-    for h in range(heads):
-        at = rows_of(h)
-        up, down = up_ref[:, at], down_ref[:, at]
-        dqz = jnp.where(half, down, up).astype(jnp.float32) * behind
-        dv = jnp.where(half, up, down).astype(jnp.float32) * ahead
+    first = slice(heads * HD, heads * HD + TAIL)
+    second = slice(heads * HD + TAIL, heads * HD + 2 * TAIL)
+    lse, delta = (
+        (joined_rows(jnp.where(half, up_ref[part], down_ref[part])), joined_rows(side_ref[part]))
+        for part in (first, second)
+    )
+    group = range(heads)
+    grads, products, tiles = [], [], []
+    for h in group:
+        at = rows_of(h)
+        up, down = up_ref[at], down_ref[at]
+        dqz = jnp.where(half, down, up).T.astype(jnp.float32) * behind
         dq_ref[:, at] = (dq_own_ref[:, at] + dqz).astype(jnp.bfloat16)
-        dv_ref[:, at] = (dv_own_ref[:, at] + side_ref[:, at].astype(jnp.float32) + dv).astype(jnp.bfloat16)
-    token_ref[...] = jnp.zeros_like(token_ref)
-
-
-def final_keys_kernel(heads, back_ref, side_ref, dk_own_ref, dk_ref):
-    ahead = (Place().me + 2 < lax.axis_size("ctx")).astype(jnp.float32)
-    for h in range(heads):
-        at = rows_of(h)
-        dk = back_ref[:, at].astype(jnp.float32) * ahead
-        dk_ref[:, at] = (dk_own_ref[:, at] + side_ref[:, at].astype(jnp.float32) + dk).astype(jnp.bfloat16)
+        grads.append(jnp.concatenate([jnp.where(half, up, down), side_ref[at]], axis=1))
+    for h, grad in zip(group, grads):
+        products.append(mm(v_ref[:, rows_of(h)], grad, NN))
+    for h, product in zip(group, products):
+        row = slice(h, h + 1)
+        probs = [jnp.exp(scores_ref[n, rows_of(h)] - lse[n][row]) for n in range(2)]
+        scores = [
+            probs[n] * (product[:, n * BLOCK : (n + 1) * BLOCK] - delta[n][row]) * SCALE for n in range(2)
+        ]
+        tiles.append([jnp.concatenate(pair, axis=1).astype(jnp.bfloat16) for pair in (probs, scores)])
+    for h, grad, (probs, scores) in zip(group, grads, tiles):
+        at = rows_of(h)
+        queries = jnp.concatenate([far_ref[FIRST, at], sideq_ref[:, at]], axis=0)
+        dk_ref[:, at] = (dk_own_ref[:, at] + mm(scores, queries, NN)).astype(jnp.bfloat16)
+        dv_ref[:, at] = (dv_own_ref[:, at] + mm(probs, grad, NT)).astype(jnp.bfloat16)
 
 
 def call(kernel, heads, flags, arrays, outs, flops, space=pltpu.VMEM, scratch=(), after=()):
-    moved = sum(math.prod(a.shape) * a.dtype.itemsize for a in (*arrays, *outs))
+    moved = sum(math.prod(a.shape) * a.dtype.itemsize for a in (*arrays, *outs)) if flops else 0
     return pl.pallas_call(
         lambda *refs: kernel(heads, *refs[len(after) :]),
         out_shape=outs,
@@ -709,8 +769,13 @@
         (message, message, wide_t, wide_t, wide_t, rows, rows, rows),
         6 * unit,
     )
+    ez, ex, en, mz, mx, mn = kept
     up_in, down_in = cycle(up_out, down_out)
-    (upstream_zt,) = call(transpose_kernel, heads, (), received, (flat_t,), 0, after=(kept[-1],))
+    (side_queries,) = call(
+        side_queries_kernel, heads, (), (queries, *received), (flat,), 0, after=(mn,)
+    )
+    side_queries = swap(side_queries)
+    (upstream_zt,) = call(transpose_kernel, heads, (), received, (flat_t,), 0, after=(mn,))
     attention, attention_z, lse, lse_z, sums = call(
         merge_kernel,
         heads,
@@ -722,39 +787,47 @@
     others = [
         lax.ppermute(sums, "head", [(i, i ^ step) for i in range(members)]) for step in range(1, members)
     ]
+    (far_queries,) = call(relay_kernel, heads, (), received, (struct(tokens + 16, width),), 0, after=(lse,))
+    far_queries = ring(far_queries, -2)
     sums = functools.reduce(jnp.add, others, sums)
-    up_out, down_out, side_dv, far_ds, side_ds, near_ds, grad_t, delta = call(
+    longer = struct(width + 2 * TAIL, tokens)
+    up_out, down_out, side_out, side_ds, grad_t, grad_zt, delta, delta_z = call(
         back_kernel,
         heads,
         (),
         (bias, sums, attention, attention_z, lse, lse_z, upstream_t, upstream_zt, *received, keys_x, values_x)
-        + tuple(kept),
-        (flat, flat, flat, flat_t, flat_t, flat_t, flat_t, rows),
-        8 * unit,
+        + (ez, ex, mz, mx),
+        (longer, longer, longer, flat_t, flat_t, flat_t, rows, rows),
+        0,
+        after=(side_queries,),
     )
     returned = cycle(up_out, down_out)
-    out_dk, side_dk = call(
-        helper_keys_kernel,
+    side_grads = swap(side_out)
+    normed, dq_own, dk_own, dv_own = call(
+        local_back_kernel,
         heads,
         (),
-        (queries, *received, far_ds, side_ds, near_ds),
-        (flat, flat),
-        3 * unit,
-    )
-    back_dk = ring(out_dk, -2)
-    side_dv, side_dk = swap(side_dv), swap(side_dk)
-    normed, dq_own, dk_own, dv_own = call(
-        diagonal_back_kernel,
+        (bias, sums, queries, keys, values, attention, lse, lse_z, grad_t, grad_zt, delta, delta_z, en, mn)
+        + (side_ds, keys_x, *received),
+        (flat, wide, wide, wide),
+        0,
+    )
+    (key_scores,) = call(
+        key_scores_kernel,
         heads,
         (),
-        (sums, queries, keys, values, attention, lse, grad_t, delta, near_ds, side_ds, keys_x, *received),
-        (flat, wide, wide, wide),
-        7 * unit,
-    )
-    grad_queries, grad_values, token = call(
-        final_first_kernel, heads, (), (*returned, side_dv, dq_own, dv_own), (flat, flat, rows), 0
-    )
-    (grad_keys,) = call(final_keys_kernel, heads, (), (back_dk, side_dk, dk_own), (flat,), 0, after=(token,))
+        (bias, keys, far_queries, side_queries),
+        (struct(2, width, tokens, dtype=jnp.float32),),
+        0,
+    )
+    grad_queries, grad_keys, grad_values = call(
+        final_kernel,
+        heads,
+        (),
+        (key_scores, far_queries, side_queries, *returned, side_grads, values, dq_own, dk_own, dv_own),
+        (flat, flat, flat),
+        6 * unit,
+    )
     return (normed, grad_queries, grad_keys, grad_values)
 
 

time: 49.2 us -> 48.3 us (0.982)
  waiting for transfers between devices: 19.4 us -> 17.2 us
  starting transfers between devices: 16.9 us -> 18 us
    ppermute x3, waiting for transfers between devices: 4.88 us -> 7.78 us  [cycle(): lax.ppermute(up_array, ('ctx', 'head'), rising)]
    ppermute x1, waiting for transfers between devices: 2.72 us -> 0.04 us  [ring(): lax.ppermute(array, 'ctx', [(i, (i + distance) % blocks) for i in range(b...]
    ppermute x3, waiting for transfers between devices: 1.83 us -> 0.01 us  [meeting_shards(): lax.ppermute(sums, 'head', [(i, i ^ step) for i in range(members)])]
    ppermute x3, starting transfers between devices: 3.48 us -> 1.91 us  [cycle(): lax.ppermute(up_array, ('ctx', 'head'), rising)]
    ppermute x3, starting transfers between devices: 3.82 us -> 5.38 us  [cycle(): lax.ppermute(down_array, ('ctx', 'head'), falling)]
    ppermute x4, starting transfers between devices: 4.05 us -> 5.18 us  [swap(): return lax.ppermute(array, 'ctx', [(i, i ^ 1) for i in range(blocks)])]
    pallas_call x10 -> x11, Pallas kernels: 11.3 us -> 11.4 us  [call(): pl.pallas_call(lambda *refs: kernel(heads, *refs[len(after):]), out_shape...]
  transfers between devices with their start and end apart: 14 -> 14, of which waited for: 9 -> 5; matrix products, arithmetic and copies ran while one was open for 0% -> 0% of each run, Pallas kernels for 13% -> 15%
where the time goes in v9:
time: 48.3 us; the launch traced here: 48.1 us
  starting transfers between devices  18 us (37%)
  waiting for transfers between devices  17.2 us (36%)
  Pallas kernels  11.4 us (24%)
  between operations  0.76 us (2%)
  local copies, waits for them, and re-layouts  0.7 us (1%)
    pallas_call x11, Pallas kernels, call(): pl.pallas_call(lambda *refs: kernel(heads, *refs[len(after):]), out_shape...  11.4 us
    ppermute x4, waiting for transfers between devices, swap(): return lax.ppermute(array, 'ctx', [(i, i ^ 1) for i in range(blocks)])  8.3 us
    ppermute x3, waiting for transfers between devices, cycle(): lax.ppermute(up_array, ('ctx', 'head'), rising)  7.78 us
    ppermute x3, starting transfers between devices, cycle(): lax.ppermute(down_array, ('ctx', 'head'), falling)  5.38 us
    ppermute x4, starting transfers between devices, swap(): return lax.ppermute(array, 'ctx', [(i, i ^ 1) for i in range(blocks)])  5.18 us
    ppermute x1, starting transfers between devices, ring(): lax.ppermute(array, 'ctx', [(i, (i + distance) % blocks) for i in range(b...  3.61 us
    ppermute x3, starting transfers between devices, meeting_shards(): lax.ppermute(sums, 'head', [(i, i ^ step) for i in range(members)])  1.92 us
    ppermute x3, starting transfers between devices, cycle(): lax.ppermute(up_array, ('ctx', 'head'), rising)  1.91 us
  transfers between devices with their start and end apart: 14, of which 5 were waited for; matrix products, arithmetic and copies ran while one was open for 0% of the time, Pallas kernels for 15%

profile of v9, /device:TPU:0, one launch (start us, length us, event | category | flops | bytes accessed | tf_op | source)
XLA Modules:
  0.0 48.1 jit_solution(12965550818040432108)
XLA Ops:
  0.7 1.3 %shard_map.84 = (bf16[256,1024]{1,0:T(8,128)(2,1)S(1)}, bf16[256,1024]{1,0:T(8,128)(2,1)S(1)}) custom-call(bf16[128,1024]{1,0:T(8,128)(2,1)} %refs_2_.5, bf16[128,1024]{1,0:T(8,128)(2,1)} %refs_1_.7, bf16[128,1024]{1,0:T(8,128)(2,1)} %refs_6_.1, bf16[128,1024]{1,0:T(8,128)(2,1)} %refs_5_.1), custom_call_target="tpu_custom_call" | custom-call | tf_op jit(solution)/shard_map/pallas_call | solution.py:688
  2.0 3.0 %collective-permute-start.1 = (bf16[256,1024]{1,0:T(8,128)(2,1)S(1)}, bf16[256,1024]{1,0:T(8,128)(2,1)S(1)}, u32[]{:S(2)}, u32[]{:S(2)}) collective-permute-start(bf16[256,1024]{1,0:T(8,128)(2,1)S(1)} %get-tuple-element.40), channel_id=1, source_target_pairs={{8,0},{9,1},{0,2},{1,3},{12,4},{13,5},{4,6},{5,7},{16,8},{17,9},{2... | collective-permute-start | bytes 1572872 | tf_op jit(solution)/shard_map/ppermute | solution.py:724
  5.1 1.9 %collective-permute-start.2 = (bf16[128,1024]{1,0:T(8,128)(2,1)S(1)}, bf16[128,1024]{1,0:T(8,128)(2,1)S(1)}, u32[]{:S(2)}, u32[]{:S(2)}) collective-permute-start(bf16[128,1024]{1,0:T(8,128)(2,1)S(1)} %copy-done.1), channel_id=1, source_target_pairs={{0,4},{4,0},{8,12},{12,8},{16,20},{20,16},{24,28},{28,24},{1,5},{5... | collective-permute-start | bytes 786440 | tf_op jit(solution)/shard_map/ppermute | solution.py:729
  7.2 0.7 %copy-done.4 = s32[8,8]{1,0:T(8,128)S(1)} copy-done((s32[8,8]{1,0:T(8,128)S(1)}, s32[8,8]{1,0:T(8,128)}, u32[]{:S(2)}) %copy-start.4) | copy-done | bytes 280
  7.9 2.4 %shard_map.85 = (f32[1024,128]{1,0:T(8,128)S(1)}, f32[8,128]{1,0:T(8,128)S(1)}, bf16[1024,128]{1,0:T(8,128)(2,1)S(1)}, f32[8,128]{1,0:T(8,128)S(1)}) custom-call(bf16[256,1024]{1,0:T(8,128)(2,1)S(1)} %get-tuple-element.38.refs_0_, s32[8,8]{1,0:T(8,128)S(1)} %copy-done.4, bf16[128,1024]{1,0:T(8,128)(2,1)S(1)} %copy-done, bf16[128,1024]{1,0:T(8,128)(2,1)S(1)} %copy-done.1, ...), custom_call_target="tpu_custom_call" | custom-call | flops 100663296 | bytes 1843200 | tf_op jit(solution)/shard_map/pallas_call | solution.py:688
  10.2 4.1 %collective-permute-done.2.refs_4_.refs_11_.refs_15_ = bf16[128,1024]{1,0:T(8,128)(2,1)S(1)} collective-permute-done((bf16[128,1024]{1,0:T(8,128)(2,1)S(1)}, bf16[128,1024]{1,0:T(8,128)(2,1)S(1)}, u32[]{:S(2)}, u32[]{:S(2)}) %collective-permute-start.2) | collective-permute-done | bytes 262176 | tf_op jit(solution)/shard_map/ppermute | solution.py:729
  14.4 4.2 %collective-permute-done.3.refs_5_.refs_12_ = bf16[128,1024]{1,0:T(8,128)(2,1)S(1)} collective-permute-done((bf16[128,1024]{1,0:T(8,128)(2,1)S(1)}, bf16[128,1024]{1,0:T(8,128)(2,1)S(1)}, u32[]{:S(2)}, u32[]{:S(2)}) %collective-permute-start.3) | collective-permute-done | bytes 262176 | tf_op jit(solution)/shard_map/ppermute | solution.py:729
  18.5 1.1 %shard_map.86 = (bf16[1056,128]{1,0:T(8,128)(2,1)S(1)}, bf16[1056,128]{1,0:T(8,128)(2,1)S(1)}, f32[1024,128]{1,0:T(8,128)S(1)}, f32[1024,128]{1,0:T(8,128)S(1)},...) custom-call(f32[8,128]{1,0:T(8,128)S(1)} %get-tuple-element.39.refs_0_.refs_1_, ...), custom_call_target="tpu_custom_call" | custom-call | flops 201326592 | bytes 4493312 | tf_op jit(solution)/shard_map/pallas_call | solution.py:688
  19.7 1.7 %collective-permute-start.4 = (bf16[1056,128]{1,0:T(8,128)(2,1)S(1)}, bf16[1056,128]{1,0:T(8,128)(2,1)S(1)}, u32[]{:S(2)}, u32[]{:S(2)}) collective-permute-start(bf16[1056,128]{1,0:T(8,128)(2,1)S(1)} %get-tuple-element.43.refs_1_), channel_id=1, source_target_pairs={{0,8},{1,9},{2,0},{3,1},{4,12},{5,13},{6,4},{7,5},{8,16},{9,17},{1... | collective-permute-start | bytes 811016 | tf_op jit(solution)/shard_map/ppermute | solution.py:724
  21.4 0.3 collective-permute-start.5
  21.9 1.7 %collective-permute-start.9 = (bf16[128,1024]{1,0:T(8,128)(2,1)S(1)}, bf16[128,1024]{1,0:T(8,128)(2,1)S(1)}, u32[]{:S(2)}, u32[]{:S(2)}) collective-permute-start(bf16[128,1024]{1,0:T(8,128)(2,1)S(1)} %shard_map.89), channel_id=1, source_target_pairs={{0,4},{4,0},{8,12},{12,8},{16,20},{20,16},{24,28},{28,24},{1,5},{5... | collective-permute-start | bytes 786440 | tf_op jit(solution)/shard_map/ppermute | solution.py:729
  23.6 3.1 %collective-permute-done.4.refs_3_ = bf16[1056,128]{1,0:T(8,128)(2,1)S(1)} collective-permute-done((bf16[1056,128]{1,0:T(8,128)(2,1)S(1)}, bf16[1056,128]{1,0:T(8,128)(2,1)S(1)}, u32[]{:S(2)}, u32[]{:S(2)}) %collective-permute-start.4) | collective-permute-done | bytes 270368 | tf_op jit(solution)/shard_map/ppermute | solution.py:724
  26.7 1.1 %collective-permute-done.5.refs_4_ = bf16[1056,128]{1,0:T(8,128)(2,1)S(1)} collective-permute-done((bf16[1056,128]{1,0:T(8,128)(2,1)S(1)}, bf16[1056,128]{1,0:T(8,128)(2,1)S(1)}, u32[]{:S(2)}, u32[]{:S(2)}) %collective-permute-start.5) | collective-permute-done | bytes 270368 | tf_op jit(solution)/shard_map/ppermute | solution.py:724
  27.9 0.5 %shard_map.88 = (bf16[1024,128]{1,0:T(8,128)(2,1)S(1)}, bf16[1024,128]{1,0:T(8,128)(2,1)S(1)}, f32[8,128]{1,0:T(8,128)S(1)}, f32[8,128]{1,0:T(8,128)S(1)}, f32[8,128]{1,0:T(8,128)S(1)}) custom-call(f32[8,128]{1,0:T(8,128)S(1)} %get-tuple-element.39.refs_0_.refs_1_, bf16[1056,128]{1,0:T(8,128)(2,1)S(1)} %get-tuple-element.43.refs_1_, ...), custom_call_target="tpu_custom_call" | custom-call | flops 524288 | bytes 2146304 | tf_op jit(solution)/shard_map/pallas_call | solution.py:688
  28.4 0.7 %collective-permute-start.7 = (f32[8,128]{1,0:T(8,128)S(1)}, f32[8,128]{1,0:T(8,128)S(1)}, u32[]{:S(2)}, u32[]{:S(2)}) collective-permute-start(f32[8,128]{1,0:T(8,128)S(1)} %get-tuple-element.47), channel_id=1, source_target_pairs={{0,2},{1,3},{2,0},{3,1},{4,6},{5,7},{6,4},{7,5},{8,10},{9,11},{10,... | collective-permute-start | bytes 12296 | tf_op jit(solution)/shard_map/ppermute | solution.py:788
  29.1 1.1 %collective-permute-start.6 = (f32[8,128]{1,0:T(8,128)S(1)}, f32[8,128]{1,0:T(8,128)S(1)}, u32[]{:S(2)}, u32[]{:S(2)}) collective-permute-start(f32[8,128]{1,0:T(8,128)S(1)} %get-tuple-element.47), channel_id=1, source_target_pairs={{0,1},{1,0},{2,3},{3,2},{4,5},{5,4},{6,7},{7,6},{8,9},{9,8},{10,11... | collective-permute-start | bytes 12296 | tf_op jit(solution)/shard_map/ppermute | solution.py:788
  30.4 3.6 %collective-permute-start.10 = (bf16[144,1024]{1,0:T(8,128)(2,1)S(1)}, bf16[144,1024]{1,0:T(8,128)(2,1)S(1)}, u32[]{:S(2)}, u32[]{:S(2)}) collective-permute-start(bf16[144,1024]{1,0:T(8,128)(2,1)S(1)} %shard_map.92), channel_id=1, source_target_pairs={{0,24},{4,28},{8,0},{12,4},{16,8},{20,12},{24,16},{28,20},{1,25},{... | collective-permute-start | bytes 884744 | tf_op jit(solution)/shard_map/ppermute | solution.py:732
  34.0 0.8 %shard_map.90 = (bf16[1088,128]{1,0:T(8,128)(2,1)S(1)}, bf16[1088,128]{1,0:T(8,128)(2,1)S(1)}, bf16[1088,128]{1,0:T(8,128)(2,1)S(1)}, bf16[1024,128]{1,0:T(8,128...) custom-call(bf16[128,1024]{1,0:T(8,128)(2,1)S(1)} %collective-permut, ...), custom_call_target="tpu_custom_call" | custom-call | tf_op jit(solution)/shard_map/pallas_call | solution.py:688
  34.9 2.0 %collective-permute-start.12 = (bf16[1088,128]{1,0:T(8,128)(2,1)S(1)}, bf16[1088,128]{1,0:T(8,128)(2,1)S(1)}, u32[]{:S(2)}, u32[]{:S(2)}) collective-permute-start(bf16[1088,128]{1,0:T(8,128)(2,1)S(1)} %get-tuple-element.64), channel_id=1, source_target_pairs={{8,0},{9,1},{0,2},{1,3},{12,4},{13,5},{4,6},{5,7},{16,8},{17,9},{2... | collective-permute-start | bytes 835592 | tf_op jit(solution)/shard_map/ppermute | solution.py:724
  36.9 1.5 %collective-permute-start.13 = (bf16[1088,128]{1,0:T(8,128)(2,1)S(1)}, bf16[1088,128]{1,0:T(8,128)(2,1)S(1)}, u32[]{:S(2)}, u32[]{:S(2)}) collective-permute-start(bf16[1088,128]{1,0:T(8,128)(2,1)S(1)} %get-tuple-element.65), channel_id=1, source_target_pairs={{0,4},{4,0},{8,12},{12,8},{16,20},{20,16},{24,28},{28,24},{1,5},{5... | collective-permute-start | bytes 835592 | tf_op jit(solution)/shard_map/ppermute | solution.py:729
  38.4 3.0 %shard_map.91 = (bf16[128,1024]{1,0:T(8,128)(2,1)}, f32[128,1024]{1,0:T(8,128)S(1)}, f32[128,1024]{1,0:T(8,128)S(1)}, f32[128,1024]{1,0:T(8,128)S(1)}) custom-call(f32[8,128]{1,0:T(8,128)S(1)} %get-tuple-element.39.refs_0_.refs_1_, f32[8,128]{1,0:T(8,128)S(1)} %add_add_fusion.refs_2_.refs_1_, bf16[128,1024]{1,0:T(8,128)(2,1)S(1)} %copy-done, ...), custom_call_target="tpu_custom_call" | custom-call | tf_op jit(solution)/shard_map/pallas_call | solution.py:688
  41.4 0.3 shard_map.93.refs_0_
  41.7 4.7 %collective-permute-done.11.refs_3_ = bf16[1088,128]{1,0:T(8,128)(2,1)S(1)} collective-permute-done((bf16[1088,128]{1,0:T(8,128)(2,1)S(1)}, bf16[1088,128]{1,0:T(8,128)(2,1)S(1)}, u32[]{:S(2)}, u32[]{:S(2)}) %collective-permute-start.11) | collective-permute-done | bytes 278560 | tf_op jit(solution)/shard_map/ppermute | solution.py:724
  46.4 1.6 %shard_map.94 = (bf16[128,1024]{1,0:T(8,128)(2,1)}, bf16[128,1024]{1,0:T(8,128)(2,1)}, bf16[128,1024]{1,0:T(8,128)(2,1)}) custom-call(f32[2,1024,128]{2,1,0:T(8,128)S(1)} %shard_map.93.refs_0_, bf16[144,1024]{1,0:T(8,128)(2,1)S(1)} %collective-permute-done.10.refs_2_.refs_1_, bf16[128,1024]{1,0:T(8,128)(2,1)S(1)} %collective-permute-done.9.refs_0_.refs_3_.refs_2_, ...), custom_call_target="tpu_custom_call" | custom-call | flops 201326592 | bytes 5062656 | tf_op jit(solution)/shard_map/pallas_call | solution.py:688
  (26 shorter events, 0.8 us)
Async XLA Ops:
  0.6 6.4 %copy-start.2 = (bf16[128,1024]{1,0:T(8,128)(2,1)S(1)}, bf16[128,1024]{1,0:T(8,128)(2,1)}, u32[]{:S(2)}) copy-start(bf16[128,1024]{1,0:T(8,128)(2,1)} %refs_6_.1) | copy-start | bytes 786436
  0.6 4.5 %copy-start.1 = (bf16[128,1024]{1,0:T(8,128)(2,1)S(1)}, bf16[128,1024]{1,0:T(8,128)(2,1)}, u32[]{:S(2)}) copy-start(bf16[128,1024]{1,0:T(8,128)(2,1)} %refs_1_.7) | copy-start | bytes 786436
  0.7 6.5 %copy-start = (bf16[128,1024]{1,0:T(8,128)(2,1)S(1)}, bf16[128,1024]{1,0:T(8,128)(2,1)}, u32[]{:S(2)}) copy-start(bf16[128,1024]{1,0:T(8,128)(2,1)} %refs_2_.5) | copy-start | bytes 786436
  0.7 6.5 %copy-start.3 = (bf16[128,1024]{1,0:T(8,128)(2,1)S(1)}, bf16[128,1024]{1,0:T(8,128)(2,1)}, u32[]{:S(2)}) copy-start(bf16[128,1024]{1,0:T(8,128)(2,1)} %refs_5_.1) | copy-start | bytes 786436
  2.0 16.5 %collective-permute-start.1 = (bf16[256,1024]{1,0:T(8,128)(2,1)S(1)}, bf16[256,1024]{1,0:T(8,128)(2,1)S(1)}, u32[]{:S(2)}, u32[]{:S(2)}) collective-permute-start(bf16[256,1024]{1,0:T(8,128)(2,1)S(1)} %get-tuple-element.40), channel_id=1, source_target_pairs={{8,0},{9,1},{0,2},{1,3},{12,4},{13,5},{4,6},{5,7},{16,8},{17,9},{2... | collective-permute-start | bytes 1572872 | tf_op jit(solution)/shard_map/ppermute | solution.py:724
  5.0 13.5 %collective-permute-start = (bf16[256,1024]{1,0:T(8,128)(2,1)S(1)}, bf16[256,1024]{1,0:T(8,128)(2,1)S(1)}, u32[]{:S(2)}, u32[]{:S(2)}) collective-permute-start(bf16[256,1024]{1,0:T(8,128)(2,1)S(1)} %get-tuple-element.38.refs_0_), channel_id=1, source_target_pairs={{0,8},{1,9},{2,0},{3,1},{4,12},{5,13},{6,4},{7,5},{8,16},{9,17},{1... | collective-permute-start | bytes 1572872 | tf_op jit(solution)/shard_map/ppermute | solution.py:724
  5.1 9.2 %collective-permute-start.2 = (bf16[128,1024]{1,0:T(8,128)(2,1)S(1)}, bf16[128,1024]{1,0:T(8,128)(2,1)S(1)}, u32[]{:S(2)}, u32[]{:S(2)}) collective-permute-start(bf16[128,1024]{1,0:T(8,128)(2,1)S(1)} %copy-done.1), channel_id=1, source_target_pairs={{0,4},{4,0},{8,12},{12,8},{16,20},{20,16},{24,28},{28,24},{1,5},{5... | collective-permute-start | bytes 786440 | tf_op jit(solution)/shard_map/ppermute | solution.py:729
  7.0 11.5 %collective-permute-start.3 = (bf16[128,1024]{1,0:T(8,128)(2,1)S(1)}, bf16[128,1024]{1,0:T(8,128)(2,1)S(1)}, u32[]{:S(2)}, u32[]{:S(2)}) collective-permute-start(bf16[128,1024]{1,0:T(8,128)(2,1)S(1)} %copy-done.2), channel_id=1, source_target_pairs={{0,4},{4,0},{8,12},{12,8},{16,20},{20,16},{24,28},{28,24},{1,5},{5... | collective-permute-start | bytes 786440 | tf_op jit(solution)/shard_map/ppermute | solution.py:729
  7.2 0.7 %copy-start.4 = (s32[8,8]{1,0:T(8,128)S(1)}, s32[8,8]{1,0:T(8,128)}, u32[]{:S(2)}) copy-start(s32[8,8]{1,0:T(8,128)} %refs_1_.5) | copy-start | bytes 772
  19.7 7.1 %collective-permute-start.4 = (bf16[1056,128]{1,0:T(8,128)(2,1)S(1)}, bf16[1056,128]{1,0:T(8,128)(2,1)S(1)}, u32[]{:S(2)}, u32[]{:S(2)}) collective-permute-start(bf16[1056,128]{1,0:T(8,128)(2,1)S(1)} %get-tuple-element.43.refs_1_), channel_id=1, source_target_pairs={{0,8},{1,9},{2,0},{3,1},{4,12},{5,13},{6,4},{7,5},{8,16},{9,17},{1... | collective-permute-start | bytes 811016 | tf_op jit(solution)/shard_map/ppermute | solution.py:724
  21.4 6.5 %collective-permute-start.5 = (bf16[1056,128]{1,0:T(8,128)(2,1)S(1)}, bf16[1056,128]{1,0:T(8,128)(2,1)S(1)}, u32[]{:S(2)}, u32[]{:S(2)}) collective-permute-start(bf16[1056,128]{1,0:T(8,128)(2,1)S(1)} %get-tuple-element.44.refs_2_), channel_id=1, source_target_pairs={{8,0},{9,1},{0,2},{1,3},{12,4},{13,5},{4,6},{5,7},{16,8},{17,9},{2... | collective-permute-start | bytes 811016 | tf_op jit(solution)/shard_map/ppermute | solution.py:724
  21.9 12.2 %collective-permute-start.9 = (bf16[128,1024]{1,0:T(8,128)(2,1)S(1)}, bf16[128,1024]{1,0:T(8,128)(2,1)S(1)}, u32[]{:S(2)}, u32[]{:S(2)}) collective-permute-start(bf16[128,1024]{1,0:T(8,128)(2,1)S(1)} %shard_map.89), channel_id=1, source_target_pairs={{0,4},{4,0},{8,12},{12,8},{16,20},{20,16},{24,28},{28,24},{1,5},{5... | collective-permute-start | bytes 786440 | tf_op jit(solution)/shard_map/ppermute | solution.py:729
  28.4 5.6 %collective-permute-start.8 = (f32[8,128]{1,0:T(8,128)S(1)}, f32[8,128]{1,0:T(8,128)S(1)}, u32[]{:S(2)}, u32[]{:S(2)}) collective-permute-start(f32[8,128]{1,0:T(8,128)S(1)} %get-tuple-element.47), channel_id=1, source_target_pairs={{0,3},{1,2},{2,1},{3,0},{4,7},{5,6},{6,5},{7,4},{8,11},{9,10},{10,... | collective-permute-start | bytes 12296 | tf_op jit(solution)/shard_map/ppermute | solution.py:788
  28.4 5.5 %collective-permute-start.7 = (f32[8,128]{1,0:T(8,128)S(1)}, f32[8,128]{1,0:T(8,128)S(1)}, u32[]{:S(2)}, u32[]{:S(2)}) collective-permute-start(f32[8,128]{1,0:T(8,128)S(1)} %get-tuple-element.47), channel_id=1, source_target_pairs={{0,2},{1,3},{2,0},{3,1},{4,6},{5,7},{6,4},{7,5},{8,10},{9,11},{10,... | collective-permute-start | bytes 12296 | tf_op jit(solution)/shard_map/ppermute | solution.py:788
  29.1 4.8 %collective-permute-start.6 = (f32[8,128]{1,0:T(8,128)S(1)}, f32[8,128]{1,0:T(8,128)S(1)}, u32[]{:S(2)}, u32[]{:S(2)}) collective-permute-start(f32[8,128]{1,0:T(8,128)S(1)} %get-tuple-element.47), channel_id=1, source_target_pairs={{0,1},{1,0},{2,3},{3,2},{4,5},{5,4},{6,7},{7,6},{8,9},{9,8},{10,11... | collective-permute-start | bytes 12296 | tf_op jit(solution)/shard_map/ppermute | solution.py:788
  30.4 11.0 %collective-permute-start.10 = (bf16[144,1024]{1,0:T(8,128)(2,1)S(1)}, bf16[144,1024]{1,0:T(8,128)(2,1)S(1)}, u32[]{:S(2)}, u32[]{:S(2)}) collective-permute-start(bf16[144,1024]{1,0:T(8,128)(2,1)S(1)} %shard_map.92), channel_id=1, source_target_pairs={{0,24},{4,28},{8,0},{12,4},{16,8},{20,12},{24,16},{28,20},{1,25},{... | collective-permute-start | bytes 884744 | tf_op jit(solution)/shard_map/ppermute | solution.py:732
  34.8 11.6 %collective-permute-start.11 = (bf16[1088,128]{1,0:T(8,128)(2,1)S(1)}, bf16[1088,128]{1,0:T(8,128)(2,1)S(1)}, u32[]{:S(2)}, u32[]{:S(2)}) collective-permute-start(bf16[1088,128]{1,0:T(8,128)(2,1)S(1)} %get-tuple-element.63), channel_id=1, source_target_pairs={{0,8},{1,9},{2,0},{3,1},{4,12},{5,13},{6,4},{7,5},{8,16},{9,17},{1... | collective-permute-start | bytes 835592 | tf_op jit(solution)/shard_map/ppermute | solution.py:724
  34.9 11.6 %collective-permute-start.12 = (bf16[1088,128]{1,0:T(8,128)(2,1)S(1)}, bf16[1088,128]{1,0:T(8,128)(2,1)S(1)}, u32[]{:S(2)}, u32[]{:S(2)}) collective-permute-start(bf16[1088,128]{1,0:T(8,128)(2,1)S(1)} %get-tuple-element.64), channel_id=1, source_target_pairs={{8,0},{9,1},{0,2},{1,3},{12,4},{13,5},{4,6},{5,7},{16,8},{17,9},{2... | collective-permute-start | bytes 835592 | tf_op jit(solution)/shard_map/ppermute | solution.py:724
  36.9 9.6 %collective-permute-start.13 = (bf16[1088,128]{1,0:T(8,128)(2,1)S(1)}, bf16[1088,128]{1,0:T(8,128)(2,1)S(1)}, u32[]{:S(2)}, u32[]{:S(2)}) collective-permute-start(bf16[1088,128]{1,0:T(8,128)(2,1)S(1)} %get-tuple-element.65), channel_id=1, source_target_pairs={{0,4},{4,0},{8,12},{12,8},{16,20},{20,16},{24,28},{28,24},{1,5},{5... | collective-permute-start | bytes 835592 | tf_op jit(solution)/shard_map/ppermute | solution.py:729

commit v10 on v9

--- a/solution.py
+++ b/solution.py
@@ -489,8 +489,7 @@
     half = Place().half
     for h in range(heads):
         at = rows_of(h)
-        out_ref[FIRST, at] = jnp.where(half, up_ref[FIRST, at], down_ref[FIRST, at])
-    out_ref[BLOCK:] = jnp.zeros_like(out_ref[BLOCK:])
+        out_ref[:, at] = jnp.where(half, up_ref[FIRST, at], down_ref[FIRST, at])
 
 
 def back_kernel(
@@ -629,7 +628,7 @@
 def key_scores_kernel(heads, bias_ref, k_ref, far_ref, side_ref, out_ref):
     for h in range(heads):
         at = rows_of(h)
-        both = score_tile(k_ref[:, at], jnp.concatenate([far_ref[FIRST, at], side_ref[:, at]], axis=0))
+        both = score_tile(k_ref[:, at], jnp.concatenate([far_ref[:, at], side_ref[:, at]], axis=0))
         out_ref[0, at] = both[:, :BLOCK] + bias_ref[KEY_FAR : KEY_FAR + 1]
         out_ref[1, at] = both[:, BLOCK:] + bias_ref[KEY_SIDE : KEY_SIDE + 1]
 
@@ -678,7 +677,7 @@
         tiles.append([jnp.concatenate(pair, axis=1).astype(jnp.bfloat16) for pair in (probs, scores)])
     for h, grad, (probs, scores) in zip(group, grads, tiles):
         at = rows_of(h)
-        queries = jnp.concatenate([far_ref[FIRST, at], sideq_ref[:, at]], axis=0)
+        queries = jnp.concatenate([far_ref[:, at], sideq_ref[:, at]], axis=0)
         dk_ref[:, at] = (dk_own_ref[:, at] + mm(scores, queries, NN)).astype(jnp.bfloat16)
         dv_ref[:, at] = (dv_own_ref[:, at] + mm(probs, grad, NT)).astype(jnp.bfloat16)
 
@@ -775,6 +774,8 @@
         side_queries_kernel, heads, (), (queries, *received), (flat,), 0, after=(mn,)
     )
     side_queries = swap(side_queries)
+    (far_queries,) = call(relay_kernel, heads, (), received, (flat,), 0, after=(mn,))
+    far_queries = lax.ppermute(far_queries, "ctx", [(i, i - 2) for i in range(2, blocks - 2)])
     (upstream_zt,) = call(transpose_kernel, heads, (), received, (flat_t,), 0, after=(mn,))
     attention, attention_z, lse, lse_z, sums = call(
         merge_kernel,
@@ -787,8 +788,6 @@
     others = [
         lax.ppermute(sums, "head", [(i, i ^ step) for i in range(members)]) for step in range(1, members)
     ]
-    (far_queries,) = call(relay_kernel, heads, (), received, (struct(tokens + 16, width),), 0, after=(lse,))
-    far_queries = ring(far_queries, -2)
     sums = functools.reduce(jnp.add, others, sums)
     longer = struct(width + 2 * TAIL, tokens)
     up_out, down_out, side_out, side_ds, grad_t, grad_zt, delta, delta_z = call(
@@ -799,7 +798,7 @@
         + (ez, ex, mz, mx),
         (longer, longer, longer, flat_t, flat_t, flat_t, rows, rows),
         0,
-        after=(side_queries,),
+        after=(side_queries, far_queries),
     )
     returned = cycle(up_out, down_out)
     side_grads = swap(side_out)

time: 48.3 us -> 46.9 us (0.971)
  starting transfers between devices: 18 us -> 16.2 us
    ppermute x3, waiting for transfers between devices: 7.78 us -> 2.32 us  [cycle(): lax.ppermute(up_array, ('ctx', 'head'), rising)]
    ppermute x3, waiting for transfers between devices: 1.11 us -> 4.72 us  [cycle(): lax.ppermute(down_array, ('ctx', 'head'), falling)]
    ppermute x1, starting transfers between devices: 3.61 us -> 1.29 us  [meeting_shards(): lax.ppermute(far_queries, 'ctx', [(i, i - 2) for i in range(2, blocks - 2)])]
    ppermute x3, waiting for transfers between devices: 0.01 us -> 1.83 us  [meeting_shards(): lax.ppermute(sums, 'head', [(i, i ^ step) for i in range(members)])]
    ppermute x3, starting transfers between devices: 1.91 us -> 3.56 us  [cycle(): lax.ppermute(up_array, ('ctx', 'head'), rising)]
    ppermute x3, starting transfers between devices: 5.38 us -> 3.74 us  [cycle(): lax.ppermute(down_array, ('ctx', 'head'), falling)]
    ppermute x4, starting transfers between devices: 5.18 us -> 5.75 us  [swap(): return lax.ppermute(array, 'ctx', [(i, i ^ 1) for i in range(blocks)])]
  transfers between devices with their start and end apart: 14 -> 14, of which waited for: 5 -> 9; matrix products, arithmetic and copies ran while one was open for 0% -> 0% of each run, Pallas kernels for 15% -> 14%
where the time goes in v10:
time: 46.9 us; the launch traced here: 46.7 us
  waiting for transfers between devices  17.6 us (38%)
  starting transfers between devices  16.2 us (35%)
  Pallas kernels  11.4 us (24%)
  between operations  0.77 us (2%)
  local copies, waits for them, and re-layouts  0.7 us (1%)
    pallas_call x11, Pallas kernels, call(): pl.pallas_call(lambda *refs: kernel(heads, *refs[len(after):]), out_shape...  11.4 us
    ppermute x4, waiting for transfers between devices, swap(): return lax.ppermute(array, 'ctx', [(i, i ^ 1) for i in range(blocks)])  8.7 us
    ppermute x4, starting transfers between devices, swap(): return lax.ppermute(array, 'ctx', [(i, i ^ 1) for i in range(blocks)])  5.75 us
    ppermute x3, waiting for transfers between devices, cycle(): lax.ppermute(down_array, ('ctx', 'head'), falling)  4.72 us
    ppermute x3, starting transfers between devices, cycle(): lax.ppermute(down_array, ('ctx', 'head'), falling)  3.74 us
    ppermute x3, starting transfers between devices, cycle(): lax.ppermute(up_array, ('ctx', 'head'), rising)  3.56 us
    ppermute x3, waiting for transfers between devices, cycle(): lax.ppermute(up_array, ('ctx', 'head'), rising)  2.32 us
    ppermute x3, starting transfers between devices, meeting_shards(): lax.ppermute(sums, 'head', [(i, i ^ step) for i in range(members)])  1.91 us
  transfers between devices with their start and end apart: 14, of which 9 were waited for; matrix products, arithmetic and copies ran while one was open for 0% of the time, Pallas kernels for 14%

profile of v10, /device:TPU:0, one launch (start us, length us, event | category | flops | bytes accessed | tf_op | source)
XLA Modules:
  0.0 46.7 jit_solution(11808219988158177597)
XLA Ops:
  0.7 1.3 %shard_map.84 = (bf16[256,1024]{1,0:T(8,128)(2,1)S(1)}, bf16[256,1024]{1,0:T(8,128)(2,1)S(1)}) custom-call(bf16[128,1024]{1,0:T(8,128)(2,1)} %refs_2_.5, bf16[128,1024]{1,0:T(8,128)(2,1)} %refs_1_.7, bf16[128,1024]{1,0:T(8,128)(2,1)} %refs_6_.1, bf16[128,1024]{1,0:T(8,128)(2,1)} %refs_5_.1), custom_call_target="tpu_custom_call" | custom-call | tf_op jit(solution)/shard_map/pallas_call | solution.py:687
  2.0 3.0 %collective-permute-start.1 = (bf16[256,1024]{1,0:T(8,128)(2,1)S(1)}, bf16[256,1024]{1,0:T(8,128)(2,1)S(1)}, u32[]{:S(2)}, u32[]{:S(2)}) collective-permute-start(bf16[256,1024]{1,0:T(8,128)(2,1)S(1)} %get-tuple-element.40), channel_id=1, source_target_pairs={{8,0},{9,1},{0,2},{1,3},{12,4},{13,5},{4,6},{5,7},{16,8},{17,9},{2... | collective-permute-start | bytes 1572872 | tf_op jit(solution)/shard_map/ppermute | solution.py:723
  5.1 1.9 %collective-permute-start.2 = (bf16[128,1024]{1,0:T(8,128)(2,1)S(1)}, bf16[128,1024]{1,0:T(8,128)(2,1)S(1)}, u32[]{:S(2)}, u32[]{:S(2)}) collective-permute-start(bf16[128,1024]{1,0:T(8,128)(2,1)S(1)} %copy-done.1), channel_id=1, source_target_pairs={{0,4},{4,0},{8,12},{12,8},{16,20},{20,16},{24,28},{28,24},{1,5},{5... | collective-permute-start | bytes 786440 | tf_op jit(solution)/shard_map/ppermute | solution.py:728
  7.2 0.7 %copy-done.4 = s32[8,8]{1,0:T(8,128)S(1)} copy-done((s32[8,8]{1,0:T(8,128)S(1)}, s32[8,8]{1,0:T(8,128)}, u32[]{:S(2)}) %copy-start.4) | copy-done | bytes 280
  7.9 2.4 %shard_map.85 = (f32[1024,128]{1,0:T(8,128)S(1)}, f32[8,128]{1,0:T(8,128)S(1)}, bf16[1024,128]{1,0:T(8,128)(2,1)S(1)}, f32[8,128]{1,0:T(8,128)S(1)}) custom-call(bf16[256,1024]{1,0:T(8,128)(2,1)S(1)} %get-tuple-element.38.refs_0_, s32[8,8]{1,0:T(8,128)S(1)} %copy-done.4, bf16[128,1024]{1,0:T(8,128)(2,1)S(1)} %copy-done, bf16[128,1024]{1,0:T(8,128)(2,1)S(1)} %copy-done.1, ...), custom_call_target="tpu_custom_call" | custom-call | flops 100663296 | bytes 1843200 | tf_op jit(solution)/shard_map/pallas_call | solution.py:687
  10.2 4.1 %collective-permute-done.2.refs_4_.refs_12_.refs_15_ = bf16[128,1024]{1,0:T(8,128)(2,1)S(1)} collective-permute-done((bf16[128,1024]{1,0:T(8,128)(2,1)S(1)}, bf16[128,1024]{1,0:T(8,128)(2,1)S(1)}, u32[]{:S(2)}, u32[]{:S(2)}) %collective-permute-start.2) | collective-permute-done | bytes 262176 | tf_op jit(solution)/shard_map/ppermute | solution.py:728
  14.4 4.2 %collective-permute-done.3.refs_5_.refs_13_ = bf16[128,1024]{1,0:T(8,128)(2,1)S(1)} collective-permute-done((bf16[128,1024]{1,0:T(8,128)(2,1)S(1)}, bf16[128,1024]{1,0:T(8,128)(2,1)S(1)}, u32[]{:S(2)}, u32[]{:S(2)}) %collective-permute-start.3) | collective-permute-done | bytes 262176 | tf_op jit(solution)/shard_map/ppermute | solution.py:728
  18.5 1.1 %shard_map.86 = (bf16[1056,128]{1,0:T(8,128)(2,1)S(1)}, bf16[1056,128]{1,0:T(8,128)(2,1)S(1)}, f32[1024,128]{1,0:T(8,128)S(1)}, f32[1024,128]{1,0:T(8,128)S(1)},...) custom-call(f32[8,128]{1,0:T(8,128)S(1)} %get-tuple-element.39.refs_0_.refs_2_, ...), custom_call_target="tpu_custom_call" | custom-call | flops 201326592 | bytes 4493312 | tf_op jit(solution)/shard_map/pallas_call | solution.py:687
  19.7 1.7 %collective-permute-start.4 = (bf16[1056,128]{1,0:T(8,128)(2,1)S(1)}, bf16[1056,128]{1,0:T(8,128)(2,1)S(1)}, u32[]{:S(2)}, u32[]{:S(2)}) collective-permute-start(bf16[1056,128]{1,0:T(8,128)(2,1)S(1)} %get-tuple-element.43.refs_1_), channel_id=1, source_target_pairs={{0,8},{1,9},{2,0},{3,1},{4,12},{5,13},{6,4},{7,5},{8,16},{9,17},{1... | collective-permute-start | bytes 811016 | tf_op jit(solution)/shard_map/ppermute | solution.py:723
  21.9 1.7 %collective-permute-start.9 = (bf16[128,1024]{1,0:T(8,128)(2,1)S(1)}, bf16[128,1024]{1,0:T(8,128)(2,1)S(1)}, u32[]{:S(2)}, u32[]{:S(2)}) collective-permute-start(bf16[128,1024]{1,0:T(8,128)(2,1)S(1)} %shard_map.89), channel_id=1, source_target_pairs={{0,4},{4,0},{8,12},{12,8},{16,20},{20,16},{24,28},{28,24},{1,5},{5... | collective-permute-start | bytes 786440 | tf_op jit(solution)/shard_map/ppermute | solution.py:728
  23.6 1.3 %collective-permute-start.10 = (bf16[128,1024]{1,0:T(8,128)(2,1)S(1)}, bf16[128,1024]{1,0:T(8,128)(2,1)S(1)}, u32[]{:S(2)}, u32[]{:S(2)}) collective-permute-start(bf16[128,1024]{1,0:T(8,128)(2,1)S(1)} %shard_map.90), channel_id=1, source_target_pairs={{8,0},{12,4},{16,8},{20,12},{9,1},{13,5},{17,9},{21,13},{10,2},{14... | collective-permute-start | bytes 786440 | tf_op jit(solution)/shard_map/ppermute | solution.py:778
  25.0 1.7 %collective-permute-done.4.refs_3_ = bf16[1056,128]{1,0:T(8,128)(2,1)S(1)} collective-permute-done((bf16[1056,128]{1,0:T(8,128)(2,1)S(1)}, bf16[1056,128]{1,0:T(8,128)(2,1)S(1)}, u32[]{:S(2)}, u32[]{:S(2)}) %collective-permute-start.4) | collective-permute-done | bytes 270368 | tf_op jit(solution)/shard_map/ppermute | solution.py:723
  26.7 3.3 %collective-permute-done.5.refs_4_ = bf16[1056,128]{1,0:T(8,128)(2,1)S(1)} collective-permute-done((bf16[1056,128]{1,0:T(8,128)(2,1)S(1)}, bf16[1056,128]{1,0:T(8,128)(2,1)S(1)}, u32[]{:S(2)}, u32[]{:S(2)}) %collective-permute-start.5) | collective-permute-done | bytes 270368 | tf_op jit(solution)/shard_map/ppermute | solution.py:723
  30.1 0.5 %shard_map.88 = (bf16[1024,128]{1,0:T(8,128)(2,1)S(1)}, bf16[1024,128]{1,0:T(8,128)(2,1)S(1)}, f32[8,128]{1,0:T(8,128)S(1)}, f32[8,128]{1,0:T(8,128)S(1)}, f32[8,128]{1,0:T(8,128)S(1)}) custom-call(f32[8,128]{1,0:T(8,128)S(1)} %get-tuple-element.39.refs_0_.refs_2_, bf16[1056,128]{1,0:T(8,128)(2,1)S(1)} %get-tuple-element.43.refs_1_, ...), custom_call_target="tpu_custom_call" | custom-call | flops 524288 | bytes 2146304 | tf_op jit(solution)/shard_map/pallas_call | solution.py:687
  30.8 1.8 %collective-permute-start.6 = (f32[8,128]{1,0:T(8,128)S(1)}, f32[8,128]{1,0:T(8,128)S(1)}, u32[]{:S(2)}, u32[]{:S(2)}) collective-permute-start(f32[8,128]{1,0:T(8,128)S(1)} %get-tuple-element.47), channel_id=1, source_target_pairs={{0,1},{1,0},{2,3},{3,2},{4,5},{5,4},{6,7},{7,6},{8,9},{9,8},{10,11... | collective-permute-start | bytes 12296 | tf_op jit(solution)/shard_map/ppermute | solution.py:789
  32.5 1.2 %collective-permute-done.8 = f32[8,128]{1,0:T(8,128)S(1)} collective-permute-done((f32[8,128]{1,0:T(8,128)S(1)}, f32[8,128]{1,0:T(8,128)S(1)}, u32[]{:S(2)}, u32[]{:S(2)}) %collective-permute-start.8) | collective-permute-done | bytes 4128 | tf_op jit(solution)/shard_map/ppermute | solution.py:789
  33.7 0.7 %collective-permute-done.7 = f32[8,128]{1,0:T(8,128)S(1)} collective-permute-done((f32[8,128]{1,0:T(8,128)S(1)}, f32[8,128]{1,0:T(8,128)S(1)}, u32[]{:S(2)}, u32[]{:S(2)}) %collective-permute-start.7) | collective-permute-done | bytes 4128 | tf_op jit(solution)/shard_map/ppermute | solution.py:789
  34.4 0.8 %shard_map.91 = (bf16[1088,128]{1,0:T(8,128)(2,1)S(1)}, bf16[1088,128]{1,0:T(8,128)(2,1)S(1)}, bf16[1088,128]{1,0:T(8,128)(2,1)S(1)}, bf16[1024,128]{1,0:T(8,128...) custom-call(bf16[128,1024]{1,0:T(8,128)(2,1)S(1)} %collective-permut, ...), custom_call_target="tpu_custom_call" | custom-call | tf_op jit(solution)/shard_map/pallas_call | solution.py:687
  35.2 1.7 %collective-permute-start.11 = (bf16[1088,128]{1,0:T(8,128)(2,1)S(1)}, bf16[1088,128]{1,0:T(8,128)(2,1)S(1)}, u32[]{:S(2)}, u32[]{:S(2)}) collective-permute-start(bf16[1088,128]{1,0:T(8,128)(2,1)S(1)} %get-tuple-element.63), channel_id=1, source_target_pairs={{0,8},{1,9},{2,0},{3,1},{4,12},{5,13},{6,4},{7,5},{8,16},{9,17},{1... | collective-permute-start | bytes 835592 | tf_op jit(solution)/shard_map/ppermute | solution.py:723
  37.2 2.1 %collective-permute-start.13 = (bf16[1088,128]{1,0:T(8,128)(2,1)S(1)}, bf16[1088,128]{1,0:T(8,128)(2,1)S(1)}, u32[]{:S(2)}, u32[]{:S(2)}) collective-permute-start(bf16[1088,128]{1,0:T(8,128)(2,1)S(1)} %get-tuple-element.65), channel_id=1, source_target_pairs={{0,4},{4,0},{8,12},{12,8},{16,20},{20,16},{24,28},{28,24},{1,5},{5... | collective-permute-start | bytes 835592 | tf_op jit(solution)/shard_map/ppermute | solution.py:728
  39.6 3.0 %shard_map.92 = (bf16[128,1024]{1,0:T(8,128)(2,1)}, f32[128,1024]{1,0:T(8,128)S(1)}, f32[128,1024]{1,0:T(8,128)S(1)}, f32[128,1024]{1,0:T(8,128)S(1)}) custom-call(f32[8,128]{1,0:T(8,128)S(1)} %get-tuple-element.39.refs_0_.refs_2_, f32[8,128]{1,0:T(8,128)S(1)} %add_add_fusion.refs_3_.refs_1_, bf16[128,1024]{1,0:T(8,128)(2,1)S(1)} %copy-done, ...), custom_call_target="tpu_custom_call" | custom-call | tf_op jit(solution)/shard_map/pallas_call | solution.py:687
  42.6 0.6 %collective-permute-done.11.refs_3_ = bf16[1088,128]{1,0:T(8,128)(2,1)S(1)} collective-permute-done((bf16[1088,128]{1,0:T(8,128)(2,1)S(1)}, bf16[1088,128]{1,0:T(8,128)(2,1)S(1)}, u32[]{:S(2)}, u32[]{:S(2)}) %collective-permute-start.11) | collective-permute-done | bytes 278560 | tf_op jit(solution)/shard_map/ppermute | solution.py:723
  43.2 1.4 %collective-permute-done.12.refs_4_ = bf16[1088,128]{1,0:T(8,128)(2,1)S(1)} collective-permute-done((bf16[1088,128]{1,0:T(8,128)(2,1)S(1)}, bf16[1088,128]{1,0:T(8,128)(2,1)S(1)}, u32[]{:S(2)}, u32[]{:S(2)}) %collective-permute-start.12) | collective-permute-done | bytes 278560 | tf_op jit(solution)/shard_map/ppermute | solution.py:723
  45.0 1.6 %shard_map.94 = (bf16[128,1024]{1,0:T(8,128)(2,1)}, bf16[128,1024]{1,0:T(8,128)(2,1)}, bf16[128,1024]{1,0:T(8,128)(2,1)}) custom-call(f32[2,1024,128]{2,1,0:T(8,128)S(1)} %shard_map.93.refs_0_, bf16[128,1024]{1,0:T(8,128)(2,1)S(1)} %collective-permute-done.10.refs_1_.refs_2_, bf16[128,1024]{1,0:T(8,128)(2,1)S(1)} %collective-permute-done.9.refs_0_.refs_3_.refs_2_, ...), custom_call_target="tpu_custom_call" | custom-call | flops 201326592 | bytes 5029888 | tf_op jit(solution)/shard_map/pallas_call | solution.py:687
  (26 shorter events, 2.2 us)
Async XLA Ops:
  0.6 6.4 %copy-start.2 = (bf16[128,1024]{1,0:T(8,128)(2,1)S(1)}, bf16[128,1024]{1,0:T(8,128)(2,1)}, u32[]{:S(2)}) copy-start(bf16[128,1024]{1,0:T(8,128)(2,1)} %refs_6_.1) | copy-start | bytes 786436
  0.6 4.5 %copy-start.1 = (bf16[128,1024]{1,0:T(8,128)(2,1)S(1)}, bf16[128,1024]{1,0:T(8,128)(2,1)}, u32[]{:S(2)}) copy-start(bf16[128,1024]{1,0:T(8,128)(2,1)} %refs_1_.7) | copy-start | bytes 786436
  0.7 6.5 %copy-start = (bf16[128,1024]{1,0:T(8,128)(2,1)S(1)}, bf16[128,1024]{1,0:T(8,128)(2,1)}, u32[]{:S(2)}) copy-start(bf16[128,1024]{1,0:T(8,128)(2,1)} %refs_2_.5) | copy-start | bytes 786436
  0.7 6.5 %copy-start.3 = (bf16[128,1024]{1,0:T(8,128)(2,1)S(1)}, bf16[128,1024]{1,0:T(8,128)(2,1)}, u32[]{:S(2)}) copy-start(bf16[128,1024]{1,0:T(8,128)(2,1)} %refs_5_.1) | copy-start | bytes 786436
  2.0 16.5 %collective-permute-start.1 = (bf16[256,1024]{1,0:T(8,128)(2,1)S(1)}, bf16[256,1024]{1,0:T(8,128)(2,1)S(1)}, u32[]{:S(2)}, u32[]{:S(2)}) collective-permute-start(bf16[256,1024]{1,0:T(8,128)(2,1)S(1)} %get-tuple-element.40), channel_id=1, source_target_pairs={{8,0},{9,1},{0,2},{1,3},{12,4},{13,5},{4,6},{5,7},{16,8},{17,9},{2... | collective-permute-start | bytes 1572872 | tf_op jit(solution)/shard_map/ppermute | solution.py:723
  5.0 13.5 %collective-permute-start = (bf16[256,1024]{1,0:T(8,128)(2,1)S(1)}, bf16[256,1024]{1,0:T(8,128)(2,1)S(1)}, u32[]{:S(2)}, u32[]{:S(2)}) collective-permute-start(bf16[256,1024]{1,0:T(8,128)(2,1)S(1)} %get-tuple-element.38.refs_0_), channel_id=1, source_target_pairs={{0,8},{1,9},{2,0},{3,1},{4,12},{5,13},{6,4},{7,5},{8,16},{9,17},{1... | collective-permute-start | bytes 1572872 | tf_op jit(solution)/shard_map/ppermute | solution.py:723
  5.1 9.2 %collective-permute-start.2 = (bf16[128,1024]{1,0:T(8,128)(2,1)S(1)}, bf16[128,1024]{1,0:T(8,128)(2,1)S(1)}, u32[]{:S(2)}, u32[]{:S(2)}) collective-permute-start(bf16[128,1024]{1,0:T(8,128)(2,1)S(1)} %copy-done.1), channel_id=1, source_target_pairs={{0,4},{4,0},{8,12},{12,8},{16,20},{20,16},{24,28},{28,24},{1,5},{5... | collective-permute-start | bytes 786440 | tf_op jit(solution)/shard_map/ppermute | solution.py:728
  7.0 11.5 %collective-permute-start.3 = (bf16[128,1024]{1,0:T(8,128)(2,1)S(1)}, bf16[128,1024]{1,0:T(8,128)(2,1)S(1)}, u32[]{:S(2)}, u32[]{:S(2)}) collective-permute-start(bf16[128,1024]{1,0:T(8,128)(2,1)S(1)} %copy-done.2), channel_id=1, source_target_pairs={{0,4},{4,0},{8,12},{12,8},{16,20},{20,16},{24,28},{28,24},{1,5},{5... | collective-permute-start | bytes 786440 | tf_op jit(solution)/shard_map/ppermute | solution.py:728
  7.2 0.7 %copy-start.4 = (s32[8,8]{1,0:T(8,128)S(1)}, s32[8,8]{1,0:T(8,128)}, u32[]{:S(2)}) copy-start(s32[8,8]{1,0:T(8,128)} %refs_1_.5) | copy-start | bytes 772
  19.7 7.1 %collective-permute-start.4 = (bf16[1056,128]{1,0:T(8,128)(2,1)S(1)}, bf16[1056,128]{1,0:T(8,128)(2,1)S(1)}, u32[]{:S(2)}, u32[]{:S(2)}) collective-permute-start(bf16[1056,128]{1,0:T(8,128)(2,1)S(1)} %get-tuple-element.43.refs_1_), channel_id=1, source_target_pairs={{0,8},{1,9},{2,0},{3,1},{4,12},{5,13},{6,4},{7,5},{8,16},{9,17},{1... | collective-permute-start | bytes 811016 | tf_op jit(solution)/shard_map/ppermute | solution.py:723
  21.4 8.7 %collective-permute-start.5 = (bf16[1056,128]{1,0:T(8,128)(2,1)S(1)}, bf16[1056,128]{1,0:T(8,128)(2,1)S(1)}, u32[]{:S(2)}, u32[]{:S(2)}) collective-permute-start(bf16[1056,128]{1,0:T(8,128)(2,1)S(1)} %get-tuple-element.44.refs_2_), channel_id=1, source_target_pairs={{8,0},{9,1},{0,2},{1,3},{12,4},{13,5},{4,6},{5,7},{16,8},{17,9},{2... | collective-permute-start | bytes 811016 | tf_op jit(solution)/shard_map/ppermute | solution.py:723
  21.9 12.5 %collective-permute-start.9 = (bf16[128,1024]{1,0:T(8,128)(2,1)S(1)}, bf16[128,1024]{1,0:T(8,128)(2,1)S(1)}, u32[]{:S(2)}, u32[]{:S(2)}) collective-permute-start(bf16[128,1024]{1,0:T(8,128)(2,1)S(1)} %shard_map.89), channel_id=1, source_target_pairs={{0,4},{4,0},{8,12},{12,8},{16,20},{20,16},{24,28},{28,24},{1,5},{5... | collective-permute-start | bytes 786440 | tf_op jit(solution)/shard_map/ppermute | solution.py:728
  23.6 10.8 %collective-permute-start.10 = (bf16[128,1024]{1,0:T(8,128)(2,1)S(1)}, bf16[128,1024]{1,0:T(8,128)(2,1)S(1)}, u32[]{:S(2)}, u32[]{:S(2)}) collective-permute-start(bf16[128,1024]{1,0:T(8,128)(2,1)S(1)} %shard_map.90), channel_id=1, source_target_pairs={{8,0},{12,4},{16,8},{20,12},{9,1},{13,5},{17,9},{21,13},{10,2},{14... | collective-permute-start | bytes 786440 | tf_op jit(solution)/shard_map/ppermute | solution.py:778
  30.6 3.1 %collective-permute-start.8 = (f32[8,128]{1,0:T(8,128)S(1)}, f32[8,128]{1,0:T(8,128)S(1)}, u32[]{:S(2)}, u32[]{:S(2)}) collective-permute-start(f32[8,128]{1,0:T(8,128)S(1)} %get-tuple-element.47), channel_id=1, source_target_pairs={{0,3},{1,2},{2,1},{3,0},{4,7},{5,6},{6,5},{7,4},{8,11},{9,10},{10,... | collective-permute-start | bytes 12296 | tf_op jit(solution)/shard_map/ppermute | solution.py:789
  30.7 3.7 %collective-permute-start.7 = (f32[8,128]{1,0:T(8,128)S(1)}, f32[8,128]{1,0:T(8,128)S(1)}, u32[]{:S(2)}, u32[]{:S(2)}) collective-permute-start(f32[8,128]{1,0:T(8,128)S(1)} %get-tuple-element.47), channel_id=1, source_target_pairs={{0,2},{1,3},{2,0},{3,1},{4,6},{5,7},{6,4},{7,5},{8,10},{9,11},{10,... | collective-permute-start | bytes 12296 | tf_op jit(solution)/shard_map/ppermute | solution.py:789
  30.8 3.6 %collective-permute-start.6 = (f32[8,128]{1,0:T(8,128)S(1)}, f32[8,128]{1,0:T(8,128)S(1)}, u32[]{:S(2)}, u32[]{:S(2)}) collective-permute-start(f32[8,128]{1,0:T(8,128)S(1)} %get-tuple-element.47), channel_id=1, source_target_pairs={{0,1},{1,0},{2,3},{3,2},{4,5},{5,4},{6,7},{7,6},{8,9},{9,8},{10,11... | collective-permute-start | bytes 12296 | tf_op jit(solution)/shard_map/ppermute | solution.py:789
  35.2 8.1 %collective-permute-start.11 = (bf16[1088,128]{1,0:T(8,128)(2,1)S(1)}, bf16[1088,128]{1,0:T(8,128)(2,1)S(1)}, u32[]{:S(2)}, u32[]{:S(2)}) collective-permute-start(bf16[1088,128]{1,0:T(8,128)(2,1)S(1)} %get-tuple-element.63), channel_id=1, source_target_pairs={{0,8},{1,9},{2,0},{3,1},{4,12},{5,13},{6,4},{7,5},{8,16},{9,17},{1... | collective-permute-start | bytes 835592 | tf_op jit(solution)/shard_map/ppermute | solution.py:723
  36.9 7.7 %collective-permute-start.12 = (bf16[1088,128]{1,0:T(8,128)(2,1)S(1)}, bf16[1088,128]{1,0:T(8,128)(2,1)S(1)}, u32[]{:S(2)}, u32[]{:S(2)}) collective-permute-start(bf16[1088,128]{1,0:T(8,128)(2,1)S(1)} %get-tuple-element.64), channel_id=1, source_target_pairs={{8,0},{9,1},{0,2},{1,3},{12,4},{13,5},{4,6},{5,7},{16,8},{17,9},{2... | collective-permute-start | bytes 835592 | tf_op jit(solution)/shard_map/ppermute | solution.py:723
  37.2 7.8 %collective-permute-start.13 = (bf16[1088,128]{1,0:T(8,128)(2,1)S(1)}, bf16[1088,128]{1,0:T(8,128)(2,1)S(1)}, u32[]{:S(2)}, u32[]{:S(2)}) collective-permute-start(bf16[1088,128]{1,0:T(8,128)(2,1)S(1)} %get-tuple-element.65), channel_id=1, source_target_pairs={{0,4},{4,0},{8,12},{12,8},{16,20},{20,16},{24,28},{28,24},{1,5},{5... | collective-permute-start | bytes 835592 | tf_op jit(solution)/shard_map/ppermute | solution.py:728

commit v11 on v10

--- a/solution.py
+++ b/solution.py
@@ -774,7 +774,7 @@
         side_queries_kernel, heads, (), (queries, *received), (flat,), 0, after=(mn,)
     )
     side_queries = swap(side_queries)
-    (far_queries,) = call(relay_kernel, heads, (), received, (flat,), 0, after=(mn,))
+    (far_queries,) = call(relay_kernel, heads, (), received, (flat,), 0, after=(down_in,))
     far_queries = lax.ppermute(far_queries, "ctx", [(i, i - 2) for i in range(2, blocks - 2)])
     (upstream_zt,) = call(transpose_kernel, heads, (), received, (flat_t,), 0, after=(mn,))
     attention, attention_z, lse, lse_z, sums = call(
@@ -798,10 +798,10 @@
         + (ez, ex, mz, mx),
         (longer, longer, longer, flat_t, flat_t, flat_t, rows, rows),
         0,
-        after=(side_queries, far_queries),
+        after=(side_queries,),
     )
     returned = cycle(up_out, down_out)
-    side_grads = swap(side_out)
+    side_grads = swap(lax.optimization_barrier((side_out, far_queries))[0])
     normed, dq_own, dk_own, dv_own = call(
         local_back_kernel,
         heads,

time: 46.9 us -> 46.8 us (level)
    ppermute x3, starting transfers between devices: 3.74 us -> 4.71 us  [cycle(): lax.ppermute(down_array, ('ctx', 'head'), falling)]
    ppermute x3, waiting for transfers between devices: 4.72 us -> 5.43 us  [cycle(): lax.ppermute(down_array, ('ctx', 'head'), falling)]
    ppermute x4, starting transfers between devices: 5.75 us -> 5.05 us  [swap(): return lax.ppermute(array, 'ctx', [(i, i ^ 1) for i in range(blocks)])]
  transfers between devices with their start and end apart: 14 -> 14, of which waited for: 9 -> 7; matrix products, arithmetic and copies ran while one was open for 0% -> 0% of each run, Pallas kernels for 14% -> 16%
where the time goes in v11:
time: 46.8 us; the launch traced here: 46.6 us
  waiting for transfers between devices  17.6 us (38%)
  starting transfers between devices  16.2 us (35%)
  Pallas kernels  11.4 us (24%)
  between operations  0.76 us (2%)
  local copies, waits for them, and re-layouts  0.7 us (1%)
    pallas_call x11, Pallas kernels, call(): pl.pallas_call(lambda *refs: kernel(heads, *refs[len(after):]), out_shape...  11.4 us
    ppermute x4, waiting for transfers between devices, swap(): return lax.ppermute(array, 'ctx', [(i, i ^ 1) for i in range(blocks)])  8.3 us
    ppermute x3, waiting for transfers between devices, cycle(): lax.ppermute(down_array, ('ctx', 'head'), falling)  5.43 us
    ppermute x4, starting transfers between devices, swap(): return lax.ppermute(array, 'ctx', [(i, i ^ 1) for i in range(blocks)])  5.05 us
    ppermute x3, starting transfers between devices, cycle(): lax.ppermute(down_array, ('ctx', 'head'), falling)  4.71 us
    ppermute x3, starting transfers between devices, cycle(): lax.ppermute(up_array, ('ctx', 'head'), rising)  3.21 us
    ppermute x3, waiting for transfers between devices, cycle(): lax.ppermute(up_array, ('ctx', 'head'), rising)  2.02 us
    ppermute x3, starting transfers between devices, meeting_shards(): lax.ppermute(sums, 'head', [(i, i ^ step) for i in range(members)])  1.92 us
  transfers between devices with their start and end apart: 14, of which 7 were waited for; matrix products, arithmetic and copies ran while one was open for 0% of the time, Pallas kernels for 16%

profile of v11, /device:TPU:0, one launch (start us, length us, event | category | flops | bytes accessed | tf_op | source)
XLA Modules:
  0.0 46.6 jit_solution(6231386176656386671)
XLA Ops:
  0.7 1.3 %shard_map.84 = (bf16[256,1024]{1,0:T(8,128)(2,1)S(1)}, bf16[256,1024]{1,0:T(8,128)(2,1)S(1)}) custom-call(bf16[128,1024]{1,0:T(8,128)(2,1)} %refs_2_.5, bf16[128,1024]{1,0:T(8,128)(2,1)} %refs_1_.7, bf16[128,1024]{1,0:T(8,128)(2,1)} %refs_6_.1, bf16[128,1024]{1,0:T(8,128)(2,1)} %refs_5_.1), custom_call_target="tpu_custom_call" | custom-call | tf_op jit(solution)/shard_map/pallas_call | solution.py:687
  2.0 3.0 %collective-permute-start.1 = (bf16[256,1024]{1,0:T(8,128)(2,1)S(1)}, bf16[256,1024]{1,0:T(8,128)(2,1)S(1)}, u32[]{:S(2)}, u32[]{:S(2)}) collective-permute-start(bf16[256,1024]{1,0:T(8,128)(2,1)S(1)} %get-tuple-element.41), channel_id=1, source_target_pairs={{8,0},{9,1},{0,2},{1,3},{12,4},{13,5},{4,6},{5,7},{16,8},{17,9},{2... | collective-permute-start | bytes 1572872 | tf_op jit(solution)/shard_map/ppermute | solution.py:723
  5.1 1.9 %collective-permute-start.2 = (bf16[128,1024]{1,0:T(8,128)(2,1)S(1)}, bf16[128,1024]{1,0:T(8,128)(2,1)S(1)}, u32[]{:S(2)}, u32[]{:S(2)}) collective-permute-start(bf16[128,1024]{1,0:T(8,128)(2,1)S(1)} %copy-done.1), channel_id=1, source_target_pairs={{0,4},{4,0},{8,12},{12,8},{16,20},{20,16},{24,28},{28,24},{1,5},{5... | collective-permute-start | bytes 786440 | tf_op jit(solution)/shard_map/ppermute | solution.py:728
  7.2 0.7 %copy-done.4 = s32[8,8]{1,0:T(8,128)S(1)} copy-done((s32[8,8]{1,0:T(8,128)S(1)}, s32[8,8]{1,0:T(8,128)}, u32[]{:S(2)}) %copy-start.4) | copy-done | bytes 280
  7.9 2.4 %shard_map.85 = (f32[1024,128]{1,0:T(8,128)S(1)}, f32[8,128]{1,0:T(8,128)S(1)}, bf16[1024,128]{1,0:T(8,128)(2,1)S(1)}, f32[8,128]{1,0:T(8,128)S(1)}) custom-call(bf16[256,1024]{1,0:T(8,128)(2,1)S(1)} %get-tuple-element.39.refs_0_, s32[8,8]{1,0:T(8,128)S(1)} %copy-done.4, bf16[128,1024]{1,0:T(8,128)(2,1)S(1)} %copy-done, bf16[128,1024]{1,0:T(8,128)(2,1)S(1)} %copy-done.1, ...), custom_call_target="tpu_custom_call" | custom-call | flops 100663296 | bytes 1843200 | tf_op jit(solution)/shard_map/pallas_call | solution.py:687
  10.2 4.1 %collective-permute-done.2.refs_4_.refs_11_.refs_15_ = bf16[128,1024]{1,0:T(8,128)(2,1)S(1)} collective-permute-done((bf16[128,1024]{1,0:T(8,128)(2,1)S(1)}, bf16[128,1024]{1,0:T(8,128)(2,1)S(1)}, u32[]{:S(2)}, u32[]{:S(2)}) %collective-permute-start.2) | collective-permute-done | bytes 262176 | tf_op jit(solution)/shard_map/ppermute | solution.py:728
  14.4 4.2 %collective-permute-done.3.refs_5_.refs_12_ = bf16[128,1024]{1,0:T(8,128)(2,1)S(1)} collective-permute-done((bf16[128,1024]{1,0:T(8,128)(2,1)S(1)}, bf16[128,1024]{1,0:T(8,128)(2,1)S(1)}, u32[]{:S(2)}, u32[]{:S(2)}) %collective-permute-start.3) | collective-permute-done | bytes 262176 | tf_op jit(solution)/shard_map/ppermute | solution.py:728
  18.5 1.1 %shard_map.86 = (bf16[1056,128]{1,0:T(8,128)(2,1)S(1)}, bf16[1056,128]{1,0:T(8,128)(2,1)S(1)}, f32[1024,128]{1,0:T(8,128)S(1)}, f32[1024,128]{1,0:T(8,128)S(1)},...) custom-call(f32[8,128]{1,0:T(8,128)S(1)} %get-tuple-element.40.refs_0_.refs_1_, ...), custom_call_target="tpu_custom_call" | custom-call | flops 201326592 | bytes 4493312 | tf_op jit(solution)/shard_map/pallas_call | solution.py:687
  19.7 1.7 %collective-permute-start.5 = (bf16[1056,128]{1,0:T(8,128)(2,1)S(1)}, bf16[1056,128]{1,0:T(8,128)(2,1)S(1)}, u32[]{:S(2)}, u32[]{:S(2)}) collective-permute-start(bf16[1056,128]{1,0:T(8,128)(2,1)S(1)} %get-tuple-element.45.refs_2_), channel_id=1, source_target_pairs={{8,0},{9,1},{0,2},{1,3},{12,4},{13,5},{4,6},{5,7},{16,8},{17,9},{2... | collective-permute-start | bytes 811016 | tf_op jit(solution)/shard_map/ppermute | solution.py:723
  21.3 0.4 collective-permute-start.4
  21.9 1.7 %collective-permute-start.9 = (bf16[128,1024]{1,0:T(8,128)(2,1)S(1)}, bf16[128,1024]{1,0:T(8,128)(2,1)S(1)}, u32[]{:S(2)}, u32[]{:S(2)}) collective-permute-start(bf16[128,1024]{1,0:T(8,128)(2,1)S(1)} %shard_map.89), channel_id=1, source_target_pairs={{0,4},{4,0},{8,12},{12,8},{16,20},{20,16},{24,28},{28,24},{1,5},{5... | collective-permute-start | bytes 786440 | tf_op jit(solution)/shard_map/ppermute | solution.py:728
  23.5 3.2 %collective-permute-done.5.refs_4_.refs_0_ = bf16[1056,128]{1,0:T(8,128)(2,1)S(1)} collective-permute-done((bf16[1056,128]{1,0:T(8,128)(2,1)S(1)}, bf16[1056,128]{1,0:T(8,128)(2,1)S(1)}, u32[]{:S(2)}, u32[]{:S(2)}) %collective-permute-start.5) | collective-permute-done | bytes 270368 | tf_op jit(solution)/shard_map/ppermute | solution.py:723
  26.8 1.3 %collective-permute-start.10 = (bf16[128,1024]{1,0:T(8,128)(2,1)S(1)}, bf16[128,1024]{1,0:T(8,128)(2,1)S(1)}, u32[]{:S(2)}, u32[]{:S(2)}) collective-permute-start(bf16[128,1024]{1,0:T(8,128)(2,1)S(1)} %shard_map.92), channel_id=1, source_target_pairs={{8,0},{12,4},{16,8},{20,12},{9,1},{13,5},{17,9},{21,13},{10,2},{14... | collective-permute-start | bytes 786440 | tf_op jit(solution)/shard_map/ppermute | solution.py:778
  28.3 0.5 %shard_map.88 = (bf16[1024,128]{1,0:T(8,128)(2,1)S(1)}, bf16[1024,128]{1,0:T(8,128)(2,1)S(1)}, f32[8,128]{1,0:T(8,128)S(1)}, f32[8,128]{1,0:T(8,128)S(1)}, f32[8,128]{1,0:T(8,128)S(1)}) custom-call(f32[8,128]{1,0:T(8,128)S(1)} %get-tuple-element.40.refs_0_.refs_1_, bf16[1056,128]{1,0:T(8,128)(2,1)S(1)} %get-tuple-element.44.refs_1_, ...), custom_call_target="tpu_custom_call" | custom-call | flops 524288 | bytes 2146304 | tf_op jit(solution)/shard_map/pallas_call | solution.py:687
  28.9 1.5 %collective-permute-start.7 = (f32[8,128]{1,0:T(8,128)S(1)}, f32[8,128]{1,0:T(8,128)S(1)}, u32[]{:S(2)}, u32[]{:S(2)}) collective-permute-start(f32[8,128]{1,0:T(8,128)S(1)} %get-tuple-element.48), channel_id=1, source_target_pairs={{0,2},{1,3},{2,0},{3,1},{4,6},{5,7},{6,4},{7,5},{8,10},{9,11},{10,... | collective-permute-start | bytes 12296 | tf_op jit(solution)/shard_map/ppermute | solution.py:789
  30.7 1.2 %collective-permute-done.8 = f32[8,128]{1,0:T(8,128)S(1)} collective-permute-done((f32[8,128]{1,0:T(8,128)S(1)}, f32[8,128]{1,0:T(8,128)S(1)}, u32[]{:S(2)}, u32[]{:S(2)}) %collective-permute-start.8) | collective-permute-done | bytes 4128 | tf_op jit(solution)/shard_map/ppermute | solution.py:789
  31.9 0.6 %collective-permute-done.7 = f32[8,128]{1,0:T(8,128)S(1)} collective-permute-done((f32[8,128]{1,0:T(8,128)S(1)}, f32[8,128]{1,0:T(8,128)S(1)}, u32[]{:S(2)}, u32[]{:S(2)}) %collective-permute-start.7) | collective-permute-done | bytes 4128 | tf_op jit(solution)/shard_map/ppermute | solution.py:789
  32.6 0.8 %shard_map.90 = (bf16[1088,128]{1,0:T(8,128)(2,1)S(1)}, bf16[1088,128]{1,0:T(8,128)(2,1)S(1)}, bf16[1088,128]{1,0:T(8,128)(2,1)S(1)}, bf16[1024,128]{1,0:T(8,128...) custom-call(bf16[128,1024]{1,0:T(8,128)(2,1)S(1)} %collective-permut, ...), custom_call_target="tpu_custom_call" | custom-call | tf_op jit(solution)/shard_map/pallas_call | solution.py:687
  33.3 2.7 %collective-permute-start.11 = (bf16[1088,128]{1,0:T(8,128)(2,1)S(1)}, bf16[1088,128]{1,0:T(8,128)(2,1)S(1)}, u32[]{:S(2)}, u32[]{:S(2)}) collective-permute-start(bf16[1088,128]{1,0:T(8,128)(2,1)S(1)} %get-tuple-element.64), channel_id=1, source_target_pairs={{0,8},{1,9},{2,0},{3,1},{4,12},{5,13},{6,4},{7,5},{8,16},{9,17},{1... | collective-permute-start | bytes 835592 | tf_op jit(solution)/shard_map/ppermute | solution.py:723
  36.0 1.4 %collective-permute-start.13 = (bf16[1088,128]{1,0:T(8,128)(2,1)S(1)}, bf16[1088,128]{1,0:T(8,128)(2,1)S(1)}, u32[]{:S(2)}, u32[]{:S(2)}) collective-permute-start(bf16[1088,128]{1,0:T(8,128)(2,1)S(1)} %get-tuple-element.67), channel_id=1, source_target_pairs={{0,4},{4,0},{8,12},{12,8},{16,20},{20,16},{24,28},{28,24},{1,5},{5... | collective-permute-start | bytes 835592 | tf_op jit(solution)/shard_map/ppermute | solution.py:728
  37.4 3.0 %shard_map.91 = (bf16[128,1024]{1,0:T(8,128)(2,1)}, f32[128,1024]{1,0:T(8,128)S(1)}, f32[128,1024]{1,0:T(8,128)S(1)}, f32[128,1024]{1,0:T(8,128)S(1)}) custom-call(f32[8,128]{1,0:T(8,128)S(1)} %get-tuple-element.40.refs_0_.refs_1_, f32[8,128]{1,0:T(8,128)S(1)} %add_add_fusion.refs_2_.refs_1_, bf16[128,1024]{1,0:T(8,128)(2,1)S(1)} %copy-done, ...), custom_call_target="tpu_custom_call" | custom-call | tf_op jit(solution)/shard_map/pallas_call | solution.py:687
  40.7 2.0 %collective-permute-done.11.refs_3_ = bf16[1088,128]{1,0:T(8,128)(2,1)S(1)} collective-permute-done((bf16[1088,128]{1,0:T(8,128)(2,1)S(1)}, bf16[1088,128]{1,0:T(8,128)(2,1)S(1)}, u32[]{:S(2)}, u32[]{:S(2)}) %collective-permute-start.11) | collective-permute-done | bytes 278560 | tf_op jit(solution)/shard_map/ppermute | solution.py:723
  42.7 2.2 %collective-permute-done.12.refs_4_ = bf16[1088,128]{1,0:T(8,128)(2,1)S(1)} collective-permute-done((bf16[1088,128]{1,0:T(8,128)(2,1)S(1)}, bf16[1088,128]{1,0:T(8,128)(2,1)S(1)}, u32[]{:S(2)}, u32[]{:S(2)}) %collective-permute-start.12) | collective-permute-done | bytes 278560 | tf_op jit(solution)/shard_map/ppermute | solution.py:723
  45.0 1.6 %shard_map.94 = (bf16[128,1024]{1,0:T(8,128)(2,1)}, bf16[128,1024]{1,0:T(8,128)(2,1)}, bf16[128,1024]{1,0:T(8,128)(2,1)}) custom-call(f32[2,1024,128]{2,1,0:T(8,128)S(1)} %shard_map.93.refs_0_, bf16[128,1024]{1,0:T(8,128)(2,1)S(1)} %collective-permute-done.10.refs_2_.refs_1_, bf16[128,1024]{1,0:T(8,128)(2,1)S(1)} %collective-permute-done.9.refs_0_.refs_3_.refs_2_, ...), custom_call_target="tpu_custom_call" | custom-call | flops 201326592 | bytes 5029888 | tf_op jit(solution)/shard_map/pallas_call | solution.py:687
  (26 shorter events, 1.3 us)
Async XLA Ops:
  0.6 6.4 %copy-start.2 = (bf16[128,1024]{1,0:T(8,128)(2,1)S(1)}, bf16[128,1024]{1,0:T(8,128)(2,1)}, u32[]{:S(2)}) copy-start(bf16[128,1024]{1,0:T(8,128)(2,1)} %refs_6_.1) | copy-start | bytes 786436
  0.6 4.5 %copy-start.1 = (bf16[128,1024]{1,0:T(8,128)(2,1)S(1)}, bf16[128,1024]{1,0:T(8,128)(2,1)}, u32[]{:S(2)}) copy-start(bf16[128,1024]{1,0:T(8,128)(2,1)} %refs_1_.7) | copy-start | bytes 786436
  0.7 6.5 %copy-start = (bf16[128,1024]{1,0:T(8,128)(2,1)S(1)}, bf16[128,1024]{1,0:T(8,128)(2,1)}, u32[]{:S(2)}) copy-start(bf16[128,1024]{1,0:T(8,128)(2,1)} %refs_2_.5) | copy-start | bytes 786436
  0.7 6.5 %copy-start.3 = (bf16[128,1024]{1,0:T(8,128)(2,1)S(1)}, bf16[128,1024]{1,0:T(8,128)(2,1)}, u32[]{:S(2)}) copy-start(bf16[128,1024]{1,0:T(8,128)(2,1)} %refs_5_.1) | copy-start | bytes 786436
  2.0 16.5 %collective-permute-start.1 = (bf16[256,1024]{1,0:T(8,128)(2,1)S(1)}, bf16[256,1024]{1,0:T(8,128)(2,1)S(1)}, u32[]{:S(2)}, u32[]{:S(2)}) collective-permute-start(bf16[256,1024]{1,0:T(8,128)(2,1)S(1)} %get-tuple-element.41), channel_id=1, source_target_pairs={{8,0},{9,1},{0,2},{1,3},{12,4},{13,5},{4,6},{5,7},{16,8},{17,9},{2... | collective-permute-start | bytes 1572872 | tf_op jit(solution)/shard_map/ppermute | solution.py:723
  5.0 13.5 %collective-permute-start = (bf16[256,1024]{1,0:T(8,128)(2,1)S(1)}, bf16[256,1024]{1,0:T(8,128)(2,1)S(1)}, u32[]{:S(2)}, u32[]{:S(2)}) collective-permute-start(bf16[256,1024]{1,0:T(8,128)(2,1)S(1)} %get-tuple-element.39.refs_0_), channel_id=1, source_target_pairs={{0,8},{1,9},{2,0},{3,1},{4,12},{5,13},{6,4},{7,5},{8,16},{9,17},{1... | collective-permute-start | bytes 1572872 | tf_op jit(solution)/shard_map/ppermute | solution.py:723
  5.1 9.2 %collective-permute-start.2 = (bf16[128,1024]{1,0:T(8,128)(2,1)S(1)}, bf16[128,1024]{1,0:T(8,128)(2,1)S(1)}, u32[]{:S(2)}, u32[]{:S(2)}) collective-permute-start(bf16[128,1024]{1,0:T(8,128)(2,1)S(1)} %copy-done.1), channel_id=1, source_target_pairs={{0,4},{4,0},{8,12},{12,8},{16,20},{20,16},{24,28},{28,24},{1,5},{5... | collective-permute-start | bytes 786440 | tf_op jit(solution)/shard_map/ppermute | solution.py:728
  7.0 11.5 %collective-permute-start.3 = (bf16[128,1024]{1,0:T(8,128)(2,1)S(1)}, bf16[128,1024]{1,0:T(8,128)(2,1)S(1)}, u32[]{:S(2)}, u32[]{:S(2)}) collective-permute-start(bf16[128,1024]{1,0:T(8,128)(2,1)S(1)} %copy-done.2), channel_id=1, source_target_pairs={{0,4},{4,0},{8,12},{12,8},{16,20},{20,16},{24,28},{28,24},{1,5},{5... | collective-permute-start | bytes 786440 | tf_op jit(solution)/shard_map/ppermute | solution.py:728
  7.2 0.7 %copy-start.4 = (s32[8,8]{1,0:T(8,128)S(1)}, s32[8,8]{1,0:T(8,128)}, u32[]{:S(2)}) copy-start(s32[8,8]{1,0:T(8,128)} %refs_1_.5) | copy-start | bytes 772
  19.7 7.1 %collective-permute-start.5 = (bf16[1056,128]{1,0:T(8,128)(2,1)S(1)}, bf16[1056,128]{1,0:T(8,128)(2,1)S(1)}, u32[]{:S(2)}, u32[]{:S(2)}) collective-permute-start(bf16[1056,128]{1,0:T(8,128)(2,1)S(1)} %get-tuple-element.45.refs_2_), channel_id=1, source_target_pairs={{8,0},{9,1},{0,2},{1,3},{12,4},{13,5},{4,6},{5,7},{16,8},{17,9},{2... | collective-permute-start | bytes 811016 | tf_op jit(solution)/shard_map/ppermute | solution.py:723
  21.3 6.9 %collective-permute-start.4 = (bf16[1056,128]{1,0:T(8,128)(2,1)S(1)}, bf16[1056,128]{1,0:T(8,128)(2,1)S(1)}, u32[]{:S(2)}, u32[]{:S(2)}) collective-permute-start(bf16[1056,128]{1,0:T(8,128)(2,1)S(1)} %get-tuple-element.44.refs_1_), channel_id=1, source_target_pairs={{0,8},{1,9},{2,0},{3,1},{4,12},{5,13},{6,4},{7,5},{8,16},{9,17},{1... | collective-permute-start | bytes 811016 | tf_op jit(solution)/shard_map/ppermute | solution.py:723
  21.9 10.7 %collective-permute-start.9 = (bf16[128,1024]{1,0:T(8,128)(2,1)S(1)}, bf16[128,1024]{1,0:T(8,128)(2,1)S(1)}, u32[]{:S(2)}, u32[]{:S(2)}) collective-permute-start(bf16[128,1024]{1,0:T(8,128)(2,1)S(1)} %shard_map.89), channel_id=1, source_target_pairs={{0,4},{4,0},{8,12},{12,8},{16,20},{20,16},{24,28},{28,24},{1,5},{5... | collective-permute-start | bytes 786440 | tf_op jit(solution)/shard_map/ppermute | solution.py:728
  26.8 9.2 %collective-permute-start.10 = (bf16[128,1024]{1,0:T(8,128)(2,1)S(1)}, bf16[128,1024]{1,0:T(8,128)(2,1)S(1)}, u32[]{:S(2)}, u32[]{:S(2)}) collective-permute-start(bf16[128,1024]{1,0:T(8,128)(2,1)S(1)} %shard_map.92), channel_id=1, source_target_pairs={{8,0},{12,4},{16,8},{20,12},{9,1},{13,5},{17,9},{21,13},{10,2},{14... | collective-permute-start | bytes 786440 | tf_op jit(solution)/shard_map/ppermute | solution.py:778
  28.8 3.1 %collective-permute-start.8 = (f32[8,128]{1,0:T(8,128)S(1)}, f32[8,128]{1,0:T(8,128)S(1)}, u32[]{:S(2)}, u32[]{:S(2)}) collective-permute-start(f32[8,128]{1,0:T(8,128)S(1)} %get-tuple-element.48), channel_id=1, source_target_pairs={{0,3},{1,2},{2,1},{3,0},{4,7},{5,6},{6,5},{7,4},{8,11},{9,10},{10,... | collective-permute-start | bytes 12296 | tf_op jit(solution)/shard_map/ppermute | solution.py:789
  28.9 3.7 %collective-permute-start.7 = (f32[8,128]{1,0:T(8,128)S(1)}, f32[8,128]{1,0:T(8,128)S(1)}, u32[]{:S(2)}, u32[]{:S(2)}) collective-permute-start(f32[8,128]{1,0:T(8,128)S(1)} %get-tuple-element.48), channel_id=1, source_target_pairs={{0,2},{1,3},{2,0},{3,1},{4,6},{5,7},{6,4},{7,5},{8,10},{9,11},{10,... | collective-permute-start | bytes 12296 | tf_op jit(solution)/shard_map/ppermute | solution.py:789
  30.4 2.2 %collective-permute-start.6 = (f32[8,128]{1,0:T(8,128)S(1)}, f32[8,128]{1,0:T(8,128)S(1)}, u32[]{:S(2)}, u32[]{:S(2)}) collective-permute-start(f32[8,128]{1,0:T(8,128)S(1)} %get-tuple-element.48), channel_id=1, source_target_pairs={{0,1},{1,0},{2,3},{3,2},{4,5},{5,4},{6,7},{7,6},{8,9},{9,8},{10,11... | collective-permute-start | bytes 12296 | tf_op jit(solution)/shard_map/ppermute | solution.py:789
  33.3 9.4 %collective-permute-start.11 = (bf16[1088,128]{1,0:T(8,128)(2,1)S(1)}, bf16[1088,128]{1,0:T(8,128)(2,1)S(1)}, u32[]{:S(2)}, u32[]{:S(2)}) collective-permute-start(bf16[1088,128]{1,0:T(8,128)(2,1)S(1)} %get-tuple-element.64), channel_id=1, source_target_pairs={{0,8},{1,9},{2,0},{3,1},{4,12},{5,13},{6,4},{7,5},{8,16},{9,17},{1... | collective-permute-start | bytes 835592 | tf_op jit(solution)/shard_map/ppermute | solution.py:723
  36.0 8.9 %collective-permute-start.12 = (bf16[1088,128]{1,0:T(8,128)(2,1)S(1)}, bf16[1088,128]{1,0:T(8,128)(2,1)S(1)}, u32[]{:S(2)}, u32[]{:S(2)}) collective-permute-start(bf16[1088,128]{1,0:T(8,128)(2,1)S(1)} %get-tuple-element.65), channel_id=1, source_target_pairs={{8,0},{9,1},{0,2},{1,3},{12,4},{13,5},{4,6},{5,7},{16,8},{17,9},{2... | collective-permute-start | bytes 835592 | tf_op jit(solution)/shard_map/ppermute | solution.py:723
  36.0 8.9 %collective-permute-start.13 = (bf16[1088,128]{1,0:T(8,128)(2,1)S(1)}, bf16[1088,128]{1,0:T(8,128)(2,1)S(1)}, u32[]{:S(2)}, u32[]{:S(2)}) collective-permute-start(bf16[1088,128]{1,0:T(8,128)(2,1)S(1)} %get-tuple-element.67), channel_id=1, source_target_pairs={{0,4},{4,0},{8,12},{12,8},{16,20},{20,16},{24,28},{28,24},{1,5},{5... | collective-permute-start | bytes 835592 | tf_op jit(solution)/shard_map/ppermute | solution.py:728

commit v12 on v10

--- a/solution.py
+++ b/solution.py
@@ -418,8 +418,8 @@
     bias_ref,
     up_ref,
     down_ref,
+    down_in_ref,
     up_in_ref,
-    down_in_ref,
     ut_ref,
     uzt_ref,
     a_ref,
@@ -781,12 +781,12 @@
         merge_kernel,
         heads,
         (),
-        (bias, up_out, down_out, up_in, down_in, upstream_t, upstream_zt),
+        (bias, up_out, down_out, down_in, up_in, upstream_t, upstream_zt),
         (flat_t, flat_t, rows, rows, rows),
         unit // 64,
     )
     others = [
-        lax.ppermute(sums, "head", [(i, i ^ step) for i in range(members)]) for step in range(1, members)
+        lax.ppermute(sums, "head", [(i, i ^ step) for i in range(members)]) for step in (2, 1, 3)
     ]
     sums = functools.reduce(jnp.add, others, sums)
     longer = struct(width + 2 * TAIL, tokens)

time: 46.9 us -> 46.9 us (level)
  no operation moved by 1% of the time
where the time goes in v12:
time: 46.9 us; the launch traced here: 46.6 us
  waiting for transfers between devices  17.3 us (37%)
  starting transfers between devices  16.5 us (35%)
  Pallas kernels  11.4 us (24%)
  between operations  0.76 us (2%)
  local copies, waits for them, and re-layouts  0.7 us (1%)
    pallas_call x11, Pallas kernels, call(): pl.pallas_call(lambda *refs: kernel(heads, *refs[len(after):]), out_shape...  11.4 us
    ppermute x4, waiting for transfers between devices, swap(): return lax.ppermute(array, 'ctx', [(i, i ^ 1) for i in range(blocks)])  8.7 us
    ppermute x4, starting transfers between devices, swap(): return lax.ppermute(array, 'ctx', [(i, i ^ 1) for i in range(blocks)])  5.75 us
    ppermute x3, waiting for transfers between devices, cycle(): lax.ppermute(down_array, ('ctx', 'head'), falling)  4.72 us
    ppermute x3, starting transfers between devices, cycle(): lax.ppermute(down_array, ('ctx', 'head'), falling)  3.77 us
    ppermute x3, starting transfers between devices, cycle(): lax.ppermute(up_array, ('ctx', 'head'), rising)  3.55 us
    ppermute x3, waiting for transfers between devices, cycle(): lax.ppermute(up_array, ('ctx', 'head'), rising)  2.22 us
    ppermute x3, starting transfers between devices, meeting_shards(): lax.ppermute(sums, 'head', [(i, i ^ step) for i in range(members)])  2.19 us
  transfers between devices with their start and end apart: 14, of which 9 were waited for; matrix products, arithmetic and copies ran while one was open for 0% of the time, Pallas kernels for 14%

profile of v12, /device:TPU:0, one launch (start us, length us, event | category | flops | bytes accessed | tf_op | source)
XLA Modules:
  0.0 46.6 jit_solution(5759800651068772993)
XLA Ops:
  0.7 1.3 %shard_map.84 = (bf16[256,1024]{1,0:T(8,128)(2,1)S(1)}, bf16[256,1024]{1,0:T(8,128)(2,1)S(1)}) custom-call(bf16[128,1024]{1,0:T(8,128)(2,1)} %refs_2_.5, bf16[128,1024]{1,0:T(8,128)(2,1)} %refs_1_.7, bf16[128,1024]{1,0:T(8,128)(2,1)} %refs_6_.1, bf16[128,1024]{1,0:T(8,128)(2,1)} %refs_5_.1), custom_call_target="tpu_custom_call" | custom-call | tf_op jit(solution)/shard_map/pallas_call | solution.py:687
  2.0 3.0 %collective-permute-start.1 = (bf16[256,1024]{1,0:T(8,128)(2,1)S(1)}, bf16[256,1024]{1,0:T(8,128)(2,1)S(1)}, u32[]{:S(2)}, u32[]{:S(2)}) collective-permute-start(bf16[256,1024]{1,0:T(8,128)(2,1)S(1)} %get-tuple-element.40), channel_id=1, source_target_pairs={{8,0},{9,1},{0,2},{1,3},{12,4},{13,5},{4,6},{5,7},{16,8},{17,9},{2... | collective-permute-start | bytes 1572872 | tf_op jit(solution)/shard_map/ppermute | solution.py:723
  5.1 1.9 %collective-permute-start.2 = (bf16[128,1024]{1,0:T(8,128)(2,1)S(1)}, bf16[128,1024]{1,0:T(8,128)(2,1)S(1)}, u32[]{:S(2)}, u32[]{:S(2)}) collective-permute-start(bf16[128,1024]{1,0:T(8,128)(2,1)S(1)} %copy-done.1), channel_id=1, source_target_pairs={{0,4},{4,0},{8,12},{12,8},{16,20},{20,16},{24,28},{28,24},{1,5},{5... | collective-permute-start | bytes 786440 | tf_op jit(solution)/shard_map/ppermute | solution.py:728
  7.2 0.7 %copy-done.4 = s32[8,8]{1,0:T(8,128)S(1)} copy-done((s32[8,8]{1,0:T(8,128)S(1)}, s32[8,8]{1,0:T(8,128)}, u32[]{:S(2)}) %copy-start.4) | copy-done | bytes 280
  7.9 2.4 %shard_map.85 = (f32[1024,128]{1,0:T(8,128)S(1)}, f32[8,128]{1,0:T(8,128)S(1)}, bf16[1024,128]{1,0:T(8,128)(2,1)S(1)}, f32[8,128]{1,0:T(8,128)S(1)}) custom-call(bf16[256,1024]{1,0:T(8,128)(2,1)S(1)} %get-tuple-element.38.refs_0_, s32[8,8]{1,0:T(8,128)S(1)} %copy-done.4, bf16[128,1024]{1,0:T(8,128)(2,1)S(1)} %copy-done, bf16[128,1024]{1,0:T(8,128)(2,1)S(1)} %copy-done.1, ...), custom_call_target="tpu_custom_call" | custom-call | flops 100663296 | bytes 1843200 | tf_op jit(solution)/shard_map/pallas_call | solution.py:687
  10.2 4.1 %collective-permute-done.2.refs_4_.refs_12_.refs_15_ = bf16[128,1024]{1,0:T(8,128)(2,1)S(1)} collective-permute-done((bf16[128,1024]{1,0:T(8,128)(2,1)S(1)}, bf16[128,1024]{1,0:T(8,128)(2,1)S(1)}, u32[]{:S(2)}, u32[]{:S(2)}) %collective-permute-start.2) | collective-permute-done | bytes 262176 | tf_op jit(solution)/shard_map/ppermute | solution.py:728
  14.4 4.2 %collective-permute-done.3.refs_5_.refs_13_ = bf16[128,1024]{1,0:T(8,128)(2,1)S(1)} collective-permute-done((bf16[128,1024]{1,0:T(8,128)(2,1)S(1)}, bf16[128,1024]{1,0:T(8,128)(2,1)S(1)}, u32[]{:S(2)}, u32[]{:S(2)}) %collective-permute-start.3) | collective-permute-done | bytes 262176 | tf_op jit(solution)/shard_map/ppermute | solution.py:728
  18.5 1.1 %shard_map.86 = (bf16[1056,128]{1,0:T(8,128)(2,1)S(1)}, bf16[1056,128]{1,0:T(8,128)(2,1)S(1)}, f32[1024,128]{1,0:T(8,128)S(1)}, f32[1024,128]{1,0:T(8,128)S(1)},...) custom-call(f32[8,128]{1,0:T(8,128)S(1)} %get-tuple-element.39.refs_0_.refs_2_, ...), custom_call_target="tpu_custom_call" | custom-call | flops 201326592 | bytes 4493312 | tf_op jit(solution)/shard_map/pallas_call | solution.py:687
  19.7 1.7 %collective-permute-start.5 = (bf16[1056,128]{1,0:T(8,128)(2,1)S(1)}, bf16[1056,128]{1,0:T(8,128)(2,1)S(1)}, u32[]{:S(2)}, u32[]{:S(2)}) collective-permute-start(bf16[1056,128]{1,0:T(8,128)(2,1)S(1)} %get-tuple-element.43.refs_1_), channel_id=1, source_target_pairs={{0,8},{1,9},{2,0},{3,1},{4,12},{5,13},{6,4},{7,5},{8,16},{9,17},{1... | collective-permute-start | bytes 811016 | tf_op jit(solution)/shard_map/ppermute | solution.py:723
  21.9 1.7 %collective-permute-start.9 = (bf16[128,1024]{1,0:T(8,128)(2,1)S(1)}, bf16[128,1024]{1,0:T(8,128)(2,1)S(1)}, u32[]{:S(2)}, u32[]{:S(2)}) collective-permute-start(bf16[128,1024]{1,0:T(8,128)(2,1)S(1)} %shard_map.89), channel_id=1, source_target_pairs={{0,4},{4,0},{8,12},{12,8},{16,20},{20,16},{24,28},{28,24},{1,5},{5... | collective-permute-start | bytes 786440 | tf_op jit(solution)/shard_map/ppermute | solution.py:728
  23.6 1.3 %collective-permute-start.10 = (bf16[128,1024]{1,0:T(8,128)(2,1)S(1)}, bf16[128,1024]{1,0:T(8,128)(2,1)S(1)}, u32[]{:S(2)}, u32[]{:S(2)}) collective-permute-start(bf16[128,1024]{1,0:T(8,128)(2,1)S(1)} %shard_map.90), channel_id=1, source_target_pairs={{8,0},{12,4},{16,8},{20,12},{9,1},{13,5},{17,9},{21,13},{10,2},{14... | collective-permute-start | bytes 786440 | tf_op jit(solution)/shard_map/ppermute | solution.py:778
  25.0 1.7 %collective-permute-done.5.refs_4_ = bf16[1056,128]{1,0:T(8,128)(2,1)S(1)} collective-permute-done((bf16[1056,128]{1,0:T(8,128)(2,1)S(1)}, bf16[1056,128]{1,0:T(8,128)(2,1)S(1)}, u32[]{:S(2)}, u32[]{:S(2)}) %collective-permute-start.5) | collective-permute-done | bytes 270368 | tf_op jit(solution)/shard_map/ppermute | solution.py:723
  26.7 3.3 %collective-permute-done.4.refs_3_ = bf16[1056,128]{1,0:T(8,128)(2,1)S(1)} collective-permute-done((bf16[1056,128]{1,0:T(8,128)(2,1)S(1)}, bf16[1056,128]{1,0:T(8,128)(2,1)S(1)}, u32[]{:S(2)}, u32[]{:S(2)}) %collective-permute-start.4) | collective-permute-done | bytes 270368 | tf_op jit(solution)/shard_map/ppermute | solution.py:723
  30.1 0.5 %shard_map.88 = (bf16[1024,128]{1,0:T(8,128)(2,1)S(1)}, bf16[1024,128]{1,0:T(8,128)(2,1)S(1)}, f32[8,128]{1,0:T(8,128)S(1)}, f32[8,128]{1,0:T(8,128)S(1)}, f32[8,128]{1,0:T(8,128)S(1)}) custom-call(f32[8,128]{1,0:T(8,128)S(1)} %get-tuple-element.39.refs_0_.refs_2_, bf16[1056,128]{1,0:T(8,128)(2,1)S(1)} %get-tuple-element.43.refs_1_, ...), custom_call_target="tpu_custom_call" | custom-call | flops 524288 | bytes 2146304 | tf_op jit(solution)/shard_map/pallas_call | solution.py:687
  30.8 2.0 %collective-permute-start.6 = (f32[8,128]{1,0:T(8,128)S(1)}, f32[8,128]{1,0:T(8,128)S(1)}, u32[]{:S(2)}, u32[]{:S(2)}) collective-permute-start(f32[8,128]{1,0:T(8,128)S(1)} %get-tuple-element.47), channel_id=1, source_target_pairs={{0,2},{1,3},{2,0},{3,1},{4,6},{5,7},{6,4},{7,5},{8,10},{9,11},{10,... | collective-permute-start | bytes 12296 | tf_op jit(solution)/shard_map/ppermute | solution.py:789
  32.8 0.9 %collective-permute-done.8 = f32[8,128]{1,0:T(8,128)S(1)} collective-permute-done((f32[8,128]{1,0:T(8,128)S(1)}, f32[8,128]{1,0:T(8,128)S(1)}, u32[]{:S(2)}, u32[]{:S(2)}) %collective-permute-start.8) | collective-permute-done | bytes 4128 | tf_op jit(solution)/shard_map/ppermute | solution.py:789
  33.7 0.7 %collective-permute-done.6 = f32[8,128]{1,0:T(8,128)S(1)} collective-permute-done((f32[8,128]{1,0:T(8,128)S(1)}, f32[8,128]{1,0:T(8,128)S(1)}, u32[]{:S(2)}, u32[]{:S(2)}) %collective-permute-start.6) | collective-permute-done | bytes 4128 | tf_op jit(solution)/shard_map/ppermute | solution.py:789
  34.5 0.8 %shard_map.91 = (bf16[1088,128]{1,0:T(8,128)(2,1)S(1)}, bf16[1088,128]{1,0:T(8,128)(2,1)S(1)}, bf16[1088,128]{1,0:T(8,128)(2,1)S(1)}, bf16[1024,128]{1,0:T(8,128...) custom-call(bf16[128,1024]{1,0:T(8,128)(2,1)S(1)} %collective-permut, ...), custom_call_target="tpu_custom_call" | custom-call | tf_op jit(solution)/shard_map/pallas_call | solution.py:687
  35.2 1.7 %collective-permute-start.11 = (bf16[1088,128]{1,0:T(8,128)(2,1)S(1)}, bf16[1088,128]{1,0:T(8,128)(2,1)S(1)}, u32[]{:S(2)}, u32[]{:S(2)}) collective-permute-start(bf16[1088,128]{1,0:T(8,128)(2,1)S(1)} %get-tuple-element.63), channel_id=1, source_target_pairs={{0,8},{1,9},{2,0},{3,1},{4,12},{5,13},{6,4},{7,5},{8,16},{9,17},{1... | collective-permute-start | bytes 835592 | tf_op jit(solution)/shard_map/ppermute | solution.py:723
  37.3 2.1 %collective-permute-start.13 = (bf16[1088,128]{1,0:T(8,128)(2,1)S(1)}, bf16[1088,128]{1,0:T(8,128)(2,1)S(1)}, u32[]{:S(2)}, u32[]{:S(2)}) collective-permute-start(bf16[1088,128]{1,0:T(8,128)(2,1)S(1)} %get-tuple-element.65), channel_id=1, source_target_pairs={{0,4},{4,0},{8,12},{12,8},{16,20},{20,16},{24,28},{28,24},{1,5},{5... | collective-permute-start | bytes 835592 | tf_op jit(solution)/shard_map/ppermute | solution.py:728
  39.7 3.0 %shard_map.92 = (bf16[128,1024]{1,0:T(8,128)(2,1)}, f32[128,1024]{1,0:T(8,128)S(1)}, f32[128,1024]{1,0:T(8,128)S(1)}, f32[128,1024]{1,0:T(8,128)S(1)}) custom-call(f32[8,128]{1,0:T(8,128)S(1)} %get-tuple-element.39.refs_0_.refs_2_, f32[8,128]{1,0:T(8,128)S(1)} %add_add_fusion.refs_3_.refs_1_, bf16[128,1024]{1,0:T(8,128)(2,1)S(1)} %copy-done, ...), custom_call_target="tpu_custom_call" | custom-call | tf_op jit(solution)/shard_map/pallas_call | solution.py:687
  42.7 0.5 %collective-permute-done.11.refs_3_ = bf16[1088,128]{1,0:T(8,128)(2,1)S(1)} collective-permute-done((bf16[1088,128]{1,0:T(8,128)(2,1)S(1)}, bf16[1088,128]{1,0:T(8,128)(2,1)S(1)}, u32[]{:S(2)}, u32[]{:S(2)}) %collective-permute-start.11) | collective-permute-done | bytes 278560 | tf_op jit(solution)/shard_map/ppermute | solution.py:723
  43.2 1.4 %collective-permute-done.12.refs_4_ = bf16[1088,128]{1,0:T(8,128)(2,1)S(1)} collective-permute-done((bf16[1088,128]{1,0:T(8,128)(2,1)S(1)}, bf16[1088,128]{1,0:T(8,128)(2,1)S(1)}, u32[]{:S(2)}, u32[]{:S(2)}) %collective-permute-start.12) | collective-permute-done | bytes 278560 | tf_op jit(solution)/shard_map/ppermute | solution.py:723
  45.0 1.6 %shard_map.94 = (bf16[128,1024]{1,0:T(8,128)(2,1)}, bf16[128,1024]{1,0:T(8,128)(2,1)}, bf16[128,1024]{1,0:T(8,128)(2,1)}) custom-call(f32[2,1024,128]{2,1,0:T(8,128)S(1)} %shard_map.93.refs_0_, bf16[128,1024]{1,0:T(8,128)(2,1)S(1)} %collective-permute-done.10.refs_1_.refs_2_, bf16[128,1024]{1,0:T(8,128)(2,1)S(1)} %collective-permute-done.9.refs_0_.refs_3_.refs_2_, ...), custom_call_target="tpu_custom_call" | custom-call | flops 201326592 | bytes 5029888 | tf_op jit(solution)/shard_map/pallas_call | solution.py:687
  (26 shorter events, 2.2 us)
Async XLA Ops:
  0.6 6.4 %copy-start.2 = (bf16[128,1024]{1,0:T(8,128)(2,1)S(1)}, bf16[128,1024]{1,0:T(8,128)(2,1)}, u32[]{:S(2)}) copy-start(bf16[128,1024]{1,0:T(8,128)(2,1)} %refs_6_.1) | copy-start | bytes 786436
  0.6 4.5 %copy-start.1 = (bf16[128,1024]{1,0:T(8,128)(2,1)S(1)}, bf16[128,1024]{1,0:T(8,128)(2,1)}, u32[]{:S(2)}) copy-start(bf16[128,1024]{1,0:T(8,128)(2,1)} %refs_1_.7) | copy-start | bytes 786436
  0.7 6.5 %copy-start = (bf16[128,1024]{1,0:T(8,128)(2,1)S(1)}, bf16[128,1024]{1,0:T(8,128)(2,1)}, u32[]{:S(2)}) copy-start(bf16[128,1024]{1,0:T(8,128)(2,1)} %refs_2_.5) | copy-start | bytes 786436
  0.7 6.5 %copy-start.3 = (bf16[128,1024]{1,0:T(8,128)(2,1)S(1)}, bf16[128,1024]{1,0:T(8,128)(2,1)}, u32[]{:S(2)}) copy-start(bf16[128,1024]{1,0:T(8,128)(2,1)} %refs_5_.1) | copy-start | bytes 786436
  2.0 16.5 %collective-permute-start.1 = (bf16[256,1024]{1,0:T(8,128)(2,1)S(1)}, bf16[256,1024]{1,0:T(8,128)(2,1)S(1)}, u32[]{:S(2)}, u32[]{:S(2)}) collective-permute-start(bf16[256,1024]{1,0:T(8,128)(2,1)S(1)} %get-tuple-element.40), channel_id=1, source_target_pairs={{8,0},{9,1},{0,2},{1,3},{12,4},{13,5},{4,6},{5,7},{16,8},{17,9},{2... | collective-permute-start | bytes 1572872 | tf_op jit(solution)/shard_map/ppermute | solution.py:723
  5.0 13.5 %collective-permute-start = (bf16[256,1024]{1,0:T(8,128)(2,1)S(1)}, bf16[256,1024]{1,0:T(8,128)(2,1)S(1)}, u32[]{:S(2)}, u32[]{:S(2)}) collective-permute-start(bf16[256,1024]{1,0:T(8,128)(2,1)S(1)} %get-tuple-element.38.refs_0_), channel_id=1, source_target_pairs={{0,8},{1,9},{2,0},{3,1},{4,12},{5,13},{6,4},{7,5},{8,16},{9,17},{1... | collective-permute-start | bytes 1572872 | tf_op jit(solution)/shard_map/ppermute | solution.py:723
  5.1 9.2 %collective-permute-start.2 = (bf16[128,1024]{1,0:T(8,128)(2,1)S(1)}, bf16[128,1024]{1,0:T(8,128)(2,1)S(1)}, u32[]{:S(2)}, u32[]{:S(2)}) collective-permute-start(bf16[128,1024]{1,0:T(8,128)(2,1)S(1)} %copy-done.1), channel_id=1, source_target_pairs={{0,4},{4,0},{8,12},{12,8},{16,20},{20,16},{24,28},{28,24},{1,5},{5... | collective-permute-start | bytes 786440 | tf_op jit(solution)/shard_map/ppermute | solution.py:728
  7.0 11.5 %collective-permute-start.3 = (bf16[128,1024]{1,0:T(8,128)(2,1)S(1)}, bf16[128,1024]{1,0:T(8,128)(2,1)S(1)}, u32[]{:S(2)}, u32[]{:S(2)}) collective-permute-start(bf16[128,1024]{1,0:T(8,128)(2,1)S(1)} %copy-done.2), channel_id=1, source_target_pairs={{0,4},{4,0},{8,12},{12,8},{16,20},{20,16},{24,28},{28,24},{1,5},{5... | collective-permute-start | bytes 786440 | tf_op jit(solution)/shard_map/ppermute | solution.py:728
  7.2 0.7 %copy-start.4 = (s32[8,8]{1,0:T(8,128)S(1)}, s32[8,8]{1,0:T(8,128)}, u32[]{:S(2)}) copy-start(s32[8,8]{1,0:T(8,128)} %refs_1_.5) | copy-start | bytes 772
  19.7 7.1 %collective-permute-start.5 = (bf16[1056,128]{1,0:T(8,128)(2,1)S(1)}, bf16[1056,128]{1,0:T(8,128)(2,1)S(1)}, u32[]{:S(2)}, u32[]{:S(2)}) collective-permute-start(bf16[1056,128]{1,0:T(8,128)(2,1)S(1)} %get-tuple-element.43.refs_1_), channel_id=1, source_target_pairs={{0,8},{1,9},{2,0},{3,1},{4,12},{5,13},{6,4},{7,5},{8,16},{9,17},{1... | collective-permute-start | bytes 811016 | tf_op jit(solution)/shard_map/ppermute | solution.py:723
  21.4 8.7 %collective-permute-start.4 = (bf16[1056,128]{1,0:T(8,128)(2,1)S(1)}, bf16[1056,128]{1,0:T(8,128)(2,1)S(1)}, u32[]{:S(2)}, u32[]{:S(2)}) collective-permute-start(bf16[1056,128]{1,0:T(8,128)(2,1)S(1)} %get-tuple-element.44.refs_2_), channel_id=1, source_target_pairs={{8,0},{9,1},{0,2},{1,3},{12,4},{13,5},{4,6},{5,7},{16,8},{17,9},{2... | collective-permute-start | bytes 811016 | tf_op jit(solution)/shard_map/ppermute | solution.py:723
  21.9 12.6 %collective-permute-start.9 = (bf16[128,1024]{1,0:T(8,128)(2,1)S(1)}, bf16[128,1024]{1,0:T(8,128)(2,1)S(1)}, u32[]{:S(2)}, u32[]{:S(2)}) collective-permute-start(bf16[128,1024]{1,0:T(8,128)(2,1)S(1)} %shard_map.89), channel_id=1, source_target_pairs={{0,4},{4,0},{8,12},{12,8},{16,20},{20,16},{24,28},{28,24},{1,5},{5... | collective-permute-start | bytes 786440 | tf_op jit(solution)/shard_map/ppermute | solution.py:728
  23.6 10.9 %collective-permute-start.10 = (bf16[128,1024]{1,0:T(8,128)(2,1)S(1)}, bf16[128,1024]{1,0:T(8,128)(2,1)S(1)}, u32[]{:S(2)}, u32[]{:S(2)}) collective-permute-start(bf16[128,1024]{1,0:T(8,128)(2,1)S(1)} %shard_map.90), channel_id=1, source_target_pairs={{8,0},{12,4},{16,8},{20,12},{9,1},{13,5},{17,9},{21,13},{10,2},{14... | collective-permute-start | bytes 786440 | tf_op jit(solution)/shard_map/ppermute | solution.py:778
  30.6 3.1 %collective-permute-start.8 = (f32[8,128]{1,0:T(8,128)S(1)}, f32[8,128]{1,0:T(8,128)S(1)}, u32[]{:S(2)}, u32[]{:S(2)}) collective-permute-start(f32[8,128]{1,0:T(8,128)S(1)} %get-tuple-element.47), channel_id=1, source_target_pairs={{0,3},{1,2},{2,1},{3,0},{4,7},{5,6},{6,5},{7,4},{8,11},{9,10},{10,... | collective-permute-start | bytes 12296 | tf_op jit(solution)/shard_map/ppermute | solution.py:789
  30.7 3.0 %collective-permute-start.7 = (f32[8,128]{1,0:T(8,128)S(1)}, f32[8,128]{1,0:T(8,128)S(1)}, u32[]{:S(2)}, u32[]{:S(2)}) collective-permute-start(f32[8,128]{1,0:T(8,128)S(1)} %get-tuple-element.47), channel_id=1, source_target_pairs={{0,1},{1,0},{2,3},{3,2},{4,5},{5,4},{6,7},{7,6},{8,9},{9,8},{10,11... | collective-permute-start | bytes 12296 | tf_op jit(solution)/shard_map/ppermute | solution.py:789
  30.8 3.7 %collective-permute-start.6 = (f32[8,128]{1,0:T(8,128)S(1)}, f32[8,128]{1,0:T(8,128)S(1)}, u32[]{:S(2)}, u32[]{:S(2)}) collective-permute-start(f32[8,128]{1,0:T(8,128)S(1)} %get-tuple-element.47), channel_id=1, source_target_pairs={{0,2},{1,3},{2,0},{3,1},{4,6},{5,7},{6,4},{7,5},{8,10},{9,11},{10,... | collective-permute-start | bytes 12296 | tf_op jit(solution)/shard_map/ppermute | solution.py:789
  35.2 8.0 %collective-permute-start.11 = (bf16[1088,128]{1,0:T(8,128)(2,1)S(1)}, bf16[1088,128]{1,0:T(8,128)(2,1)S(1)}, u32[]{:S(2)}, u32[]{:S(2)}) collective-permute-start(bf16[1088,128]{1,0:T(8,128)(2,1)S(1)} %get-tuple-element.63), channel_id=1, source_target_pairs={{0,8},{1,9},{2,0},{3,1},{4,12},{5,13},{6,4},{7,5},{8,16},{9,17},{1... | collective-permute-start | bytes 835592 | tf_op jit(solution)/shard_map/ppermute | solution.py:723
  36.9 7.7 %collective-permute-start.12 = (bf16[1088,128]{1,0:T(8,128)(2,1)S(1)}, bf16[1088,128]{1,0:T(8,128)(2,1)S(1)}, u32[]{:S(2)}, u32[]{:S(2)}) collective-permute-start(bf16[1088,128]{1,0:T(8,128)(2,1)S(1)} %get-tuple-element.64), channel_id=1, source_target_pairs={{8,0},{9,1},{0,2},{1,3},{12,4},{13,5},{4,6},{5,7},{16,8},{17,9},{2... | collective-permute-start | bytes 835592 | tf_op jit(solution)/shard_map/ppermute | solution.py:723
  37.3 7.7 %collective-permute-start.13 = (bf16[1088,128]{1,0:T(8,128)(2,1)S(1)}, bf16[1088,128]{1,0:T(8,128)(2,1)S(1)}, u32[]{:S(2)}, u32[]{:S(2)}) collective-permute-start(bf16[1088,128]{1,0:T(8,128)(2,1)S(1)} %get-tuple-element.65), channel_id=1, source_target_pairs={{0,4},{4,0},{8,12},{12,8},{16,20},{20,16},{24,28},{28,24},{1,5},{5... | collective-permute-start | bytes 835592 | tf_op jit(solution)/shard_map/ppermute | solution.py:728

commit v13 on v11

--- a/solution.py
+++ b/solution.py
@@ -645,9 +645,13 @@
     dq_own_ref,
     dk_own_ref,
     dv_own_ref,
+    dq_out,
+    dk_out,
+    dv_out,
     dq_ref,
     dk_ref,
     dv_ref,
+    sems,
 ):
     place = Place()
     half = place.half
@@ -659,13 +663,19 @@
         for part in (first, second)
     )
     group = range(heads)
-    grads, products, tiles = [], [], []
+    grads, products, tiles, copies = [], [], [], []
+
+    def leave(stage, out, columns):
+        copies.append(pltpu.make_async_copy(stage.at[:, columns], out.at[:, columns], sems.at[len(copies)]))
+        copies[-1].start()
+
     for h in group:
         at = rows_of(h)
         up, down = up_ref[at], down_ref[at]
         dqz = jnp.where(half, down, up).T.astype(jnp.float32) * behind
         dq_ref[:, at] = (dq_own_ref[:, at] + dqz).astype(jnp.bfloat16)
         grads.append(jnp.concatenate([jnp.where(half, up, down), side_ref[at]], axis=1))
+    leave(dq_ref, dq_out, slice(0, heads * HD))
     for h, grad in zip(group, grads):
         products.append(mm(v_ref[:, rows_of(h)], grad, NN))
     for h, product in zip(group, products):
@@ -680,9 +690,15 @@
         queries = jnp.concatenate([far_ref[:, at], sideq_ref[:, at]], axis=0)
         dk_ref[:, at] = (dk_own_ref[:, at] + mm(scores, queries, NN)).astype(jnp.bfloat16)
         dv_ref[:, at] = (dv_own_ref[:, at] + mm(probs, grad, NT)).astype(jnp.bfloat16)
-
-
-def call(kernel, heads, flags, arrays, outs, flops, space=pltpu.VMEM, scratch=(), after=()):
+        if h % (heads // 2) == heads // 2 - 1:
+            columns = slice((h + 1 - heads // 2) * HD, (h + 1) * HD)
+            leave(dk_ref, dk_out, columns)
+            leave(dv_ref, dv_out, columns)
+    for copy in copies:
+        copy.wait()
+
+
+def call(kernel, heads, flags, arrays, outs, flops, space=pltpu.VMEM, scratch=(), after=(), out_space=pltpu.VMEM):
     moved = sum(math.prod(a.shape) * a.dtype.itemsize for a in (*arrays, *outs)) if flops else 0
     return pl.pallas_call(
         lambda *refs: kernel(heads, *refs[len(after) :]),
@@ -690,7 +706,7 @@
         in_specs=[pl.BlockSpec(memory_space=pl.ANY)] * len(after)
         + [pl.BlockSpec(memory_space=pltpu.SMEM)] * len(flags)
         + [pl.BlockSpec(memory_space=space)] * len(arrays),
-        out_specs=[pl.BlockSpec(memory_space=pltpu.VMEM)] * len(outs),
+        out_specs=[pl.BlockSpec(memory_space=out_space)] * len(outs),
         scratch_shapes=scratch,
         compiler_params=pltpu.CompilerParams(vmem_limit_bytes=24 * 2**20),
         cost_estimate=pl.CostEstimate(flops=flops, bytes_accessed=moved, transcendentals=0),
@@ -826,6 +842,8 @@
         (key_scores, far_queries, side_queries, *returned, side_grads, values, dq_own, dk_own, dv_own),
         (flat, flat, flat),
         6 * unit,
+        scratch=(pltpu.VMEM((tokens, width), jnp.bfloat16),) * 3 + (pltpu.SemaphoreType.DMA((5,)),),
+        out_space=pltpu.HBM,
     )
     return (normed, grad_queries, grad_keys, grad_values)
 

time: 46.8 us -> 46.8 us (level)
  no operation moved by 1% of the time
where the time goes in v13:
time: 46.8 us; the launch traced here: 46.6 us
  waiting for transfers between devices  17.6 us (38%)
  starting transfers between devices  16.2 us (35%)
  Pallas kernels  11.3 us (24%)
  between operations  0.76 us (2%)
  local copies, waits for them, and re-layouts  0.7 us (1%)
    pallas_call x11, Pallas kernels, call(): pl.pallas_call(lambda *refs: kernel(heads, *refs[len(after):]), out_shape...  11.3 us
    ppermute x4, waiting for transfers between devices, swap(): return lax.ppermute(array, 'ctx', [(i, i ^ 1) for i in range(blocks)])  8.3 us
    ppermute x3, waiting for transfers between devices, cycle(): lax.ppermute(down_array, ('ctx', 'head'), falling)  5.43 us
    ppermute x4, starting transfers between devices, swap(): return lax.ppermute(array, 'ctx', [(i, i ^ 1) for i in range(blocks)])  5.05 us
    ppermute x3, starting transfers between devices, cycle(): lax.ppermute(down_array, ('ctx', 'head'), falling)  4.71 us
    ppermute x3, starting transfers between devices, cycle(): lax.ppermute(up_array, ('ctx', 'head'), rising)  3.21 us
    ppermute x3, waiting for transfers between devices, cycle(): lax.ppermute(up_array, ('ctx', 'head'), rising)  2.02 us
    ppermute x3, starting transfers between devices, meeting_shards(): lax.ppermute(sums, 'head', [(i, i ^ step) for i in range(members)])  1.92 us
  transfers between devices with their start and end apart: 14, of which 7 were waited for; matrix products, arithmetic and copies ran while one was open for 0% of the time, Pallas kernels for 16%

profile of v13, /device:TPU:0, one launch (start us, length us, event | category | flops | bytes accessed | tf_op | source)
XLA Modules:
  0.0 46.6 jit_solution(18386337977272739321)
XLA Ops:
  0.7 1.3 %shard_map.84 = (bf16[256,1024]{1,0:T(8,128)(2,1)S(1)}, bf16[256,1024]{1,0:T(8,128)(2,1)S(1)}) custom-call(bf16[128,1024]{1,0:T(8,128)(2,1)} %refs_2_.5, bf16[128,1024]{1,0:T(8,128)(2,1)} %refs_1_.7, bf16[128,1024]{1,0:T(8,128)(2,1)} %refs_6_.1, bf16[128,1024]{1,0:T(8,128)(2,1)} %refs_5_.1), custom_call_target="tpu_custom_call" | custom-call | tf_op jit(solution)/shard_map/pallas_call | solution.py:703
  2.0 3.0 %collective-permute-start.1 = (bf16[256,1024]{1,0:T(8,128)(2,1)S(1)}, bf16[256,1024]{1,0:T(8,128)(2,1)S(1)}, u32[]{:S(2)}, u32[]{:S(2)}) collective-permute-start(bf16[256,1024]{1,0:T(8,128)(2,1)S(1)} %get-tuple-element.41), channel_id=1, source_target_pairs={{8,0},{9,1},{0,2},{1,3},{12,4},{13,5},{4,6},{5,7},{16,8},{17,9},{2... | collective-permute-start | bytes 1572872 | tf_op jit(solution)/shard_map/ppermute | solution.py:739
  5.1 1.9 %collective-permute-start.2 = (bf16[128,1024]{1,0:T(8,128)(2,1)S(1)}, bf16[128,1024]{1,0:T(8,128)(2,1)S(1)}, u32[]{:S(2)}, u32[]{:S(2)}) collective-permute-start(bf16[128,1024]{1,0:T(8,128)(2,1)S(1)} %copy-done.1), channel_id=1, source_target_pairs={{0,4},{4,0},{8,12},{12,8},{16,20},{20,16},{24,28},{28,24},{1,5},{5... | collective-permute-start | bytes 786440 | tf_op jit(solution)/shard_map/ppermute | solution.py:744
  7.2 0.7 %copy-done.4 = s32[8,8]{1,0:T(8,128)S(1)} copy-done((s32[8,8]{1,0:T(8,128)S(1)}, s32[8,8]{1,0:T(8,128)}, u32[]{:S(2)}) %copy-start.4) | copy-done | bytes 280
  7.9 2.4 %shard_map.85 = (f32[1024,128]{1,0:T(8,128)S(1)}, f32[8,128]{1,0:T(8,128)S(1)}, bf16[1024,128]{1,0:T(8,128)(2,1)S(1)}, f32[8,128]{1,0:T(8,128)S(1)}) custom-call(bf16[256,1024]{1,0:T(8,128)(2,1)S(1)} %get-tuple-element.39.refs_0_, s32[8,8]{1,0:T(8,128)S(1)} %copy-done.4, bf16[128,1024]{1,0:T(8,128)(2,1)S(1)} %copy-done, bf16[128,1024]{1,0:T(8,128)(2,1)S(1)} %copy-done.1, ...), custom_call_target="tpu_custom_call" | custom-call | flops 100663296 | bytes 1843200 | tf_op jit(solution)/shard_map/pallas_call | solution.py:703
  10.2 4.1 %collective-permute-done.2.refs_4_.refs_11_.refs_15_ = bf16[128,1024]{1,0:T(8,128)(2,1)S(1)} collective-permute-done((bf16[128,1024]{1,0:T(8,128)(2,1)S(1)}, bf16[128,1024]{1,0:T(8,128)(2,1)S(1)}, u32[]{:S(2)}, u32[]{:S(2)}) %collective-permute-start.2) | collective-permute-done | bytes 262176 | tf_op jit(solution)/shard_map/ppermute | solution.py:744
  14.4 4.2 %collective-permute-done.3.refs_5_.refs_12_ = bf16[128,1024]{1,0:T(8,128)(2,1)S(1)} collective-permute-done((bf16[128,1024]{1,0:T(8,128)(2,1)S(1)}, bf16[128,1024]{1,0:T(8,128)(2,1)S(1)}, u32[]{:S(2)}, u32[]{:S(2)}) %collective-permute-start.3) | collective-permute-done | bytes 262176 | tf_op jit(solution)/shard_map/ppermute | solution.py:744
  18.5 1.1 %shard_map.86 = (bf16[1056,128]{1,0:T(8,128)(2,1)S(1)}, bf16[1056,128]{1,0:T(8,128)(2,1)S(1)}, f32[1024,128]{1,0:T(8,128)S(1)}, f32[1024,128]{1,0:T(8,128)S(1)},...) custom-call(f32[8,128]{1,0:T(8,128)S(1)} %get-tuple-element.40.refs_0_.refs_1_, ...), custom_call_target="tpu_custom_call" | custom-call | flops 201326592 | bytes 4493312 | tf_op jit(solution)/shard_map/pallas_call | solution.py:703
  19.7 1.7 %collective-permute-start.5 = (bf16[1056,128]{1,0:T(8,128)(2,1)S(1)}, bf16[1056,128]{1,0:T(8,128)(2,1)S(1)}, u32[]{:S(2)}, u32[]{:S(2)}) collective-permute-start(bf16[1056,128]{1,0:T(8,128)(2,1)S(1)} %get-tuple-element.45.refs_2_), channel_id=1, source_target_pairs={{8,0},{9,1},{0,2},{1,3},{12,4},{13,5},{4,6},{5,7},{16,8},{17,9},{2... | collective-permute-start | bytes 811016 | tf_op jit(solution)/shard_map/ppermute | solution.py:739
  21.3 0.4 collective-permute-start.4
  21.9 1.7 %collective-permute-start.9 = (bf16[128,1024]{1,0:T(8,128)(2,1)S(1)}, bf16[128,1024]{1,0:T(8,128)(2,1)S(1)}, u32[]{:S(2)}, u32[]{:S(2)}) collective-permute-start(bf16[128,1024]{1,0:T(8,128)(2,1)S(1)} %shard_map.89), channel_id=1, source_target_pairs={{0,4},{4,0},{8,12},{12,8},{16,20},{20,16},{24,28},{28,24},{1,5},{5... | collective-permute-start | bytes 786440 | tf_op jit(solution)/shard_map/ppermute | solution.py:744
  23.5 3.2 %collective-permute-done.5.refs_4_.refs_0_ = bf16[1056,128]{1,0:T(8,128)(2,1)S(1)} collective-permute-done((bf16[1056,128]{1,0:T(8,128)(2,1)S(1)}, bf16[1056,128]{1,0:T(8,128)(2,1)S(1)}, u32[]{:S(2)}, u32[]{:S(2)}) %collective-permute-start.5) | collective-permute-done | bytes 270368 | tf_op jit(solution)/shard_map/ppermute | solution.py:739
  26.8 1.3 %collective-permute-start.10 = (bf16[128,1024]{1,0:T(8,128)(2,1)S(1)}, bf16[128,1024]{1,0:T(8,128)(2,1)S(1)}, u32[]{:S(2)}, u32[]{:S(2)}) collective-permute-start(bf16[128,1024]{1,0:T(8,128)(2,1)S(1)} %shard_map.92), channel_id=1, source_target_pairs={{8,0},{12,4},{16,8},{20,12},{9,1},{13,5},{17,9},{21,13},{10,2},{14... | collective-permute-start | bytes 786440 | tf_op jit(solution)/shard_map/ppermute | solution.py:794
  28.3 0.5 %shard_map.88 = (bf16[1024,128]{1,0:T(8,128)(2,1)S(1)}, bf16[1024,128]{1,0:T(8,128)(2,1)S(1)}, f32[8,128]{1,0:T(8,128)S(1)}, f32[8,128]{1,0:T(8,128)S(1)}, f32[8,128]{1,0:T(8,128)S(1)}) custom-call(f32[8,128]{1,0:T(8,128)S(1)} %get-tuple-element.40.refs_0_.refs_1_, bf16[1056,128]{1,0:T(8,128)(2,1)S(1)} %get-tuple-element.44.refs_1_, ...), custom_call_target="tpu_custom_call" | custom-call | flops 524288 | bytes 2146304 | tf_op jit(solution)/shard_map/pallas_call | solution.py:703
  28.9 1.5 %collective-permute-start.7 = (f32[8,128]{1,0:T(8,128)S(1)}, f32[8,128]{1,0:T(8,128)S(1)}, u32[]{:S(2)}, u32[]{:S(2)}) collective-permute-start(f32[8,128]{1,0:T(8,128)S(1)} %get-tuple-element.48), channel_id=1, source_target_pairs={{0,2},{1,3},{2,0},{3,1},{4,6},{5,7},{6,4},{7,5},{8,10},{9,11},{10,... | collective-permute-start | bytes 12296 | tf_op jit(solution)/shard_map/ppermute | solution.py:805
  30.7 1.2 %collective-permute-done.8 = f32[8,128]{1,0:T(8,128)S(1)} collective-permute-done((f32[8,128]{1,0:T(8,128)S(1)}, f32[8,128]{1,0:T(8,128)S(1)}, u32[]{:S(2)}, u32[]{:S(2)}) %collective-permute-start.8) | collective-permute-done | bytes 4128 | tf_op jit(solution)/shard_map/ppermute | solution.py:805
  31.9 0.6 %collective-permute-done.7 = f32[8,128]{1,0:T(8,128)S(1)} collective-permute-done((f32[8,128]{1,0:T(8,128)S(1)}, f32[8,128]{1,0:T(8,128)S(1)}, u32[]{:S(2)}, u32[]{:S(2)}) %collective-permute-start.7) | collective-permute-done | bytes 4128 | tf_op jit(solution)/shard_map/ppermute | solution.py:805
  32.6 0.8 %shard_map.90 = (bf16[1088,128]{1,0:T(8,128)(2,1)S(1)}, bf16[1088,128]{1,0:T(8,128)(2,1)S(1)}, bf16[1088,128]{1,0:T(8,128)(2,1)S(1)}, bf16[1024,128]{1,0:T(8,128...) custom-call(bf16[128,1024]{1,0:T(8,128)(2,1)S(1)} %collective-permut, ...), custom_call_target="tpu_custom_call" | custom-call | tf_op jit(solution)/shard_map/pallas_call | solution.py:703
  33.3 2.7 %collective-permute-start.11 = (bf16[1088,128]{1,0:T(8,128)(2,1)S(1)}, bf16[1088,128]{1,0:T(8,128)(2,1)S(1)}, u32[]{:S(2)}, u32[]{:S(2)}) collective-permute-start(bf16[1088,128]{1,0:T(8,128)(2,1)S(1)} %get-tuple-element.64), channel_id=1, source_target_pairs={{0,8},{1,9},{2,0},{3,1},{4,12},{5,13},{6,4},{7,5},{8,16},{9,17},{1... | collective-permute-start | bytes 835592 | tf_op jit(solution)/shard_map/ppermute | solution.py:739
  36.0 1.4 %collective-permute-start.13 = (bf16[1088,128]{1,0:T(8,128)(2,1)S(1)}, bf16[1088,128]{1,0:T(8,128)(2,1)S(1)}, u32[]{:S(2)}, u32[]{:S(2)}) collective-permute-start(bf16[1088,128]{1,0:T(8,128)(2,1)S(1)} %get-tuple-element.67), channel_id=1, source_target_pairs={{0,4},{4,0},{8,12},{12,8},{16,20},{20,16},{24,28},{28,24},{1,5},{5... | collective-permute-start | bytes 835592 | tf_op jit(solution)/shard_map/ppermute | solution.py:744
  37.4 3.0 %shard_map.91 = (bf16[128,1024]{1,0:T(8,128)(2,1)}, f32[128,1024]{1,0:T(8,128)S(1)}, f32[128,1024]{1,0:T(8,128)S(1)}, f32[128,1024]{1,0:T(8,128)S(1)}) custom-call(f32[8,128]{1,0:T(8,128)S(1)} %get-tuple-element.40.refs_0_.refs_1_, f32[8,128]{1,0:T(8,128)S(1)} %add_add_fusion.refs_2_.refs_1_, bf16[128,1024]{1,0:T(8,128)(2,1)S(1)} %copy-done, ...), custom_call_target="tpu_custom_call" | custom-call | tf_op jit(solution)/shard_map/pallas_call | solution.py:703
  40.7 2.0 %collective-permute-done.11.refs_3_ = bf16[1088,128]{1,0:T(8,128)(2,1)S(1)} collective-permute-done((bf16[1088,128]{1,0:T(8,128)(2,1)S(1)}, bf16[1088,128]{1,0:T(8,128)(2,1)S(1)}, u32[]{:S(2)}, u32[]{:S(2)}) %collective-permute-start.11) | collective-permute-done | bytes 278560 | tf_op jit(solution)/shard_map/ppermute | solution.py:739
  42.7 2.2 %collective-permute-done.12.refs_4_ = bf16[1088,128]{1,0:T(8,128)(2,1)S(1)} collective-permute-done((bf16[1088,128]{1,0:T(8,128)(2,1)S(1)}, bf16[1088,128]{1,0:T(8,128)(2,1)S(1)}, u32[]{:S(2)}, u32[]{:S(2)}) %collective-permute-start.12) | collective-permute-done | bytes 278560 | tf_op jit(solution)/shard_map/ppermute | solution.py:739
  45.0 1.6 %shard_map.94 = (bf16[128,1024]{1,0:T(8,128)(2,1)}, bf16[128,1024]{1,0:T(8,128)(2,1)}, bf16[128,1024]{1,0:T(8,128)(2,1)}) custom-call(f32[2,1024,128]{2,1,0:T(8,128)S(1)} %shard_map.93.refs_0_, bf16[128,1024]{1,0:T(8,128)(2,1)S(1)} %collective-permute-done.10.refs_2_.refs_1_, bf16[128,1024]{1,0:T(8,128)(2,1)S(1)} %collective-permute-done.9.refs_0_.refs_3_.refs_2_, ...), custom_call_target="tpu_custom_call" | custom-call | flops 201326592 | bytes 5029888 | tf_op jit(solution)/shard_map/pallas_call | solution.py:703
  (26 shorter events, 1.3 us)
Async XLA Ops:
  0.6 6.4 %copy-start.2 = (bf16[128,1024]{1,0:T(8,128)(2,1)S(1)}, bf16[128,1024]{1,0:T(8,128)(2,1)}, u32[]{:S(2)}) copy-start(bf16[128,1024]{1,0:T(8,128)(2,1)} %refs_6_.1) | copy-start | bytes 786436
  0.6 4.5 %copy-start.1 = (bf16[128,1024]{1,0:T(8,128)(2,1)S(1)}, bf16[128,1024]{1,0:T(8,128)(2,1)}, u32[]{:S(2)}) copy-start(bf16[128,1024]{1,0:T(8,128)(2,1)} %refs_1_.7) | copy-start | bytes 786436
  0.7 6.5 %copy-start = (bf16[128,1024]{1,0:T(8,128)(2,1)S(1)}, bf16[128,1024]{1,0:T(8,128)(2,1)}, u32[]{:S(2)}) copy-start(bf16[128,1024]{1,0:T(8,128)(2,1)} %refs_2_.5) | copy-start | bytes 786436
  0.7 6.5 %copy-start.3 = (bf16[128,1024]{1,0:T(8,128)(2,1)S(1)}, bf16[128,1024]{1,0:T(8,128)(2,1)}, u32[]{:S(2)}) copy-start(bf16[128,1024]{1,0:T(8,128)(2,1)} %refs_5_.1) | copy-start | bytes 786436
  2.0 16.5 %collective-permute-start.1 = (bf16[256,1024]{1,0:T(8,128)(2,1)S(1)}, bf16[256,1024]{1,0:T(8,128)(2,1)S(1)}, u32[]{:S(2)}, u32[]{:S(2)}) collective-permute-start(bf16[256,1024]{1,0:T(8,128)(2,1)S(1)} %get-tuple-element.41), channel_id=1, source_target_pairs={{8,0},{9,1},{0,2},{1,3},{12,4},{13,5},{4,6},{5,7},{16,8},{17,9},{2... | collective-permute-start | bytes 1572872 | tf_op jit(solution)/shard_map/ppermute | solution.py:739
  5.0 13.5 %collective-permute-start = (bf16[256,1024]{1,0:T(8,128)(2,1)S(1)}, bf16[256,1024]{1,0:T(8,128)(2,1)S(1)}, u32[]{:S(2)}, u32[]{:S(2)}) collective-permute-start(bf16[256,1024]{1,0:T(8,128)(2,1)S(1)} %get-tuple-element.39.refs_0_), channel_id=1, source_target_pairs={{0,8},{1,9},{2,0},{3,1},{4,12},{5,13},{6,4},{7,5},{8,16},{9,17},{1... | collective-permute-start | bytes 1572872 | tf_op jit(solution)/shard_map/ppermute | solution.py:739
  5.1 9.2 %collective-permute-start.2 = (bf16[128,1024]{1,0:T(8,128)(2,1)S(1)}, bf16[128,1024]{1,0:T(8,128)(2,1)S(1)}, u32[]{:S(2)}, u32[]{:S(2)}) collective-permute-start(bf16[128,1024]{1,0:T(8,128)(2,1)S(1)} %copy-done.1), channel_id=1, source_target_pairs={{0,4},{4,0},{8,12},{12,8},{16,20},{20,16},{24,28},{28,24},{1,5},{5... | collective-permute-start | bytes 786440 | tf_op jit(solution)/shard_map/ppermute | solution.py:744
  7.0 11.5 %collective-permute-start.3 = (bf16[128,1024]{1,0:T(8,128)(2,1)S(1)}, bf16[128,1024]{1,0:T(8,128)(2,1)S(1)}, u32[]{:S(2)}, u32[]{:S(2)}) collective-permute-start(bf16[128,1024]{1,0:T(8,128)(2,1)S(1)} %copy-done.2), channel_id=1, source_target_pairs={{0,4},{4,0},{8,12},{12,8},{16,20},{20,16},{24,28},{28,24},{1,5},{5... | collective-permute-start | bytes 786440 | tf_op jit(solution)/shard_map/ppermute | solution.py:744
  7.2 0.7 %copy-start.4 = (s32[8,8]{1,0:T(8,128)S(1)}, s32[8,8]{1,0:T(8,128)}, u32[]{:S(2)}) copy-start(s32[8,8]{1,0:T(8,128)} %refs_1_.5) | copy-start | bytes 772
  19.7 7.1 %collective-permute-start.5 = (bf16[1056,128]{1,0:T(8,128)(2,1)S(1)}, bf16[1056,128]{1,0:T(8,128)(2,1)S(1)}, u32[]{:S(2)}, u32[]{:S(2)}) collective-permute-start(bf16[1056,128]{1,0:T(8,128)(2,1)S(1)} %get-tuple-element.45.refs_2_), channel_id=1, source_target_pairs={{8,0},{9,1},{0,2},{1,3},{12,4},{13,5},{4,6},{5,7},{16,8},{17,9},{2... | collective-permute-start | bytes 811016 | tf_op jit(solution)/shard_map/ppermute | solution.py:739
  21.3 6.9 %collective-permute-start.4 = (bf16[1056,128]{1,0:T(8,128)(2,1)S(1)}, bf16[1056,128]{1,0:T(8,128)(2,1)S(1)}, u32[]{:S(2)}, u32[]{:S(2)}) collective-permute-start(bf16[1056,128]{1,0:T(8,128)(2,1)S(1)} %get-tuple-element.44.refs_1_), channel_id=1, source_target_pairs={{0,8},{1,9},{2,0},{3,1},{4,12},{5,13},{6,4},{7,5},{8,16},{9,17},{1... | collective-permute-start | bytes 811016 | tf_op jit(solution)/shard_map/ppermute | solution.py:739
  21.9 10.7 %collective-permute-start.9 = (bf16[128,1024]{1,0:T(8,128)(2,1)S(1)}, bf16[128,1024]{1,0:T(8,128)(2,1)S(1)}, u32[]{:S(2)}, u32[]{:S(2)}) collective-permute-start(bf16[128,1024]{1,0:T(8,128)(2,1)S(1)} %shard_map.89), channel_id=1, source_target_pairs={{0,4},{4,0},{8,12},{12,8},{16,20},{20,16},{24,28},{28,24},{1,5},{5... | collective-permute-start | bytes 786440 | tf_op jit(solution)/shard_map/ppermute | solution.py:744
  26.8 9.2 %collective-permute-start.10 = (bf16[128,1024]{1,0:T(8,128)(2,1)S(1)}, bf16[128,1024]{1,0:T(8,128)(2,1)S(1)}, u32[]{:S(2)}, u32[]{:S(2)}) collective-permute-start(bf16[128,1024]{1,0:T(8,128)(2,1)S(1)} %shard_map.92), channel_id=1, source_target_pairs={{8,0},{12,4},{16,8},{20,12},{9,1},{13,5},{17,9},{21,13},{10,2},{14... | collective-permute-start | bytes 786440 | tf_op jit(solution)/shard_map/ppermute | solution.py:794
  28.8 3.1 %collective-permute-start.8 = (f32[8,128]{1,0:T(8,128)S(1)}, f32[8,128]{1,0:T(8,128)S(1)}, u32[]{:S(2)}, u32[]{:S(2)}) collective-permute-start(f32[8,128]{1,0:T(8,128)S(1)} %get-tuple-element.48), channel_id=1, source_target_pairs={{0,3},{1,2},{2,1},{3,0},{4,7},{5,6},{6,5},{7,4},{8,11},{9,10},{10,... | collective-permute-start | bytes 12296 | tf_op jit(solution)/shard_map/ppermute | solution.py:805
  28.9 3.7 %collective-permute-start.7 = (f32[8,128]{1,0:T(8,128)S(1)}, f32[8,128]{1,0:T(8,128)S(1)}, u32[]{:S(2)}, u32[]{:S(2)}) collective-permute-start(f32[8,128]{1,0:T(8,128)S(1)} %get-tuple-element.48), channel_id=1, source_target_pairs={{0,2},{1,3},{2,0},{3,1},{4,6},{5,7},{6,4},{7,5},{8,10},{9,11},{10,... | collective-permute-start | bytes 12296 | tf_op jit(solution)/shard_map/ppermute | solution.py:805
  30.4 2.2 %collective-permute-start.6 = (f32[8,128]{1,0:T(8,128)S(1)}, f32[8,128]{1,0:T(8,128)S(1)}, u32[]{:S(2)}, u32[]{:S(2)}) collective-permute-start(f32[8,128]{1,0:T(8,128)S(1)} %get-tuple-element.48), channel_id=1, source_target_pairs={{0,1},{1,0},{2,3},{3,2},{4,5},{5,4},{6,7},{7,6},{8,9},{9,8},{10,11... | collective-permute-start | bytes 12296 | tf_op jit(solution)/shard_map/ppermute | solution.py:805
  33.3 9.4 %collective-permute-start.11 = (bf16[1088,128]{1,0:T(8,128)(2,1)S(1)}, bf16[1088,128]{1,0:T(8,128)(2,1)S(1)}, u32[]{:S(2)}, u32[]{:S(2)}) collective-permute-start(bf16[1088,128]{1,0:T(8,128)(2,1)S(1)} %get-tuple-element.64), channel_id=1, source_target_pairs={{0,8},{1,9},{2,0},{3,1},{4,12},{5,13},{6,4},{7,5},{8,16},{9,17},{1... | collective-permute-start | bytes 835592 | tf_op jit(solution)/shard_map/ppermute | solution.py:739
  36.0 8.9 %collective-permute-start.12 = (bf16[1088,128]{1,0:T(8,128)(2,1)S(1)}, bf16[1088,128]{1,0:T(8,128)(2,1)S(1)}, u32[]{:S(2)}, u32[]{:S(2)}) collective-permute-start(bf16[1088,128]{1,0:T(8,128)(2,1)S(1)} %get-tuple-element.65), channel_id=1, source_target_pairs={{8,0},{9,1},{0,2},{1,3},{12,4},{13,5},{4,6},{5,7},{16,8},{17,9},{2... | collective-permute-start | bytes 835592 | tf_op jit(solution)/shard_map/ppermute | solution.py:739
  36.0 8.9 %collective-permute-start.13 = (bf16[1088,128]{1,0:T(8,128)(2,1)S(1)}, bf16[1088,128]{1,0:T(8,128)(2,1)S(1)}, u32[]{:S(2)}, u32[]{:S(2)}) collective-permute-start(bf16[1088,128]{1,0:T(8,128)(2,1)S(1)} %get-tuple-element.67), channel_id=1, source_target_pairs={{0,4},{4,0},{8,12},{12,8},{16,20},{20,16},{24,28},{28,24},{1,5},{5... | collective-permute-start | bytes 835592 | tf_op jit(solution)/shard_map/ppermute | solution.py:744
